TPU v7x, 32 devices: a whole 2x2x4 slice. The times are simulated.
32 devices in a mesh: fsdp: 8 (over y, x, core), seq: 4 (over z).
Axes of the slice: x: 2, y: 2, z: 4, core: 2. Of those that a mesh axis runs over, the one named last changes fastest.
Arguments:
- tokens: bfloat16 [8192, 1536], P(('fsdp', 'seq')), may hold values from -6 to 6
- cotangent: bfloat16 [8192, 1536], P(('fsdp', 'seq')), may hold values from -6 to 6
- lengths: int32 [8, 3], P('fsdp'), may hold values from 1 to 768, as said below
- balance: int32 [8192], P(('fsdp', 'seq')), may hold values from 0 to 8191, as said below
- norm1_gain: bfloat16 [1536], P('fsdp'), may hold values from 0.5 to 1.5
- w_query: bfloat16 [1536, 1536], P('fsdp'), may hold values from -0.15625 to 0.15625
- b_query: bfloat16 [1536], P('fsdp'), may hold values from -3 to 3
- w_key: bfloat16 [1536, 256], P('fsdp'), may hold values from -0.15625 to 0.15625
- b_key: bfloat16 [256], P('fsdp'), may hold values from -3 to 3
- w_value: bfloat16 [1536, 256], P('fsdp'), may hold values from -0.15625 to 0.15625
- b_value: bfloat16 [256], P('fsdp'), may hold values from -3 to 3
- w_out: bfloat16 [1536, 1536], P('fsdp'), may hold values from -0.625 to 0.625
- norm2_gain: bfloat16 [1536], P('fsdp'), may hold values from 0.5 to 1.5
- w_gate: bfloat16 [1536, 8960], P('fsdp'), may hold values from -0.15625 to 0.15625
- w_up: bfloat16 [1536, 8960], P('fsdp'), may hold values from -0.15625 to 0.15625
- w_down: bfloat16 [8960, 1536], P('fsdp'), may hold values from -0.109375 to 0.109375
Outputs:
- layer_out: bfloat16 [8192, 1536], P(('fsdp', 'seq'))
- input_grad: bfloat16 [8192, 1536], P(('fsdp', 'seq'))
- grad_norm1: float32 [1536], P(('fsdp', 'seq'))
- grad_w_query: float32 [1536, 1536], P(('fsdp', 'seq'))
- grad_b_query: float32 [1536], P(('fsdp', 'seq'))
- grad_w_key: float32 [1536, 256], P(('fsdp', 'seq'))
- grad_b_key: float32 [256], replicated
- grad_w_value: float32 [1536, 256], P(('fsdp', 'seq'))
- grad_b_value: float32 [256], replicated
- grad_w_out: float32 [1536, 1536], P(('fsdp', 'seq'))
- grad_norm2: float32 [1536], P(('fsdp', 'seq'))
- grad_w_gate: float32 [1536, 8960], P(('fsdp', 'seq'))
- grad_w_up: float32 [1536, 8960], P(('fsdp', 'seq'))
- grad_w_down: float32 [8960, 1536], P(('fsdp', 'seq'))
Inputs may be any that keep to these rules, and one draw needn't show every extreme that they name: Row g gives, in order, the lengths of the three sequences that fill balanced rows g * 1024 to (g + 1) * 1024 - 1; each row sums to 1024 and its middle entry is 768. balance is a permutation that keeps every row within its block of 1024 rows. Of the rows of one device, at most 96 go to any one device of the block, and in every block some device sends exactly 96 rows to some device.
All inputs are finite; a program needn't handle non-finite values.
Results may differ from a plain program's by a relative error of at most 0.025.
Values may be sent and summed in bfloat16 or wider, within the bound.
A program may use at most 512 MiB of HBM per device.

v0:
```python
import jax
import jax.numpy as jnp
import numpy as np
from jax import lax
from jax.sharding import PartitionSpec as P

HEADS = 12
KV_HEADS = 2
HEAD_DIM = 128


epsilon = 1e-06
rope_base = 1000000.0


def norm_piece(values, gain):
    return values * lax.rsqrt(jnp.mean(values * values, -1, keepdims=True) + epsilon) * gain


def rope_tables(position):
    half = HEAD_DIM // 2
    inverse = rope_base ** (-(jnp.arange(half, dtype=jnp.float32) * 2.0 / HEAD_DIM))
    angle = position.astype(jnp.float32)[:, None] * inverse[None, :]
    cosine = jnp.concatenate([jnp.cos(angle), jnp.cos(angle)], -1)
    sine = jnp.concatenate([jnp.sin(angle), jnp.sin(angle)], -1)
    return (cosine, sine)


def turn_half(values):
    half = values.shape[-1] // 2
    return jnp.concatenate([-values[..., half:], values[..., :half]], -1)


def rotate(values, cosine, sine):
    return values * cosine[:, None, :] + turn_half(values) * sine[:, None, :]


def rotate_back(grads, cosine, sine):
    return grads * cosine[:, None, :] - turn_half(grads * sine[:, None, :])


def segment_of(slots, starts):
    return (slots >= starts[1]).astype(jnp.int32) + (slots >= starts[2]).astype(jnp.int32)


def contract_rows(left, right):
    return lax.dot_general(
        left, right, (((0,), (0,)), ((), ())), preferred_element_type=jnp.float32
    )


def contract_columns(left, right):
    return lax.dot_general(
        left, right, (((1,), (1,)), ((), ())), preferred_element_type=jnp.float32
    )


def block_scores(query_block, keys_head, row_start, segments, score_scale):
    block = query_block.shape[0]
    raw = (
        jnp.einsum("qhd,kd->hqk", query_block, keys_head, preferred_element_type=jnp.float32)
        * score_scale
    )
    rows_now = row_start + jnp.arange(block, dtype=jnp.int32)
    columns = jnp.arange(segments.shape[0], dtype=jnp.int32)
    segment_rows = lax.dynamic_slice_in_dim(segments, row_start, block, 0)
    allowed = (segment_rows[:, None] == segments[None, :]) & (columns[None, :] <= rows_now[:, None])
    return (raw, allowed)


def per_device(
    tokens,
    cotangent,
    lengths,
    balance,
    norm1_gain,
    w_query,
    b_query,
    w_key,
    b_key,
    w_value,
    b_value,
    w_out,
    norm2_gain,
    w_gate,
    w_up,
    w_down,
):
    seq_count = lax.axis_size("seq")
    seq_rank = lax.axis_index("seq")
    rows_here = tokens.shape[0]
    width = tokens.shape[1]
    group = seq_count * rows_here
    capacity = 3 * rows_here // (2 * seq_count)
    local_heads = HEADS // seq_count
    kv_width = KV_HEADS * HEAD_DIM
    hidden_width = w_gate.shape[1]
    score_scale = HEAD_DIM ** (-0.5)
    block = min(512, group)
    block_count = group // block
    group_slot = balance % group
    target = group_slot // rows_here
    target_row = group_slot % rows_here
    onehot = (target[:, None] == jnp.arange(seq_count)[None, :]).astype(jnp.int32)
    order = jnp.sum(jnp.cumsum(onehot, 0) * onehot, 1) - 1
    send_tokens = (
        jnp.zeros((seq_count, capacity, width), jnp.bfloat16).at[target, order].set(tokens)
    )
    send_upstream = (
        jnp.zeros((seq_count, capacity, width), jnp.bfloat16).at[target, order].set(cotangent)
    )
    send_rows = (
        jnp.full((seq_count, capacity), rows_here, jnp.int32).at[target, order].set(target_row)
    )
    got_tokens, got_upstream, got_rows = (
        lax.all_to_all(send_tokens, "seq", split_axis=0, concat_axis=0, tiled=True),
        lax.all_to_all(send_upstream, "seq", split_axis=0, concat_axis=0, tiled=True),
        lax.all_to_all(send_rows, "seq", split_axis=0, concat_axis=0, tiled=True),
    )
    arrived = got_rows.reshape(-1)
    placed = (
        jnp.zeros((rows_here, width), jnp.bfloat16)
        .at[arrived]
        .set(got_tokens.reshape(-1, width), mode="drop")
    )
    placed_upstream = (
        jnp.zeros((rows_here, width), jnp.bfloat16)
        .at[arrived]
        .set(got_upstream.reshape(-1, width), mode="drop")
    )
    seq_lengths = lengths[0]
    starts = jnp.cumsum(seq_lengths) - seq_lengths
    own_slots = seq_rank * rows_here + jnp.arange(rows_here, dtype=jnp.int32)
    own_segment = segment_of(own_slots, starts)
    first_row = jnp.where(
        own_segment == 0, starts[0], jnp.where(own_segment == 1, starts[1], starts[2])
    )
    position = own_slots - first_row
    segments = segment_of(jnp.arange(group, dtype=jnp.int32), starts)
    cosine, sine = rope_tables(position)
    (
        gain_one,
        weight_query,
        bias_query,
        weight_key,
        bias_key,
        weight_value,
        bias_value,
        weight_out,
        gain_two,
    ) = (
        lax.all_gather(norm1_gain, "fsdp", axis=0, tiled=True),
        lax.all_gather(w_query, "fsdp", axis=0, tiled=True),
        lax.all_gather(b_query, "fsdp", axis=0, tiled=True),
        lax.all_gather(w_key, "fsdp", axis=0, tiled=True),
        lax.all_gather(b_key, "fsdp", axis=0, tiled=True),
        lax.all_gather(w_value, "fsdp", axis=0, tiled=True),
        lax.all_gather(b_value, "fsdp", axis=0, tiled=True),
        lax.all_gather(w_out, "fsdp", axis=0, tiled=True),
        lax.all_gather(norm2_gain, "fsdp", axis=0, tiled=True),
    )
    gain_one = gain_one.astype(jnp.float32)
    gain_two = gain_two.astype(jnp.float32)
    weight_qkv = jnp.concatenate([weight_query, weight_key, weight_value], 1)
    bias_qkv = jnp.concatenate([bias_query, bias_key, bias_value], 0).astype(jnp.float32)
    inputs = placed.astype(jnp.float32)
    normed_one = norm_piece(inputs, gain_one).astype(jnp.bfloat16)
    projected = jnp.dot(normed_one, weight_qkv, preferred_element_type=jnp.float32) + bias_qkv
    query_pre = projected[:, :width].reshape(rows_here, HEADS, HEAD_DIM)
    key_pre = projected[:, width : width + kv_width].reshape(rows_here, KV_HEADS, HEAD_DIM)
    value_pre = projected[:, width + kv_width :].reshape(rows_here, KV_HEADS, HEAD_DIM)
    queries = rotate(query_pre, cosine, sine).astype(jnp.bfloat16).reshape(rows_here, width)
    keys = rotate(key_pre, cosine, sine).astype(jnp.bfloat16)
    values = value_pre.astype(jnp.bfloat16)
    paired = jnp.concatenate([keys, values], -1)
    picked = np.arange(seq_count) * KV_HEADS // seq_count
    paired_send = paired[:, picked].reshape(rows_here, seq_count * 2 * HEAD_DIM)
    queries_head, paired_head = (
        lax.all_to_all(queries, "seq", split_axis=1, concat_axis=0, tiled=True),
        lax.all_to_all(paired_send, "seq", split_axis=1, concat_axis=0, tiled=True),
    )
    queries_head = queries_head.reshape(group, local_heads, HEAD_DIM)
    keys_head = paired_head[:, :HEAD_DIM]
    values_head = paired_head[:, HEAD_DIM:]

    def attend_block(index):
        row_start = index * block
        query_block = lax.dynamic_slice_in_dim(queries_head, row_start, block, 0)
        raw, allowed = block_scores(query_block, keys_head, row_start, segments, score_scale)
        scores = jnp.where(allowed[None], raw, -jnp.inf)
        top_score = jnp.max(scores, -1, keepdims=True)
        expo = jnp.exp(scores - top_score)
        total = jnp.sum(expo, -1, keepdims=True)
        weights_low = (expo / total).astype(jnp.bfloat16)
        result = jnp.einsum(
            "hqk,kd->qhd", weights_low, values_head, preferred_element_type=jnp.float32
        )
        return (result.astype(jnp.bfloat16), (top_score + jnp.log(total))[..., 0])

    heads_out, logsums = lax.map(attend_block, jnp.arange(block_count))
    heads_out = heads_out.reshape(group, local_heads * HEAD_DIM)
    attended = lax.all_to_all(heads_out, "seq", split_axis=0, concat_axis=1, tiled=True)
    resid = inputs + jnp.dot(attended, weight_out, preferred_element_type=jnp.float32)
    normed_two = norm_piece(resid, gain_two).astype(jnp.bfloat16)
    pieces = (
        lax.all_gather(w_gate, "fsdp", axis=0, tiled=True),
        lax.all_gather(w_up, "fsdp", axis=0, tiled=True),
    )
    columns = normed_two
    gate = jnp.dot(columns, pieces[0], preferred_element_type=jnp.float32)
    up = jnp.dot(columns, pieces[1], preferred_element_type=jnp.float32)
    sigma = jax.nn.sigmoid(gate)
    activated = gate * sigma
    hidden = (activated * up).astype(jnp.bfloat16)
    columns = hidden
    branch = jnp.dot(
        columns,
        lax.all_gather(w_down, "fsdp", axis=0, tiled=True),
        preferred_element_type=jnp.float32,
    )
    layer_rows = (resid + branch).astype(jnp.bfloat16)
    grad_down = lax.psum_scatter(
        contract_rows(hidden, placed_upstream), ("fsdp", "seq"), scatter_dimension=0, tiled=True
    )
    d_hidden = contract_columns(placed_upstream, lax.all_gather(w_down, "fsdp", axis=0, tiled=True))
    d_gate = (d_hidden * up * sigma * (1.0 + gate * (1.0 - sigma))).astype(jnp.bfloat16)
    d_up = (d_hidden * activated).astype(jnp.bfloat16)
    d_both = jnp.concatenate([d_gate, d_up], 1)
    grad_pair = lax.psum_scatter(
        contract_rows(normed_two, d_both), ("fsdp", "seq"), scatter_dimension=0, tiled=True
    )
    grad_gate = grad_pair[:, :hidden_width]
    grad_up = grad_pair[:, hidden_width:]
    pieces = (
        lax.all_gather(w_gate, "fsdp", axis=0, tiled=True),
        lax.all_gather(w_up, "fsdp", axis=0, tiled=True),
    )
    columns = contract_columns(d_gate, pieces[0]) + contract_columns(d_up, pieces[1])
    _, pull_two = jax.vjp(norm_piece, resid, gain_two)
    d_resid_norm, grad_gain_two = pull_two(columns)
    d_resid = placed_upstream.astype(jnp.float32) + d_resid_norm
    d_branch = d_resid.astype(jnp.bfloat16)
    grad_out = contract_rows(attended, d_branch)
    d_attended = contract_columns(d_branch, weight_out).astype(jnp.bfloat16)
    d_attended_head = lax.all_to_all(d_attended, "seq", split_axis=1, concat_axis=0, tiled=True)
    d_attended_head = d_attended_head.reshape(group, local_heads, HEAD_DIM)

    def back_block(carry, index):
        keys_grad, values_grad = carry
        row_start = index * block
        query_block = lax.dynamic_slice_in_dim(queries_head, row_start, block, 0)
        grad_block = lax.dynamic_slice_in_dim(d_attended_head, row_start, block, 0)
        raw, allowed = block_scores(query_block, keys_head, row_start, segments, score_scale)
        probs = jnp.where(allowed[None], jnp.exp(raw - logsums[index][:, :, None]), 0.0)
        weights_low = probs.astype(jnp.bfloat16)
        d_probs = jnp.einsum(
            "qhd,kd->hqk", grad_block, values_head, preferred_element_type=jnp.float32
        )
        delta = jnp.sum(probs * d_probs, -1, keepdims=True)
        d_score = (probs * (d_probs - delta)).astype(jnp.bfloat16)
        query_grad = (
            jnp.einsum("hqk,kd->qhd", d_score, keys_head, preferred_element_type=jnp.float32)
            * score_scale
        )
        keys_grad = (
            keys_grad
            + jnp.einsum("hqk,qhd->kd", d_score, query_block, preferred_element_type=jnp.float32)
            * score_scale
        )
        values_grad = values_grad + jnp.einsum(
            "hqk,qhd->kd", weights_low, grad_block, preferred_element_type=jnp.float32
        )
        return ((keys_grad, values_grad), query_grad)

    zero_head = jnp.zeros((group, HEAD_DIM), jnp.float32)
    (keys_grad, values_grad), query_grads = lax.scan(
        back_block, (zero_head, zero_head), jnp.arange(block_count)
    )
    query_grads = query_grads.reshape(group, local_heads * HEAD_DIM)
    paired_grads = jnp.concatenate([keys_grad, values_grad], 1)
    d_queries, d_paired = (
        lax.all_to_all(
            query_grads.astype(jnp.bfloat16), "seq", split_axis=0, concat_axis=1, tiled=True
        ).astype(query_grads.dtype),
        lax.all_to_all(
            paired_grads.astype(jnp.bfloat16), "seq", split_axis=0, concat_axis=1, tiled=True
        ).astype(paired_grads.dtype),
    )
    d_paired = jnp.sum(
        d_paired.reshape(rows_here, KV_HEADS, seq_count // KV_HEADS, 2 * HEAD_DIM), 2
    )
    d_query_pre = rotate_back(d_queries.reshape(rows_here, HEADS, HEAD_DIM), cosine, sine).astype(
        jnp.bfloat16
    )
    d_key_pre = rotate_back(d_paired[..., :HEAD_DIM], cosine, sine).astype(jnp.bfloat16)
    d_value_pre = d_paired[..., HEAD_DIM:].astype(jnp.bfloat16)
    d_qkv = jnp.concatenate(
        [
            d_query_pre.reshape(rows_here, width),
            d_key_pre.reshape(rows_here, kv_width),
            d_value_pre.reshape(rows_here, kv_width),
        ],
        1,
    )
    grad_qkv = contract_rows(normed_one, d_qkv)
    grad_bias = jnp.sum(d_qkv.astype(jnp.float32), 0)
    d_normed_one = contract_columns(d_qkv, weight_qkv)
    _, pull_one = jax.vjp(norm_piece, inputs, gain_one)
    d_input_norm, grad_gain_one = pull_one(d_normed_one)
    input_rows = (d_resid + d_input_norm).astype(jnp.bfloat16)
    summed = (
        lax.psum_scatter(grad_gain_one, ("fsdp", "seq"), scatter_dimension=0, tiled=True),
        lax.psum_scatter(grad_qkv[:, :width], ("fsdp", "seq"), scatter_dimension=0, tiled=True),
        lax.psum_scatter(grad_bias[:width], ("fsdp", "seq"), scatter_dimension=0, tiled=True),
        lax.psum_scatter(
            grad_qkv[:, width : width + kv_width], ("fsdp", "seq"), scatter_dimension=0, tiled=True
        ),
        lax.psum_scatter(
            grad_qkv[:, width + kv_width :], ("fsdp", "seq"), scatter_dimension=0, tiled=True
        ),
        lax.psum_scatter(grad_out, ("fsdp", "seq"), scatter_dimension=0, tiled=True),
        lax.psum_scatter(grad_gain_two, ("fsdp", "seq"), scatter_dimension=0, tiled=True),
    )
    key_bias_grad, value_bias_grad = lax.psum(
        (grad_bias[width : width + kv_width], grad_bias[width + kv_width :]), ("fsdp", "seq")
    )
    valid = arrived < rows_here
    safe_rows = jnp.minimum(arrived, rows_here - 1)
    out_send = jnp.where(valid[:, None], layer_rows[safe_rows], 0).reshape(
        seq_count, capacity, width
    )
    grad_send = jnp.where(valid[:, None], input_rows[safe_rows], 0).reshape(
        seq_count, capacity, width
    )
    back_out, back_grad = (
        lax.all_to_all(out_send, "seq", split_axis=0, concat_axis=0, tiled=True),
        lax.all_to_all(grad_send, "seq", split_axis=0, concat_axis=0, tiled=True),
    )
    layer_out = back_out[target, order]
    input_grad = back_grad[target, order]
    return (
        layer_out,
        input_grad,
        summed[0],
        summed[1],
        summed[2],
        summed[3],
        key_bias_grad,
        summed[4],
        value_bias_grad,
        summed[5],
        summed[6],
        grad_gate,
        grad_up,
        grad_down,
    )


def solution(mesh):
    placed = (
        P(("fsdp", "seq"), None),
        P(("fsdp", "seq"), None),
        P("fsdp", None),
        P(("fsdp", "seq")),
        P("fsdp"),
        P("fsdp", None),
        P("fsdp"),
        P("fsdp", None),
        P("fsdp"),
        P("fsdp", None),
        P("fsdp"),
        P("fsdp", None),
        P("fsdp"),
        P("fsdp", None),
        P("fsdp", None),
        P("fsdp", None),
    )
    return jax.shard_map(
        per_device,
        mesh=mesh,
        in_specs=placed,
        out_specs=(
            P(("fsdp", "seq"), None),
            P(("fsdp", "seq"), None),
            P(("fsdp", "seq")),
            P(("fsdp", "seq"), None),
            P(("fsdp", "seq")),
            P(("fsdp", "seq"), None),
            P(),
            P(("fsdp", "seq"), None),
            P(),
            P(("fsdp", "seq"), None),
            P(("fsdp", "seq")),
            P(("fsdp", "seq"), None),
            P(("fsdp", "seq"), None),
            P(("fsdp", "seq"), None),
        ),
        check_vma=False,
    )
```

profile of v0, /device:TPU:0, one launch (start us, length us, event | category | flops | bytes accessed | tf_op | source)
XLA Modules:
  0.0 2497.5 jit_solution(11681611396258412380)
XLA Ops:
  13.5 38.3 %scatter_fusion = s32[4,96]{1,0:T(4,128)} fusion(s32[4,96]{1,0:T(4,128)} %broadcast_in_dim.81, s32[256]{0:T(256)S(1)} %bitcast.257, s32[256]{0:T(256)S(1)} %get-tuple-element.287), kind=kCustom, calls=%fused_computation.5 | custom fusion | bytes 5120 | tf_op jit(solution)/shard_map/scatter | solution.py:113
  51.8 6.3 all-to-all-start
  59.2 43.1 %scatter_fusion.1 = bf16[4,96,1536]{2,1,0:T(8,128)(2,1)} fusion(bf16[4,96,1536]{2,1,0:T(8,128)(2,1)} %broadcast.332.clone, s32[256]{0:T(256)S(1)} %bitcast.258, bf16[256,1536]{1,0:T(8,128)(2,1)S(1)} %copy-done.30), kind=kCustom, calls=%fused_computation.6 | custom fusion | bytes 2361344 | tf_op jit(solution)/shard_map/scatter | solution.py:107
  102.4 4.7 all-to-all-start.1
  110.5 25.7 %all-reduce.10 = (bf16[256]{0:T(256)(128)(2,1)S(1)}, bf16[256]{0:T(256)(128)(2,1)S(1)}, bf16[1536]{0:T(1024)(128)(2,1)S(1)}, bf16[1536]{0:T(1024)(128)(2,1)S(1)}, bf16[1536]{0:T(1024)(128)(2,1)S(1)}) all-reduce(bf16[256]{0:T(256)(128)(2,1)S(1)} %dynamic-update-slice.3, ...), channel_id=1, replica_groups=mesh['fsdp'=8,'seq'=4] {'fsdp'}, use_global_device_ids=true, to_apply=%add.3 | all-reduce | flops 5120 | bytes 20480
  141.5 9.6 all_gather.41
  151.1 14.3 all_gather.42
  167.3 3.5 scatter_custom_fusion.2
  183.0 4.9 all-to-all-start.3
  193.7 3.2 add_convert_fusion
  199.2 3.7 all-to-all-done.3
  202.9 3.5 all-to-all-start.2
  207.5 43.1 %scatter_fusion.2 = bf16[4,96,1536]{2,1,0:T(8,128)(2,1)} fusion(bf16[4,96,1536]{2,1,0:T(8,128)(2,1)} %broadcast.332.clone.1, s32[256]{0:T(256)S(1)} %bitcast.259, bf16[256,1536]{1,0:T(8,128)(2,1)S(1)} %copy-done.31), kind=kCustom, calls=%fused_computation.8 | custom fusion | bytes 2361344 | tf_op jit(solution)/shard_map/scatter | solution.py:110
  252.7 4.6 all-to-all-start.6
  259.6 18.8 while.27
  265.7 3.3 fusion.149
  275.1 3.3 fusion.149
  280.4 5.3 all-to-all-done.6
  285.7 3.5 all-to-all-start.4
  289.5 4.0 scatter_custom_fusion.4
  293.5 15.3 all-to-all-done.4
  308.8 4.1 multiply_reduce_fusion.2
  313.7 15.2 fusion.99
  328.9 42.3 %all-gather.12.cloned.1.call-done = bf16[1536,8960]{1,0:T(8,128)(2,1)} async-done(((bf16[192,8960]{1,0:T(8,128)(2,1)}), bf16[1536,8960]{1,0:T(8,128)(2,1)}) %all-gather.12.cloned.1.call-update) | async-done | bytes 27525136 | tf_op jit(solution)/shard_map/all_gather | solution.py:207
  371.1 15.7 fusion.100
  386.8 121.4 %all-gather.14.cloned.1.call-done = bf16[8960,1536]{1,0:T(8,128)(2,1)} async-done(((bf16[1120,1536]{1,0:T(8,128)(2,1)}), bf16[8960,1536]{1,0:T(8,128)(2,1)}) %all-gather.14.cloned.1.call-update) | async-done | bytes 27525136 | tf_op jit(solution)/shard_map/all_gather | solution.py:218
  508.2 21.4 multiply_convert_fusion
  529.6 40.0 %fusion.49 = f32[1536,17920]{1,0:T(8,128)} fusion(bf16[256,1536]{1,0:T(8,128)(2,1)S(1)} %multiply_convert_fusion.3, bf16[256,8960]{1,0:T(8,128)(2,1)} %get-tuple-element.297, bf16[256,8960]{1,0:T(8,128)(2,1)} %get-tuple-element.298), kind=kOutput, calls=%fused_computation.69 | convolution fusion | flops 14111211520 | bytes 120061952 | tf_op jit(solution)/shard_map/dot_general | solution.py:47
  569.6 19.2 fusion.101
  588.8 21.5 multiply_reduce_fusion
  612.0 4.7 convolution_convert_fusion
  617.9 4.9 all-to-all-start.7
  622.8 20.5 all-to-all-done.7
  645.3 61.5 %while.28 = (s32[]{:T(128)}, f32[1024,128]{1,0:T(8,128)}, f32[1024,128]{1,0:T(8,128)}, bf16[2,512,3,128]{3,1,2,0:T(8,128)(2,1)}, s32[2]{0:T(128)S(1)}, /*index=5...) while((s32[]{:T(128)}, f32[1024,128]{1,0:T(8,128)}, ...), condition=%wide.region_18.19_spmd.clone, body=%wide.region_16.18_spmd.clone.sunk | while | flops 2039282688 | bytes 88138240 | solution.py:276
  646.6 5.7 fusion.158
  654.9 7.5 fusion.160
  664.8 3.1 fusion.162
  667.9 6.5 fusion.163
  677.7 5.7 fusion.158
  686.1 7.6 fusion.160
  696.1 3.3 fusion.162
  699.4 5.3 fusion.163
  709.9 3.5 all-to-all-start.9
  715.3 26.7 %all-to-all-done.9 = bf16[4,256,256]{2,1,0:T(8,128)(2,1)S(1)} async-done(((bf16[4,256,256]{2,1,0:T(8,128)(2,1)}), bf16[4,256,256]{2,1,0:T(8,128)(2,1)S(1)}, u32[]{:S(2)}, u32[]{:S(2)}) %all-to-all-start.9) | async-done | bytes 524320 | tf_op jit(solution)/shard_map/all_to_all | solution.py:285
  742.1 4.2 all-to-all-start.8
  747.2 37.9 %all-to-all-done.8 = bf16[4,256,384]{1,2,0:T(8,128)(2,1)S(1)} async-done(((bf16[4,256,384]{1,2,0:T(8,128)(2,1)}), bf16[4,256,384]{1,2,0:T(8,128)(2,1)S(1)}, u32[]{:S(2)}, u32[]{:S(2)}) %all-to-all-start.8) | async-done | bytes 786464 | tf_op jit(solution)/shard_map/all_to_all | solution.py:282
  789.6 4.5 copy-done.5
  797.5 5.0 fusion.66
  802.6 8.2 slice.150
  812.0 23.3 fusion.102
  836.7 14.4 fusion.54
  854.0 5.2 fusion.58
  865.4 59.6 %all_to_all.116 = bf16[4,96,1536]{2,1,0:T(8,128)(2,1)S(1)} all-to-all(bf16[4,96,1536]{2,1,0:T(8,128)(2,1)S(1)} %get-tuple-element.321), channel_id=1, replica_groups=mesh['fsdp'=8,'seq'=4] {'seq'}, dimensions={0} | all-to-all | bytes 2359296 | tf_op jit(solution)/shard_map/all_to_all | solution.py:336
  925.0 3.7 all-to-all-start.10
  929.0 77.9 %all-reduce.9 = (f32[1536]{0:T(1024)S(1)}, f32[1536]{0:T(1024)S(1)}, f32[256]{0:T(256)}, f32[256]{0:T(256)}, f32[1536]{0:T(1024)S(1)}) all-reduce(f32[1536]{0:T(1024)S(1)} %get-tuple-element.235, f32[1536]{0:T(1024)S(1)} %bitcast.282, f32[256]{0:T(256)S(1)} %get-tuple-element.315, ...), channel_id=2, replica_groups=mesh['fsdp'=8,'seq'=4] {'fsdp','seq'}, use_global_device_ids=true, to_apply=%region_22.23.clone | all-reduce | flops 5120 | bytes 40960
  1008.7 4.4 gather_fusion.2
  1013.1 4.4 gather_fusion.4
  1017.5 515.2 %reduce-scatter.17.cloned.1.call-done = f32[48,17920]{1,0:T(8,128)} async-done(((f32[1536,17920]{1,0:T(8,128)}), f32[48,17920]{1,0:T(8,128)}) %reduce-scatter.17.cloned.1.call-update) | async-done | bytes 3440656 | tf_op jit(solution)/shard_map/reduce_scatter | solution.py:229
  1532.7 4.0 fusion.95
  1536.6 98.9 %reduce-scatter.11.cloned.1.call-done = f32[48,256]{1,0:T(8,128)} async-done(((f32[1536,256]{1,0:T(8,128)}), f32[48,256]{1,0:T(8,128)}) %reduce-scatter.11.cloned.1.call-update) | async-done | bytes 49168 | tf_op jit(solution)/shard_map/reduce_scatter | solution.py:315
  1635.5 102.7 %reduce-scatter.13.cloned.1.call-done = f32[48,256]{1,0:T(8,128)} async-done(((f32[1536,256]{1,0:T(8,128)}), f32[48,256]{1,0:T(8,128)}) %reduce-scatter.13.cloned.1.call-update) | async-done | bytes 49168 | tf_op jit(solution)/shard_map/reduce_scatter | solution.py:318
  1738.3 142.1 %reduce-scatter.15.cloned.1.call-done = f32[48,1536]{1,0:T(8,128)} async-done(((f32[1536,1536]{1,0:T(8,128)}), f32[48,1536]{1,0:T(8,128)}) %reduce-scatter.15.cloned.1.call-update) | async-done | bytes 294928 | tf_op jit(solution)/shard_map/reduce_scatter | solution.py:321
  1880.4 140.9 %reduce-scatter.9.cloned.1.call-done = f32[48,1536]{1,0:T(8,128)} async-done(((f32[1536,1536]{1,0:T(8,128)}), f32[48,1536]{1,0:T(8,128)}) %reduce-scatter.9.cloned.1.call-update) | async-done | bytes 294928 | tf_op jit(solution)/shard_map/reduce_scatter | solution.py:313
  2021.3 469.3 %reduce-scatter.19.cloned.1.call-done = f32[280,1536]{1,0:T(8,128)} async-done(((f32[8960,1536]{1,0:T(8,128)}), f32[280,1536]{1,0:T(8,128)}) %reduce-scatter.19.cloned.1.call-update) | async-done | bytes 1720336
  (323 shorter events, 99.5 us)
Async XLA Ops:
  7.2 163.9 %all-gather.6.cloned.1.call-start = ((), (), s32[]{:S(2)}) async-start(), calls=%async_computation.17 | async-start | bytes 5308416 | tf_op jit(solution)/shard_map/all_gather | solution.py:153
  7.9 285.6 %all-gather.8.cloned.1.call-start = ((), (), s32[]{:S(2)}) async-start(), calls=%async_computation.18 | async-start | bytes 5308416 | tf_op jit(solution)/shard_map/all_gather | solution.py:159
  8.7 305.0 %all-gather.10.cloned.1.call-start = ((), (), s32[]{:S(2)}) async-start(), calls=%async_computation.19 | async-start | bytes 30965760 | tf_op jit(solution)/shard_map/all_gather | solution.py:206
  9.4 361.7 %all-gather.12.cloned.1.call-start = ((), (), s32[]{:S(2)}) async-start(), calls=%async_computation.20 | async-start | bytes 30965760 | tf_op jit(solution)/shard_map/all_gather | solution.py:207
  10.0 498.2 %all-gather.14.cloned.1.call-start = ((), (), s32[]{:S(2)}) async-start(), calls=%async_computation.21 | async-start | bytes 30965760 | tf_op jit(solution)/shard_map/all_gather | solution.py:218
  10.7 48.6 %copy-start.30 = (bf16[256,1536]{1,0:T(8,128)(2,1)S(1)}, bf16[256,1536]{1,0:T(8,128)(2,1)}, u32[]{:S(2)}) copy-start(bf16[256,1536]{1,0:T(8,128)(2,1)} %param.22) | copy-start | bytes 2359300
  51.8 50.6 %all-to-all-start = ((s32[4,1,96]{2,1,0:T(1,128)}), s32[4,1,96]{2,1,0:T(1,128)S(1)}, u32[]{:S(2)}, u32[]{:S(2)}) async-start(s32[4,1,96]{2,1,0:T(1,128)} %bitcast.15), calls=%async_computation | async-start | bytes 4096 | tf_op jit(solution)/shard_map/all_to_all | solution.py:118
  102.3 4.8 copy-start.61
  102.3 5.0 copy-start.62
  102.3 6.9 copy-start.56
  102.3 7.2 copy-start.57
  102.3 7.4 copy-start.58
  102.3 7.6 copy-start.59
  102.4 7.9 copy-start.60
  102.4 63.6 %copy-start.44 = (s32[4,1,96]{2,1,0:T(1,128)}, s32[4,1,96]{2,1,0:T(1,128)S(1)}, u32[]{:S(2)}) copy-start(s32[4,1,96]{2,1,0:T(1,128)S(1)} %all-to-all-done) | copy-start | bytes 4612
  102.4 64.9 %all-to-all-start.1 = ((bf16[4,96,1536]{2,1,0:T(8,128)(2,1)}), bf16[4,96,1536]{2,1,0:T(8,128)(2,1)}, u32[]{:S(2)}, u32[]{:S(2)}) async-start(bf16[4,96,1536]{2,1,0:T(8,128)(2,1)} %scatter_fusion.1), calls=%async_computation.1 | async-start | bytes 2359296 | tf_op jit(solution)/shard_map/all_to_all | solution.py:116
  136.2 38.0 %copy-start.38 = (f32[1536]{0:T(1024)}, f32[1536]{0:T(1024)S(1)}, u32[]{:S(2)}) copy-start(f32[1536]{0:T(1024)S(1)} %convert_element_type.158) | copy-start | bytes 18436
  139.4 42.0 %copy-start.20 = (f32[256,128]{1,0:T(8,128)}, f32[256,128]{1,0:T(8,128)S(1)}, u32[]{:S(2)}) copy-start(f32[256,128]{1,0:T(8,128)S(1)} %get-tuple-element.330) | copy-start | bytes 393220
  139.4 42.0 %copy-start.22 = (f32[256,128]{1,0:T(8,128)}, f32[256,128]{1,0:T(8,128)S(1)}, u32[]{:S(2)}) copy-start(f32[256,128]{1,0:T(8,128)S(1)} %get-tuple-element.329) | copy-start | bytes 393220
  139.6 49.8 %copy-start.24 = (f32[256,128]{0,1:T(8,128)}, f32[256,128]{0,1:T(8,128)S(1)}, u32[]{:S(2)}) copy-start(f32[256,128]{0,1:T(8,128)S(1)} %copy.120) | copy-start | bytes 393220
  139.8 11.3 copy-start.43
  170.8 138.0 %copy-start.6 = (bf16[256,1536]{1,0:T(8,128)(2,1)}, bf16[256,1536]{1,0:T(8,128)(2,1)S(1)}, u32[]{:S(2)}) copy-start(bf16[256,1536]{1,0:T(8,128)(2,1)S(1)} %scatter_custom_fusion.2) | copy-start | bytes 2359300
  171.0 3.2 copy-start.46
  183.0 19.9 all-to-all-start.3
  196.9 10.7 copy-start.31
  202.9 49.8 %all-to-all-start.2 = ((bf16[256,4,384]{0,2,1:T(8,128)(2,1)}), bf16[256,4,384]{0,2,1:T(8,128)(2,1)S(1)}, u32[]{:S(2)}, u32[]{:S(2)}) async-start(bf16[256,4,384]{0,2,1:T(8,128)(2,1)} %bitcast.28), calls=%async_computation.2 | async-start | bytes 1572864 | tf_op jit(solution)/shard_map/all_to_all | solution.py:179
  252.7 33.0 %all-to-all-start.6 = ((bf16[4,96,1536]{2,1,0:T(8,128)(2,1)}), bf16[4,96,1536]{2,1,0:T(8,128)(2,1)}, u32[]{:S(2)}, u32[]{:S(2)}) async-start(bf16[4,96,1536]{2,1,0:T(8,128)(2,1)} %scatter_fusion.2), calls=%async_computation.6 | async-start | bytes 2359296 | tf_op jit(solution)/shard_map/all_to_all | solution.py:117
  285.7 23.1 all-to-all-start.4
  289.2 1243.5 %reduce-scatter.17.cloned.1.call-start = ((), (), s32[]{:S(2)}) async-start(), calls=%async_computation.26 | async-start | bytes 113541120 | tf_op jit(solution)/shard_map/reduce_scatter | solution.py:229
  308.7 4.1 copy-start.13
  312.9 297.5 %copy-start.8 = (f32[256,1536]{1,0:T(8,128)}, f32[256,1536]{1,0:T(8,128)S(1)}, u32[]{:S(2)}) copy-start(f32[256,1536]{1,0:T(8,128)S(1)} %get-tuple-element.326) | copy-start | bytes 4718596
  328.9 179.4 %copy-start.15 = (bf16[256,1536]{1,0:T(8,128)(2,1)S(1)}, bf16[256,1536]{1,0:T(8,128)(2,1)}, u32[]{:S(2)}) copy-start(bf16[256,1536]{1,0:T(8,128)(2,1)} %scatter_custom_fusion.4) | copy-start | bytes 2359300
  588.8 21.5 copy-start.51
  617.9 27.4 %copy-start.4 = (bf16[1024,128]{1,0:T(8,128)(2,1)S(1)}, bf16[1024,128]{1,0:T(8,128)(2,1)}, u32[]{:S(2)}) copy-start(bf16[1024,128]{1,0:T(8,128)(2,1)} %copy-done.3) | copy-start | bytes 786436
  617.9 27.4 %copy-start.29 = (s32[1024]{0:T(1024)S(1)}, s32[1024]{0:T(1024)}, u32[]{:S(2)}) copy-start(s32[1024]{0:T(1024)} %copy-done.28) | copy-start | bytes 12292
  617.9 27.4 %copy-start.41 = (f32[2,3,512]{2,1,0:T(4,128)S(1)}, f32[2,3,512]{2,1,0:T(4,128)}, u32[]{:S(2)}) copy-start(f32[2,3,512]{2,1,0:T(4,128)} %copy-done.40) | copy-start | bytes 36868
  617.9 25.4 %all-to-all-start.7 = ((bf16[256,4,384]{0,2,1:T(8,128)(2,1)}), bf16[256,4,384]{0,2,1:T(8,128)(2,1)S(1)}, u32[]{:S(2)}, u32[]{:S(2)}) async-start(bf16[256,4,384]{0,2,1:T(8,128)(2,1)} %bitcast.39), calls=%async_computation.7 | async-start | bytes 1572864 | tf_op jit(solution)/shard_map/all_to_all | solution.py:245
  654.9 7.5 copy-start
  654.9 7.5 slice-start
  654.9 8.0 slice-start.1
  667.9 6.5 copy-start.33
  686.1 7.6 copy-start
  686.1 7.6 slice-start
  686.1 8.1 slice-start.1
  696.0 3.3 copy-start.1
  696.1 3.3 copy-start.36
  699.4 5.3 copy-start.33
  706.8 6.6 copy-start.35
  709.9 32.2 %all-to-all-start.9 = ((bf16[4,256,256]{2,1,0:T(8,128)(2,1)}), bf16[4,256,256]{2,1,0:T(8,128)(2,1)S(1)}, u32[]{:S(2)}, u32[]{:S(2)}) async-start(bf16[4,256,256]{2,1,0:T(8,128)(2,1)} %pad_maximum_fusion.2), calls=%async_computation.9 | async-start | bytes 1048576 | tf_op jit(solution)/shard_map/all_to_all | solution.py:285
  714.3 32.4 %copy-start.21 = (f32[256,128]{1,0:T(8,128)S(1)}, f32[256,128]{1,0:T(8,128)}, u32[]{:S(2)}) copy-start(f32[256,128]{1,0:T(8,128)} %copy-done.20) | copy-start | bytes 393220
  715.3 31.6 %copy-start.23 = (f32[256,128]{1,0:T(8,128)S(1)}, f32[256,128]{1,0:T(8,128)}, u32[]{:S(2)}) copy-start(f32[256,128]{1,0:T(8,128)} %copy-done.22) | copy-start | bytes 393220
  742.1 43.1 %all-to-all-start.8 = ((bf16[4,256,384]{1,2,0:T(8,128)(2,1)}), bf16[4,256,384]{1,2,0:T(8,128)(2,1)S(1)}, u32[]{:S(2)}, u32[]{:S(2)}) async-start(bf16[4,256,384]{1,2,0:T(8,128)(2,1)} %copy.136), calls=%async_computation.8 | async-start | bytes 1572864 | tf_op jit(solution)/shard_map/all_to_all | solution.py:282
  746.3 889.2 %reduce-scatter.11.cloned.1.call-start = ((), (), s32[]{:S(2)}) async-start(), calls=%async_computation.23 | async-start | bytes 1622016 | tf_op jit(solution)/shard_map/reduce_scatter | solution.py:315
  746.9 38.3 %copy-start.25 = (f32[256,128]{0,1:T(8,128)S(1)}, f32[256,128]{0,1:T(8,128)}, u32[]{:S(2)}) copy-start(f32[256,128]{0,1:T(8,128)} %copy-done.24) | copy-start | bytes 393220
  789.6 4.5 copy-start.5
  795.9 942.3 %reduce-scatter.13.cloned.1.call-start = ((), (), s32[]{:S(2)}) async-start(), calls=%async_computation.24 | async-start | bytes 1622016 | tf_op jit(solution)/shard_map/reduce_scatter | solution.py:318
  796.7 1083.7 %reduce-scatter.15.cloned.1.call-start = ((), (), s32[]{:S(2)}) async-start(), calls=%async_computation.25 | async-start | bytes 9732096 | tf_op jit(solution)/shard_map/reduce_scatter | solution.py:321
  802.6 1218.7 %reduce-scatter.9.cloned.1.call-start = ((), (), s32[]{:S(2)}) async-start(), calls=%async_computation.22 | async-start | bytes 9732096 | tf_op jit(solution)/shard_map/reduce_scatter | solution.py:313
  810.9 1679.6 %reduce-scatter.19.cloned.1.call-start = ((), (), s32[]{:S(2)}) async-start(), calls=%async_computation.27 | async-start | bytes 56770560
  853.9 5.2 copy-start.49
  853.9 5.3 copy-start.12
  925.0 4.1 copy-start.52
  925.0 83.7 %copy-start.2 = (s32[256,1]{0,1:T(1,128)S(1)}, s32[256,1]{0,1:T(1,128)}, u32[]{:S(2)}) copy-start(s32[256,1]{0,1:T(1,128)} %get-tuple-element.290) | copy-start | bytes 3076
  925.0 88.1 %all-to-all-start.10 = ((bf16[4,96,1536]{2,1,0:T(8,128)(2,1)}), bf16[4,96,1536]{2,1,0:T(8,128)(2,1)S(1)}, u32[]{:S(2)}, u32[]{:S(2)}) async-start(bf16[4,96,1536]{2,1,0:T(8,128)(2,1)} %get-tuple-element.320), calls=%async_computation.10 | async-start | bytes 2359296 | tf_op jit(solution)/shard_map/all_to_all | solution.py:337
  (30 other events, 48.9 us)
Sparse Core Ops, SparseCore 0:
  9.9 41.6 all-gather.5
  53.4 38.9 all-gather.7
  94.3 139.7 all-gather.9
  235.8 135.2 all-gather.11
  372.9 135.2 all-gather.13
  569.8 962.8 reduce-scatter.16
  1539.3 96.1 reduce-scatter.10
  1642.2 96.0 reduce-scatter.12
  1745.7 134.5 reduce-scatter.14
  1886.7 134.5 reduce-scatter.8
  2029.4 461.0 reduce-scatter.18
where the time goes:
time: 2510 us; the launch traced here: 2500 us
  waiting for transfers between devices  1750 us (70%)
  matrix products  252 us (10%)
  local copies, waits for them, and re-layouts  212 us (8%)
  blocking collectives  187 us (7%)
  starting transfers between devices  44.5 us (2%)
  other arithmetic  32.1 us (1%)
    reduce_scatter x1, waiting for transfers between devices, per_device(): lax.psum_scatter(contract_rows(normed_two, d_both), ('fsdp', 'seq'), scat...  515 us
    unnamed x12, waiting for transfers between devices  473 us
    reduce_scatter x1, waiting for transfers between devices, per_device(): lax.psum_scatter(grad_out, ('fsdp', 'seq'), scatter_dimension=0, tiled=True)  142 us
    reduce_scatter x1, waiting for transfers between devices, per_device(): lax.psum_scatter(grad_qkv[:, :width], ('fsdp', 'seq'), scatter_dimension=...  141 us
    all_gather x1, waiting for transfers between devices, per_device(): lax.all_gather(w_down, 'fsdp', axis=0, tiled=True)  121 us
    unnamed x2, blocking collectives  104 us
    reduce_scatter x1, waiting for transfers between devices, per_device(): lax.psum_scatter(grad_qkv[:, width + kv_width:], ('fsdp', 'seq'), scatter...  103 us
    reduce_scatter x1, waiting for transfers between devices, per_device(): lax.psum_scatter(grad_qkv[:, width:width + kv_width], ('fsdp', 'seq'), sc...  98.9 us
  transfers between devices with their start and end apart: 21, of which 14 were waited for; matrix products, arithmetic and copies ran while one was open for 17% of the time, Pallas kernels for 0%

commit v1 on v0

v1 whole, which is shorter than its diff:
```python
import jax
import jax.numpy as jnp
from jax import lax
from jax.sharding import PartitionSpec as P

HEADS = 12
KV_HEADS = 2
HEAD_DIM = 128

epsilon = 1e-06
rope_base = 1000000.0


def norm_piece(values, gain):
    return values * lax.rsqrt(jnp.mean(values * values, -1, keepdims=True) + epsilon) * gain


def rope_tables(position):
    half = HEAD_DIM // 2
    inverse = rope_base ** (-(jnp.arange(half, dtype=jnp.float32) * 2.0 / HEAD_DIM))
    angle = position.astype(jnp.float32)[:, None] * inverse[None, :]
    cosine = jnp.concatenate([jnp.cos(angle), jnp.cos(angle)], -1)
    sine = jnp.concatenate([jnp.sin(angle), jnp.sin(angle)], -1)
    return (cosine, sine)


def turn_half(values):
    half = values.shape[-1] // 2
    return jnp.concatenate([-values[..., half:], values[..., :half]], -1)


def rotate(values, cosine, sine):
    return values * cosine[:, None, :] + turn_half(values) * sine[:, None, :]


def rotate_back(grads, cosine, sine):
    return grads * cosine[:, None, :] - turn_half(grads * sine[:, None, :])


def segment_of(slots, starts):
    return (slots >= starts[1]).astype(jnp.int32) + (slots >= starts[2]).astype(jnp.int32)


def contract_rows(left, right):
    return lax.dot_general(
        left, right, (((0,), (0,)), ((), ())), preferred_element_type=jnp.float32
    )


def contract_columns(left, right):
    return lax.dot_general(
        left, right, (((1,), (1,)), ((), ())), preferred_element_type=jnp.float32
    )


def per_device(
    tokens, cotangent, lengths, balance, norm1_gain, w_query, b_query, w_key, b_key,
    w_value, b_value, w_out, norm2_gain, w_gate, w_up, w_down,
):
    seq_count = lax.axis_size("seq")
    fsdp_count = lax.axis_size("fsdp")
    seq_rank = lax.axis_index("seq")
    rows_here, width = tokens.shape
    group = seq_count * rows_here
    kv_width = KV_HEADS * HEAD_DIM
    qkv_width = width + 2 * kv_width
    hidden_width = w_gate.shape[1]
    unit = hidden_width // (fsdp_count * seq_count)
    own_units = hidden_width // seq_count
    weight_rows = w_gate.shape[0]
    score_scale = HEAD_DIM ** (-0.5)
    repeat = HEADS // KV_HEADS

    slot = balance % group
    slots_all = lax.all_gather(slot, "seq", axis=0, tiled=True)
    seq_lengths = lengths[0]
    starts = jnp.cumsum(seq_lengths) - seq_lengths
    segment = segment_of(slot, starts)
    segments_all = segment_of(slots_all, starts)
    first_row = jnp.where(segment == 0, starts[0], jnp.where(segment == 1, starts[1], starts[2]))
    cosine, sine = rope_tables(slot - first_row)
    allowed = (segment[:, None] == segments_all[None, :]) & (slots_all[None, :] <= slot[:, None])

    small = jnp.concatenate([norm1_gain, norm2_gain, b_query, b_key, b_value], 0)[None]
    small = lax.all_gather(small, "fsdp", axis=0, tiled=True)
    piece = norm1_gain.shape[0]
    bias_piece = b_key.shape[0]
    gain_one = small[:, :piece].reshape(-1).astype(jnp.float32)
    gain_two = small[:, piece : 2 * piece].reshape(-1).astype(jnp.float32)
    bias_qkv = jnp.concatenate(
        [
            small[:, 2 * piece : 3 * piece].reshape(-1),
            small[:, 3 * piece : 3 * piece + bias_piece].reshape(-1),
            small[:, 3 * piece + bias_piece :].reshape(-1),
        ],
        0,
    ).astype(jnp.float32)
    weight_qkv = lax.all_gather(
        jnp.concatenate([w_query, w_key, w_value], 1), "fsdp", axis=0, tiled=True
    )
    weight_out = lax.all_gather(w_out, "fsdp", axis=0, tiled=True)
    upstream_all = lax.all_gather(cotangent, "seq", axis=0, tiled=True)

    def own_columns(weight):
        cut = weight.reshape(weight_rows, fsdp_count, seq_count, unit)
        return lax.dynamic_index_in_dim(cut, seq_rank, 2, False).reshape(weight_rows, own_units)

    weight_gu = lax.all_gather(
        jnp.concatenate([own_columns(w_gate), own_columns(w_up)], 1), "fsdp", axis=0, tiled=True
    )
    weight_down = lax.all_gather(
        lax.dynamic_slice_in_dim(w_down, seq_rank * unit, unit, 0), "fsdp", axis=0, tiled=True
    )

    inputs = tokens.astype(jnp.float32)
    normed_one = norm_piece(inputs, gain_one).astype(jnp.bfloat16)
    projected = jnp.dot(normed_one, weight_qkv, preferred_element_type=jnp.float32) + bias_qkv
    query_pre = projected[:, :width].reshape(rows_here, HEADS, HEAD_DIM)
    key_pre = projected[:, width : width + kv_width].reshape(rows_here, KV_HEADS, HEAD_DIM)
    value_pre = projected[:, width + kv_width :]
    queries = rotate(query_pre, cosine, sine).astype(jnp.bfloat16)
    keys = rotate(key_pre, cosine, sine).astype(jnp.bfloat16).reshape(rows_here, kv_width)
    values = value_pre.astype(jnp.bfloat16)
    paired = lax.all_gather(jnp.concatenate([keys, values], 1), "seq", axis=0, tiled=True)
    keys_all = paired[:, :kv_width].reshape(group, KV_HEADS, HEAD_DIM)
    values_all = paired[:, kv_width:].reshape(group, KV_HEADS, HEAD_DIM)
    grouped = queries.reshape(rows_here, KV_HEADS, repeat, HEAD_DIM)
    raw = (
        jnp.einsum("qgrd,kgd->grqk", grouped, keys_all, preferred_element_type=jnp.float32)
        * score_scale
    )
    scores = jnp.where(allowed, raw, -jnp.inf)
    expo = jnp.exp(scores - jnp.max(scores, -1, keepdims=True))
    probs = expo / jnp.sum(expo, -1, keepdims=True)
    probs_low = probs.astype(jnp.bfloat16)
    attended = jnp.einsum(
        "grqk,kgd->qgrd", probs_low, values_all, preferred_element_type=jnp.float32
    )
    attended = attended.astype(jnp.bfloat16).reshape(rows_here, width)
    resid = inputs + jnp.dot(attended, weight_out, preferred_element_type=jnp.float32)
    normed_two = norm_piece(resid, gain_two).astype(jnp.bfloat16)

    normed_all = lax.all_gather(normed_two, "seq", axis=0, tiled=True)
    both = jnp.dot(normed_all, weight_gu, preferred_element_type=jnp.float32)
    gate = both[:, :own_units]
    up = both[:, own_units:]
    sigma = jax.nn.sigmoid(gate)
    activated = gate * sigma
    hidden = (activated * up).astype(jnp.bfloat16)
    d_hidden = contract_columns(upstream_all, weight_down)
    d_gate = (d_hidden * up * sigma * (1.0 + gate * (1.0 - sigma))).astype(jnp.bfloat16)
    d_up = (d_hidden * activated).astype(jnp.bfloat16)
    d_both = jnp.concatenate([d_gate, d_up], 1)
    columns = lax.psum_scatter(
        contract_columns(d_both, weight_gu).astype(jnp.bfloat16),
        "seq", scatter_dimension=0, tiled=True,
    ).astype(jnp.float32)
    branch = lax.psum_scatter(
        jnp.dot(hidden, weight_down, preferred_element_type=jnp.float32).astype(jnp.bfloat16),
        "seq", scatter_dimension=0, tiled=True,
    ).astype(jnp.float32)
    layer_out = (resid + branch).astype(jnp.bfloat16)
    grad_down = lax.psum_scatter(
        contract_rows(hidden, upstream_all).astype(jnp.bfloat16),
        "fsdp", scatter_dimension=0, tiled=True,
    ).astype(jnp.float32)
    grad_pair = lax.psum_scatter(
        contract_rows(normed_all, d_both).astype(jnp.bfloat16),
        "fsdp", scatter_dimension=0, tiled=True,
    )
    grad_pair = lax.all_to_all(grad_pair, "seq", split_axis=0, concat_axis=0, tiled=True)
    grad_pair = grad_pair.reshape(seq_count, weight_rows // seq_count, 2, fsdp_count, unit)
    grad_pair = grad_pair.transpose(2, 1, 3, 0, 4).astype(jnp.float32)
    grad_pair = grad_pair.reshape(2, weight_rows // seq_count, hidden_width)

    _, pull_two = jax.vjp(norm_piece, resid, gain_two)
    d_resid_norm, grad_gain_two = pull_two(columns)
    d_resid = cotangent.astype(jnp.float32) + d_resid_norm
    d_branch = d_resid.astype(jnp.bfloat16)
    grad_out = contract_rows(attended, d_branch).astype(jnp.bfloat16)
    d_attended = contract_columns(d_branch, weight_out).astype(jnp.bfloat16)
    d_attended = d_attended.reshape(rows_here, KV_HEADS, repeat, HEAD_DIM)
    d_probs = jnp.einsum(
        "qgrd,kgd->grqk", d_attended, values_all, preferred_element_type=jnp.float32
    )
    delta = jnp.sum(probs * d_probs, -1, keepdims=True)
    d_score = (probs * (d_probs - delta)).astype(jnp.bfloat16)
    d_queries = (
        jnp.einsum("grqk,kgd->qgrd", d_score, keys_all, preferred_element_type=jnp.float32)
        * score_scale
    )
    d_keys = (
        jnp.einsum("grqk,qgrd->kgd", d_score, grouped, preferred_element_type=jnp.float32)
        * score_scale
    )
    d_values = jnp.einsum(
        "grqk,qgrd->kgd", probs_low, d_attended, preferred_element_type=jnp.float32
    )
    d_paired = jnp.concatenate([d_keys.reshape(group, kv_width), d_values.reshape(group, kv_width)], 1)
    d_paired = lax.psum_scatter(
        d_paired.astype(jnp.bfloat16), "seq", scatter_dimension=0, tiled=True
    ).astype(jnp.float32)
    d_query_pre = rotate_back(
        d_queries.reshape(rows_here, HEADS, HEAD_DIM), cosine, sine
    ).astype(jnp.bfloat16)
    d_key_pre = rotate_back(
        d_paired[:, :kv_width].reshape(rows_here, KV_HEADS, HEAD_DIM), cosine, sine
    ).astype(jnp.bfloat16)
    d_value_pre = d_paired[:, kv_width:].astype(jnp.bfloat16)
    d_qkv = jnp.concatenate(
        [
            d_query_pre.reshape(rows_here, width),
            d_key_pre.reshape(rows_here, kv_width),
            d_value_pre,
        ],
        1,
    )
    grad_qkv = contract_rows(normed_one, d_qkv).astype(jnp.bfloat16)
    grad_bias = jnp.sum(d_qkv.astype(jnp.float32), 0)
    d_normed_one = contract_columns(d_qkv, weight_qkv)
    _, pull_one = jax.vjp(norm_piece, inputs, gain_one)
    d_input_norm, grad_gain_one = pull_one(d_normed_one)
    input_grad = (d_resid + d_input_norm).astype(jnp.bfloat16)

    def summed(value):
        value = lax.psum_scatter(value, "fsdp", scatter_dimension=0, tiled=True)
        return lax.psum_scatter(value, "seq", scatter_dimension=0, tiled=True).astype(jnp.float32)

    grad_out = summed(grad_out)
    grad_qkv = summed(grad_qkv)
    vectors = lax.psum(
        jnp.concatenate([grad_gain_one, grad_gain_two, grad_bias], 0), ("fsdp", "seq")
    )
    own = width // (fsdp_count * seq_count)
    first = (lax.axis_index("fsdp") * seq_count + seq_rank) * own

    def own_part(offset):
        return lax.dynamic_slice_in_dim(vectors, offset + first, own, 0)

    biases = 2 * width
    return (
        layer_out,
        input_grad,
        own_part(0),
        grad_qkv[:, :width],
        own_part(biases),
        grad_qkv[:, width : width + kv_width],
        vectors[biases + width : biases + width + kv_width],
        grad_qkv[:, width + kv_width :],
        vectors[biases + width + kv_width :],
        grad_out,
        own_part(width),
        grad_pair[0],
        grad_pair[1],
        grad_down,
    )


def solution(mesh):
    both = P(("fsdp", "seq"), None)
    both_one = P(("fsdp", "seq"))
    placed = (
        both, both, P("fsdp", None), both_one, P("fsdp"), P("fsdp", None), P("fsdp"),
        P("fsdp", None), P("fsdp"), P("fsdp", None), P("fsdp"), P("fsdp", None), P("fsdp"),
        P("fsdp", None), P("fsdp", None), P("fsdp", None),
    )
    return jax.shard_map(
        per_device,
        mesh=mesh,
        in_specs=placed,
        out_specs=(
            both, both, both_one, both, both_one, both, P(), both, P(), both, both_one,
            both, both, both,
        ),
        check_vma=False,
    )
```

time: 2510 us -> 1010 us (0.40)
  waiting for transfers between devices: 1750 us -> 585 us
  blocking collectives: 187 us -> 62 us
  local copies, waits for them, and re-layouts: 212 us -> 111 us
  matrix products: 252 us -> 179 us
  starting transfers between devices: 44.5 us -> 6.67 us
    reduce_scatter x5 -> x9, waiting for transfers between devices: 1000 us -> 358 us  [the longest x1 102 us: per_device(): lax.psum_scatter(contract_rows(normed_all, d_both).astype(jnp.bfloat16),...]
    unnamed x12 -> x16, waiting for transfers between devices: 473 us -> 1.43 us
    scatter x5 -> x0, local copies, waits for them, and re-layouts: 132 us -> none  [the longest x2 86.2 us: per_device(): jnp.zeros((seq_count, capacity, width), jnp.bfloat16).at[target, order]]
    all_to_all x10 -> x1, waiting for transfers between devices: 109 us -> 0.01 us  [per_device(): lax.all_to_all(grad_pair, 'seq', split_axis=0, concat_axis=0, tiled=True)]
    unnamed x2 -> x0, blocking collectives: 104 us -> none
    all_gather x5 -> x7, waiting for transfers between devices: 164 us -> 225 us  [the longest x1 78.1 us: per_device(): lax.all_gather(jnp.concatenate([own_columns(w_gate), own_columns(w_up)],...]
    all_to_all x1 -> x0, blocking collectives: 59.6 us -> none  [per_device(): lax.all_to_all(out_send, 'seq', split_axis=0, concat_axis=0, tiled=True)]
    psum x0 -> x1, blocking collectives: none -> 40.3 us  [per_device(): lax.psum(jnp.concatenate([grad_gain_one, grad_gain_two, grad_bias], 0), (...]
  transfers between devices with their start and end apart: 21 -> 17, of which waited for: 14 -> 15; matrix products, arithmetic and copies ran while one was open for 17% -> 21% of each run, Pallas kernels for 0% -> 0%
where the time goes in v1:
time: 1010 us
  waiting for transfers between devices  585 us (58%)
  matrix products  179 us (18%)
  local copies, waits for them, and re-layouts  111 us (11%)
  blocking collectives  62 us (6%)
  other arithmetic  52.1 us (5%)
  between operations  14.6 us (1%)
    reduce_scatter x1, waiting for transfers between devices, per_device(): lax.psum_scatter(contract_rows(normed_all, d_both).astype(jnp.bfloat16),...  102 us
    reduce_scatter x2, waiting for transfers between devices, summed(): value = lax.psum_scatter(value, 'fsdp', scatter_dimension=0, tiled=True)  84.9 us
    all_gather x1, waiting for transfers between devices, per_device(): lax.all_gather(jnp.concatenate([own_columns(w_gate), own_columns(w_up)],...  78.1 us
    reduce_scatter x1, waiting for transfers between devices, per_device(): lax.psum_scatter(jnp.dot(hidden, weight_down, preferred_element_type=jnp....  61 us
    dot_general x4, matrix products, contract_columns(): lax.dot_general(left, right, (((1,), (1,)), ((), ())), preferred_element_...  51.5 us
    all_gather x1, waiting for transfers between devices, per_device(): lax.all_gather(lax.dynamic_slice_in_dim(w_down, seq_rank * unit, unit, 0)...  49.2 us
    reduce_scatter x1, waiting for transfers between devices, per_device(): lax.psum_scatter(contract_columns(d_both, weight_gu).astype(jnp.bfloat16)...  47.8 us
    reduce_scatter x2, waiting for transfers between devices, summed(): lax.psum_scatter(value, 'seq', scatter_dimension=0, tiled=True)  43.8 us
  transfers between devices with their start and end apart: 17, of which 15 were waited for; matrix products, arithmetic and copies ran while one was open for 21% of the time, Pallas kernels for 0%

profile of v1, /device:TPU:0, one launch (start us, length us, event | category | flops | bytes accessed | tf_op | source)
XLA Modules:
  0.0 1009.4 jit_solution(3517443093025868273)
XLA Ops:
  7.2 2.3 pad_maximum_fusion.9
  11.7 2.0 fusion.58
  13.7 1.9 fusion.60
  18.3 3.4 concatenate.65
  21.7 10.5 %all-gather.1 = bf16[8,1,640]{2,1,0:T(2,128)(2,1)S(1)} all-gather(bf16[1,1,640]{2,1,0:T(2,128)(2,1)S(1)} %reshape.252), channel_id=2, replica_groups=mesh['fsdp'=8,'seq'=4] {'fsdp'}, dimensions={0}, use_global_device_ids=true | all-gather | bytes 11520 | tf_op jit(solution)/shard_map/all_gather | solution.py:85
  36.4 22.4 %all-gather.11.cloned.1.call-done = bf16[1536,2048]{1,0:T(8,128)(2,1)} async-done(((bf16[192,2048]{1,0:T(8,128)(2,1)}), bf16[1536,2048]{1,0:T(8,128)(2,1)}) %all-gather.11.cloned.1.call-update) | async-done | bytes 6291472 | tf_op jit(solution)/shard_map/all_gather | solution.py:98
  58.8 4.9 convolution_add_fusion
  74.6 11.2 %all-gather.2 = s32[4,1,256]{2,1,0:T(1,128)S(1)} all-gather(s32[1,1,256]{2,1,0:T(1,128)S(1)} %bitcast.162), channel_id=1, replica_groups=mesh['fsdp'=8,'seq'=4] {'seq'}, dimensions={0}, use_global_device_ids=true | all-gather | bytes 5120 | tf_op jit(solution)/shard_map/all_gather | solution.py:75
  88.2 2.7 slice.150
  90.9 3.0 copy.75
  97.0 4.9 all-gather.13.cloned.1.call-done
  101.9 2.2 fusion.70
  104.1 2.0 reshape.234
  106.1 2.1 copy.101
  108.1 2.0 reshape.233
  110.1 9.9 fusion.76
  120.0 6.8 fusion.38
  126.8 15.3 %all-gather.15.cloned.1.call-done = bf16[1536,1536]{1,0:T(8,128)(2,1)} async-done(((bf16[192,1536]{1,0:T(8,128)(2,1)}), bf16[1536,1536]{1,0:T(8,128)(2,1)}) %all-gather.15.cloned.1.call-update) | async-done | bytes 4718608 | tf_op jit(solution)/shard_map/all_gather | solution.py:101
  142.2 4.3 multiply_reduce_fusion
  149.0 11.3 %reshape.238 = bf16[192,8,4,280]{3,2,1,0:T(4,128)(2,1)} reshape(bf16[192,8960]{1,0:T(8,128)(2,1)} %param.29) | data formatting | bytes 6881280 | tf_op jit(solution)/shard_map/reshape | solution.py:105
  160.4 11.3 %reshape.240 = bf16[192,8,4,280]{3,2,1,0:T(4,128)(2,1)} reshape(bf16[192,8960]{1,0:T(8,128)(2,1)} %param.30) | data formatting | bytes 6881280 | tf_op jit(solution)/shard_map/reshape | solution.py:105
  171.7 18.3 %dynamic-slice_reduce_fusion = (bf16[192,8,280]{2,1,0:T(8,128)(2,1)}, bf16[192,8,280]{2,1,0:T(8,128)(2,1)}) fusion(bf16[192,8,4,280]{3,2,1,0:T(4,128)(2,1)} %reshape.240, s32[]{:T(128)S(6)} %select_n.40, bf16[192,8,4,280]{3,2,1,0:T(4,128)(2,1)} %reshape.238), kind=kLoop, calls=%fused_computation.44 | loop fusion | bytes 3440644 | tf_op jit(solution)/shard_map/jit(dynamic_index_in_dim)/dynamic_slice | solution.py:106
  190.0 2.8 reshape.239
  192.9 2.8 reshape.241
  195.7 3.0 pad_maximum_fusion.5
  200.9 11.5 %all-gather.17.cloned.1.call-done = bf16[1024,1536]{1,0:T(8,128)(2,1)} async-done(((bf16[256,1536]{1,0:T(8,128)(2,1)}), bf16[1024,1536]{1,0:T(8,128)(2,1)}) %all-gather.17.cloned.1.call-update) | async-done | bytes 3145744 | tf_op jit(solution)/shard_map/all_gather | solution.py:143
  212.4 78.1 %all-gather.19.cloned.1.call-done = bf16[1536,4480]{1,0:T(8,128)(2,1)} async-done(((bf16[192,4480]{1,0:T(8,128)(2,1)}), bf16[1536,4480]{1,0:T(8,128)(2,1)}) %all-gather.19.cloned.1.call-update) | async-done | bytes 13762576 | tf_op jit(solution)/shard_map/all_gather | solution.py:108
  290.5 21.2 %fusion.77 = f32[1024,4480]{1,0:T(8,128)} fusion(bf16[1024,1536]{1,0:T(8,128)(2,1)} %all-gather.17.cloned.1.call-done, bf16[1536,4480]{1,0:T(8,128)(2,1)} %all-gather.19.cloned.1.call-done), kind=kOutput, calls=%fused_computation.150 | convolution fusion | flops 14092861440 | bytes 35258368 | tf_op jit(solution)/shard_map/dot_general | solution.py:144
  311.7 43.8 %all-gather.23.cloned.1.call-done = bf16[1024,1536]{1,0:T(8,128)(2,1)} async-done(((bf16[256,1536]{1,0:T(8,128)(2,1)}), bf16[1024,1536]{1,0:T(8,128)(2,1)}) %all-gather.23.cloned.1.call-update) | async-done | bytes 3145744 | tf_op jit(solution)/shard_map/all_gather | solution.py:102
  355.4 49.2 %all-gather.21.cloned.1.call-done = bf16[2240,1536]{1,0:T(8,128)(2,1)} async-done(((bf16[280,1536]{1,0:T(8,128)(2,1)}), bf16[2240,1536]{1,0:T(8,128)(2,1)}) %all-gather.21.cloned.1.call-update) | async-done | bytes 6881296 | tf_op jit(solution)/shard_map/all_gather | solution.py:111
  404.6 19.8 %fusion.7 = (bf16[1024,2240]{1,0:T(8,128)(2,1)}, bf16[1024,2240]{1,0:T(8,128)(2,1)}, bf16[1024,2240]{1,0:T(8,128)(2,1)}) fusion(f32[1024,4480]{1,0:T(8,128)} %fusion.77, bf16[2240,1536]{1,0:T(8,128)(2,1)} %all-gather.21.cloned.1.call-done, bf16[1024,1536]{1,0:T(8,128)(2,1)} %all-gather.23.cloned.1.call-done), kind=kOutput, calls=%fused_computation.15 | convolution fusion | flops 7080837120 | bytes 42139648 | tf_op jit(solution)/shard_map/dot_general | solution.py:51
  424.4 22.0 %fusion.14 = bf16[1024,1536]{1,0:T(8,128)(2,1)} fusion(bf16[1536,4480]{1,0:T(8,128)(2,1)} %all-gather.19.cloned.1.call-done, bf16[1024,2240]{1,0:T(8,128)(2,1)} %get-tuple-element.21, bf16[1024,2240]{1,0:T(8,128)(2,1)} %get-tuple-element.20), kind=kOutput, calls=%fused_computation.29 | convolution fusion | flops 14112784384 | bytes 26083328 | tf_op jit(solution)/shard_map/dot_general | solution.py:51
  446.6 12.3 %convolution_convert_fusion.4 = bf16[1024,1536]{1,0:T(8,128)(2,1)} fusion(bf16[1024,2240]{1,0:T(8,128)(2,1)} %get-tuple-element.22, bf16[2240,1536]{1,0:T(8,128)(2,1)} %all-gather.21.cloned.1.call-done), kind=kOutput, calls=%fused_computation.30 | convolution fusion | flops 7048003584 | bytes 14614528 | tf_op jit(solution)/shard_map/dot_general | solution.py:159
  459.1 47.8 %reduce-scatter.12.cloned.1.call-done = bf16[256,1536]{1,0:T(8,128)(2,1)} async-done(((bf16[1024,1536]{1,0:T(8,128)(2,1)}), bf16[256,1536]{1,0:T(8,128)(2,1)}) %reduce-scatter.12.cloned.1.call-update) | async-done | bytes 786448 | tf_op jit(solution)/shard_map/reduce_scatter | solution.py:154
  508.6 61.0 %reduce-scatter.10.cloned.1.call-done = bf16[256,1536]{1,0:T(8,128)(2,1)} async-done(((bf16[1024,1536]{1,0:T(8,128)(2,1)}), bf16[256,1536]{1,0:T(8,128)(2,1)}) %reduce-scatter.10.cloned.1.call-update) | async-done | bytes 786448 | tf_op jit(solution)/shard_map/reduce_scatter | solution.py:158
  569.5 3.0 fusion.27
  572.6 3.8 convolution_convert_fusion.5
  576.7 10.3 %fusion.1 = (f32[2,6,256]{2,1,0:T(8,128)S(1)}, f32[2,1024,256,6]{2,1,3,0:T(8,128)}) fusion(f32[2,6,256,1024]{2,3,1,0:T(8,128)} %get-tuple-element.57, f32[2,6,256]{2,1,0:T(8,128)S(1)} %copy-done.21, bf16[256,2,6,128]{0,3,2,1:T(8,128)(2,1)S(1)} %bitcast.153, bf16[1024,2,128,1]{2,1,0,3:T(2,128)(2,1)} %bitcast.156), kind=kOutput, calls=%fused_computation.4 | convolution fusion | flops 814740480 | bytes 26501120 | tf_op jit(solution)/shard_map/qgrd,kgd->grqk/dot_general | solution.py:183
  586.9 7.8 fusion.45
  594.8 6.5 fusion.3
  601.3 2.9 fusion.48
  605.6 2.0 copy.116
  607.6 2.1 pad_maximum_fusion.7
  609.8 3.5 convolution_convert_fusion.3
  613.6 22.4 %convolution_convert_fusion = bf16[1536,4480]{1,0:T(8,128)(2,1)} fusion(bf16[1024,1536]{1,0:T(8,128)(2,1)} %all-gather.17.cloned.1.call-done, bf16[1024,2240]{1,0:T(8,128)(2,1)} %get-tuple-element.21, bf16[1024,2240]{1,0:T(8,128)(2,1)} %get-tuple-element.20), kind=kOutput, calls=%fused_computation.1 | convolution fusion | flops 14118092800 | bytes 26083328 | tf_op jit(solution)/shard_map/dot_general | solution.py:45
  636.1 4.0 convolution_multiply_fusion
  651.9 4.6 convolution_convert_fusion.2
  656.8 12.3 %convolution_convert_fusion.1 = bf16[2240,1536]{1,0:T(8,128)(2,1)} fusion(bf16[1024,2240]{1,0:T(8,128)(2,1)} %get-tuple-element.22, bf16[1024,1536]{1,0:T(8,128)(2,1)} %all-gather.23.cloned.1.call-done), kind=kOutput, calls=%fused_computation.9 | convolution fusion | flops 7049871360 | bytes 14614528 | tf_op jit(solution)/shard_map/dot_general | solution.py:45
  669.1 24.4 %reduce-scatter.20.cloned.1.call-done = bf16[192,1536]{1,0:T(8,128)(2,1)} async-done(((bf16[1536,1536]{1,0:T(8,128)(2,1)}), bf16[192,1536]{1,0:T(8,128)(2,1)}) %reduce-scatter.20.cloned.1.call-update) | async-done | bytes 589840 | tf_op jit(solution)/shard_map/reduce_scatter | solution.py:226
  693.5 102.0 %reduce-scatter.24.cloned.1.call-done = bf16[192,4480]{1,0:T(8,128)(2,1)} async-done(((bf16[1536,4480]{1,0:T(8,128)(2,1)}), bf16[192,4480]{1,0:T(8,128)(2,1)}) %reduce-scatter.24.cloned.1.call-update) | async-done | bytes 1720336 | tf_op jit(solution)/shard_map/reduce_scatter | solution.py:167
  795.6 4.6 all-to-all-start
  800.2 60.5 %reduce-scatter.16.cloned.1.call-done = bf16[192,2048]{1,0:T(8,128)(2,1)} async-done(((bf16[1536,2048]{1,0:T(8,128)(2,1)}), bf16[192,2048]{1,0:T(8,128)(2,1)}) %reduce-scatter.16.cloned.1.call-update) | async-done | bytes 786448 | tf_op jit(solution)/shard_map/reduce_scatter | solution.py:226
  860.7 5.9 fusion.24
  867.0 40.3 %psum.7 = f32[5120]{0:T(1024)S(1)} all-reduce(f32[5120]{0:T(1024)S(1)} %pad_maximum_fusion.14), channel_id=1, replica_groups=mesh['fsdp'=8,'seq'=4] {'fsdp','seq'}, use_global_device_ids=true, to_apply=%region_14.15 | all-reduce | flops 5120 | bytes 40960 | tf_op jit(solution)/shard_map/psum | solution.py:231
  908.4 2.7 fusion.29
  911.2 18.6 %reduce-scatter.26.cloned.1.call-done = bf16[280,1536]{1,0:T(8,128)(2,1)} async-done(((bf16[2240,1536]{1,0:T(8,128)(2,1)}), bf16[280,1536]{1,0:T(8,128)(2,1)}) %reduce-scatter.26.cloned.1.call-update) | async-done | bytes 860176 | tf_op jit(solution)/shard_map/reduce_scatter | solution.py:163
  929.7 2.6 convert_element_type.195
  932.3 21.5 %reduce-scatter.22.cloned.1.call-done = bf16[48,1536]{1,0:T(8,128)(2,1)} async-done(((bf16[192,1536]{1,0:T(8,128)(2,1)}), bf16[48,1536]{1,0:T(8,128)(2,1)}) %reduce-scatter.22.cloned.1.call-update) | async-done | bytes 147472 | tf_op jit(solution)/shard_map/reduce_scatter | solution.py:227
  955.4 22.3 %reduce-scatter.18.cloned.1.call-done = bf16[48,2048]{1,0:T(8,128)(2,1)} async-done(((bf16[192,2048]{1,0:T(8,128)(2,1)}), bf16[48,2048]{1,0:T(8,128)(2,1)}) %reduce-scatter.18.cloned.1.call-update) | async-done | bytes 196624 | tf_op jit(solution)/shard_map/reduce_scatter | solution.py:227
  980.7 5.8 reshape.250
  986.5 5.4 copy.133
  991.9 3.0 fusion.69
  994.8 4.0 squeeze.29
  998.9 3.9 squeeze.30
  (153 shorter events, 52.1 us)
Async XLA Ops:
  7.2 192.2 %copy-start = (bf16[1120,1536]{1,0:T(8,128)(2,1)S(1)}, bf16[1120,1536]{1,0:T(8,128)(2,1)}, u32[]{:S(2)}) copy-start(bf16[1120,1536]{1,0:T(8,128)(2,1)} %param.31) | copy-start | bytes 10321924
  7.2 51.6 %all-gather.11.cloned.1.call-start = ((), (), s32[]{:S(2)}) async-start(), calls=%async_computation.10 | async-start | bytes 7077888 | tf_op jit(solution)/shard_map/all_gather | solution.py:98
  9.6 92.3 %all-gather.13.cloned.1.call-start = ((), (), s32[]{:S(2)}) async-start(), calls=%async_computation.11 | async-start | bytes 1310720 | tf_op jit(solution)/shard_map/all_gather | solution.py:124
  32.7 31.0 %copy-start.18 = (f32[1536]{0:T(1024)}, f32[1536]{0:T(1024)S(1)}, u32[]{:S(2)}) copy-start(f32[1536]{0:T(1024)S(1)} %reshape.248) | copy-start | bytes 18436
  36.4 27.3 %copy-start.24 = (f32[256]{0:T(256)}, f32[256]{0:T(256)S(1)}, u32[]{:S(2)}) copy-start(f32[256]{0:T(256)S(1)} %fusion.30) | copy-start | bytes 3076
  36.4 27.3 %copy-start.22 = (f32[256]{0:T(256)}, f32[256]{0:T(256)S(1)}, u32[]{:S(2)}) copy-start(f32[256]{0:T(256)S(1)} %fusion.62) | copy-start | bytes 3076
  63.7 1.4 copy-start.10
  67.6 5.4 copy-start.17
  71.3 0.7 copy-start.11
  73.8 68.4 %all-gather.15.cloned.1.call-start = ((), (), s32[]{:S(2)}) async-start(), calls=%async_computation.12 | async-start | bytes 5308416 | tf_op jit(solution)/shard_map/all_gather | solution.py:101
  74.5 137.9 %all-gather.17.cloned.1.call-start = ((), (), s32[]{:S(2)}) async-start(), calls=%async_computation.13 | async-start | bytes 3932160 | tf_op jit(solution)/shard_map/all_gather | solution.py:143
  93.9 1.9 copy-start.6
  93.9 1.9 copy-start.13
  93.9 1.9 copy-start.15
  120.0 6.8 copy-start.20
  146.4 1.1 copy-start.3
  148.7 141.8 %all-gather.19.cloned.1.call-start = ((), (), s32[]{:S(2)}) async-start(), calls=%async_computation.14 | async-start | bytes 15482880 | tf_op jit(solution)/shard_map/all_gather | solution.py:108
  198.7 156.7 %all-gather.23.cloned.1.call-start = ((), (), s32[]{:S(2)}) async-start(), calls=%async_computation.17 | async-start | bytes 3932160 | tf_op jit(solution)/shard_map/all_gather | solution.py:102
  199.3 205.3 %all-gather.21.cloned.1.call-start = ((), (), s32[]{:S(2)}) async-start(), calls=%async_computation.15 | async-start | bytes 7741440 | tf_op jit(solution)/shard_map/all_gather | solution.py:111
  200.3 306.6 %reduce-scatter.12.cloned.1.call-start = ((), (), s32[]{:S(2)}) async-start(), calls=%async_computation.18 | async-start | bytes 3932160 | tf_op jit(solution)/shard_map/reduce_scatter | solution.py:154
  446.5 123.0 %reduce-scatter.10.cloned.1.call-start = ((), (), s32[]{:S(2)}) async-start(), calls=%async_computation.16 | async-start | bytes 3932160 | tf_op jit(solution)/shard_map/reduce_scatter | solution.py:158
  458.8 48.1 %copy-start.4 = (f32[256,1536]{1,0:T(8,128)S(1)}, f32[256,1536]{1,0:T(8,128)}, u32[]{:S(2)}) copy-start(f32[256,1536]{1,0:T(8,128)} %copy-done.3) | copy-start | bytes 4718596
  458.9 183.7 %reduce-scatter.14.cloned.1.call-start = ((), (), s32[]{:S(2)}) async-start(), calls=%async_computation.19 | async-start | bytes 1310720 | tf_op jit(solution)/shard_map/reduce_scatter | solution.py:200
  572.6 4.0 copy-start.21
  576.6 18.1 %slice-start = ((s8[12582912]{0:T(1024)(128)(4,1)}), s8[4194304]{0:T(1024)(128)(4,1)S(1)}, s32[]{:S(2)}) async-start(s8[12582912]{0:T(1024)(128)(4,1)} %bitcast.140), calls=%async_computation.26 | async-start | bytes 8388608
  576.6 18.1 %slice-start.1 = ((s8[12582912]{0:T(1024)(128)(4,1)}), s8[4194304]{0:T(1024)(128)(4,1)S(1)}, s32[]{:S(2)}) async-start(s8[12582912]{0:T(1024)(128)(4,1)} %bitcast.140), calls=%async_computation.27 | async-start | bytes 8388608
  586.9 7.8 slice-start.2
  594.8 6.6 copy-start.9
  601.3 3.0 copy-start.2
  604.3 5.5 copy-start.7
  609.8 83.8 %reduce-scatter.20.cloned.1.call-start = ((), (), s32[]{:S(2)}) async-start(), calls=%async_computation.22 | async-start | bytes 5308416 | tf_op jit(solution)/shard_map/reduce_scatter | solution.py:226
  613.4 182.2 %reduce-scatter.24.cloned.1.call-start = ((), (), s32[]{:S(2)}) async-start(), calls=%async_computation.24 | async-start | bytes 15482880 | tf_op jit(solution)/shard_map/reduce_scatter | solution.py:167
  636.1 4.1 copy-start.14
  636.1 224.6 %reduce-scatter.16.cloned.1.call-start = ((), (), s32[]{:S(2)}) async-start(), calls=%async_computation.20 | async-start | bytes 7077888 | tf_op jit(solution)/shard_map/reduce_scatter | solution.py:226
  640.3 0.9 copy-start.16
  641.2 6.9 copy-start.12
  642.5 9.3 copy-start.5
  642.5 9.3 copy-start.8
  642.5 9.3 copy-start.19
  642.5 9.3 copy-start.23
  656.5 273.2 %reduce-scatter.26.cloned.1.call-start = ((), (), s32[]{:S(2)}) async-start(), calls=%async_computation.25 | async-start | bytes 7741440 | tf_op jit(solution)/shard_map/reduce_scatter | solution.py:163
  669.1 284.7 %reduce-scatter.22.cloned.1.call-start = ((), (), s32[]{:S(2)}) async-start(), calls=%async_computation.23 | async-start | bytes 737280 | tf_op jit(solution)/shard_map/reduce_scatter | solution.py:227
  795.6 185.2 %all-to-all-start = ((bf16[4,48,4480]{2,1,0:T(8,128)(2,1)}), bf16[4,48,4480]{2,1,0:T(8,128)(2,1)}, u32[]{:S(2)}, u32[]{:S(2)}) async-start(bf16[4,48,4480]{2,1,0:T(8,128)(2,1)} %bitcast.150), calls=%async_computation.8 | async-start | bytes 3440640 | tf_op jit(solution)/shard_map/all_to_all | solution.py:171
  800.2 177.5 %reduce-scatter.18.cloned.1.call-start = ((), (), s32[]{:S(2)}) async-start(), calls=%async_computation.21 | async-start | bytes 983040 | tf_op jit(solution)/shard_map/reduce_scatter | solution.py:227
  860.7 47.1 %copy-start.25 = (f32[256]{0:T(256)S(1)}, f32[256]{0:T(256)}, u32[]{:S(2)}) copy-start(f32[256]{0:T(256)} %copy-done.24) | copy-start | bytes 3076
  994.8 7.9 copy-start.1
Sparse Core Ops, SparseCore 0:
  10.5 48.2 all-gather.10
  73.9 27.9 all-gather.12
  103.8 38.3 all-gather.14
  148.8 63.4 all-gather.16
  214.7 75.7 all-gather.18
  291.9 63.4 all-gather.22
  357.9 46.6 all-gather.20
  446.6 60.2 reduce-scatter.11
  509.2 60.2 reduce-scatter.9
  609.9 27.1 reduce-scatter.13
  640.9 52.5 reduce-scatter.19
  696.9 98.6 reduce-scatter.23
  799.0 61.7 reduce-scatter.15
  864.4 65.2 reduce-scatter.25
  931.9 21.8 reduce-scatter.21
  955.9 21.7 reduce-scatter.17

commit v2 on v1

v2 whole, which is shorter than its diff:
```python
import jax
import jax.numpy as jnp
from jax import lax
from jax.experimental import pallas as pl
from jax.experimental.pallas import tpu as pltpu
from jax.sharding import PartitionSpec as P

HEADS = 12
KV_HEADS = 2
HEAD_DIM = 128

epsilon = 1e-06
rope_base = 1000000.0


def norm_piece(values, gain):
    return values * lax.rsqrt(jnp.mean(values * values, -1, keepdims=True) + epsilon) * gain


def rope_tables(position):
    half = HEAD_DIM // 2
    inverse = rope_base ** (-(jnp.arange(half, dtype=jnp.float32) * 2.0 / HEAD_DIM))
    angle = position.astype(jnp.float32)[:, None] * inverse[None, :]
    cosine = jnp.concatenate([jnp.cos(angle), jnp.cos(angle)], -1)
    sine = jnp.concatenate([jnp.sin(angle), jnp.sin(angle)], -1)
    return (cosine, sine)


def turn_half(values):
    half = values.shape[-1] // 2
    return jnp.concatenate([-values[..., half:], values[..., :half]], -1)


def rotate(values, cosine, sine):
    return values * cosine[:, None, :] + turn_half(values) * sine[:, None, :]


def rotate_back(grads, cosine, sine):
    return grads * cosine[:, None, :] - turn_half(grads * sine[:, None, :])


def segment_of(slots, starts):
    return (slots >= starts[1]).astype(jnp.int32) + (slots >= starts[2]).astype(jnp.int32)


def contract_rows(left, right):
    return lax.dot_general(
        left, right, (((0,), (0,)), ((), ())), preferred_element_type=jnp.float32
    )


def contract_columns(left, right):
    return lax.dot_general(
        left, right, (((1,), (1,)), ((), ())), preferred_element_type=jnp.float32
    )


def after(value, *earlier):
    return lax.optimization_barrier((value, *earlier))[0]


def add_low(*values):
    return sum(value.astype(jnp.float32) for value in values).astype(jnp.bfloat16)


def cross(value, bits):
    count = lax.axis_size("fsdp")
    return lax.ppermute(value, "fsdp", [(i, i ^ bits) for i in range(count)])


def shift(value, step):
    count = lax.axis_size("seq")
    return lax.ppermute(value, "seq", [(i, (i + step) % count) for i in range(count)])


def place(parts, rank):
    rows = parts[0].shape[0]
    whole = jnp.zeros((len(parts) * rows,) + parts[0].shape[1:], parts[0].dtype)
    for k, part in enumerate(parts):
        whole = lax.dynamic_update_slice_in_dim(whole, part, (rank ^ k) * rows, 0)
    return whole


def gather_plane(block, earlier=()):
    if lax.axis_size("fsdp") != 8:
        whole = lax.all_gather(block, "fsdp", axis=0, tiled=True)
        return whole, ()
    rank = lax.axis_index("fsdp")
    half = block.shape[0] // 2
    if earlier:
        block = after(block, *earlier)
    from_x = cross(block, 2)
    from_y = cross(block, 4)
    diagonal = (cross(from_x[:half], 4), cross(from_y[half:], 2))
    from_core = cross(block, 1)
    both = cross(jnp.concatenate([from_x, from_y], 0), 1)
    diagonal = jnp.concatenate(diagonal, 0)
    rows = block.shape[0]
    parts = [
        block, from_core, from_x, both[:rows], from_y, both[rows:], diagonal, cross(diagonal, 1),
    ]
    return place(parts, rank), (from_x, from_y)


def scatter_plane(whole, earlier=()):
    count = lax.axis_size("fsdp")
    if count != 8:
        return lax.psum_scatter(whole, "fsdp", scatter_dimension=0, tiled=True)
    rank = lax.axis_index("fsdp")
    rows = whole.shape[0] // count
    half = whole.shape[1] // 2
    if earlier:
        whole = after(whole, *earlier)

    def part(k):
        return lax.dynamic_slice_in_dim(whole, (rank ^ k) * rows, rows, 0)

    arrived = cross(jnp.concatenate([part(1), part(3), part(5), part(7)], 0), 1)
    own, to_x, to_y, to_both = [
        add_low(part(2 * i), arrived[i * rows : (i + 1) * rows]) for i in range(4)
    ]
    got_x = cross(jnp.concatenate([to_x[:, :half], to_both[:, :half]], 0), 2)
    got_y = cross(jnp.concatenate([to_y[:, half:], to_both[:, half:]], 0), 4)
    last_y = cross(add_low(to_y[:, :half], got_x[rows:]), 4)
    last_x = cross(add_low(to_x[:, half:], got_y[rows:]), 2)
    return jnp.concatenate(
        [
            add_low(own[:, :half], got_x[:rows], last_y),
            add_low(own[:, half:], got_y[:rows], last_x),
        ],
        1,
    )


def chain_step(up, down, step):
    count = lax.axis_size("seq")
    up = lax.ppermute(up, "seq", [(i, i + 1) for i in range(step - 1, count - 1)])
    down = lax.ppermute(down, "seq", [(i, i - 1) for i in range(1, count - step + 1)])
    return up, down


def gather_seq(block, pause=None):
    count = lax.axis_size("seq")
    rank = lax.axis_index("seq")
    up, down = block, block
    ups, downs = [], []
    for step in range(1, count):
        if pause is not None and step == count - 1:
            up, down = pause(up), pause(down)
        up, down = chain_step(up, down, step)
        ups.append(up)
        downs.append(down)
    rest = [jnp.where(rank >= j, ups[j - 1], downs[count - j - 1]) for j in range(1, count)]
    return [block] + rest


def scatter_seq(parts, earlier=()):
    count = lax.axis_size("seq")
    up, down = None, None
    for step in range(1, count):
        send_up = parts[step] if up is None else add_low(parts[step], up)
        send_down = parts[count - step] if down is None else add_low(parts[count - step], down)
        if up is None and earlier:
            send_up = after(send_up, *earlier)
            send_down = after(send_down, *earlier)
        up = lax.ppermute(send_up, "seq", [(i, i + 1) for i in range(min(step, count - 1))])
        down = lax.ppermute(
            send_down, "seq", [(i, i - 1) for i in range(count - 1, max(count - 1 - step, 0), -1)]
        )
    return parts[0].astype(jnp.float32) + up.astype(jnp.float32) + down.astype(jnp.float32)


def exchange_seq(whole):
    count = lax.axis_size("seq")
    rank = lax.axis_index("seq")
    rows = whole.shape[0] // count

    def part(step):
        return lax.dynamic_slice_in_dim(whole, ((rank + step) % count) * rows, rows, 0)

    return [part(0)] + [shift(part(step), step) for step in range(1, count)]


def attend_kernel(query, key, value, bias, out, logsum):
    scale = HEAD_DIM ** (-0.5)
    raw = lax.dot_general(
        key[...], query[...], (((1,), (1,)), ((), ())), preferred_element_type=jnp.float32
    )
    scores = raw * scale + bias[...]
    top = jnp.max(scores, 0, keepdims=True)
    expo = jnp.exp(scores - top)
    total = jnp.sum(expo, 0, keepdims=True)
    probs = (expo * (1.0 / total)).astype(jnp.bfloat16)
    turned = lax.dot_general(
        value[...], probs, (((0,), (0,)), ((), ())), preferred_element_type=jnp.float32
    )
    out[...] = turned.T.astype(jnp.bfloat16)
    logsum[...] = jnp.broadcast_to(top + jnp.log(total), logsum.shape)


def attend(queries, paired, bias):
    rows, width = queries.shape
    group = paired.shape[0]
    repeat = HEADS // KV_HEADS
    return pl.pallas_call(
        attend_kernel,
        grid=(HEADS,),
        in_specs=[
            pl.BlockSpec((rows, HEAD_DIM), lambda h: (0, h)),
            pl.BlockSpec((group, HEAD_DIM), lambda h: (0, h // repeat)),
            pl.BlockSpec((group, HEAD_DIM), lambda h: (0, KV_HEADS + h // repeat)),
            pl.BlockSpec((group, rows), lambda h: (0, 0)),
        ],
        out_specs=[
            pl.BlockSpec((rows, HEAD_DIM), lambda h: (0, h)),
            pl.BlockSpec((8, rows), lambda h: (h, 0)),
        ],
        out_shape=[
            jax.ShapeDtypeStruct((rows, width), jnp.bfloat16),
            jax.ShapeDtypeStruct((8 * HEADS, rows), jnp.float32),
        ],
        compiler_params=pltpu.CompilerParams(vmem_limit_bytes=48 * 2**20),
        cost_estimate=pl.CostEstimate(
            flops=4 * HEADS * rows * group * HEAD_DIM * 3, bytes_accessed=4 * 2**20, transcendentals=HEADS * rows * group
        ),
        name="attend",
    )(queries, paired, paired, bias)


def attend_back_kernel(query, key, value, bias, logsum, grad, d_query, d_key, d_value):
    scale = HEAD_DIM ** (-0.5)
    repeat = HEADS // KV_HEADS
    raw = lax.dot_general(
        key[...], query[...], (((1,), (1,)), ((), ())), preferred_element_type=jnp.float32
    )
    probs = jnp.exp(raw * scale + bias[...] - logsum[0:1])
    d_probs = lax.dot_general(
        value[...], grad[...], (((1,), (1,)), ((), ())), preferred_element_type=jnp.float32
    )
    delta = jnp.sum(probs * d_probs, 0, keepdims=True)
    d_score = (probs * (d_probs - delta)).astype(jnp.bfloat16)
    turned = lax.dot_general(
        key[...], d_score, (((0,), (0,)), ((), ())), preferred_element_type=jnp.float32
    )
    d_query[...] = (turned * scale).T.astype(jnp.bfloat16)
    key_part = jnp.dot(d_score, query[...], preferred_element_type=jnp.float32) * scale
    value_part = jnp.dot(
        probs.astype(jnp.bfloat16), grad[...], preferred_element_type=jnp.float32
    )

    @pl.when(pl.program_id(0) % repeat == 0)
    def _():
        d_key[...] = key_part
        d_value[...] = value_part

    @pl.when(pl.program_id(0) % repeat != 0)
    def _():
        d_key[...] += key_part
        d_value[...] += value_part


def attend_back(queries, paired, bias, logsum, grads):
    rows, width = queries.shape
    group = paired.shape[0]
    repeat = HEADS // KV_HEADS
    return pl.pallas_call(
        attend_back_kernel,
        grid=(HEADS,),
        in_specs=[
            pl.BlockSpec((rows, HEAD_DIM), lambda h: (0, h)),
            pl.BlockSpec((group, HEAD_DIM), lambda h: (0, h // repeat)),
            pl.BlockSpec((group, HEAD_DIM), lambda h: (0, KV_HEADS + h // repeat)),
            pl.BlockSpec((group, rows), lambda h: (0, 0)),
            pl.BlockSpec((8, rows), lambda h: (h, 0)),
            pl.BlockSpec((rows, HEAD_DIM), lambda h: (0, h)),
        ],
        out_specs=[
            pl.BlockSpec((rows, HEAD_DIM), lambda h: (0, h)),
            pl.BlockSpec((group, HEAD_DIM), lambda h: (0, h // repeat)),
            pl.BlockSpec((group, HEAD_DIM), lambda h: (0, h // repeat)),
        ],
        out_shape=[
            jax.ShapeDtypeStruct((rows, width), jnp.bfloat16),
            jax.ShapeDtypeStruct((group, KV_HEADS * HEAD_DIM), jnp.float32),
            jax.ShapeDtypeStruct((group, KV_HEADS * HEAD_DIM), jnp.float32),
        ],
        compiler_params=pltpu.CompilerParams(vmem_limit_bytes=48 * 2**20),
        cost_estimate=pl.CostEstimate(
            flops=10 * HEADS * rows * group * HEAD_DIM * 3, bytes_accessed=8 * 2**20, transcendentals=HEADS * rows * group
        ),
        name="attend_back",
    )(queries, paired, paired, bias, logsum, grads)


def pick_kernel(starts, gate, up, out, *, unit, stride, pieces, window):
    rank = lax.axis_index("seq")
    units = unit * pieces
    padded = out.shape[1] // 2
    tile = 128
    for first in range(0, 2 * padded, tile):
        source = gate if first < padded else up
        local = first % padded
        total = jnp.zeros((out.shape[0], tile), jnp.float32)
        for f in range(pieces):
            low, high = max(local, f * unit), min(local + tile, (f + 1) * unit)
            if low >= high:
                continue
            begin = f * stride + rank * unit
            base = jnp.minimum(begin // 128, (source.shape[1] - window) // 128) * 128
            base = pl.multiple_of(base, 128)
            rows = lax.broadcasted_iota(jnp.int32, (window, tile), 0)
            columns = lax.broadcasted_iota(jnp.int32, (window, tile), 1)
            wanted = columns + (local - f * unit + begin - base)
            inside = (columns >= low - local) & (columns < high - local)
            chosen = jnp.where((rows == wanted) & inside, 1.0, 0.0).astype(jnp.bfloat16)
            total += jnp.dot(
                source[:, pl.ds(base, window)], chosen, preferred_element_type=jnp.float32
            )
        out[:, first : first + tile] = total.astype(jnp.bfloat16)


def pick_columns(w_gate, w_up, unit, stride, pieces, padded):
    rows, width = w_gate.shape
    window = 512
    return pl.pallas_call(
        lambda gate, up, out: pick_kernel(
            None, gate, up, out, unit=unit, stride=stride, pieces=pieces, window=window
        ),
        in_specs=[pl.BlockSpec(memory_space=pltpu.VMEM)] * 2,
        out_specs=pl.BlockSpec(memory_space=pltpu.VMEM),
        out_shape=jax.ShapeDtypeStruct((rows, 2 * padded), jnp.bfloat16),
        compiler_params=pltpu.CompilerParams(vmem_limit_bytes=48 * 2**20),
        cost_estimate=pl.CostEstimate(
            flops=2 * 2 * rows * 2 * padded * window, bytes_accessed=12 * 2**20, transcendentals=0
        ),
        name="pick_columns",
    )(w_gate, w_up)


def per_device(
    tokens, cotangent, lengths, balance, norm1_gain, w_query, b_query, w_key, b_key,
    w_value, b_value, w_out, norm2_gain, w_gate, w_up, w_down,
):
    seq_count = lax.axis_size("seq")
    fsdp_count = lax.axis_size("fsdp")
    seq_rank = lax.axis_index("seq")
    fsdp_rank = lax.axis_index("fsdp")
    rows_here, width = tokens.shape
    group = seq_count * rows_here
    kv_width = KV_HEADS * HEAD_DIM
    qkv_width = width + 2 * kv_width
    hidden_width = w_gate.shape[1]
    unit = hidden_width // (fsdp_count * seq_count)
    own_units = hidden_width // seq_count
    padded = -(-own_units // 256) * 256
    weight_rows = w_gate.shape[0]

    weight_qkv, first_got = gather_plane(jnp.concatenate([w_query, w_key, w_value], 1))
    small = jnp.concatenate([norm1_gain, norm2_gain, b_query, b_key, b_value], 0)[None]
    if fsdp_count == 8:
        small = place([small] + [cross(small, k) for k in range(1, 8)], fsdp_rank)
    else:
        small = lax.all_gather(small, "fsdp", axis=0, tiled=True)
    piece = norm1_gain.shape[0]
    bias_piece = b_key.shape[0]
    gain_one = small[:, :piece].reshape(-1).astype(jnp.float32)
    gain_two = small[:, piece : 2 * piece].reshape(-1).astype(jnp.float32)
    bias_qkv = jnp.concatenate(
        [
            small[:, 2 * piece : 3 * piece].reshape(-1),
            small[:, 3 * piece : 3 * piece + bias_piece].reshape(-1),
            small[:, 3 * piece + bias_piece :].reshape(-1),
        ],
        0,
    ).astype(jnp.float32)
    weight_out, second_got = gather_plane(w_out, first_got)
    picked = pick_columns(
        w_gate, w_up, unit, hidden_width // fsdp_count, fsdp_count, padded
    )
    weight_gu, third_got = gather_plane(picked, second_got)
    weight_down, _ = gather_plane(
        lax.dynamic_slice_in_dim(w_down, seq_rank * unit, unit, 0), third_got
    )
    weight_down = jnp.pad(weight_down, ((0, padded - own_units), (0, 0)))

    slot = (balance % group)[None]
    slots_all = jnp.concatenate([slot] + [shift(slot, j) for j in range(1, seq_count)], 1)[0]
    slot = slot[0]
    seq_lengths = lengths[0]
    starts = jnp.cumsum(seq_lengths) - seq_lengths
    segment = segment_of(slot, starts)
    first_row = jnp.where(segment == 0, starts[0], jnp.where(segment == 1, starts[1], starts[2]))
    cosine, sine = rope_tables(slot - first_row)
    allowed = (slots_all[:, None] <= slot[None, :]) & (slots_all[:, None] >= first_row[None, :])
    bias = jnp.where(allowed, 0.0, -1e30).astype(jnp.float32)

    inputs = tokens.astype(jnp.float32)
    normed_one = norm_piece(inputs, gain_one).astype(jnp.bfloat16)
    projected = jnp.dot(normed_one, weight_qkv, preferred_element_type=jnp.float32) + bias_qkv
    query_pre = projected[:, :width].reshape(rows_here, HEADS, HEAD_DIM)
    key_pre = projected[:, width : width + kv_width].reshape(rows_here, KV_HEADS, HEAD_DIM)
    value_pre = projected[:, width + kv_width :]
    queries = rotate(query_pre, cosine, sine).astype(jnp.bfloat16).reshape(rows_here, width)
    keys = rotate(key_pre, cosine, sine).astype(jnp.bfloat16).reshape(rows_here, kv_width)
    values = value_pre.astype(jnp.bfloat16)
    paired = jnp.concatenate([keys, values], 1)
    paired = [paired] + [shift(paired, j) for j in range(1, seq_count)]
    upstream_all = gather_seq(cotangent, lambda value: after(value, *paired[1:]))
    upstream_all = jnp.concatenate(upstream_all, 0)
    paired = jnp.concatenate(paired, 0)
    attended, logsum = attend(queries, paired, bias)
    resid = inputs + jnp.dot(attended, weight_out, preferred_element_type=jnp.float32)
    normed_two = norm_piece(resid, gain_two).astype(jnp.bfloat16)

    normed_all = jnp.concatenate(gather_seq(normed_two), 0)
    both = jnp.dot(normed_all, weight_gu, preferred_element_type=jnp.float32)
    gate = both[:, :padded]
    up = both[:, padded:]
    sigma = jax.nn.sigmoid(gate)
    activated = gate * sigma
    hidden = (activated * up).astype(jnp.bfloat16)
    d_hidden = contract_columns(upstream_all, weight_down)
    d_gate = (d_hidden * up * sigma * (1.0 + gate * (1.0 - sigma))).astype(jnp.bfloat16)
    d_up = (d_hidden * activated).astype(jnp.bfloat16)
    d_both = jnp.concatenate([d_gate, d_up], 1)
    columns = contract_columns(d_both, weight_gu).astype(jnp.bfloat16)
    columns = scatter_seq([columns[j * rows_here : (j + 1) * rows_here] for j in range(seq_count)])

    grad_down = contract_rows(hidden, upstream_all).astype(jnp.bfloat16)
    grad_down = scatter_plane(grad_down[:own_units]).astype(jnp.float32)
    grad_pair = scatter_plane(contract_rows(normed_all, d_both).astype(jnp.bfloat16))
    branch = jnp.dot(hidden, weight_down, preferred_element_type=jnp.float32).astype(jnp.bfloat16)
    branch = scatter_seq(
        [branch[j * rows_here : (j + 1) * rows_here] for j in range(seq_count)], (columns,)
    )
    layer_out = (resid + branch).astype(jnp.bfloat16)
    grad_pair = exchange_seq(grad_pair)
    own_rows = weight_rows // seq_count
    grad_pair = jnp.stack(grad_pair, 0).reshape(seq_count, own_rows, 2, padded)[..., :own_units]
    order = (seq_rank - jnp.arange(seq_count)) % seq_count
    grad_pair = grad_pair[order]
    grad_pair = grad_pair.reshape(seq_count, own_rows, 2, fsdp_count, unit)
    grad_pair = grad_pair.transpose(2, 1, 3, 0, 4).astype(jnp.float32)
    grad_pair = grad_pair.reshape(2, own_rows, hidden_width)

    _, pull_two = jax.vjp(norm_piece, resid, gain_two)
    d_resid_norm, grad_gain_two = pull_two(columns)
    d_resid = cotangent.astype(jnp.float32) + d_resid_norm
    d_branch = d_resid.astype(jnp.bfloat16)
    d_attended = contract_columns(d_branch, weight_out).astype(jnp.bfloat16)
    d_queries, d_keys, d_values = attend_back(queries, paired, bias, logsum, d_attended)
    d_paired = jnp.concatenate([d_keys, d_values], 1).astype(jnp.bfloat16)
    d_paired = [d_paired[j * rows_here : (j + 1) * rows_here] for j in range(seq_count)]
    d_paired = sum(
        part.astype(jnp.float32)
        for part in [d_paired[0]] + [shift(d_paired[j], -j) for j in range(1, seq_count)]
    )
    d_query_pre = rotate_back(
        d_queries.astype(jnp.float32).reshape(rows_here, HEADS, HEAD_DIM), cosine, sine
    ).astype(jnp.bfloat16)
    d_key_pre = rotate_back(
        d_paired[:, :kv_width].reshape(rows_here, KV_HEADS, HEAD_DIM), cosine, sine
    ).astype(jnp.bfloat16)
    d_value_pre = d_paired[:, kv_width:].astype(jnp.bfloat16)
    d_qkv = jnp.concatenate(
        [
            d_query_pre.reshape(rows_here, width),
            d_key_pre.reshape(rows_here, kv_width),
            d_value_pre,
        ],
        1,
    )
    grad_out = contract_rows(attended, d_branch).astype(jnp.bfloat16)
    grad_qkv = contract_rows(normed_one, d_qkv).astype(jnp.bfloat16)
    grad_bias = jnp.sum(d_qkv.astype(jnp.float32), 0)
    d_normed_one = contract_columns(d_qkv, weight_qkv)
    _, pull_one = jax.vjp(norm_piece, inputs, gain_one)
    d_input_norm, grad_gain_one = pull_one(d_normed_one)
    input_grad = (d_resid + d_input_norm).astype(jnp.bfloat16)

    def summed(value):
        return sum(part.astype(jnp.float32) for part in exchange_seq(scatter_plane(value)))

    grad_out = summed(grad_out)
    grad_qkv = summed(grad_qkv)
    vectors = jnp.concatenate([grad_gain_one, grad_gain_two, grad_bias], 0)
    if fsdp_count == 8:
        for bits in (1, 2, 4):
            vectors = vectors + cross(vectors, bits)
        vectors = vectors + sum(shift(vectors, j) for j in range(1, seq_count))
    else:
        vectors = lax.psum(vectors, ("fsdp", "seq"))
    own = width // (fsdp_count * seq_count)
    first = (fsdp_rank * seq_count + seq_rank) * own

    def own_part(offset):
        return lax.dynamic_slice_in_dim(vectors, offset + first, own, 0)

    biases = 2 * width
    return (
        layer_out,
        input_grad,
        own_part(0),
        grad_qkv[:, :width],
        own_part(biases),
        grad_qkv[:, width : width + kv_width],
        vectors[biases + width : biases + width + kv_width],
        grad_qkv[:, width + kv_width :],
        vectors[biases + width + kv_width :],
        grad_out,
        own_part(width),
        grad_pair[0],
        grad_pair[1],
        grad_down,
    )


def solution(mesh):
    both = P(("fsdp", "seq"), None)
    both_one = P(("fsdp", "seq"))
    placed = (
        both, both, P("fsdp", None), both_one, P("fsdp"), P("fsdp", None), P("fsdp"),
        P("fsdp", None), P("fsdp"), P("fsdp", None), P("fsdp"), P("fsdp", None), P("fsdp"),
        P("fsdp", None), P("fsdp", None), P("fsdp", None),
    )
    return jax.shard_map(
        per_device,
        mesh=mesh,
        in_specs=placed,
        out_specs=(
            both, both, both_one, both, both_one, both, P(), both, P(), both, both_one,
            both, both, both,
        ),
        check_vma=False,
    )
```

time: 1010 us -> 825 us (0.82)
  waiting for transfers between devices: 585 us -> 285 us
  starting transfers between devices: 6.67 us -> 135 us
  blocking collectives: 62 us -> 0 us
  matrix products: 179 us -> 126 us
  local copies, waits for them, and re-layouts: 111 us -> 152 us
  Pallas kernels: 0 us -> 35.6 us
  other arithmetic: 52.1 us -> 79.1 us
  between operations: 14.6 us -> 3.36 us
    reduce_scatter x9 -> x0, waiting for transfers between devices: 358 us -> none  [the longest x1 102 us: per_device(): lax.psum_scatter(contract_rows(normed_all, d_both).astype(jnp.bfloat16),...]
    ppermute x0 -> x103, waiting for transfers between devices: none -> 285 us  [the longest x58 157 us: cross(): return lax.ppermute(value, 'fsdp', [(i, i ^ bits) for i in range(count)])]
    all_gather x7 -> x0, waiting for transfers between devices: 225 us -> none  [the longest x1 78.1 us: per_device(): lax.all_gather(jnp.concatenate([own_columns(w_gate), own_columns(w_up)],...]
    ppermute x0 -> x103, starting transfers between devices: none -> 135 us  [the longest x58 45.7 us: cross(): return lax.ppermute(value, 'fsdp', [(i, i ^ bits) for i in range(count)])]
    psum x1 -> x0, blocking collectives: 40.3 us -> none  [per_device(): lax.psum(jnp.concatenate([grad_gain_one, grad_gain_two, grad_bias], 0), (...]
    dynamic_update_slice x0 -> x39, local copies, waits for them, and re-layouts: none -> 40 us  [place(): whole = lax.dynamic_update_slice_in_dim(whole, part, (rank ^ k) * rows, 0)]
    reshape x9 -> x0, local copies, waits for them, and re-layouts: 37.6 us -> none  [the longest x2 22.6 us: own_columns(): cut = weight.reshape(weight_rows, fsdp_count, seq_count, unit)]
    pallas_call x0 -> x3, Pallas kernels: none -> 35.6 us  [the longest x1 17.9 us: attend_back(): pl.pallas_call(attend_back_kernel, grid=(HEADS,), in_specs=[pl.BlockSpec(...]
  transfers between devices with their start and end apart: 17 -> 103, of which waited for: 15 -> 36; matrix products, arithmetic and copies ran while one was open for 21% -> 30% of each run, Pallas kernels for 0% -> 4%
where the time goes in v2:
time: 825 us; the launch traced here: 816 us
  waiting for transfers between devices  285 us (35%)
  local copies, waits for them, and re-layouts  152 us (18%)
  starting transfers between devices  135 us (16%)
  matrix products  126 us (15%)
  other arithmetic  79.1 us (10%)
  Pallas kernels  35.6 us (4%)
    ppermute x58, waiting for transfers between devices, cross(): return lax.ppermute(value, 'fsdp', [(i, i ^ bits) for i in range(count)])  157 us
    ppermute x6, waiting for transfers between devices, chain_step(): lax.ppermute(down, 'seq', [(i, i - 1) for i in range(1, count - step + 1)])  56.3 us
    dot_general x4, matrix products, contract_columns(): lax.dot_general(left, right, (((1,), (1,)), ((), ())), preferred_element_...  50.2 us
    ppermute x21, waiting for transfers between devices, shift(): lax.ppermute(value, 'seq', [(i, (i + step) % count) for i in range(count)])  46.5 us
    ppermute x58, starting transfers between devices, cross(): return lax.ppermute(value, 'fsdp', [(i, i ^ bits) for i in range(count)])  45.7 us
    dynamic_update_slice x39, local copies, waits for them, and re-layouts, place(): whole = lax.dynamic_update_slice_in_dim(whole, part, (rank ^ k) * rows, 0)  40 us
    ppermute x21, starting transfers between devices, shift(): lax.ppermute(value, 'seq', [(i, (i + step) % count) for i in range(count)])  36.7 us
    dot_general x4, matrix products, contract_rows(): lax.dot_general(left, right, (((0,), (0,)), ((), ())), preferred_element_...  36.5 us
  transfers between devices with their start and end apart: 103, of which 36 were waited for; matrix products, arithmetic and copies ran while one was open for 30% of the time, Pallas kernels for 4%

profile of v2, /device:TPU:0, one launch (start us, length us, event | category | flops | bytes accessed | tf_op | source)
XLA Modules:
  0.0 815.8 jit_solution(14478019812330044227)
XLA Ops:
  5.6 5.1 collective-permute-start.19
  18.2 3.4 concatenate.142
  28.2 3.0 copy.31
  33.5 3.4 broadcast_in_dim.36
  41.0 5.2 pick_columns.1
  56.4 14.6 %collective-permute-done.4 = bf16[1,640]{1,0:T(2,128)(2,1)S(1)} collective-permute-done((bf16[1,640]{1,0:T(2,128)(2,1)S(1)}, bf16[1,640]{1,0:T(2,128)(2,1)S(1)}, u32[]{:S(2)}, u32[]{:S(2)}) %collective-permute-start.4) | collective-permute-done | bytes 1312 | tf_op jit(solution)/shard_map/ppermute | solution.py:68
  71.8 5.3 collective-permute-start.47
  93.5 10.5 %collective-permute-done.12 = bf16[96,2048]{1,0:T(8,128)(2,1)S(1)} collective-permute-done((bf16[96,2048]{1,0:T(8,128)(2,1)S(1)}, bf16[96,2048]{1,0:T(8,128)(2,1)S(1)}, u32[]{:S(2)}, u32[]{:S(2)}) %collective-permute-start.12) | collective-permute-done | bytes 393248 | tf_op jit(solution)/shard_map/ppermute | solution.py:68
  113.3 5.9 broadcast_in_dim.72
  122.1 8.4 %collective-permute-done.49 = bf16[256,1536]{1,0:T(8,128)(2,1)} collective-permute-done((bf16[256,1536]{1,0:T(8,128)(2,1)}, bf16[256,1536]{1,0:T(8,128)(2,1)}, u32[]{:S(2)}, u32[]{:S(2)}) %collective-permute-start.49) | collective-permute-done | bytes 786464 | tf_op jit(solution)/shard_map/ppermute | solution.py:138
  134.0 4.9 collective-permute-done.25
  149.2 4.6 convolution_add_fusion
  168.9 3.0 copy.33
  188.1 12.5 %attend.1 = (bf16[256,1536]{1,0:T(8,128)(2,1)S(1)}, f32[96,256]{1,0:T(8,128)S(1)}) custom-call(bf16[256,1536]{1,0:T(8,128)(2,1)S(1)} %add_convert_fusion.21.query, bf16[1024,512]{1,0:T(8,128)(2,1)S(1)} %pad_maximum_fusion.21.key.value, bf16[1024,512]{1,0:T(8,128)(2,1)S(1)} %pad_maximum_fusion.21.key.value, f32[1024,256]{1,0:T(8,128)S(1)} %and_select_fusion.bias), custom_call_target="tpu_custom_call" | custom-call | flops 4831838208 | bytes 4194304 | tf_op jit(solution)/shard_map/attend/pallas_call | solution.py:205
  200.6 4.1 multiply_reduce_fusion.2
  207.6 14.6 %collective-permute-done.34 = bf16[192,4608]{1,0:T(8,128)(2,1)S(1)} collective-permute-done((bf16[192,4608]{1,0:T(8,128)(2,1)S(1)}, bf16[192,4608]{1,0:T(8,128)(2,1)S(1)}, u32[]{:S(2)}, u32[]{:S(2)}) %collective-permute-start.34) | collective-permute-done | bytes 1769504 | tf_op jit(solution)/shard_map/ppermute | solution.py:68
  230.5 3.3 broadcast_in_dim.73
  238.2 4.5 collective-permute-done.50
  247.9 8.9 %collective-permute-done.42 = bf16[280,1536]{1,0:T(8,128)(2,1)S(1)} collective-permute-done((bf16[280,1536]{1,0:T(8,128)(2,1)S(1)}, bf16[280,1536]{1,0:T(8,128)(2,1)S(1)}, u32[]{:S(2)}, u32[]{:S(2)}) %collective-permute-start.42) | collective-permute-done | bytes 860192 | tf_op jit(solution)/shard_map/ppermute | solution.py:68
  260.1 7.2 collective-permute-done.28
  268.1 6.9 collective-permute-done.37
  279.1 16.5 %collective-permute-done.29 = bf16[256,1536]{1,0:T(8,128)(2,1)S(1)} collective-permute-done((bf16[256,1536]{1,0:T(8,128)(2,1)S(1)}, bf16[256,1536]{1,0:T(8,128)(2,1)S(1)}, u32[]{:S(2)}, u32[]{:S(2)}) %collective-permute-start.29) | collective-permute-done | bytes 786464 | tf_op jit(solution)/shard_map/ppermute | solution.py:138
  302.5 19.6 %collective-permute-done.30 = bf16[256,1536]{1,0:T(8,128)(2,1)S(1)} collective-permute-done((bf16[256,1536]{1,0:T(8,128)(2,1)S(1)}, bf16[256,1536]{1,0:T(8,128)(2,1)S(1)}, u32[]{:S(2)}, u32[]{:S(2)}) %collective-permute-start.30) | collective-permute-done | bytes 786464 | tf_op jit(solution)/shard_map/ppermute | solution.py:138
  324.4 5.0 copy-done.15
  329.4 17.8 %fusion.24 = f32[1024,4608]{1,0:T(8,128)} fusion(bf16[1536,4608]{1,0:T(8,128)(2,1)S(1)} %constant_dynamic-update-slice_fusion.6, bf16[256,1536]{1,0:T(8,128)(2,1)S(1)} %broadcast_select_fusion.1, bf16[256,1536]{1,0:T(8,128)(2,1)S(1)} %broadcast_select_fusion.3, bf16[256,1536]{1,0:T(8,128)(2,1)S(1)} %broadcast_select_fusion.5, ...), kind=kOutput, calls=%fused_computation.166 | convolution fusion | flops 14508097536 | bytes 36175872 | tf_op jit(solution)/shard_map/dot_general | solution.py:416
  347.3 20.4 %multiply_convert_fusion.1 = (bf16[1024,2304]{1,0:T(8,128)(2,1)}, bf16[1024,2304]{1,0:T(8,128)(2,1)}, bf16[1024,2304]{1,0:T(8,128)(2,1)}) fusion(f32[1024,4608]{1,0:T(8,128)} %fusion.24, bf16[2240,1536]{1,0:T(8,128)(2,1)} %constant_dynamic-update-slice_fusion, bf16[256,1536]{1,0:T(8,128)(2,1)S(1)} %copy-done.52, bf16[256,1536]{1,0:T(8,128)(2,1)S(1)} %copy-done.51, ...), kind=kOutput, calls=%fused_computation.5 | convolution fusion | flops 7295729664 | bytes 43057152 | tf_op jit(solution)/shard_map/dot_general | solution.py:53
  367.6 20.3 %fusion.6 = bf16[1024,1536]{1,0:T(8,128)(2,1)S(1)} fusion(bf16[1536,4608]{1,0:T(8,128)(2,1)} %copy-done.15, bf16[1024,2304]{1,0:T(8,128)(2,1)} %get-tuple-element.49, bf16[1024,2304]{1,0:T(8,128)(2,1)} %get-tuple-element.48), kind=kOutput, calls=%fused_computation.18 | convolution fusion | flops 14515961856 | bytes 26738688 | tf_op jit(solution)/shard_map/dot_general | solution.py:53
  390.5 12.4 %fusion.7 = bf16[1024,1536]{1,0:T(8,128)(2,1)} fusion(bf16[1024,2304]{1,0:T(8,128)(2,1)} %get-tuple-element.54, bf16[2240,1536]{1,0:T(8,128)(2,1)} %constant_dynamic-update-slice_fusion), kind=kOutput, calls=%fused_computation.19 | convolution fusion | flops 7249330176 | bytes 14745600 | tf_op jit(solution)/shard_map/dot_general | solution.py:432
  403.0 3.5 collective-permute-done.53
  407.9 4.4 collective-permute-start.54
  414.0 9.5 %fusion.23 = bf16[2304,1536]{1,0:T(8,128)(2,1)} fusion(bf16[1024,2304]{1,0:T(8,128)(2,1)S(1)} %bitcast.73, bf16[256,1536]{1,0:T(8,128)(2,1)S(1)} %copy-done.52, bf16[256,1536]{1,0:T(8,128)(2,1)S(1)} %copy-done.51, bf16[256,1536]{1,0:T(8,128)(2,1)S(1)} %copy-done.53, bf16[256,1536]{1,0:T(8,128)(2,1)S(1)} %copy-done.62), kind=kOutput, calls=%fused_computation.165 | convolution fusion | flops 7260340224 | bytes 14942208 | tf_op jit(solution)/shard_map/dot_general | solution.py:47
  423.5 3.4 slice.732
  432.5 6.0 collective-permute-start.55
  442.9 9.5 %collective-permute-done.58 = bf16[256,1536]{1,0:T(8,128)(2,1)S(1)} collective-permute-done((bf16[256,1536]{1,0:T(8,128)(2,1)S(1)}, bf16[256,1536]{1,0:T(8,128)(2,1)S(1)}, u32[]{:S(2)}, u32[]{:S(2)}) %collective-permute-start.58) | collective-permute-done | bytes 786464 | tf_op jit(solution)/shard_map/ppermute | solution.py:167
  455.2 5.3 collective-permute-start.59
  462.3 22.1 %convolution_convert_fusion = bf16[1536,4608]{1,0:T(8,128)(2,1)} fusion(bf16[1024,2304]{1,0:T(8,128)(2,1)} %get-tuple-element.49, bf16[1024,2304]{1,0:T(8,128)(2,1)} %get-tuple-element.48, bf16[256,1536]{1,0:T(8,128)(2,1)S(1)} %copy-done.57, bf16[256,1536]{1,0:T(8,128)(2,1)S(1)} %copy-done.55, bf16[256,1536]{1,0:T(8,128)(2,1)} %copy-done.58, ...), kind=kOutput, calls=%fused_computation.1 | convolution fusion | flops 14534049792 | bytes 26738688 | tf_op jit(solution)/shard_map/dot_general | solution.py:47
  484.4 3.7 constant_dynamic-slice_fusion.7
  492.1 4.9 add_convert_fusion.11
  499.3 6.2 collective-permute-done.60
  507.2 7.7 collective-permute-start.61
  514.9 3.5 pad_maximum_fusion.1
  522.5 3.5 collective-permute-done.64
  529.1 4.4 convolution_convert_fusion.3.grad
  533.5 17.9 %attend_back.1 = (bf16[256,1536]{1,0:T(8,128)(2,1)S(1)}, f32[1024,256]{1,0:T(8,128)S(1)}, f32[1024,256]{1,0:T(8,128)S(1)}) custom-call(bf16[256,1536]{1,0:T(8,128)(2,1)S(1)} %copy-done.11, bf16[1024,512]{1,0:T(8,128)(2,1)S(1)} %copy-done.9, bf16[1024,512]{1,0:T(8,128)(2,1)S(1)} %copy-done.9, f32[1024,256]{1,0:T(8,128)} %copy-done.7, ...), custom_call_target="tpu_custom_call" | custom-call | flops 12079595520 | bytes 8388608 | tf_op jit(solution)/shard_map/attend_back/pallas_call | solution.py:266
  579.6 5.1 fusion.13
  594.0 4.0 collective-permute-start.73
  600.4 3.1 collective-permute-done.71
  604.8 4.3 add_convert_fusion.3
  615.0 12.8 %collective-permute-done.85 = bf16[384,768]{1,0:T(8,128)(2,1)S(1)} collective-permute-done((bf16[384,768]{1,0:T(8,128)(2,1)S(1)}, bf16[384,768]{1,0:T(8,128)(2,1)S(1)}, u32[]{:S(2)}, u32[]{:S(2)}) %collective-permute-start.85) | collective-permute-done | bytes 589856 | tf_op jit(solution)/shard_map/ppermute | solution.py:68
  632.3 5.6 collective-permute-done.86
  637.9 30.8 %collective-permute-done.84 = bf16[192,768]{1,0:T(8,128)(2,1)S(1)} collective-permute-done((bf16[192,768]{1,0:T(8,128)(2,1)S(1)}, bf16[192,768]{1,0:T(8,128)(2,1)S(1)}, u32[]{:S(2)}, u32[]{:S(2)}) %collective-permute-start.84) | collective-permute-done | bytes 294944 | tf_op jit(solution)/shard_map/ppermute | solution.py:68
  668.9 3.3 collective-permute-start.89
  678.5 16.1 %collective-permute-done.77 = bf16[384,1024]{1,0:T(8,128)(2,1)S(1)} collective-permute-done((bf16[384,1024]{1,0:T(8,128)(2,1)S(1)}, bf16[384,1024]{1,0:T(8,128)(2,1)S(1)}, u32[]{:S(2)}, u32[]{:S(2)}) %collective-permute-start.77) | collective-permute-done | bytes 786464 | tf_op jit(solution)/shard_map/ppermute | solution.py:68
  700.1 23.5 %collective-permute-done.78 = bf16[192,1024]{1,0:T(8,128)(2,1)S(1)} collective-permute-done((bf16[192,1024]{1,0:T(8,128)(2,1)S(1)}, bf16[192,1024]{1,0:T(8,128)(2,1)S(1)}, u32[]{:S(2)}, u32[]{:S(2)}) %collective-permute-start.78) | collective-permute-done | bytes 393248 | tf_op jit(solution)/shard_map/ppermute | solution.py:68
  724.4 3.3 collective-permute-start.81
  730.0 3.2 collective-permute-start.97
  737.1 6.3 collective-permute-done.80
  745.0 6.1 collective-permute-done.97
  752.2 28.2 %collective-permute-done.96 = bf16[48,4608]{1,0:T(8,128)(2,1)} collective-permute-done((bf16[48,4608]{1,0:T(8,128)(2,1)S(1)}, bf16[48,4608]{1,0:T(8,128)(2,1)}, u32[]{:S(2)}, u32[]{:S(2)}) %collective-permute-start.96) | collective-permute-done | bytes 442400 | tf_op jit(solution)/shard_map/ppermute | solution.py:73
  786.3 5.4 gather_fusion
  791.7 7.2 reshape.251
  798.9 5.4 copy.48
  807.3 4.3 squeeze.24
  811.5 3.9 squeeze.25
  (571 shorter events, 264.0 us)
Async XLA Ops:
  5.6 42.8 %collective-permute-start.19 = (s32[1,256]{1,0:T(1,128)S(1)}, s32[1,256]{1,0:T(1,128)S(1)}, u32[]{:S(2)}, u32[]{:S(2)}) collective-permute-start(s32[1,256]{1,0:T(1,128)S(1)} %bitcast.67), channel_id=1, source_target_pairs={{0,3},{1,0},{2,1},{3,2},{4,7},{5,4},{6,5},{7,6},{8,11},{9,8},{10,9... | collective-permute-start | bytes 3080 | tf_op jit(solution)/shard_map/ppermute | solution.py:73
  10.7 38.2 %collective-permute-start.18 = (s32[1,256]{1,0:T(1,128)S(1)}, s32[1,256]{1,0:T(1,128)S(1)}, u32[]{:S(2)}, u32[]{:S(2)}) collective-permute-start(s32[1,256]{1,0:T(1,128)S(1)} %bitcast.68), channel_id=1, source_target_pairs={{0,2},{1,3},{2,0},{3,1},{4,6},{5,7},{6,4},{7,5},{8,10},{9,11},{10,... | collective-permute-start | bytes 3080 | tf_op jit(solution)/shard_map/ppermute | solution.py:73
  10.7 39.3 %collective-permute-start.17 = (s32[1,256]{1,0:T(1,128)S(1)}, s32[1,256]{1,0:T(1,128)S(1)}, u32[]{:S(2)}, u32[]{:S(2)}) collective-permute-start(s32[1,256]{1,0:T(1,128)S(1)} %bitcast.69), channel_id=1, source_target_pairs={{0,1},{1,2},{2,3},{3,0},{4,5},{5,6},{6,7},{7,4},{8,9},{9,10},{10,1... | collective-permute-start | bytes 3080 | tf_op jit(solution)/shard_map/ppermute | solution.py:73
  16.7 62.4 %collective-permute-start.8 = (bf16[192,2048]{1,0:T(8,128)(2,1)}, bf16[192,2048]{1,0:T(8,128)(2,1)}, u32[]{:S(2)}, u32[]{:S(2)}) collective-permute-start(bf16[192,2048]{1,0:T(8,128)(2,1)} %constant_dynamic-update-slice_fusion.24), channel_id=1, source_target_pairs={{0,8},{4,12},{8,0},{12,4},{16,24},{20,28},{24,16},{28,20},{1,9},{5... | collective-permute-start | bytes 2359304 | tf_op jit(solution)/shard_map/ppermute | solution.py:68
  21.6 30.0 %collective-permute-start = (bf16[1,640]{1,0:T(2,128)(2,1)S(1)}, bf16[1,640]{1,0:T(2,128)(2,1)S(1)}, u32[]{:S(2)}, u32[]{:S(2)}) collective-permute-start(bf16[1,640]{1,0:T(2,128)(2,1)S(1)} %broadcast_in_dim.35), channel_id=1, source_target_pairs={{0,4},{4,0},{8,12},{12,8},{16,20},{20,16},{24,28},{28,24},{1,5},{5... | collective-permute-start | bytes 3848 | tf_op jit(solution)/shard_map/ppermute | solution.py:68
  51.6 29.1 %collective-permute-start.9 = (bf16[192,2048]{1,0:T(8,128)(2,1)}, bf16[192,2048]{1,0:T(8,128)(2,1)S(1)}, u32[]{:S(2)}, u32[]{:S(2)}) collective-permute-start(bf16[192,2048]{1,0:T(8,128)(2,1)} %constant_dynamic-update-slice_fusion.24), channel_id=1, source_target_pairs={{0,16},{4,20},{8,24},{12,28},{16,0},{20,4},{24,8},{28,12},{1,17},{... | collective-permute-start | bytes 2359304 | tf_op jit(solution)/shard_map/ppermute | solution.py:68
  54.4 22.7 %collective-permute-start.6 = (bf16[1,640]{1,0:T(2,128)(2,1)S(1)}, bf16[1,640]{1,0:T(2,128)(2,1)S(1)}, u32[]{:S(2)}, u32[]{:S(2)}) collective-permute-start(bf16[1,640]{1,0:T(2,128)(2,1)S(1)} %broadcast_in_dim.35), channel_id=1, source_target_pairs={{0,28},{4,24},{8,20},{12,16},{16,12},{20,8},{24,4},{28,0},{1,29},{... | collective-permute-start | bytes 3848 | tf_op jit(solution)/shard_map/ppermute | solution.py:68
  71.8 33.7 %collective-permute-start.47 = (bf16[256,1536]{1,0:T(8,128)(2,1)}, bf16[256,1536]{1,0:T(8,128)(2,1)}, u32[]{:S(2)}, u32[]{:S(2)}) collective-permute-start(bf16[256,1536]{1,0:T(8,128)(2,1)} %param.17), channel_id=1, source_target_pairs={{0,1},{1,2},{2,3},{4,5},{5,6},{6,7},{8,9},{9,10},{10,11},{12,13},{... | collective-permute-start | bytes 2359304 | tf_op jit(solution)/shard_map/ppermute | solution.py:137
  77.1 28.9 %collective-permute-start.48 = (bf16[256,1536]{1,0:T(8,128)(2,1)}, bf16[256,1536]{1,0:T(8,128)(2,1)}, u32[]{:S(2)}, u32[]{:S(2)}) collective-permute-start(bf16[256,1536]{1,0:T(8,128)(2,1)} %param.17), channel_id=1, source_target_pairs={{1,0},{2,1},{3,2},{5,4},{6,5},{7,6},{9,8},{10,9},{11,10},{13,12},{... | collective-permute-start | bytes 2359304 | tf_op jit(solution)/shard_map/ppermute | solution.py:138
  80.7 26.9 %collective-permute-start.21 = (bf16[192,1536]{1,0:T(8,128)(2,1)}, bf16[192,1536]{1,0:T(8,128)(2,1)S(1)}, u32[]{:S(2)}, u32[]{:S(2)}) collective-permute-start(bf16[192,1536]{1,0:T(8,128)(2,1)} %param.27), channel_id=1, source_target_pairs={{0,8},{4,12},{8,0},{12,4},{16,24},{20,28},{24,16},{28,20},{1,9},{5... | collective-permute-start | bytes 1769480 | tf_op jit(solution)/shard_map/ppermute | solution.py:68
  105.5 34.1 %collective-permute-start.10 = (bf16[384,2048]{1,0:T(8,128)(2,1)}, bf16[384,2048]{1,0:T(8,128)(2,1)}, u32[]{:S(2)}, u32[]{:S(2)}) collective-permute-start(bf16[384,2048]{1,0:T(8,128)(2,1)} %pad_maximum_fusion.18), channel_id=1, source_target_pairs={{0,4},{4,0},{8,12},{12,8},{16,20},{20,16},{24,28},{28,24},{1,5},{5... | collective-permute-start | bytes 4718600 | tf_op jit(solution)/shard_map/ppermute | solution.py:68
  107.6 22.9 %collective-permute-start.49 = (bf16[256,1536]{1,0:T(8,128)(2,1)}, bf16[256,1536]{1,0:T(8,128)(2,1)}, u32[]{:S(2)}, u32[]{:S(2)}) collective-permute-start(bf16[256,1536]{1,0:T(8,128)(2,1)} %collective-permute-done.48), channel_id=1, source_target_pairs={{1,0},{2,1},{5,4},{6,5},{9,8},{10,9},{13,12},{14,13},{17,16},{18,1... | collective-permute-start | bytes 2359304 | tf_op jit(solution)/shard_map/ppermute | solution.py:138
  109.1 37.9 %collective-permute-start.13 = (bf16[192,2048]{1,0:T(8,128)(2,1)}, bf16[192,2048]{1,0:T(8,128)(2,1)}, u32[]{:S(2)}, u32[]{:S(2)}) collective-permute-start(bf16[192,2048]{1,0:T(8,128)(2,1)} %constant_dynamic-update-slice_fusion.27), channel_id=1, source_target_pairs={{0,4},{4,0},{8,12},{12,8},{16,20},{20,16},{24,28},{28,24},{1,5},{5... | collective-permute-start | bytes 2359304 | tf_op jit(solution)/shard_map/ppermute | solution.py:68
  111.1 113.5 %collective-permute-start.33 = (bf16[192,4608]{1,0:T(8,128)(2,1)S(1)}, bf16[192,4608]{1,0:T(8,128)(2,1)}, u32[]{:S(2)}, u32[]{:S(2)}) collective-permute-start(bf16[192,4608]{1,0:T(8,128)(2,1)S(1)} %copy-done.3), channel_id=1, source_target_pairs={{0,4},{4,0},{8,12},{12,8},{16,20},{20,16},{24,28},{28,24},{1,5},{5... | collective-permute-start | bytes 5308424 | tf_op jit(solution)/shard_map/ppermute | solution.py:68
  133.2 41.5 %collective-permute-start.23 = (bf16[384,1536]{1,0:T(8,128)(2,1)}, bf16[384,1536]{1,0:T(8,128)(2,1)}, u32[]{:S(2)}, u32[]{:S(2)}) collective-permute-start(bf16[384,1536]{1,0:T(8,128)(2,1)} %pad_maximum_fusion.20), channel_id=1, source_target_pairs={{0,4},{4,0},{8,12},{12,8},{16,20},{20,16},{24,28},{28,24},{1,5},{5... | collective-permute-start | bytes 3538952 | tf_op jit(solution)/shard_map/ppermute | solution.py:68
  139.6 42.0 %collective-permute-start.26 = (bf16[192,1536]{1,0:T(8,128)(2,1)}, bf16[192,1536]{1,0:T(8,128)(2,1)}, u32[]{:S(2)}, u32[]{:S(2)}) collective-permute-start(bf16[192,1536]{1,0:T(8,128)(2,1)} %constant_dynamic-update-slice_fusion.29), channel_id=1, source_target_pairs={{0,4},{4,0},{8,12},{12,8},{16,20},{20,16},{24,28},{28,24},{1,5},{5... | collective-permute-start | bytes 1769480 | tf_op jit(solution)/shard_map/ppermute | solution.py:68
  160.2 23.9 %collective-permute-start.16 = (bf16[256,512]{1,0:T(8,128)(2,1)}, bf16[256,512]{1,0:T(8,128)(2,1)}, u32[]{:S(2)}, u32[]{:S(2)}) collective-permute-start(bf16[256,512]{1,0:T(8,128)(2,1)} %pad_maximum_fusion.35), channel_id=1, source_target_pairs={{0,3},{1,0},{2,1},{3,2},{4,7},{5,4},{6,5},{7,6},{8,11},{9,8},{10,9... | collective-permute-start | bytes 786440 | tf_op jit(solution)/shard_map/ppermute | solution.py:73
  161.1 25.9 %collective-permute-start.15 = (bf16[256,512]{1,0:T(8,128)(2,1)}, bf16[256,512]{1,0:T(8,128)(2,1)}, u32[]{:S(2)}, u32[]{:S(2)}) collective-permute-start(bf16[256,512]{1,0:T(8,128)(2,1)} %pad_maximum_fusion.35), channel_id=1, source_target_pairs={{0,2},{1,3},{2,0},{3,1},{4,6},{5,7},{6,4},{7,5},{8,10},{9,11},{10,... | collective-permute-start | bytes 786440 | tf_op jit(solution)/shard_map/ppermute | solution.py:73
  181.6 40.5 %collective-permute-start.34 = (bf16[192,4608]{1,0:T(8,128)(2,1)S(1)}, bf16[192,4608]{1,0:T(8,128)(2,1)S(1)}, u32[]{:S(2)}, u32[]{:S(2)}) collective-permute-start(bf16[192,4608]{1,0:T(8,128)(2,1)S(1)} %copy-done.3), channel_id=1, source_target_pairs={{0,8},{4,12},{8,0},{12,4},{16,24},{20,28},{24,16},{28,20},{1,9},{5... | collective-permute-start | bytes 5308424 | tf_op jit(solution)/shard_map/ppermute | solution.py:68
  184.2 40.2 %collective-permute-start.35 = (bf16[192,4608]{1,0:T(8,128)(2,1)S(1)}, bf16[192,4608]{1,0:T(8,128)(2,1)S(1)}, u32[]{:S(2)}, u32[]{:S(2)}) collective-permute-start(bf16[192,4608]{1,0:T(8,128)(2,1)S(1)} %copy-done.3), channel_id=1, source_target_pairs={{0,16},{4,20},{8,24},{12,28},{16,0},{20,4},{24,8},{28,12},{1,17},{... | collective-permute-start | bytes 5308424 | tf_op jit(solution)/shard_map/ppermute | solution.py:68
  205.0 54.5 %collective-permute-start.27 = (bf16[256,1536]{1,0:T(8,128)(2,1)S(1)}, bf16[256,1536]{1,0:T(8,128)(2,1)S(1)}, u32[]{:S(2)}, u32[]{:S(2)}) collective-permute-start(bf16[256,1536]{1,0:T(8,128)(2,1)S(1)} %multiply_convert_fusion.3), channel_id=1, source_target_pairs={{0,1},{1,2},{2,3},{4,5},{5,6},{6,7},{8,9},{9,10},{10,11},{12,13},{... | collective-permute-start | bytes 2359304 | tf_op jit(solution)/shard_map/ppermute | solution.py:137
  206.8 28.0 %collective-permute-start.52 = (bf16[256,1536]{1,0:T(8,128)(2,1)}, bf16[256,1536]{1,0:T(8,128)(2,1)S(1)}, u32[]{:S(2)}, u32[]{:S(2)}) collective-permute-start(bf16[256,1536]{1,0:T(8,128)(2,1)} %collective-permute-done.51), channel_id=1, source_target_pairs={{2,3},{6,7},{10,11},{14,15},{18,19},{22,23},{26,27},{30,31}} | collective-permute-start | bytes 2359304 | tf_op jit(solution)/shard_map/ppermute | solution.py:137
  222.1 20.6 %collective-permute-start.50 = (bf16[256,1536]{1,0:T(8,128)(2,1)}, bf16[256,1536]{1,0:T(8,128)(2,1)S(1)}, u32[]{:S(2)}, u32[]{:S(2)}) collective-permute-start(bf16[256,1536]{1,0:T(8,128)(2,1)} %collective-permute-done.49), channel_id=1, source_target_pairs={{1,0},{5,4},{9,8},{13,12},{17,16},{21,20},{25,24},{29,28}} | collective-permute-start | bytes 2359304 | tf_op jit(solution)/shard_map/ppermute | solution.py:138
  224.3 33.0 %collective-permute-start.40 = (bf16[280,1536]{1,0:T(8,128)(2,1)S(1)}, bf16[280,1536]{1,0:T(8,128)(2,1)S(1)}, u32[]{:S(2)}, u32[]{:S(2)}) collective-permute-start(bf16[280,1536]{1,0:T(8,128)(2,1)S(1)} %copy-done.34), channel_id=1, source_target_pairs={{0,4},{4,0},{8,12},{12,8},{16,20},{20,16},{24,28},{28,24},{1,5},{5... | collective-permute-start | bytes 2580488 | tf_op jit(solution)/shard_map/ppermute | solution.py:68
  224.6 21.6 %collective-permute-start.41 = (bf16[280,1536]{1,0:T(8,128)(2,1)S(1)}, bf16[280,1536]{1,0:T(8,128)(2,1)S(1)}, u32[]{:S(2)}, u32[]{:S(2)}) collective-permute-start(bf16[280,1536]{1,0:T(8,128)(2,1)S(1)} %copy-done.34), channel_id=1, source_target_pairs={{0,8},{4,12},{8,0},{12,4},{16,24},{20,28},{24,16},{28,20},{1,9},{5... | collective-permute-start | bytes 2580488 | tf_op jit(solution)/shard_map/ppermute | solution.py:68
  234.8 22.0 %collective-permute-start.42 = (bf16[280,1536]{1,0:T(8,128)(2,1)S(1)}, bf16[280,1536]{1,0:T(8,128)(2,1)S(1)}, u32[]{:S(2)}, u32[]{:S(2)}) collective-permute-start(bf16[280,1536]{1,0:T(8,128)(2,1)S(1)} %copy-done.34), channel_id=1, source_target_pairs={{0,16},{4,20},{8,24},{12,28},{16,0},{20,4},{24,8},{28,12},{1,17},{... | collective-permute-start | bytes 2580488 | tf_op jit(solution)/shard_map/ppermute | solution.py:68
  242.8 32.2 %collective-permute-start.37 = (bf16[96,4608]{1,0:T(8,128)(2,1)S(1)}, bf16[96,4608]{1,0:T(8,128)(2,1)S(1)}, u32[]{:S(2)}, u32[]{:S(2)}) collective-permute-start(bf16[96,4608]{1,0:T(8,128)(2,1)S(1)} %slice.526), channel_id=1, source_target_pairs={{0,16},{4,20},{8,24},{12,28},{16,0},{20,4},{24,8},{28,12},{1,17},{... | collective-permute-start | bytes 2654216 | tf_op jit(solution)/shard_map/ppermute | solution.py:68
  246.2 21.2 %collective-permute-start.28 = (bf16[256,1536]{1,0:T(8,128)(2,1)S(1)}, bf16[256,1536]{1,0:T(8,128)(2,1)S(1)}, u32[]{:S(2)}, u32[]{:S(2)}) collective-permute-start(bf16[256,1536]{1,0:T(8,128)(2,1)S(1)} %multiply_convert_fusion.3), channel_id=1, source_target_pairs={{1,0},{2,1},{3,2},{5,4},{6,5},{7,6},{9,8},{10,9},{11,10},{13,12},{... | collective-permute-start | bytes 2359304 | tf_op jit(solution)/shard_map/ppermute | solution.py:138
  257.4 38.3 %collective-permute-start.43 = (bf16[560,1536]{1,0:T(8,128)(2,1)S(1)}, bf16[560,1536]{1,0:T(8,128)(2,1)S(1)}, u32[]{:S(2)}, u32[]{:S(2)}) collective-permute-start(bf16[560,1536]{1,0:T(8,128)(2,1)S(1)} %pad_maximum_fusion.17), channel_id=1, source_target_pairs={{0,4},{4,0},{8,12},{12,8},{16,20},{20,16},{24,28},{28,24},{1,5},{5... | collective-permute-start | bytes 5160968 | tf_op jit(solution)/shard_map/ppermute | solution.py:68
  259.5 63.8 %collective-permute-start.36 = (bf16[384,4608]{1,0:T(8,128)(2,1)S(1)}, bf16[384,4608]{1,0:T(8,128)(2,1)S(1)}, u32[]{:S(2)}, u32[]{:S(2)}) collective-permute-start(bf16[384,4608]{1,0:T(8,128)(2,1)S(1)} %pad_maximum_fusion.6), channel_id=1, source_target_pairs={{0,4},{4,0},{8,12},{12,8},{16,20},{20,16},{24,28},{28,24},{1,5},{5... | collective-permute-start | bytes 10616840 | tf_op jit(solution)/shard_map/ppermute | solution.py:68
  275.0 20.6 %collective-permute-start.29 = (bf16[256,1536]{1,0:T(8,128)(2,1)S(1)}, bf16[256,1536]{1,0:T(8,128)(2,1)S(1)}, u32[]{:S(2)}, u32[]{:S(2)}) collective-permute-start(bf16[256,1536]{1,0:T(8,128)(2,1)S(1)} %collective-permute-done.28), channel_id=1, source_target_pairs={{1,0},{2,1},{5,4},{6,5},{9,8},{10,9},{13,12},{14,13},{17,16},{18,1... | collective-permute-start | bytes 2359304 | tf_op jit(solution)/shard_map/ppermute | solution.py:138
  276.9 22.5 %collective-permute-start.45 = (bf16[140,1536]{1,0:T(8,128)(2,1)S(1)}, bf16[140,1536]{1,0:T(8,128)(2,1)S(1)}, u32[]{:S(2)}, u32[]{:S(2)}) collective-permute-start(bf16[140,1536]{1,0:T(8,128)(2,1)S(1)} %slice.533), channel_id=1, source_target_pairs={{0,8},{4,12},{8,0},{12,4},{16,24},{20,28},{24,16},{28,20},{1,9},{5... | collective-permute-start | bytes 1290248 | tf_op jit(solution)/shard_map/ppermute | solution.py:68
  277.7 23.1 %collective-permute-start.44 = (bf16[140,1536]{1,0:T(8,128)(2,1)S(1)}, bf16[140,1536]{1,0:T(8,128)(2,1)S(1)}, u32[]{:S(2)}, u32[]{:S(2)}) collective-permute-start(bf16[140,1536]{1,0:T(8,128)(2,1)S(1)} %slice.532), channel_id=1, source_target_pairs={{0,16},{4,20},{8,24},{12,28},{16,0},{20,4},{24,8},{28,12},{1,17},{... | collective-permute-start | bytes 1290248 | tf_op jit(solution)/shard_map/ppermute | solution.py:68
  295.6 28.6 %collective-permute-start.39 = (bf16[192,4608]{1,0:T(8,128)(2,1)S(1)}, bf16[192,4608]{1,0:T(8,128)(2,1)S(1)}, u32[]{:S(2)}, u32[]{:S(2)}) collective-permute-start(bf16[192,4608]{1,0:T(8,128)(2,1)S(1)} %constant_dynamic-update-slice_fusion.31), channel_id=1, source_target_pairs={{0,4},{4,0},{8,12},{12,8},{16,20},{20,16},{24,28},{28,24},{1,5},{5... | collective-permute-start | bytes 5308424 | tf_op jit(solution)/shard_map/ppermute | solution.py:68
  299.4 22.7 %collective-permute-start.30 = (bf16[256,1536]{1,0:T(8,128)(2,1)S(1)}, bf16[256,1536]{1,0:T(8,128)(2,1)S(1)}, u32[]{:S(2)}, u32[]{:S(2)}) collective-permute-start(bf16[256,1536]{1,0:T(8,128)(2,1)S(1)} %collective-permute-done.29), channel_id=1, source_target_pairs={{1,0},{5,4},{9,8},{13,12},{17,16},{21,20},{25,24},{29,28}} | collective-permute-start | bytes 2359304 | tf_op jit(solution)/shard_map/ppermute | solution.py:138
  301.8 20.3 %collective-permute-start.46 = (bf16[280,1536]{1,0:T(8,128)(2,1)S(1)}, bf16[280,1536]{1,0:T(8,128)(2,1)S(1)}, u32[]{:S(2)}, u32[]{:S(2)}) collective-permute-start(bf16[280,1536]{1,0:T(8,128)(2,1)S(1)} %get-tuple-element.44), channel_id=1, source_target_pairs={{0,4},{4,0},{8,12},{12,8},{16,20},{20,16},{24,28},{28,24},{1,5},{5... | collective-permute-start | bytes 2580488 | tf_op jit(solution)/shard_map/ppermute | solution.py:68
  407.9 21.8 %collective-permute-start.54 = (bf16[256,1536]{1,0:T(8,128)(2,1)}, bf16[256,1536]{1,0:T(8,128)(2,1)S(1)}, u32[]{:S(2)}, u32[]{:S(2)}) collective-permute-start(bf16[256,1536]{1,0:T(8,128)(2,1)} %get-tuple-element.93), channel_id=1, source_target_pairs={{0,1},{1,2},{4,5},{5,6},{8,9},{9,10},{12,13},{13,14},{16,17},{17,1... | collective-permute-start | bytes 2359304 | tf_op jit(solution)/shard_map/ppermute | solution.py:166
  431.2 21.2 %collective-permute-start.58 = (bf16[256,1536]{1,0:T(8,128)(2,1)S(1)}, bf16[256,1536]{1,0:T(8,128)(2,1)S(1)}, u32[]{:S(2)}, u32[]{:S(2)}) collective-permute-start(bf16[256,1536]{1,0:T(8,128)(2,1)S(1)} %get-tuple-element.92), channel_id=1, source_target_pairs={{3,2},{2,1},{1,0},{7,6},{6,5},{5,4},{11,10},{10,9},{9,8},{15,14},{... | collective-permute-start | bytes 2359304 | tf_op jit(solution)/shard_map/ppermute | solution.py:167
  432.5 21.0 %collective-permute-start.55 = (bf16[256,1536]{1,0:T(8,128)(2,1)S(1)}, bf16[256,1536]{1,0:T(8,128)(2,1)S(1)}, u32[]{:S(2)}, u32[]{:S(2)}) collective-permute-start(bf16[256,1536]{1,0:T(8,128)(2,1)S(1)} %get-tuple-element.91), channel_id=1, source_target_pairs={{0,1},{1,2},{2,3},{4,5},{5,6},{6,7},{8,9},{9,10},{10,11},{12,13},{... | collective-permute-start | bytes 2359304 | tf_op jit(solution)/shard_map/ppermute | solution.py:166
  440.6 51.5 %collective-permute-start.98 = (bf16[1120,1536]{1,0:T(8,128)(2,1)}, bf16[1120,1536]{1,0:T(8,128)(2,1)}, u32[]{:S(2)}, u32[]{:S(2)}) collective-permute-start(bf16[1120,1536]{1,0:T(8,128)(2,1)} %pad_maximum_fusion.7), channel_id=1, source_target_pairs={{0,4},{4,0},{8,12},{12,8},{16,20},{20,16},{24,28},{28,24},{1,5},{5... | collective-permute-start | bytes 10321928 | tf_op jit(solution)/shard_map/ppermute | solution.py:68
  455.2 32.8 %collective-permute-start.59 = (bf16[256,1536]{1,0:T(8,128)(2,1)}, bf16[256,1536]{1,0:T(8,128)(2,1)}, u32[]{:S(2)}, u32[]{:S(2)}) collective-permute-start(bf16[256,1536]{1,0:T(8,128)(2,1)} %get-tuple-element.32), channel_id=1, source_target_pairs={{0,1},{4,5},{8,9},{12,13},{16,17},{20,21},{24,25},{28,29}} | collective-permute-start | bytes 2359304 | tf_op jit(solution)/shard_map/ppermute | solution.py:166
  460.5 27.5 %collective-permute-start.62 = (bf16[256,1536]{1,0:T(8,128)(2,1)}, bf16[256,1536]{1,0:T(8,128)(2,1)}, u32[]{:S(2)}, u32[]{:S(2)}) collective-permute-start(bf16[256,1536]{1,0:T(8,128)(2,1)} %get-tuple-element.33), channel_id=1, source_target_pairs={{3,2},{7,6},{11,10},{15,14},{19,18},{23,22},{27,26},{31,30}} | collective-permute-start | bytes 2359304 | tf_op jit(solution)/shard_map/ppermute | solution.py:167
  497.1 21.4 %collective-permute-start.99 = (bf16[560,768]{1,0:T(8,128)(2,1)S(1)}, bf16[560,768]{1,0:T(8,128)(2,1)S(1)}, u32[]{:S(2)}, u32[]{:S(2)}) collective-permute-start(bf16[560,768]{1,0:T(8,128)(2,1)S(1)} %pad_maximum_fusion.24), channel_id=1, source_target_pairs={{0,8},{4,12},{8,0},{12,4},{16,24},{20,28},{24,16},{28,20},{1,9},{5... | collective-permute-start | bytes 2580488 | tf_op jit(solution)/shard_map/ppermute | solution.py:68
  498.1 23.4 %collective-permute-start.101 = (bf16[560,768]{1,0:T(8,128)(2,1)S(1)}, bf16[560,768]{1,0:T(8,128)(2,1)S(1)}, u32[]{:S(2)}, u32[]{:S(2)}) collective-permute-start(bf16[560,768]{1,0:T(8,128)(2,1)S(1)} %pad_maximum_fusion.25), channel_id=1, source_target_pairs={{0,16},{4,20},{8,24},{12,28},{16,0},{20,4},{24,8},{28,12},{1,17},{... | collective-permute-start | bytes 2580488 | tf_op jit(solution)/shard_map/ppermute | solution.py:68
  505.9 20.1 %collective-permute-start.64 = (bf16[256,1536]{1,0:T(8,128)(2,1)S(1)}, bf16[256,1536]{1,0:T(8,128)(2,1)S(1)}, u32[]{:S(2)}, u32[]{:S(2)}) collective-permute-start(bf16[256,1536]{1,0:T(8,128)(2,1)S(1)} %get-tuple-element.86), channel_id=1, source_target_pairs={{3,2},{2,1},{1,0},{7,6},{6,5},{5,4},{11,10},{10,9},{9,8},{15,14},{... | collective-permute-start | bytes 2359304 | tf_op jit(solution)/shard_map/ppermute | solution.py:167
  518.5 86.2 %collective-permute-start.90 = (bf16[768,4608]{1,0:T(8,128)(2,1)}, bf16[768,4608]{1,0:T(8,128)(2,1)}, u32[]{:S(2)}, u32[]{:S(2)}) collective-permute-start(bf16[768,4608]{1,0:T(8,128)(2,1)} %pad_maximum_fusion.1), channel_id=1, source_target_pairs={{0,4},{4,0},{8,12},{12,8},{16,20},{20,16},{24,28},{28,24},{1,5},{5... | collective-permute-start | bytes 21233672 | tf_op jit(solution)/shard_map/ppermute | solution.py:68
  519.4 49.5 %collective-permute-start.100 = (bf16[280,768]{1,0:T(8,128)(2,1)}, bf16[280,768]{1,0:T(8,128)(2,1)}, u32[]{:S(2)}, u32[]{:S(2)}) collective-permute-start(bf16[280,768]{1,0:T(8,128)(2,1)} %add_convert_fusion.29), channel_id=1, source_target_pairs={{0,16},{4,20},{8,24},{12,28},{16,0},{20,4},{24,8},{28,12},{1,17},{... | collective-permute-start | bytes 1290248 | tf_op jit(solution)/shard_map/ppermute | solution.py:68
  522.5 49.2 %collective-permute-start.102 = (bf16[280,768]{1,0:T(8,128)(2,1)}, bf16[280,768]{1,0:T(8,128)(2,1)}, u32[]{:S(2)}, u32[]{:S(2)}) collective-permute-start(bf16[280,768]{1,0:T(8,128)(2,1)} %add_convert_fusion.27), channel_id=1, source_target_pairs={{0,8},{4,12},{8,0},{12,4},{16,24},{20,28},{24,16},{28,20},{1,9},{5... | collective-permute-start | bytes 1290248 | tf_op jit(solution)/shard_map/ppermute | solution.py:68
  553.2 21.5 %collective-permute-start.67 = (bf16[256,512]{1,0:T(8,128)(2,1)}, bf16[256,512]{1,0:T(8,128)(2,1)}, u32[]{:S(2)}, u32[]{:S(2)}) collective-permute-start(bf16[256,512]{1,0:T(8,128)(2,1)} %get-tuple-element.112), channel_id=1, source_target_pairs={{0,1},{1,2},{2,3},{3,0},{4,5},{5,6},{6,7},{7,4},{8,9},{9,10},{10,1... | collective-permute-start | bytes 786440 | tf_op jit(solution)/shard_map/ppermute | solution.py:73
  571.7 37.4 %collective-permute-start.82 = (bf16[768,1536]{1,0:T(8,128)(2,1)}, bf16[768,1536]{1,0:T(8,128)(2,1)}, u32[]{:S(2)}, u32[]{:S(2)}) collective-permute-start(bf16[768,1536]{1,0:T(8,128)(2,1)} %pad_maximum_fusion.11), channel_id=1, source_target_pairs={{0,4},{4,0},{8,12},{12,8},{16,20},{20,16},{24,28},{28,24},{1,5},{5... | collective-permute-start | bytes 7077896 | tf_op jit(solution)/shard_map/ppermute | solution.py:68
  600.4 73.8 %collective-permute-start.74 = (bf16[768,2048]{1,0:T(8,128)(2,1)}, bf16[768,2048]{1,0:T(8,128)(2,1)S(1)}, u32[]{:S(2)}, u32[]{:S(2)}) collective-permute-start(bf16[768,2048]{1,0:T(8,128)(2,1)} %pad_maximum_fusion.10), channel_id=1, source_target_pairs={{0,4},{4,0},{8,12},{12,8},{16,20},{20,16},{24,28},{28,24},{1,5},{5... | collective-permute-start | bytes 9437192 | tf_op jit(solution)/shard_map/ppermute | solution.py:68
  614.3 61.6 %collective-permute-start.93 = (bf16[384,2304]{1,0:T(8,128)(2,1)S(1)}, bf16[384,2304]{1,0:T(8,128)(2,1)S(1)}, u32[]{:S(2)}, u32[]{:S(2)}) collective-permute-start(bf16[384,2304]{1,0:T(8,128)(2,1)S(1)} %pad_maximum_fusion.16), channel_id=1, source_target_pairs={{0,16},{4,20},{8,24},{12,28},{16,0},{20,4},{24,8},{28,12},{1,17},{... | collective-permute-start | bytes 5308424 | tf_op jit(solution)/shard_map/ppermute | solution.py:68
  628.9 39.8 %collective-permute-start.84 = (bf16[192,768]{1,0:T(8,128)(2,1)S(1)}, bf16[192,768]{1,0:T(8,128)(2,1)S(1)}, u32[]{:S(2)}, u32[]{:S(2)}) collective-permute-start(bf16[192,768]{1,0:T(8,128)(2,1)S(1)} %add_convert_fusion.37), channel_id=1, source_target_pairs={{0,16},{4,20},{8,24},{12,28},{16,0},{20,4},{24,8},{28,12},{1,17},{... | collective-permute-start | bytes 884744 | tf_op jit(solution)/shard_map/ppermute | solution.py:68
  630.5 47.4 %collective-permute-start.91 = (bf16[384,2304]{1,0:T(8,128)(2,1)S(1)}, bf16[384,2304]{1,0:T(8,128)(2,1)S(1)}, u32[]{:S(2)}, u32[]{:S(2)}) collective-permute-start(bf16[384,2304]{1,0:T(8,128)(2,1)S(1)} %pad_maximum_fusion.15), channel_id=1, source_target_pairs={{0,8},{4,12},{8,0},{12,4},{16,24},{20,28},{24,16},{28,20},{1,9},{5... | collective-permute-start | bytes 5308424 | tf_op jit(solution)/shard_map/ppermute | solution.py:68
  668.9 27.9 %collective-permute-start.89 = (bf16[48,1536]{1,0:T(8,128)(2,1)S(1)}, bf16[48,1536]{1,0:T(8,128)(2,1)S(1)}, u32[]{:S(2)}, u32[]{:S(2)}) collective-permute-start(bf16[48,1536]{1,0:T(8,128)(2,1)S(1)} %get-tuple-element.127), channel_id=1, source_target_pairs={{0,3},{1,0},{2,1},{3,2},{4,7},{5,4},{6,5},{7,6},{8,11},{9,8},{10,9... | collective-permute-start | bytes 442376 | tf_op jit(solution)/shard_map/ppermute | solution.py:73
  672.2 26.4 %collective-permute-start.88 = (bf16[48,1536]{1,0:T(8,128)(2,1)S(1)}, bf16[48,1536]{1,0:T(8,128)(2,1)S(1)}, u32[]{:S(2)}, u32[]{:S(2)}) collective-permute-start(bf16[48,1536]{1,0:T(8,128)(2,1)S(1)} %get-tuple-element.126), channel_id=1, source_target_pairs={{0,2},{1,3},{2,0},{3,1},{4,6},{5,7},{6,4},{7,5},{8,10},{9,11},{10,... | collective-permute-start | bytes 442376 | tf_op jit(solution)/shard_map/ppermute | solution.py:73
  674.2 25.1 %collective-permute-start.87 = (bf16[48,1536]{1,0:T(8,128)(2,1)S(1)}, bf16[48,1536]{1,0:T(8,128)(2,1)S(1)}, u32[]{:S(2)}, u32[]{:S(2)}) collective-permute-start(bf16[48,1536]{1,0:T(8,128)(2,1)S(1)} %get-tuple-element.125), channel_id=1, source_target_pairs={{0,1},{1,2},{2,3},{3,0},{4,5},{5,6},{6,7},{7,4},{8,9},{9,10},{10,1... | collective-permute-start | bytes 442376 | tf_op jit(solution)/shard_map/ppermute | solution.py:73
  694.6 33.8 %collective-permute-start.94 = (bf16[192,2304]{1,0:T(8,128)(2,1)S(1)}, bf16[192,2304]{1,0:T(8,128)(2,1)S(1)}, u32[]{:S(2)}, u32[]{:S(2)}) collective-permute-start(bf16[192,2304]{1,0:T(8,128)(2,1)S(1)} %add_convert_fusion.5), channel_id=1, source_target_pairs={{0,8},{4,12},{8,0},{12,4},{16,24},{20,28},{24,16},{28,20},{1,9},{5... | collective-permute-start | bytes 2654216 | tf_op jit(solution)/shard_map/ppermute | solution.py:68
  696.7 31.6 %collective-permute-start.92 = (bf16[192,2304]{1,0:T(8,128)(2,1)S(1)}, bf16[192,2304]{1,0:T(8,128)(2,1)S(1)}, u32[]{:S(2)}, u32[]{:S(2)}) collective-permute-start(bf16[192,2304]{1,0:T(8,128)(2,1)S(1)} %add_convert_fusion.7), channel_id=1, source_target_pairs={{0,16},{4,20},{8,24},{12,28},{16,0},{20,4},{24,8},{28,12},{1,17},{... | collective-permute-start | bytes 2654216 | tf_op jit(solution)/shard_map/ppermute | solution.py:68
  696.9 26.6 %collective-permute-start.78 = (bf16[192,1024]{1,0:T(8,128)(2,1)S(1)}, bf16[192,1024]{1,0:T(8,128)(2,1)S(1)}, u32[]{:S(2)}, u32[]{:S(2)}) collective-permute-start(bf16[192,1024]{1,0:T(8,128)(2,1)S(1)} %add_convert_fusion.31), channel_id=1, source_target_pairs={{0,8},{4,12},{8,0},{12,4},{16,24},{20,28},{24,16},{28,20},{1,9},{5... | collective-permute-start | bytes 1179656 | tf_op jit(solution)/shard_map/ppermute | solution.py:68
  698.6 25.4 %collective-permute-start.76 = (bf16[192,1024]{1,0:T(8,128)(2,1)S(1)}, bf16[192,1024]{1,0:T(8,128)(2,1)S(1)}, u32[]{:S(2)}, u32[]{:S(2)}) collective-permute-start(bf16[192,1024]{1,0:T(8,128)(2,1)S(1)} %add_convert_fusion.33), channel_id=1, source_target_pairs={{0,16},{4,20},{8,24},{12,28},{16,0},{20,4},{24,8},{28,12},{1,17},{... | collective-permute-start | bytes 1179656 | tf_op jit(solution)/shard_map/ppermute | solution.py:68
  730.0 21.1 %collective-permute-start.97 = (bf16[48,4608]{1,0:T(8,128)(2,1)}, bf16[48,4608]{1,0:T(8,128)(2,1)}, u32[]{:S(2)}, u32[]{:S(2)}) collective-permute-start(bf16[48,4608]{1,0:T(8,128)(2,1)} %get-tuple-element.100), channel_id=1, source_target_pairs={{0,3},{1,0},{2,1},{3,2},{4,7},{5,4},{6,5},{7,6},{8,11},{9,8},{10,9... | collective-permute-start | bytes 1327112 | tf_op jit(solution)/shard_map/ppermute | solution.py:73
  733.2 47.2 %collective-permute-start.96 = (bf16[48,4608]{1,0:T(8,128)(2,1)S(1)}, bf16[48,4608]{1,0:T(8,128)(2,1)}, u32[]{:S(2)}, u32[]{:S(2)}) collective-permute-start(bf16[48,4608]{1,0:T(8,128)(2,1)S(1)} %get-tuple-element.99), channel_id=1, source_target_pairs={{0,2},{1,3},{2,0},{3,1},{4,6},{5,7},{6,4},{7,5},{8,10},{9,11},{10,... | collective-permute-start | bytes 1327112 | tf_op jit(solution)/shard_map/ppermute | solution.py:73
  734.3 47.2 %collective-permute-start.95 = (bf16[48,4608]{1,0:T(8,128)(2,1)S(1)}, bf16[48,4608]{1,0:T(8,128)(2,1)}, u32[]{:S(2)}, u32[]{:S(2)}) collective-permute-start(bf16[48,4608]{1,0:T(8,128)(2,1)S(1)} %get-tuple-element.98), channel_id=1, source_target_pairs={{0,1},{1,2},{2,3},{3,0},{4,5},{5,6},{6,7},{7,4},{8,9},{9,10},{10,1... | collective-permute-start | bytes 1327112 | tf_op jit(solution)/shard_map/ppermute | solution.py:73
  (135 other events, 2044.5 us)

commit v3 on v1

--- a/solution.py
+++ b/solution.py
@@ -1,11 +1,16 @@
 import jax
 import jax.numpy as jnp
+import numpy as np
 from jax import lax
+from jax.experimental import pallas as pl
+from jax.experimental.pallas import tpu as pltpu
 from jax.sharding import PartitionSpec as P
 
 HEADS = 12
 KV_HEADS = 2
 HEAD_DIM = 128
+
+MESH = pl.DeviceIdType.MESH
 
 epsilon = 1e-06
 rope_base = 1000000.0
@@ -53,7 +58,198 @@
     )
 
 
-def per_device(
+def after(value, *earlier):
+    return lax.optimization_barrier((value, *earlier))[0]
+
+
+def add_low(*values):
+    return sum(value.astype(jnp.float32) for value in values).astype(jnp.bfloat16)
+
+
+def cross(value, bits):
+    count = lax.axis_size("fsdp")
+    return lax.ppermute(value, "fsdp", [(i, i ^ bits) for i in range(count)])
+
+
+def shift(value, step):
+    count = lax.axis_size("seq")
+    return lax.ppermute(value, "seq", [(i, (i + step) % count) for i in range(count)])
+
+
+def place(parts, rank):
+    rows = parts[0].shape[0]
+    whole = jnp.zeros((len(parts) * rows,) + parts[0].shape[1:], parts[0].dtype)
+    for k, part in enumerate(parts):
+        whole = lax.dynamic_update_slice_in_dim(whole, part, (rank ^ k) * rows, 0)
+    return whole
+
+
+def gather_plane(block, earlier=()):
+    if lax.axis_size("fsdp") != 8:
+        whole = lax.all_gather(block, "fsdp", axis=0, tiled=True)
+        return whole, ()
+    rank = lax.axis_index("fsdp")
+    half = block.shape[0] // 2
+    if earlier:
+        block = after(block, *earlier)
+    from_x = cross(block, 2)
+    from_y = cross(block, 4)
+    diagonal = (cross(from_x[:half], 4), cross(from_y[half:], 2))
+    from_core = cross(block, 1)
+    both = cross(jnp.concatenate([from_x, from_y], 0), 1)
+    diagonal = jnp.concatenate(diagonal, 0)
+    rows = block.shape[0]
+    parts = [
+        block, from_core, from_x, both[:rows], from_y, both[rows:], diagonal, cross(diagonal, 1),
+    ]
+    return place(parts, rank), (from_x, from_y)
+
+
+def scatter_plane(whole, earlier=()):
+    count = lax.axis_size("fsdp")
+    if count != 8:
+        return lax.psum_scatter(whole, "fsdp", scatter_dimension=0, tiled=True)
+    rank = lax.axis_index("fsdp")
+    rows = whole.shape[0] // count
+    half = whole.shape[1] // 2
+    if earlier:
+        whole = after(whole, *earlier)
+
+    def part(k):
+        return lax.dynamic_slice_in_dim(whole, (rank ^ k) * rows, rows, 0)
+
+    arrived = cross(jnp.concatenate([part(1), part(3), part(5), part(7)], 0), 1)
+    own, to_x, to_y, to_both = [
+        add_low(part(2 * i), arrived[i * rows : (i + 1) * rows]) for i in range(4)
+    ]
+    got_x = cross(jnp.concatenate([to_x[:, :half], to_both[:, :half]], 0), 2)
+    got_y = cross(jnp.concatenate([to_y[:, half:], to_both[:, half:]], 0), 4)
+    last_y = cross(add_low(to_y[:, :half], got_x[rows:]), 4)
+    last_x = cross(add_low(to_x[:, half:], got_y[rows:]), 2)
+    return jnp.concatenate(
+        [
+            add_low(own[:, :half], got_x[:rows], last_y),
+            add_low(own[:, half:], got_y[:rows], last_x),
+        ],
+        1,
+    )
+
+
+def chain_step(up, down, step):
+    count = lax.axis_size("seq")
+    up = lax.ppermute(up, "seq", [(i, i + 1) for i in range(step - 1, count - 1)])
+    down = lax.ppermute(down, "seq", [(i, i - 1) for i in range(1, count - step + 1)])
+    return up, down
+
+
+def gather_seq(block, pause=None):
+    count = lax.axis_size("seq")
+    rank = lax.axis_index("seq")
+    up, down = block, block
+    ups, downs = [], []
+    for step in range(1, count):
+        if pause is not None and step == count - 1:
+            up, down = pause(up), pause(down)
+        up, down = chain_step(up, down, step)
+        ups.append(up)
+        downs.append(down)
+    rest = [jnp.where(rank >= j, ups[j - 1], downs[count - j - 1]) for j in range(1, count)]
+    return [block] + rest
+
+
+def scatter_seq(parts, earlier=()):
+    count = lax.axis_size("seq")
+    up, down = None, None
+    for step in range(1, count):
+        send_up = parts[step] if up is None else add_low(parts[step], up)
+        send_down = parts[count - step] if down is None else add_low(parts[count - step], down)
+        if up is None and earlier:
+            send_up = after(send_up, *earlier)
+            send_down = after(send_down, *earlier)
+        up = lax.ppermute(send_up, "seq", [(i, i + 1) for i in range(min(step, count - 1))])
+        down = lax.ppermute(
+            send_down, "seq", [(i, i - 1) for i in range(count - 1, max(count - 1 - step, 0), -1)]
+        )
+    return parts[0].astype(jnp.float32) + up.astype(jnp.float32) + down.astype(jnp.float32)
+
+
+def exchange_seq(whole):
+    count = lax.axis_size("seq")
+    rank = lax.axis_index("seq")
+    rows = whole.shape[0] // count
+
+    def part(step):
+        return lax.dynamic_slice_in_dim(whole, ((rank + step) % count) * rows, rows, 0)
+
+    return [part(0)] + [shift(part(step), step) for step in range(1, count)]
+
+
+def attend_back_kernel(query, key, value, bias, logsum, grad, d_query, d_key, d_value):
+    scale = HEAD_DIM ** (-0.5)
+    repeat = HEADS // KV_HEADS
+    raw = lax.dot_general(
+        key[...], query[...], (((1,), (1,)), ((), ())), preferred_element_type=jnp.float32
+    )
+    probs = jnp.exp(raw * scale + bias[...] - logsum[0:1])
+    d_probs = lax.dot_general(
+        value[...], grad[...], (((1,), (1,)), ((), ())), preferred_element_type=jnp.float32
+    )
+    delta = jnp.sum(probs * d_probs, 0, keepdims=True)
+    d_score = (probs * (d_probs - delta)).astype(jnp.bfloat16)
+    turned = lax.dot_general(
+        key[...], d_score, (((0,), (0,)), ((), ())), preferred_element_type=jnp.float32
+    )
+    d_query[...] = (turned * scale).T.astype(jnp.bfloat16)
+    key_part = jnp.dot(d_score, query[...], preferred_element_type=jnp.float32) * scale
+    value_part = jnp.dot(
+        probs.astype(jnp.bfloat16), grad[...], preferred_element_type=jnp.float32
+    )
+
+    @pl.when(pl.program_id(0) % repeat == 0)
+    def _():
+        d_key[...] = key_part
+        d_value[...] = value_part
+
+    @pl.when(pl.program_id(0) % repeat != 0)
+    def _():
+        d_key[...] += key_part
+        d_value[...] += value_part
+
+
+def attend_back(queries, paired, bias, logsum, grads):
+    rows, width = queries.shape
+    group = paired.shape[0]
+    repeat = HEADS // KV_HEADS
+    return pl.pallas_call(
+        attend_back_kernel,
+        grid=(HEADS,),
+        in_specs=[
+            pl.BlockSpec((rows, HEAD_DIM), lambda h: (0, h)),
+            pl.BlockSpec((group, HEAD_DIM), lambda h: (0, h // repeat)),
+            pl.BlockSpec((group, HEAD_DIM), lambda h: (0, KV_HEADS + h // repeat)),
+            pl.BlockSpec((group, rows), lambda h: (0, 0)),
+            pl.BlockSpec((8, rows), lambda h: (h, 0)),
+            pl.BlockSpec((rows, HEAD_DIM), lambda h: (0, h)),
+        ],
+        out_specs=[
+            pl.BlockSpec((rows, HEAD_DIM), lambda h: (0, h)),
+            pl.BlockSpec((group, HEAD_DIM), lambda h: (0, h // repeat)),
+            pl.BlockSpec((group, HEAD_DIM), lambda h: (0, h // repeat)),
+        ],
+        out_shape=[
+            jax.ShapeDtypeStruct((rows, width), jnp.bfloat16),
+            jax.ShapeDtypeStruct((group, KV_HEADS * HEAD_DIM), jnp.float32),
+            jax.ShapeDtypeStruct((group, KV_HEADS * HEAD_DIM), jnp.float32),
+        ],
+        compiler_params=pltpu.CompilerParams(vmem_limit_bytes=48 * 2**20),
+        cost_estimate=pl.CostEstimate(
+            flops=10 * HEADS * rows * group * HEAD_DIM * 3, bytes_accessed=8 * 2**20, transcendentals=HEADS * rows * group
+        ),
+        name="attend_back",
+    )(queries, paired, paired, bias, logsum, grads)
+
+
+def plain_device(
     tokens, cotangent, lengths, balance, norm1_gain, w_query, b_query, w_key, b_key,
     w_value, b_value, w_out, norm2_gain, w_gate, w_up, w_down,
 ):
@@ -256,6 +452,575 @@
     )
 
 
+def front_kernel(
+    tokens, cotangent, small, slot_keys, slot_row, first_row, cosine, sine,
+    w_query, w_key, w_value, w_out, w_gate, w_up, w_down,
+    gu_all, down_all, upstream_all, normed_all, qkv_out, out_out,
+    queries, paired_out, slots_out, logsum, attended, resid, normed_one, gain_one, gain_two,
+    qkv, out_w, gate_v, up_v, gu_own, kv, small_all, slots_all, bias, normed_own,
+    local, ssem, rsem, zsend, zrecv,
+):
+    f = lax.axis_index("fsdp")
+    s = lax.axis_index("seq")
+    rows, width = tokens.shape
+    n_f, n_s = 8, slots_all.shape[0]
+    block = w_query.shape[0]
+    unit = w_down.shape[0]
+    kv_width = KV_HEADS * HEAD_DIM
+    qkv_width = width + 2 * kv_width
+    scale = HEAD_DIM ** (-0.5)
+    repeat = HEADS // KV_HEADS
+    plane = [f ^ k for k in range(n_f)]
+
+    entry = pltpu.get_barrier_semaphore()
+    for k in range(1, n_f):
+        pl.semaphore_signal(entry, inc=1, device_id={"fsdp": plane[k]}, device_id_type=MESH)
+    for j in range(1, n_s):
+        pl.semaphore_signal(
+            entry, inc=1, device_id={"seq": lax.rem(s + j, n_s)}, device_id_type=MESH
+        )
+
+    def here(source, target, index):
+        return pltpu.make_async_copy(source, target, local.at[index])
+
+    def there(source, target, index, **device):
+        return pltpu.make_async_remote_copy(
+            src_ref=source, dst_ref=target, send_sem=ssem.at[index], recv_sem=rsem.at[index],
+            device_id=device, device_id_type=MESH,
+        )
+
+    def own_rows(ref, owner, size, start=0, count=None):
+        first = pl.multiple_of(owner * size + start, 16)
+        return ref.at[pl.ds(first, size if count is None else count)]
+
+    class Gather:
+        def __init__(self, source, target, size, index):
+            half = size // 2
+            x, y, c = plane[2], plane[4], plane[1]
+            self.own = here(source, own_rows(target, f, size), index // 8) if source is not None else None
+            if source is None:
+                source = own_rows(target, f, size)
+            mine = own_rows(target, f, size)
+            self.first = [
+                there(source, mine, index, fsdp=x),
+                there(source, mine, index + 1, fsdp=y),
+                there(source, mine, index + 2, fsdp=c),
+            ]
+            from_x, from_y = own_rows(target, x, size), own_rows(target, y, size)
+            part_x = own_rows(target, x, size, 0, half)
+            part_y = own_rows(target, y, size, half, half)
+            self.second = [
+                there(part_x, part_x, index + 3, fsdp=y),
+                there(part_y, part_y, index + 4, fsdp=x),
+                there(from_x, from_x, index + 5, fsdp=c),
+                there(from_y, from_y, index + 6, fsdp=c),
+            ]
+            diagonal = own_rows(target, plane[6], size)
+            self.third = there(diagonal, diagonal, index + 7, fsdp=c)
+
+        def start(self):
+            if self.own is not None:
+                self.own.start()
+            for copy in self.first:
+                copy.start()
+
+        def forward(self):
+            self.first[0].wait_recv()
+            self.second[0].start()
+            self.second[2].start()
+            self.first[1].wait_recv()
+            self.second[1].start()
+            self.second[3].start()
+
+        def last(self):
+            self.second[0].wait_recv()
+            self.second[1].wait_recv()
+            self.third.start()
+
+        def finish(self):
+            if self.own is not None:
+                self.own.wait()
+            self.first[2].wait_recv()
+            self.second[2].wait_recv()
+            self.second[3].wait_recv()
+            self.third.wait_recv()
+
+        def sent(self):
+            for copy in self.first + self.second + [self.third]:
+                copy.wait_send()
+
+    class Chain:
+        def __init__(self, target, index):
+            self.steps = []
+            for step in range(1, n_s):
+                up = own_rows(target, s - (step - 1), rows)
+                down = own_rows(target, s + (step - 1), rows)
+                i = index + 2 * (step - 1)
+                self.steps.append((
+                    pltpu.make_async_remote_copy(
+                        src_ref=up, dst_ref=up, send_sem=zsend.at[i], recv_sem=zrecv.at[i],
+                        device_id={"seq": s + 1}, device_id_type=MESH,
+                    ),
+                    pltpu.make_async_remote_copy(
+                        src_ref=down, dst_ref=down, send_sem=zsend.at[i + 1], recv_sem=zrecv.at[i + 1],
+                        device_id={"seq": s - 1}, device_id_type=MESH,
+                    ),
+                    (s >= step - 1) & (s < n_s - 1),
+                    (s >= 1) & (s <= n_s - step),
+                    s >= step,
+                    s <= n_s - 1 - step,
+                ))
+
+        def send(self, step):
+            up, down, can_up, can_down, _, _ = self.steps[step - 1]
+            pl.when(can_up)(up.start)
+            pl.when(can_down)(down.start)
+
+        def receive(self, step):
+            up, down, _, _, from_below, from_above = self.steps[step - 1]
+            pl.when(from_below)(up.wait_recv)
+            pl.when(from_above)(down.wait_recv)
+
+        def sent(self):
+            for up, down, can_up, can_down, _, _ in self.steps:
+                pl.when(can_up)(up.wait_send)
+                pl.when(can_down)(down.wait_send)
+
+    pieces = [
+        here(w_query, qkv.at[pl.ds(pl.multiple_of(f * block, 16), block), pl.ds(0, width)], 5),
+        here(w_key, qkv.at[pl.ds(pl.multiple_of(f * block, 16), block), pl.ds(width, kv_width)], 6),
+        here(w_value, qkv.at[pl.ds(pl.multiple_of(f * block, 16), block), pl.ds(width + kv_width, kv_width)], 7),
+        here(cotangent, own_rows(upstream_all, s, rows), 8),
+    ]
+    load_gate = here(w_gate, gate_v, 9)
+    load_up = here(w_up, up_v, 10)
+    for copy in pieces:
+        copy.start()
+    load_gate.start()
+    load_up.start()
+    small_all[f] = small[...]
+    slots_all[s] = slot_keys[...]
+
+    gather_qkv = Gather(None, qkv, block, 0)
+    gather_out = Gather(w_out, out_w, block, 8)
+    gather_gu = Gather(gu_own, gu_all, block, 16)
+    gather_down = Gather(w_down, down_all, unit, 24)
+    chain_up = Chain(upstream_all, 0)
+    chain_normed = Chain(normed_all, 6)
+    send_small = [
+        there(small, small_all.at[f], 32 + k, fsdp=plane[k]) for k in range(1, n_f)
+    ]
+    send_slots = [
+        there(slot_keys, slots_all.at[s], 40 + j, seq=lax.rem(s + j, n_s)) for j in range(1, n_s)
+    ]
+    send_kv = [
+        there(kv.at[s], kv.at[s], 44 + j, seq=lax.rem(s + j, n_s)) for j in range(1, n_s)
+    ]
+    for copy in pieces[:3]:
+        copy.wait()
+    pl.semaphore_wait(entry, n_f - 1 + n_s - 1)
+    gather_qkv.start()
+    for copy in send_small + send_slots:
+        copy.start()
+    pieces[3].wait()
+    chain_up.send(1)
+
+    load_gate.wait()
+    load_up.wait()
+    pick_units(gate_v, up_v, gu_own, w_gate.shape[1] // n_f, w_gate.shape[1] // (n_f * n_s), unit)
+
+    for copy in send_small + send_slots:
+        copy.wait_recv()
+    third = 2 * block
+    for i in range(n_f // 2):
+        columns = slice(i * third, (i + 1) * third)
+        gain_one[:, columns] = (
+            small_all[2 * i, 0:1, :third].astype(jnp.float32)
+            + small_all[2 * i + 1, 0:1, :third].astype(jnp.float32)
+        )
+        gain_two[:, columns] = (
+            small_all[2 * i, 0:1, third : 2 * third].astype(jnp.float32)
+            + small_all[2 * i + 1, 0:1, third : 2 * third].astype(jnp.float32)
+        )
+    bias_query = [
+        small_all[2 * i, 0:1, 2 * third : 3 * third].astype(jnp.float32)
+        + small_all[2 * i + 1, 0:1, 2 * third : 3 * third].astype(jnp.float32)
+        for i in range(n_f // 2)
+    ]
+    bias_query = jnp.concatenate(bias_query, 1)
+    bias_pair = sum(small_all[i, 0:1, 3 * third :].astype(jnp.float32) for i in range(n_f))
+
+    inputs = tokens[...].astype(jnp.float32)
+    root = lax.rsqrt(jnp.mean(inputs * inputs, -1, keepdims=True) + epsilon)
+    normed_one[...] = (inputs * root * gain_one[...]).astype(jnp.bfloat16)
+    for j in range(n_s):
+        keys_slot = slots_all[j]
+        keys_slot = jnp.concatenate([keys_slot] * (rows // 128), 1)
+        ok = (keys_slot <= slot_row[0:1]) & (keys_slot >= first_row[0:1])
+        bias[j * rows : (j + 1) * rows] = jnp.where(ok, 0.0, -1e30)
+
+    gather_qkv.forward()
+    gather_out.start()
+    chain_up.receive(1)
+    chain_up.send(2)
+    gather_qkv.last()
+    gather_qkv.finish()
+    save_qkv = here(qkv, qkv_out, 11)
+    save_qkv.start()
+
+    def turned(value):
+        return value * cosine[...] + pltpu.roll(value, HEAD_DIM // 2, 1) * sine[...]
+
+    normed = normed_one[...]
+    pair = jnp.dot(normed, qkv[:, width : width + kv_width], preferred_element_type=jnp.float32)
+    pair = pair + bias_pair[:, :kv_width]
+    for g in range(KV_HEADS):
+        columns = slice(g * HEAD_DIM, (g + 1) * HEAD_DIM)
+        kv[s, :, columns] = turned(pair[:, columns]).astype(jnp.bfloat16)
+    pair = jnp.dot(normed, qkv[:, width + kv_width :], preferred_element_type=jnp.float32)
+    kv[s, :, kv_width:] = (pair + bias_pair[:, kv_width:]).astype(jnp.bfloat16)
+    for copy in send_kv:
+        copy.start()
+    for g in range(HEADS // 2):
+        columns = slice(g * 2 * HEAD_DIM, (g + 1) * 2 * HEAD_DIM)
+        pair = jnp.dot(normed, qkv[:, columns], preferred_element_type=jnp.float32)
+        pair = pair + bias_query[:, columns]
+        for h in range(2):
+            part = turned(pair[:, h * HEAD_DIM : (h + 1) * HEAD_DIM]).astype(jnp.bfloat16)
+            queries[:, (2 * g + h) * HEAD_DIM : (2 * g + h + 1) * HEAD_DIM] = part
+
+    gather_out.forward()
+    gather_gu.start()
+    chain_up.receive(2)
+    gather_out.last()
+    for copy in send_kv:
+        copy.wait_recv()
+    chain_up.send(3)
+    save_kv = here(kv, paired_out, 12)
+    save_kv.start()
+    slots_out[...] = slots_all[...]
+
+    for g in range(KV_HEADS):
+        keys = kv[:, :, g * HEAD_DIM : (g + 1) * HEAD_DIM].reshape(n_s * rows, HEAD_DIM)
+        values = kv[:, :, kv_width + g * HEAD_DIM : kv_width + (g + 1) * HEAD_DIM]
+        values = values.reshape(n_s * rows, HEAD_DIM)
+
+        def head(i, carry, g=g, keys=keys, values=values):
+            h = g * repeat + i
+            columns = pl.ds(pl.multiple_of(h * HEAD_DIM, HEAD_DIM), HEAD_DIM)
+            raw = lax.dot_general(
+                keys, queries[:, columns], (((1,), (1,)), ((), ())),
+                preferred_element_type=jnp.float32,
+            )
+            scores = raw * scale + bias[...]
+            top = jnp.max(scores, 0, keepdims=True)
+            expo = jnp.exp(scores - top)
+            total = jnp.sum(expo, 0, keepdims=True)
+            probs = (expo * (1.0 / total)).astype(jnp.bfloat16)
+            mixed = lax.dot_general(
+                values, probs, (((0,), (0,)), ((), ())), preferred_element_type=jnp.float32
+            )
+            attended[:, columns] = mixed.T.astype(jnp.bfloat16)
+            logsum[pl.ds(pl.multiple_of(h * 8, 8), 8)] = jnp.broadcast_to(
+                top + jnp.log(total), (8, rows)
+            )
+            return carry
+
+        lax.fori_loop(0, repeat, head, 0)
+
+    gather_out.finish()
+    save_out = here(out_w, out_out, 13)
+    save_out.start()
+    mixed = attended[...]
+    for g in range(width // 256):
+        columns = slice(g * 256, (g + 1) * 256)
+        part = jnp.dot(mixed, out_w[:, columns], preferred_element_type=jnp.float32)
+        resid[:, columns] = tokens[:, columns].astype(jnp.float32) + part
+    value = resid[...]
+    root = lax.rsqrt(jnp.mean(value * value, -1, keepdims=True) + epsilon)
+    normed_own[...] = (value * root * gain_two[...]).astype(jnp.bfloat16)
+    place_normed = here(normed_own, own_rows(normed_all, s, rows), 14)
+    place_normed.start()
+    place_normed.wait()
+    chain_normed.send(1)
+
+    gather_gu.forward()
+    gather_down.start()
+    chain_normed.receive(1)
+    chain_normed.send(2)
+    gather_gu.last()
+    chain_normed.receive(2)
+    chain_normed.send(3)
+    chain_up.receive(3)
+    gather_down.forward()
+    gather_gu.finish()
+    gather_down.last()
+    chain_normed.receive(3)
+    gather_down.finish()
+    save_qkv.wait()
+    save_kv.wait()
+    save_out.wait()
+    for part in (gather_qkv, gather_out, gather_gu, gather_down, chain_up, chain_normed):
+        part.sent()
+    for copy in send_small + send_slots + send_kv:
+        copy.wait_send()
+
+
+def pick_units(gate, up, out, stride, unit, padded):
+    rank = lax.axis_index("seq")
+    pieces = gate.shape[1] // stride
+    half = out.shape[1] // 2
+    window, tile = 512, 128
+    rows = lax.broadcasted_iota(jnp.int32, (window, tile), 0)
+    columns = lax.broadcasted_iota(jnp.int32, (window, tile), 1)
+    for first in range(0, 2 * half, tile):
+        source = gate if first < half else up
+        local = first % half
+        total = jnp.zeros((out.shape[0], tile), jnp.float32)
+        for f in range(pieces):
+            low = max(local, f * padded)
+            high = min(local + tile, f * padded + unit)
+            if low >= high:
+                continue
+            begin = f * stride + rank * unit
+            base = jnp.minimum(begin // 128, (source.shape[1] - window) // 128) * 128
+            base = pl.multiple_of(base, 128)
+            wanted = columns + (local - f * padded + begin - base)
+            inside = (columns >= low - local) & (columns < high - local)
+            chosen = jnp.where((rows == wanted) & inside, 1.0, 0.0).astype(jnp.bfloat16)
+            total += jnp.dot(
+                source[:, pl.ds(base, window)], chosen, preferred_element_type=jnp.float32
+            )
+        out[:, first : first + tile] = total.astype(jnp.bfloat16)
+
+
+def front(tokens, cotangent, small, slot, first_row, cosine, sine, weights, w_down_own):
+    rows, width = tokens.shape
+    n_s = lax.axis_size("seq")
+    w_query, w_key, w_value, w_out, w_gate, w_up = weights
+    block = w_query.shape[0]
+    unit = w_down_own.shape[0]
+    kv_width = KV_HEADS * HEAD_DIM
+    qkv_width = width + 2 * kv_width
+    units = 8 * unit
+    group = n_s * rows
+    low, full = jnp.bfloat16, jnp.float32
+    slot_f = slot.astype(full)
+    slot_keys = jnp.broadcast_to(slot_f[:, None], (rows, 128))
+    slot_row = jnp.broadcast_to(slot_f[None], (8, rows))
+    first_f = jnp.broadcast_to(first_row.astype(full)[None], (8, rows))
+    half = HEAD_DIM // 2
+    sine = jnp.concatenate([-sine[:, :half], sine[:, half:]], 1)
+    vmem = pl.BlockSpec(memory_space=pltpu.VMEM)
+    hbm = pl.BlockSpec(memory_space=pl.ANY)
+    shape = jax.ShapeDtypeStruct
+    return pl.pallas_call(
+        front_kernel,
+        in_specs=[vmem, hbm] + [vmem] * 6 + [hbm] * 7,
+        out_specs=[hbm] * 6 + [vmem, hbm] + [vmem] * 7,
+        out_shape=[
+            shape((8 * block, 2 * units), low),
+            shape((units, width), low),
+            shape((group, width), low),
+            shape((group, width), low),
+            shape((width, qkv_width), low),
+            shape((width, width), low),
+            shape((rows, width), low),
+            shape((n_s, rows, 2 * kv_width), low),
+            shape((n_s, rows, 128), full),
+            shape((8 * HEADS, rows), full),
+            shape((rows, width), low),
+            shape((rows, width), full),
+            shape((rows, width), low),
+            shape((1, width), full),
+            shape((1, width), full),
+        ],
+        scratch_shapes=[
+            pltpu.VMEM((width, qkv_width), low),
+            pltpu.VMEM((width, width), low),
+            pltpu.VMEM(w_gate.shape, low),
+            pltpu.VMEM(w_up.shape, low),
+            pltpu.VMEM((block, 2 * units), low),
+            pltpu.VMEM((n_s, rows, 2 * kv_width), low),
+            pltpu.VMEM((8,) + small.shape, low),
+            pltpu.VMEM((n_s, rows, 128), full),
+            pltpu.VMEM((group, rows), full),
+            pltpu.VMEM((rows, width), low),
+            pltpu.SemaphoreType.DMA((16,)),
+            pltpu.SemaphoreType.DMA((48,)),
+            pltpu.SemaphoreType.DMA((48,)),
+            pltpu.SemaphoreType.DMA((12,)),
+            pltpu.SemaphoreType.DMA((12,)),
+        ],
+        compiler_params=pltpu.CompilerParams(
+            collective_id=0, has_side_effects=True, vmem_limit_bytes=56 * 2**20
+        ),
+        name="front",
+    )(
+        tokens, cotangent, small, slot_keys, slot_row, first_f, cosine, sine,
+        w_query, w_key, w_value, w_out, w_gate, w_up, w_down_own,
+    )
+
+
+def per_device(
+    tokens, cotangent, lengths, balance, norm1_gain, w_query, b_query, w_key, b_key,
+    w_value, b_value, w_out, norm2_gain, w_gate, w_up, w_down,
+):
+    seq_count = lax.axis_size("seq")
+    fsdp_count = lax.axis_size("fsdp")
+    seq_rank = lax.axis_index("seq")
+    fsdp_rank = lax.axis_index("fsdp")
+    rows_here, width = tokens.shape
+    group = seq_count * rows_here
+    kv_width = KV_HEADS * HEAD_DIM
+    qkv_width = width + 2 * kv_width
+    hidden_width = w_gate.shape[1]
+    unit = hidden_width // (fsdp_count * seq_count)
+    own_units = hidden_width // seq_count
+    padded = fsdp_count * (-(-unit // 16) * 16)
+    weight_rows = w_gate.shape[0]
+
+    unit_pad = -(-unit // 16) * 16
+    pair_bias = jnp.concatenate([jnp.tile(b_key, fsdp_count), jnp.tile(b_value, fsdp_count)])
+    small = jnp.concatenate([norm1_gain] * 2 + [norm2_gain] * 2 + [b_query] * 2 + [pair_bias])
+    place_of = np.concatenate(
+        [np.repeat([0, 1], weight_rows)] * 3 + [8 + np.repeat(np.arange(8), b_key.shape[0])] * 2
+    )
+    place_of = jnp.asarray(place_of, jnp.int32)
+    mine = (place_of == fsdp_rank % 2) | (place_of == 8 + fsdp_rank)
+    small = jnp.broadcast_to(jnp.where(mine, small, 0)[None], (16, small.shape[0]))
+
+    slot = balance % group
+    seq_lengths = lengths[0]
+    starts = jnp.cumsum(seq_lengths) - seq_lengths
+    segment = segment_of(slot, starts)
+    first_row = jnp.where(segment == 0, starts[0], jnp.where(segment == 1, starts[1], starts[2]))
+    cosine, sine = rope_tables(slot - first_row)
+    down_own = lax.dynamic_slice_in_dim(w_down, seq_rank * unit, unit, 0)
+    down_own = jnp.pad(down_own, ((0, unit_pad - unit), (0, 0)))
+    (
+        weight_gu, weight_down, upstream_all, normed_all, weight_qkv, weight_out,
+        queries, paired, slots_all, logsum, attended, resid, normed_one, gain_one, gain_two,
+    ) = front(
+        tokens, cotangent, small, slot, first_row, cosine, sine,
+        (w_query, w_key, w_value, w_out, w_gate, w_up), down_own,
+    )
+    gain_one, gain_two = gain_one[0], gain_two[0]
+    paired = paired.reshape(group, 2 * kv_width)
+    slots_all = slots_all[:, :, 0].reshape(group)
+    slot = slot.astype(jnp.float32)
+    allowed = (slots_all[:, None] <= slot[None, :]) & (
+        slots_all[:, None] >= first_row.astype(jnp.float32)[None, :]
+    )
+    bias = jnp.where(allowed, 0.0, -1e30).astype(jnp.float32)
+    inputs = tokens.astype(jnp.float32)
+
+    def blocks_back(value):
+        return [
+            lax.dynamic_slice_in_dim(value, ((seq_rank - j) % seq_count) * rows_here, rows_here, 0)
+            for j in range(seq_count)
+        ]
+
+    both = jnp.dot(normed_all, weight_gu, preferred_element_type=jnp.float32)
+    gate = both[:, :padded]
+    up = both[:, padded:]
+    sigma = jax.nn.sigmoid(gate)
+    activated = gate * sigma
+    hidden = (activated * up).astype(jnp.bfloat16)
+    d_hidden = contract_columns(upstream_all, weight_down)
+    d_gate = (d_hidden * up * sigma * (1.0 + gate * (1.0 - sigma))).astype(jnp.bfloat16)
+    d_up = (d_hidden * activated).astype(jnp.bfloat16)
+    d_both = jnp.concatenate([d_gate, d_up], 1)
+    columns = contract_columns(d_both, weight_gu).astype(jnp.bfloat16)
+    columns = scatter_seq(blocks_back(columns))
+
+    grad_down = contract_rows(hidden, upstream_all).astype(jnp.bfloat16)
+    grad_down = scatter_plane(grad_down)[:unit].astype(jnp.float32)
+    grad_pair = scatter_plane(contract_rows(normed_all, d_both).astype(jnp.bfloat16))
+    branch = jnp.dot(hidden, weight_down, preferred_element_type=jnp.float32).astype(jnp.bfloat16)
+    branch = scatter_seq(blocks_back(branch), (columns,))
+    layer_out = (resid + branch).astype(jnp.bfloat16)
+    grad_pair = exchange_seq(grad_pair)
+    own_rows = weight_rows // seq_count
+    grad_pair = jnp.stack(grad_pair, 0).reshape(seq_count, own_rows, 2, padded)
+    order = (seq_rank - jnp.arange(seq_count)) % seq_count
+    grad_pair = grad_pair[order]
+    grad_pair = grad_pair.reshape(seq_count, own_rows, 2, fsdp_count, unit_pad)[..., :unit]
+    grad_pair = grad_pair.transpose(2, 1, 3, 0, 4).astype(jnp.float32)
+    grad_pair = grad_pair.reshape(2, own_rows, hidden_width)
+
+    _, pull_two = jax.vjp(norm_piece, resid, gain_two)
+    d_resid_norm, grad_gain_two = pull_two(columns)
+    d_resid = cotangent.astype(jnp.float32) + d_resid_norm
+    d_branch = d_resid.astype(jnp.bfloat16)
+    d_attended = contract_columns(d_branch, weight_out).astype(jnp.bfloat16)
+    d_queries, d_keys, d_values = attend_back(queries, paired, bias, logsum, d_attended)
+    d_paired = jnp.concatenate([d_keys, d_values], 1).astype(jnp.bfloat16)
+    d_paired = blocks_back(d_paired)
+    d_paired = sum(
+        part.astype(jnp.float32)
+        for part in [d_paired[0]] + [shift(d_paired[j], -j) for j in range(1, seq_count)]
+    )
+    d_query_pre = rotate_back(
+        d_queries.astype(jnp.float32).reshape(rows_here, HEADS, HEAD_DIM), cosine, sine
+    ).astype(jnp.bfloat16)
+    d_key_pre = rotate_back(
+        d_paired[:, :kv_width].reshape(rows_here, KV_HEADS, HEAD_DIM), cosine, sine
+    ).astype(jnp.bfloat16)
+    d_value_pre = d_paired[:, kv_width:].astype(jnp.bfloat16)
+    d_qkv = jnp.concatenate(
+        [
+            d_query_pre.reshape(rows_here, width),
+            d_key_pre.reshape(rows_here, kv_width),
+            d_value_pre,
+        ],
+        1,
+    )
+    grad_out = contract_rows(attended, d_branch).astype(jnp.bfloat16)
+    grad_qkv = contract_rows(normed_one, d_qkv).astype(jnp.bfloat16)
+    grad_bias = jnp.sum(d_qkv.astype(jnp.float32), 0)
+    d_normed_one = contract_columns(d_qkv, weight_qkv)
+    _, pull_one = jax.vjp(norm_piece, inputs, gain_one)
+    d_input_norm, grad_gain_one = pull_one(d_normed_one)
+    input_grad = (d_resid + d_input_norm).astype(jnp.bfloat16)
+
+    def summed(value):
+        return sum(part.astype(jnp.float32) for part in exchange_seq(scatter_plane(value)))
+
+    grad_out = summed(grad_out)
+    grad_qkv = summed(grad_qkv)
+    vectors = jnp.concatenate([grad_gain_one, grad_gain_two, grad_bias], 0)
+    if fsdp_count == 8:
+        for bits in (1, 2, 4):
+            vectors = vectors + cross(vectors, bits)
+        vectors = vectors + sum(shift(vectors, j) for j in range(1, seq_count))
+    else:
+        vectors = lax.psum(vectors, ("fsdp", "seq"))
+    own = width // (fsdp_count * seq_count)
+    first = (fsdp_rank * seq_count + seq_rank) * own
+
+    def own_part(offset):
+        return lax.dynamic_slice_in_dim(vectors, offset + first, own, 0)
+
+    biases = 2 * width
+    return (
+        layer_out,
+        input_grad,
+        own_part(0),
+        grad_qkv[:, :width],
+        own_part(biases),
+        grad_qkv[:, width : width + kv_width],
+        vectors[biases + width : biases + width + kv_width],
+        grad_qkv[:, width + kv_width :],
+        vectors[biases + width + kv_width :],
+        grad_out,
+        own_part(width),
+        grad_pair[0],
+        grad_pair[1],
+        grad_down,
+    )
+
+
 def solution(mesh):
     both = P(("fsdp", "seq"), None)
     both_one = P(("fsdp", "seq"))
@@ -265,7 +1030,7 @@
         P("fsdp", None), P("fsdp", None), P("fsdp", None),
     )
     return jax.shard_map(
-        per_device,
+        per_device if mesh.shape["fsdp"] == 8 else plain_device,
         mesh=mesh,
         in_specs=placed,
         out_specs=(

time: 1010 us -> 678 us (0.67)
  waiting for transfers between devices: 585 us -> 145 us
  Pallas kernels: 0 us -> 179 us
  matrix products: 179 us -> 114 us
  starting transfers between devices: 6.67 us -> 70.4 us
  blocking collectives: 62 us -> 0 us
  local copies, waits for them, and re-layouts: 111 us -> 63.2 us
  other arithmetic: 52.1 us -> 95.9 us
  between operations: 14.6 us -> 2.42 us
    reduce_scatter x9 -> x0, waiting for transfers between devices: 358 us -> none  [the longest x1 102 us: per_device(): lax.psum_scatter(contract_rows(normed_all, d_both).astype(jnp.bfloat16),...]
    all_gather x7 -> x0, waiting for transfers between devices: 225 us -> none  [the longest x1 78.1 us: per_device(): lax.all_gather(jnp.concatenate([own_columns(w_gate), own_columns(w_up)],...]
    pallas_call x0 -> x2, Pallas kernels: none -> 179 us  [the longest x1 161 us: front(): pl.pallas_call(front_kernel, in_specs=[vmem, hbm] + [vmem] * 6 + [hbm] *...]
    ppermute x0 -> x50, waiting for transfers between devices: none -> 145 us  [the longest x15 51.7 us: shift(): lax.ppermute(value, 'seq', [(i, (i + step) % count) for i in range(count)])]
    ppermute x0 -> x50, starting transfers between devices: none -> 70.4 us  [the longest x15 24.3 us: shift(): lax.ppermute(value, 'seq', [(i, (i + step) % count) for i in range(count)])]
    dot_general x7 -> x0, matrix products: 41 us -> none  [the longest x1 10.3 us: per_device(): jnp.einsum('qgrd,kgd->grqk', d_attended, values_all, preferred_element_ty...]
    psum x1 -> x0, blocking collectives: 40.3 us -> none  [per_device(): lax.psum(jnp.concatenate([grad_gain_one, grad_gain_two, grad_bias], 0), (...]
    convert_element_type x9 -> x28, other arithmetic: 15.4 us -> 51.4 us  [the longest x24 47.3 us: add_low(): sum((value.astype(jnp.float32) for value in values)).astype(jnp.bfloat16)]
  transfers between devices with their start and end apart: 17 -> 50, of which waited for: 15 -> 18; matrix products, arithmetic and copies ran while one was open for 21% -> 28% of each run, Pallas kernels for 0% -> 3%
where the time goes in v3:
time: 678 us; the launch traced here: 670 us
  Pallas kernels  179 us (26%)
  waiting for transfers between devices  145 us (21%)
  matrix products  114 us (17%)
  other arithmetic  95.9 us (14%)
  starting transfers between devices  70.4 us (10%)
  local copies, waits for them, and re-layouts  63.2 us (9%)
    pallas_call x1, Pallas kernels, front(): pl.pallas_call(front_kernel, in_specs=[vmem, hbm] + [vmem] * 6 + [hbm] *...  161 us
    ppermute x15, waiting for transfers between devices, shift(): lax.ppermute(value, 'seq', [(i, (i + step) % count) for i in range(count)])  51.7 us
    convert_element_type x24, other arithmetic, add_low(): sum((value.astype(jnp.float32) for value in values)).astype(jnp.bfloat16)  47.3 us
    dot_general x4, matrix products, contract_columns(): lax.dot_general(left, right, (((1,), (1,)), ((), ())), preferred_element_...  45.5 us
    ppermute x23, waiting for transfers between devices, cross(): return lax.ppermute(value, 'fsdp', [(i, i ^ bits) for i in range(count)])  40.4 us
    dot_general x4, matrix products, contract_rows(): lax.dot_general(left, right, (((0,), (0,)), ((), ())), preferred_element_...  36.9 us
    ppermute x6, waiting for transfers between devices, scatter_seq(): lax.ppermute(send_up, 'seq', [(i, i + 1) for i in range(min(step, count -...  27.9 us
    ppermute x6, waiting for transfers between devices, scatter_seq(): lax.ppermute(send_down, 'seq', [(i, i - 1) for i in range(count - 1, max(...  24.5 us
  transfers between devices with their start and end apart: 50, of which 18 were waited for; matrix products, arithmetic and copies ran while one was open for 28% of the time, Pallas kernels for 3%

profile of v3, /device:TPU:0, one launch (start us, length us, event | category | flops | bytes accessed | tf_op | source)
XLA Modules:
  0.0 669.5 jit_solution(12104513377741043875)
XLA Ops:
  4.5 2.6 subtract_convert_fusion.1
  7.2 1.9 fusion.43
  15.1 160.7 %front.1 = (bf16[1536,4608]{1,0:T(8,128)(2,1)}, bf16[2304,1536]{1,0:T(8,128)(2,1)}, bf16[1024,1536]{1,0:T(8,128)(2,1)}, bf16[1024,1536]{1,0:T(8,128)(2,1)}, bf16...) custom-call(bf16[256,1536]{1,0:T(8,128)(2,1)} %tokens.1, ...), custom_call_target="tpu_custom_call" | custom-call | tf_op jit(solution)/shard_map/front/pallas_call | solution.py:817
  175.9 21.3 %fusion.54 = f32[1024,4608]{1,0:T(8,128)} fusion(bf16[1024,1536]{1,0:T(8,128)(2,1)} %get-tuple-element.35, bf16[1536,4608]{1,0:T(8,128)(2,1)} %get-tuple-element.36), kind=kOutput, calls=%fused_computation.230 | convolution fusion | flops 14495514624 | bytes 36175872 | tf_op jit(solution)/shard_map/dot_general | solution.py:924
  197.1 18.7 %multiply_convert_fusion.1 = (bf16[1024,2304]{1,0:T(8,128)(2,1)}, bf16[1024,2304]{1,0:T(8,128)(2,1)}, bf16[1024,2304]{1,0:T(8,128)(2,1)}) fusion(f32[1024,4608]{1,0:T(8,128)} %fusion.54, bf16[1024,1536]{1,0:T(8,128)(2,1)S(1)} %copy-done.59, bf16[2304,1536]{1,0:T(8,128)(2,1)} %get-tuple-element.37), kind=kOutput, calls=%fused_computation.5 | convolution fusion | flops 7283146752 | bytes 43253760 | tf_op jit(solution)/shard_map/dot_general | solution.py:56
  215.8 20.3 %fusion.2 = bf16[1024,1536]{1,0:T(8,128)(2,1)S(1)} fusion(bf16[1536,4608]{1,0:T(8,128)(2,1)} %get-tuple-element.36, bf16[1024,2304]{1,0:T(8,128)(2,1)} %get-tuple-element.66, bf16[1024,2304]{1,0:T(8,128)(2,1)} %get-tuple-element.65), kind=kOutput, calls=%fused_computation.14 | convolution fusion | flops 14515961856 | bytes 26738688 | tf_op jit(solution)/shard_map/dot_general | solution.py:56
  237.2 2.3 collective-permute-start
  239.5 21.8 %convolution_convert_fusion = bf16[1536,4608]{1,0:T(8,128)(2,1)} fusion(bf16[1024,1536]{1,0:T(8,128)(2,1)} %get-tuple-element.35, bf16[1024,2304]{1,0:T(8,128)(2,1)} %get-tuple-element.66, bf16[1024,2304]{1,0:T(8,128)(2,1)} %get-tuple-element.65), kind=kOutput, calls=%fused_computation.1 | convolution fusion | flops 14521466880 | bytes 26738688 | tf_op jit(solution)/shard_map/dot_general | solution.py:50
  261.4 2.2 fusion.5
  263.6 2.2 collective-permute-start.1
  265.8 3.5 constant_dynamic-slice_fusion.7
  269.3 3.4 pad_maximum_fusion.1
  272.7 9.2 %collective-permute-done.1 = bf16[256,1536]{1,0:T(8,128)(2,1)} collective-permute-done((bf16[256,1536]{1,0:T(8,128)(2,1)}, bf16[256,1536]{1,0:T(8,128)(2,1)}, u32[]{:S(2)}, u32[]{:S(2)}) %collective-permute-start.1) | collective-permute-done | bytes 786464 | tf_op jit(solution)/shard_map/ppermute | solution.py:169
  281.9 2.5 add_convert_fusion.20
  285.9 11.8 %convolution_convert_fusion.1 = bf16[2304,1536]{1,0:T(8,128)(2,1)} fusion(bf16[1024,2304]{1,0:T(8,128)(2,1)} %get-tuple-element.71, bf16[1024,1536]{1,0:T(8,128)(2,1)S(1)} %copy-done.60), kind=kOutput, calls=%fused_computation.2 | convolution fusion | flops 7251296256 | bytes 14942208 | tf_op jit(solution)/shard_map/dot_general | solution.py:50
  299.8 2.4 constant_dynamic-slice_fusion.3
  302.1 2.1 pad_maximum_fusion.6
  304.2 6.0 collective-permute-start.2
  312.7 10.9 %convolution_convert_fusion.4 = bf16[1024,1536]{1,0:T(8,128)(2,1)} fusion(bf16[1024,2304]{1,0:T(8,128)(2,1)} %get-tuple-element.71, bf16[2304,1536]{1,0:T(8,128)(2,1)S(1)} %bitcast.58), kind=kOutput, calls=%fused_computation.15 | convolution fusion | flops 7249330176 | bytes 14942208 | tf_op jit(solution)/shard_map/dot_general | solution.py:940
  323.8 2.1 constant_dynamic-slice_fusion.18
  326.9 18.1 %collective-permute-done.5 = bf16[256,1536]{1,0:T(8,128)(2,1)S(1)} collective-permute-done((bf16[256,1536]{1,0:T(8,128)(2,1)}, bf16[256,1536]{1,0:T(8,128)(2,1)S(1)}, u32[]{:S(2)}, u32[]{:S(2)}) %collective-permute-start.5) | collective-permute-done | bytes 786464 | tf_op jit(solution)/shard_map/ppermute | solution.py:170
  345.0 3.0 multiply_reduce_fusion
  348.1 3.7 collective-permute-start.6
  353.3 12.5 %collective-permute-done.6 = bf16[256,1536]{1,0:T(8,128)(2,1)S(1)} collective-permute-done((bf16[256,1536]{1,0:T(8,128)(2,1)}, bf16[256,1536]{1,0:T(8,128)(2,1)S(1)}, u32[]{:S(2)}, u32[]{:S(2)}) %collective-permute-start.6) | collective-permute-done | bytes 786464 | tf_op jit(solution)/shard_map/ppermute | solution.py:169
  367.1 4.3 collective-permute-start.7
  371.4 5.0 add_convert_fusion.7
  379.0 5.2 collective-permute-done.7
  384.2 2.5 add_convert_fusion.18
  392.3 2.9 collective-permute-done.46
  396.5 2.5 collective-permute-done.48
  400.2 2.4 collective-permute-start.49
  405.8 3.1 collective-permute-done.49
  415.3 7.2 %add_convert_fusion.3 = (bf16[192,4608]{1,0:T(8,128)(2,1)}, bf16[192,4608]{1,0:T(8,128)(2,1)S(1)}, bf16[192,4608]{1,0:T(8,128)(2,1)S(1)}, bf16[192,4608]{1,0:T(8,128)(2,1)S(1)}) fusion(bf16[768,4608]{1,0:T(8,128)(2,1)} %collective-permute-done.37, bf16[1536,4608]{1,0:T(8,128)(2,1)} %convolution_convert_fusion, s32[]{:T(128)S(6)} %select_n.246, ...), kind=kLoop, calls=%fused_computation.20 | loop fusion | flops 14155776 | bytes 21233680 | tf_op jit(solution)/shard_map/convert_element_type | solution.py:66
  426.9 2.0 collective-permute-start.38
  428.9 6.4 collective-permute-done.11
  439.1 17.9 %attend_back.1 = (bf16[256,1536]{1,0:T(8,128)(2,1)S(1)}, f32[1024,256]{1,0:T(8,128)S(1)}, f32[1024,256]{1,0:T(8,128)S(1)}) custom-call(bf16[256,1536]{1,0:T(8,128)(2,1)S(1)} %copy-done.3, bf16[1024,512]{1,0:T(8,128)(2,1)S(1)} %bitcast.43, bf16[1024,512]{1,0:T(8,128)(2,1)S(1)} %bitcast.44, f32[1024,256]{1,0:T(8,128)} %and_select_fusion.bias, ...), custom_call_target="tpu_custom_call" | custom-call | flops 12079595520 | bytes 8388608 | tf_op jit(solution)/shard_map/attend_back/pallas_call | solution.py:223
  458.0 3.2 collective-permute-start.14
  461.2 2.5 collective-permute-start.13
  469.8 3.2 copy.36
  474.6 2.2 copy-done.5
  485.6 5.0 fusion.13
  493.3 2.4 copy-done.6
  501.4 2.1 collective-permute-start.39
  504.5 17.1 %collective-permute-done.16 = f32[5120]{0:T(1024)S(1)} collective-permute-done((f32[5120]{0:T(1024)S(1)}, f32[5120]{0:T(1024)S(1)}, u32[]{:S(2)}, u32[]{:S(2)}) %collective-permute-start.16) | collective-permute-done | bytes 20512 | tf_op jit(solution)/shard_map/ppermute | solution.py:71
  527.4 2.1 add_convert_fusion.8
  529.7 3.0 collective-permute-start.44
  532.6 2.0 collective-permute-start.43
  536.2 7.1 %collective-permute-done.44 = bf16[48,4608]{1,0:T(8,128)(2,1)S(1)} collective-permute-done((bf16[48,4608]{1,0:T(8,128)(2,1)S(1)}, bf16[48,4608]{1,0:T(8,128)(2,1)S(1)}, u32[]{:S(2)}, u32[]{:S(2)}) %collective-permute-start.44) | collective-permute-done | bytes 442400 | tf_op jit(solution)/shard_map/ppermute | solution.py:76
  543.4 27.5 %collective-permute-done.43 = bf16[48,4608]{1,0:T(8,128)(2,1)S(1)} collective-permute-done((bf16[48,4608]{1,0:T(8,128)(2,1)S(1)}, bf16[48,4608]{1,0:T(8,128)(2,1)S(1)}, u32[]{:S(2)}, u32[]{:S(2)}) %collective-permute-start.43) | collective-permute-done | bytes 442400 | tf_op jit(solution)/shard_map/ppermute | solution.py:76
  572.9 4.2 pad_maximum_fusion.11
  577.1 5.3 gather_fusion
  582.4 5.9 reshape.195
  588.8 3.0 copy.46
  591.9 3.2 add_convert_fusion.24
  599.0 3.2 add_convert_fusion.15
  606.6 2.2 fusion.45
  608.8 3.9 squeeze.24
  612.6 3.1 squeeze.25
  620.1 9.3 %collective-permute-done.24 = bf16[384,1024]{1,0:T(8,128)(2,1)} collective-permute-done((bf16[384,1024]{1,0:T(8,128)(2,1)}, bf16[384,1024]{1,0:T(8,128)(2,1)}, u32[]{:S(2)}, u32[]{:S(2)}) %collective-permute-start.24) | collective-permute-done | bytes 786464 | tf_op jit(solution)/shard_map/ppermute | solution.py:71
  633.9 3.3 collective-permute-done.33
  640.5 1.9 collective-permute-start.34
  647.5 2.2 collective-permute-start.26
  649.7 4.1 collective-permute-done.35
  654.6 13.0 %collective-permute-done.27 = bf16[48,2048]{1,0:T(8,128)(2,1)S(1)} collective-permute-done((bf16[48,2048]{1,0:T(8,128)(2,1)S(1)}, bf16[48,2048]{1,0:T(8,128)(2,1)S(1)}, u32[]{:S(2)}, u32[]{:S(2)}) %collective-permute-start.27) | collective-permute-done | bytes 196640 | tf_op jit(solution)/shard_map/ppermute | solution.py:76
  (330 shorter events, 113.3 us)
Async XLA Ops:
  175.9 21.3 %copy-start.59 = (bf16[1024,1536]{1,0:T(8,128)(2,1)S(1)}, bf16[1024,1536]{1,0:T(8,128)(2,1)}, u32[]{:S(2)}) copy-start(bf16[1024,1536]{1,0:T(8,128)(2,1)} %get-tuple-element.38) | copy-start | bytes 9437188
  236.2 74.0 %copy-start.11 = (bf16[1024,1536]{1,0:T(8,128)(2,1)}, bf16[1024,1536]{1,0:T(8,128)(2,1)S(1)}, u32[]{:S(2)}) copy-start(bf16[1024,1536]{1,0:T(8,128)(2,1)S(1)} %fusion.2) | copy-start | bytes 9437188
  237.2 24.1 %collective-permute-start = (bf16[256,1536]{1,0:T(8,128)(2,1)}, bf16[256,1536]{1,0:T(8,128)(2,1)}, u32[]{:S(2)}, u32[]{:S(2)}) collective-permute-start(bf16[256,1536]{1,0:T(8,128)(2,1)} %constant_dynamic-slice_fusion.16), channel_id=1, source_target_pairs={{0,1},{4,5},{8,9},{12,13},{16,17},{20,21},{24,25},{28,29}} | collective-permute-start | bytes 2359304 | tf_op jit(solution)/shard_map/ppermute | solution.py:169
  263.6 18.3 %collective-permute-start.1 = (bf16[256,1536]{1,0:T(8,128)(2,1)}, bf16[256,1536]{1,0:T(8,128)(2,1)}, u32[]{:S(2)}, u32[]{:S(2)}) collective-permute-start(bf16[256,1536]{1,0:T(8,128)(2,1)} %fusion.5), channel_id=1, source_target_pairs={{0,1},{1,2},{4,5},{5,6},{8,9},{9,10},{12,13},{13,14},{16,17},{17,1... | collective-permute-start | bytes 2359304 | tf_op jit(solution)/shard_map/ppermute | solution.py:169
  272.7 142.6 %collective-permute-start.37 = (bf16[768,4608]{1,0:T(8,128)(2,1)}, bf16[768,4608]{1,0:T(8,128)(2,1)}, u32[]{:S(2)}, u32[]{:S(2)}) collective-permute-start(bf16[768,4608]{1,0:T(8,128)(2,1)} %pad_maximum_fusion.1), channel_id=1, source_target_pairs={{0,4},{4,0},{8,12},{12,8},{16,20},{20,16},{24,28},{28,24},{1,5},{5... | collective-permute-start | bytes 21233672 | tf_op jit(solution)/shard_map/ppermute | solution.py:71
  272.7 13.2 %copy-start.60 = (bf16[1024,1536]{1,0:T(8,128)(2,1)S(1)}, bf16[1024,1536]{1,0:T(8,128)(2,1)}, u32[]{:S(2)}) copy-start(bf16[1024,1536]{1,0:T(8,128)(2,1)} %get-tuple-element.38) | copy-start | bytes 9437188
  284.4 13.3 %collective-permute-start.3 = (bf16[256,1536]{1,0:T(8,128)(2,1)}, bf16[256,1536]{1,0:T(8,128)(2,1)}, u32[]{:S(2)}, u32[]{:S(2)}) collective-permute-start(bf16[256,1536]{1,0:T(8,128)(2,1)} %get-tuple-element.62), channel_id=1, source_target_pairs={{3,2},{7,6},{11,10},{15,14},{19,18},{23,22},{27,26},{31,30}} | collective-permute-start | bytes 2359304 | tf_op jit(solution)/shard_map/ppermute | solution.py:170
  299.0 11.2 %collective-permute-start.4 = (bf16[256,1536]{1,0:T(8,128)(2,1)S(1)}, bf16[256,1536]{1,0:T(8,128)(2,1)S(1)}, u32[]{:S(2)}, u32[]{:S(2)}) collective-permute-start(bf16[256,1536]{1,0:T(8,128)(2,1)S(1)} %fusion.6), channel_id=1, source_target_pairs={{3,2},{2,1},{7,6},{6,5},{11,10},{10,9},{15,14},{14,13},{19,18},{18... | collective-permute-start | bytes 2359304 | tf_op jit(solution)/shard_map/ppermute | solution.py:170
  299.7 12.9 %slice-start.4 = ((s8[7077888]{0:T(1024)(128)(4,1)}), s8[4194304]{0:T(1024)(128)(4,1)S(1)}, s32[]{:S(2)}) async-start(s8[7077888]{0:T(1024)(128)(4,1)} %bitcast.57), calls=%async_computation.4 | async-start | bytes 8388608
  304.2 67.2 %collective-permute-start.45 = (bf16[1152,1536]{1,0:T(8,128)(2,1)}, bf16[1152,1536]{1,0:T(8,128)(2,1)}, u32[]{:S(2)}, u32[]{:S(2)}) collective-permute-start(bf16[1152,1536]{1,0:T(8,128)(2,1)} %pad_maximum_fusion.6), channel_id=1, source_target_pairs={{0,4},{4,0},{8,12},{12,8},{16,20},{20,16},{24,28},{28,24},{1,5},{5... | collective-permute-start | bytes 10616840 | tf_op jit(solution)/shard_map/ppermute | solution.py:71
  304.2 22.7 %collective-permute-start.2 = (bf16[256,1536]{1,0:T(8,128)(2,1)}, bf16[256,1536]{1,0:T(8,128)(2,1)}, u32[]{:S(2)}, u32[]{:S(2)}) collective-permute-start(bf16[256,1536]{1,0:T(8,128)(2,1)} %get-tuple-element.61), channel_id=1, source_target_pairs={{0,1},{1,2},{2,3},{4,5},{5,6},{6,7},{8,9},{9,10},{10,11},{12,13},{... | collective-permute-start | bytes 2359304 | tf_op jit(solution)/shard_map/ppermute | solution.py:169
  311.3 12.3 %copy-start.55 = (f32[1,1536]{1,0:T(1,128)S(1)}, f32[1,1536]{1,0:T(1,128)}, u32[]{:S(2)}) copy-start(f32[1,1536]{1,0:T(1,128)} %get-tuple-element.41) | copy-start | bytes 18436
  311.3 12.3 %copy-start.7 = (f32[256,1536]{1,0:T(8,128)S(1)}, f32[256,1536]{1,0:T(8,128)}, u32[]{:S(2)}) copy-start(f32[256,1536]{1,0:T(8,128)} %get-tuple-element.34) | copy-start | bytes 4718596
  311.3 33.8 %collective-permute-start.5 = (bf16[256,1536]{1,0:T(8,128)(2,1)}, bf16[256,1536]{1,0:T(8,128)(2,1)S(1)}, u32[]{:S(2)}, u32[]{:S(2)}) collective-permute-start(bf16[256,1536]{1,0:T(8,128)(2,1)} %add_convert_fusion.19), channel_id=1, source_target_pairs={{3,2},{2,1},{1,0},{7,6},{6,5},{5,4},{11,10},{10,9},{9,8},{15,14},{... | collective-permute-start | bytes 2359304 | tf_op jit(solution)/shard_map/ppermute | solution.py:170
  325.9 27.2 %copy-start.13 = (bf16[256,1536]{1,0:T(8,128)(2,1)S(1)}, bf16[256,1536]{1,0:T(8,128)(2,1)}, u32[]{:S(2)}) copy-start(bf16[256,1536]{1,0:T(8,128)(2,1)} %tokens.1) | copy-start | bytes 2359300
  348.1 17.7 %collective-permute-start.6 = (bf16[256,1536]{1,0:T(8,128)(2,1)}, bf16[256,1536]{1,0:T(8,128)(2,1)S(1)}, u32[]{:S(2)}, u32[]{:S(2)}) collective-permute-start(bf16[256,1536]{1,0:T(8,128)(2,1)} %constant_dynamic-slice_fusion.18), channel_id=1, source_target_pairs={{0,1},{4,5},{8,9},{12,13},{16,17},{20,21},{24,25},{28,29}} | collective-permute-start | bytes 2359304 | tf_op jit(solution)/shard_map/ppermute | solution.py:169
  367.1 17.1 %collective-permute-start.7 = (bf16[256,1536]{1,0:T(8,128)(2,1)S(1)}, bf16[256,1536]{1,0:T(8,128)(2,1)S(1)}, u32[]{:S(2)}, u32[]{:S(2)}) collective-permute-start(bf16[256,1536]{1,0:T(8,128)(2,1)S(1)} %fusion.3), channel_id=1, source_target_pairs={{0,1},{1,2},{4,5},{5,6},{8,9},{9,10},{12,13},{13,14},{16,17},{17,1... | collective-permute-start | bytes 2359304 | tf_op jit(solution)/shard_map/ppermute | solution.py:169
  377.7 17.5 %collective-permute-start.46 = (bf16[576,768]{1,0:T(8,128)(2,1)}, bf16[576,768]{1,0:T(8,128)(2,1)}, u32[]{:S(2)}, u32[]{:S(2)}) collective-permute-start(bf16[576,768]{1,0:T(8,128)(2,1)} %pad_maximum_fusion.14), channel_id=1, source_target_pairs={{0,8},{4,12},{8,0},{12,4},{16,24},{20,28},{24,16},{28,20},{1,9},{5... | collective-permute-start | bytes 2654216 | tf_op jit(solution)/shard_map/ppermute | solution.py:71
  379.0 20.0 %collective-permute-start.48 = (bf16[576,768]{1,0:T(8,128)(2,1)}, bf16[576,768]{1,0:T(8,128)(2,1)}, u32[]{:S(2)}, u32[]{:S(2)}) collective-permute-start(bf16[576,768]{1,0:T(8,128)(2,1)} %pad_maximum_fusion.15), channel_id=1, source_target_pairs={{0,16},{4,20},{8,24},{12,28},{16,0},{20,4},{24,8},{28,12},{1,17},{... | collective-permute-start | bytes 2654216 | tf_op jit(solution)/shard_map/ppermute | solution.py:71
  386.7 15.9 %collective-permute-start.9 = (bf16[256,1536]{1,0:T(8,128)(2,1)}, bf16[256,1536]{1,0:T(8,128)(2,1)}, u32[]{:S(2)}, u32[]{:S(2)}) collective-permute-start(bf16[256,1536]{1,0:T(8,128)(2,1)} %get-tuple-element.40), channel_id=1, source_target_pairs={{3,2},{7,6},{11,10},{15,14},{19,18},{23,22},{27,26},{31,30}} | collective-permute-start | bytes 2359304 | tf_op jit(solution)/shard_map/ppermute | solution.py:170
  391.1 11.6 %copy-start.10 = (bf16[1024,1536]{1,0:T(8,128)(2,1)S(1)}, bf16[1024,1536]{1,0:T(8,128)(2,1)}, u32[]{:S(2)}) copy-start(bf16[1024,1536]{1,0:T(8,128)(2,1)} %convolution_convert_fusion.4) | copy-start | bytes 9437188
  396.4 12.5 %copy-start.26 = (bf16[288,1536]{1,0:T(8,128)(2,1)S(1)}, bf16[288,1536]{1,0:T(8,128)(2,1)}, u32[]{:S(2)}) copy-start(bf16[288,1536]{1,0:T(8,128)(2,1)} %get-tuple-element.76) | copy-start | bytes 2654212
  396.4 9.4 %collective-permute-start.47 = (bf16[288,768]{1,0:T(8,128)(2,1)S(1)}, bf16[288,768]{1,0:T(8,128)(2,1)S(1)}, u32[]{:S(2)}, u32[]{:S(2)}) collective-permute-start(bf16[288,768]{1,0:T(8,128)(2,1)S(1)} %add_convert_fusion.28), channel_id=1, source_target_pairs={{0,16},{4,20},{8,24},{12,28},{16,0},{20,4},{24,8},{28,12},{1,17},{... | collective-permute-start | bytes 1327112 | tf_op jit(solution)/shard_map/ppermute | solution.py:71
  400.2 8.7 %collective-permute-start.49 = (bf16[288,768]{1,0:T(8,128)(2,1)S(1)}, bf16[288,768]{1,0:T(8,128)(2,1)S(1)}, u32[]{:S(2)}, u32[]{:S(2)}) collective-permute-start(bf16[288,768]{1,0:T(8,128)(2,1)S(1)} %add_convert_fusion.26), channel_id=1, source_target_pairs={{0,8},{4,12},{8,0},{12,4},{16,24},{20,28},{24,16},{28,20},{1,9},{5... | collective-permute-start | bytes 1327112 | tf_op jit(solution)/shard_map/ppermute | solution.py:71
  404.0 9.7 %collective-permute-start.10 = (bf16[256,1536]{1,0:T(8,128)(2,1)S(1)}, bf16[256,1536]{1,0:T(8,128)(2,1)S(1)}, u32[]{:S(2)}, u32[]{:S(2)}) collective-permute-start(bf16[256,1536]{1,0:T(8,128)(2,1)S(1)} %fusion.4), channel_id=1, source_target_pairs={{3,2},{2,1},{7,6},{6,5},{11,10},{10,9},{15,14},{14,13},{19,18},{18... | collective-permute-start | bytes 2359304 | tf_op jit(solution)/shard_map/ppermute | solution.py:170
  411.9 17.1 %collective-permute-start.8 = (bf16[256,1536]{1,0:T(8,128)(2,1)S(1)}, bf16[256,1536]{1,0:T(8,128)(2,1)S(1)}, u32[]{:S(2)}, u32[]{:S(2)}) collective-permute-start(bf16[256,1536]{1,0:T(8,128)(2,1)S(1)} %copy-done.44), channel_id=1, source_target_pairs={{0,1},{1,2},{2,3},{4,5},{5,6},{6,7},{8,9},{9,10},{10,11},{12,13},{... | collective-permute-start | bytes 2359304 | tf_op jit(solution)/shard_map/ppermute | solution.py:169
  414.0 21.3 %collective-permute-start.11 = (bf16[256,1536]{1,0:T(8,128)(2,1)S(1)}, bf16[256,1536]{1,0:T(8,128)(2,1)S(1)}, u32[]{:S(2)}, u32[]{:S(2)}) collective-permute-start(bf16[256,1536]{1,0:T(8,128)(2,1)S(1)} %add_convert_fusion.17), channel_id=1, source_target_pairs={{3,2},{2,1},{1,0},{7,6},{6,5},{5,4},{11,10},{10,9},{9,8},{15,14},{... | collective-permute-start | bytes 2359304 | tf_op jit(solution)/shard_map/ppermute | solution.py:170
  425.2 72.4 %collective-permute-start.40 = (bf16[384,2304]{1,0:T(8,128)(2,1)}, bf16[384,2304]{1,0:T(8,128)(2,1)}, u32[]{:S(2)}, u32[]{:S(2)}) collective-permute-start(bf16[384,2304]{1,0:T(8,128)(2,1)} %pad_maximum_fusion.10), channel_id=1, source_target_pairs={{0,16},{4,20},{8,24},{12,28},{16,0},{20,4},{24,8},{28,12},{1,17},{... | collective-permute-start | bytes 5308424 | tf_op jit(solution)/shard_map/ppermute | solution.py:71
  425.5 11.5 %slice-start.6 = ((s8[4718592]{0:T(1024)(128)(4,1)}), s8[4194304]{0:T(1024)(128)(4,1)S(1)}, s32[]{:S(2)}) async-start(s8[4718592]{0:T(1024)(128)(4,1)} %bitcast.59), calls=%async_computation.6 | async-start | bytes 8388608
  426.9 73.1 %collective-permute-start.38 = (bf16[384,2304]{1,0:T(8,128)(2,1)}, bf16[384,2304]{1,0:T(8,128)(2,1)}, u32[]{:S(2)}, u32[]{:S(2)}) collective-permute-start(bf16[384,2304]{1,0:T(8,128)(2,1)} %pad_maximum_fusion.9), channel_id=1, source_target_pairs={{0,8},{4,12},{8,0},{12,4},{16,24},{20,28},{24,16},{28,20},{1,9},{5... | collective-permute-start | bytes 5308424 | tf_op jit(solution)/shard_map/ppermute | solution.py:71
  458.0 22.1 %collective-permute-start.14 = (bf16[256,512]{1,0:T(8,128)(2,1)}, bf16[256,512]{1,0:T(8,128)(2,1)}, u32[]{:S(2)}, u32[]{:S(2)}) collective-permute-start(bf16[256,512]{1,0:T(8,128)(2,1)} %get-tuple-element.116), channel_id=1, source_target_pairs={{0,1},{1,2},{2,3},{3,0},{4,5},{5,6},{6,7},{7,4},{8,9},{9,10},{10,1... | collective-permute-start | bytes 786440 | tf_op jit(solution)/shard_map/ppermute | solution.py:76
  461.2 18.8 %collective-permute-start.13 = (bf16[256,512]{1,0:T(8,128)(2,1)}, bf16[256,512]{1,0:T(8,128)(2,1)}, u32[]{:S(2)}, u32[]{:S(2)}) collective-permute-start(bf16[256,512]{1,0:T(8,128)(2,1)} %get-tuple-element.115), channel_id=1, source_target_pairs={{0,2},{1,3},{2,0},{3,1},{4,6},{5,7},{6,4},{7,5},{8,10},{9,11},{10,... | collective-permute-start | bytes 786440 | tf_op jit(solution)/shard_map/ppermute | solution.py:76
  463.8 16.3 %collective-permute-start.12 = (bf16[256,512]{1,0:T(8,128)(2,1)}, bf16[256,512]{1,0:T(8,128)(2,1)}, u32[]{:S(2)}, u32[]{:S(2)}) collective-permute-start(bf16[256,512]{1,0:T(8,128)(2,1)} %get-tuple-element.114), channel_id=1, source_target_pairs={{0,3},{1,0},{2,1},{3,2},{4,7},{5,4},{6,5},{7,6},{8,11},{9,8},{10,9... | collective-permute-start | bytes 786440 | tf_op jit(solution)/shard_map/ppermute | solution.py:76
  480.0 111.8 %collective-permute-start.29 = (bf16[768,1536]{1,0:T(8,128)(2,1)}, bf16[768,1536]{1,0:T(8,128)(2,1)}, u32[]{:S(2)}, u32[]{:S(2)}) collective-permute-start(bf16[768,1536]{1,0:T(8,128)(2,1)} %pad_maximum_fusion.8), channel_id=1, source_target_pairs={{0,4},{4,0},{8,12},{12,8},{16,20},{20,16},{24,28},{28,24},{1,5},{5... | collective-permute-start | bytes 7077896 | tf_op jit(solution)/shard_map/ppermute | solution.py:71
  490.6 12.9 %collective-permute-start.15 = (f32[5120]{0:T(1024)S(1)}, f32[5120]{0:T(1024)S(1)}, u32[]{:S(2)}, u32[]{:S(2)}) collective-permute-start(f32[5120]{0:T(1024)S(1)} %pad_maximum_fusion.25), channel_id=1, source_target_pairs={{0,4},{4,0},{8,12},{12,8},{16,20},{20,16},{24,28},{28,24},{1,5},{5... | collective-permute-start | bytes 61448 | tf_op jit(solution)/shard_map/ppermute | solution.py:71
  499.5 27.0 %collective-permute-start.41 = (bf16[192,2304]{1,0:T(8,128)(2,1)S(1)}, bf16[192,2304]{1,0:T(8,128)(2,1)S(1)}, u32[]{:S(2)}, u32[]{:S(2)}) collective-permute-start(bf16[192,2304]{1,0:T(8,128)(2,1)S(1)} %add_convert_fusion.9), channel_id=1, source_target_pairs={{0,8},{4,12},{8,0},{12,4},{16,24},{20,28},{24,16},{28,20},{1,9},{5... | collective-permute-start | bytes 2654216 | tf_op jit(solution)/shard_map/ppermute | solution.py:71
  501.4 26.0 %collective-permute-start.39 = (bf16[192,2304]{1,0:T(8,128)(2,1)S(1)}, bf16[192,2304]{1,0:T(8,128)(2,1)S(1)}, u32[]{:S(2)}, u32[]{:S(2)}) collective-permute-start(bf16[192,2304]{1,0:T(8,128)(2,1)S(1)} %add_convert_fusion.11), channel_id=1, source_target_pairs={{0,16},{4,20},{8,24},{12,28},{16,0},{20,4},{24,8},{28,12},{1,17},{... | collective-permute-start | bytes 2654216 | tf_op jit(solution)/shard_map/ppermute | solution.py:71
  503.5 18.0 %collective-permute-start.16 = (f32[5120]{0:T(1024)S(1)}, f32[5120]{0:T(1024)S(1)}, u32[]{:S(2)}, u32[]{:S(2)}) collective-permute-start(f32[5120]{0:T(1024)S(1)} %fusion.69), channel_id=1, source_target_pairs={{0,8},{4,12},{8,0},{12,4},{16,24},{20,28},{24,16},{28,20},{1,9},{5... | collective-permute-start | bytes 61448 | tf_op jit(solution)/shard_map/ppermute | solution.py:71
  504.4 94.5 %collective-permute-start.21 = (bf16[768,2048]{1,0:T(8,128)(2,1)}, bf16[768,2048]{1,0:T(8,128)(2,1)}, u32[]{:S(2)}, u32[]{:S(2)}) collective-permute-start(bf16[768,2048]{1,0:T(8,128)(2,1)} %pad_maximum_fusion.7), channel_id=1, source_target_pairs={{0,4},{4,0},{8,12},{12,8},{16,20},{20,16},{24,28},{28,24},{1,5},{5... | collective-permute-start | bytes 9437192 | tf_op jit(solution)/shard_map/ppermute | solution.py:71
  521.6 3.8 collective-permute-start.17
  525.4 4.3 collective-permute-start.20
  526.5 6.1 collective-permute-start.18
  527.4 7.3 %collective-permute-start.19 = (f32[5120]{0:T(1024)S(1)}, f32[5120]{0:T(1024)S(1)}, u32[]{:S(2)}, u32[]{:S(2)}) collective-permute-start(f32[5120]{0:T(1024)S(1)} %add.492), channel_id=1, source_target_pairs={{0,2},{1,3},{2,0},{3,1},{4,6},{5,7},{6,4},{7,5},{8,10},{9,11},{10,... | collective-permute-start | bytes 61448 | tf_op jit(solution)/shard_map/ppermute | solution.py:76
  529.7 13.6 %collective-permute-start.44 = (bf16[48,4608]{1,0:T(8,128)(2,1)S(1)}, bf16[48,4608]{1,0:T(8,128)(2,1)S(1)}, u32[]{:S(2)}, u32[]{:S(2)}) collective-permute-start(bf16[48,4608]{1,0:T(8,128)(2,1)S(1)} %get-tuple-element.105), channel_id=1, source_target_pairs={{0,3},{1,0},{2,1},{3,2},{4,7},{5,4},{6,5},{7,6},{8,11},{9,8},{10,9... | collective-permute-start | bytes 1327112 | tf_op jit(solution)/shard_map/ppermute | solution.py:76
  532.6 38.2 %collective-permute-start.43 = (bf16[48,4608]{1,0:T(8,128)(2,1)S(1)}, bf16[48,4608]{1,0:T(8,128)(2,1)S(1)}, u32[]{:S(2)}, u32[]{:S(2)}) collective-permute-start(bf16[48,4608]{1,0:T(8,128)(2,1)S(1)} %get-tuple-element.104), channel_id=1, source_target_pairs={{0,2},{1,3},{2,0},{3,1},{4,6},{5,7},{6,4},{7,5},{8,10},{9,11},{10,... | collective-permute-start | bytes 1327112 | tf_op jit(solution)/shard_map/ppermute | solution.py:76
  534.7 36.3 %collective-permute-start.42 = (bf16[48,4608]{1,0:T(8,128)(2,1)S(1)}, bf16[48,4608]{1,0:T(8,128)(2,1)}, u32[]{:S(2)}, u32[]{:S(2)}) collective-permute-start(bf16[48,4608]{1,0:T(8,128)(2,1)S(1)} %get-tuple-element.103), channel_id=1, source_target_pairs={{0,1},{1,2},{2,3},{3,0},{4,5},{5,6},{6,7},{7,4},{8,9},{9,10},{10,1... | collective-permute-start | bytes 1327112 | tf_op jit(solution)/shard_map/ppermute | solution.py:76
  596.1 19.6 %collective-permute-start.32 = (bf16[384,768]{1,0:T(8,128)(2,1)}, bf16[384,768]{1,0:T(8,128)(2,1)}, u32[]{:S(2)}, u32[]{:S(2)}) collective-permute-start(bf16[384,768]{1,0:T(8,128)(2,1)} %pad_maximum_fusion.20), channel_id=1, source_target_pairs={{0,16},{4,20},{8,24},{12,28},{16,0},{20,4},{24,8},{28,12},{1,17},{... | collective-permute-start | bytes 1769480 | tf_op jit(solution)/shard_map/ppermute | solution.py:71
  597.9 19.9 %collective-permute-start.30 = (bf16[384,768]{1,0:T(8,128)(2,1)}, bf16[384,768]{1,0:T(8,128)(2,1)}, u32[]{:S(2)}, u32[]{:S(2)}) collective-permute-start(bf16[384,768]{1,0:T(8,128)(2,1)} %pad_maximum_fusion.19), channel_id=1, source_target_pairs={{0,8},{4,12},{8,0},{12,4},{16,24},{20,28},{24,16},{28,20},{1,9},{5... | collective-permute-start | bytes 1769480 | tf_op jit(solution)/shard_map/ppermute | solution.py:71
  603.4 26.0 %collective-permute-start.24 = (bf16[384,1024]{1,0:T(8,128)(2,1)}, bf16[384,1024]{1,0:T(8,128)(2,1)}, u32[]{:S(2)}, u32[]{:S(2)}) collective-permute-start(bf16[384,1024]{1,0:T(8,128)(2,1)} %pad_maximum_fusion.18), channel_id=1, source_target_pairs={{0,16},{4,20},{8,24},{12,28},{16,0},{20,4},{24,8},{28,12},{1,17},{... | collective-permute-start | bytes 2359304 | tf_op jit(solution)/shard_map/ppermute | solution.py:71
  605.2 26.3 %collective-permute-start.22 = (bf16[384,1024]{1,0:T(8,128)(2,1)}, bf16[384,1024]{1,0:T(8,128)(2,1)}, u32[]{:S(2)}, u32[]{:S(2)}) collective-permute-start(bf16[384,1024]{1,0:T(8,128)(2,1)} %pad_maximum_fusion.17), channel_id=1, source_target_pairs={{0,8},{4,12},{8,0},{12,4},{16,24},{20,28},{24,16},{28,20},{1,9},{5... | collective-permute-start | bytes 2359304 | tf_op jit(solution)/shard_map/ppermute | solution.py:71
  615.7 13.7 %copy-start.33 = (bf16[192,2048]{1,0:T(8,128)(2,1)S(1)}, bf16[192,2048]{1,0:T(8,128)(2,1)}, u32[]{:S(2)}) copy-start(bf16[192,2048]{1,0:T(8,128)(2,1)} %copy-done.32) | copy-start | bytes 2359300
  615.7 15.7 %copy-start.31 = (bf16[192,2048]{1,0:T(8,128)(2,1)S(1)}, bf16[192,2048]{1,0:T(8,128)(2,1)}, u32[]{:S(2)}) copy-start(bf16[192,2048]{1,0:T(8,128)(2,1)} %copy-done.30) | copy-start | bytes 2359300
  617.0 20.2 %copy-start.38 = (bf16[192,1536]{1,0:T(8,128)(2,1)S(1)}, bf16[192,1536]{1,0:T(8,128)(2,1)}, u32[]{:S(2)}) copy-start(bf16[192,1536]{1,0:T(8,128)(2,1)} %get-tuple-element.88) | copy-start | bytes 1769476
  617.0 20.2 %collective-permute-start.33 = (bf16[192,768]{1,0:T(8,128)(2,1)S(1)}, bf16[192,768]{1,0:T(8,128)(2,1)S(1)}, u32[]{:S(2)}, u32[]{:S(2)}) collective-permute-start(bf16[192,768]{1,0:T(8,128)(2,1)S(1)} %add_convert_fusion.34), channel_id=1, source_target_pairs={{0,8},{4,12},{8,0},{12,4},{16,24},{20,28},{24,16},{28,20},{1,9},{5... | collective-permute-start | bytes 884744 | tf_op jit(solution)/shard_map/ppermute | solution.py:71
  618.9 18.3 %collective-permute-start.31 = (bf16[192,768]{1,0:T(8,128)(2,1)S(1)}, bf16[192,768]{1,0:T(8,128)(2,1)S(1)}, u32[]{:S(2)}, u32[]{:S(2)}) collective-permute-start(bf16[192,768]{1,0:T(8,128)(2,1)S(1)} %add_convert_fusion.36), channel_id=1, source_target_pairs={{0,16},{4,20},{8,24},{12,28},{16,0},{20,4},{24,8},{28,12},{1,17},{... | collective-permute-start | bytes 884744 | tf_op jit(solution)/shard_map/ppermute | solution.py:71
  630.6 11.9 %collective-permute-start.25 = (bf16[192,1024]{1,0:T(8,128)(2,1)S(1)}, bf16[192,1024]{1,0:T(8,128)(2,1)S(1)}, u32[]{:S(2)}, u32[]{:S(2)}) collective-permute-start(bf16[192,1024]{1,0:T(8,128)(2,1)S(1)} %add_convert_fusion.30), channel_id=1, source_target_pairs={{0,8},{4,12},{8,0},{12,4},{16,24},{20,28},{24,16},{28,20},{1,9},{5... | collective-permute-start | bytes 1179656 | tf_op jit(solution)/shard_map/ppermute | solution.py:71
  632.6 9.9 %collective-permute-start.23 = (bf16[192,1024]{1,0:T(8,128)(2,1)S(1)}, bf16[192,1024]{1,0:T(8,128)(2,1)S(1)}, u32[]{:S(2)}, u32[]{:S(2)}) collective-permute-start(bf16[192,1024]{1,0:T(8,128)(2,1)S(1)} %add_convert_fusion.32), channel_id=1, source_target_pairs={{0,16},{4,20},{8,24},{12,28},{16,0},{20,4},{24,8},{28,12},{1,17},{... | collective-permute-start | bytes 1179656 | tf_op jit(solution)/shard_map/ppermute | solution.py:71
  638.5 9.0 %collective-permute-start.36 = (bf16[48,1536]{1,0:T(8,128)(2,1)S(1)}, bf16[48,1536]{1,0:T(8,128)(2,1)S(1)}, u32[]{:S(2)}, u32[]{:S(2)}) collective-permute-start(bf16[48,1536]{1,0:T(8,128)(2,1)S(1)} %get-tuple-element.130), channel_id=1, source_target_pairs={{0,3},{1,0},{2,1},{3,2},{4,7},{5,4},{6,5},{7,6},{8,11},{9,8},{10,9... | collective-permute-start | bytes 442376 | tf_op jit(solution)/shard_map/ppermute | solution.py:76
  638.6 15.2 %collective-permute-start.35 = (bf16[48,1536]{1,0:T(8,128)(2,1)S(1)}, bf16[48,1536]{1,0:T(8,128)(2,1)S(1)}, u32[]{:S(2)}, u32[]{:S(2)}) collective-permute-start(bf16[48,1536]{1,0:T(8,128)(2,1)S(1)} %get-tuple-element.129), channel_id=1, source_target_pairs={{0,2},{1,3},{2,0},{3,1},{4,6},{5,7},{6,4},{7,5},{8,10},{9,11},{10,... | collective-permute-start | bytes 442376 | tf_op jit(solution)/shard_map/ppermute | solution.py:76
  640.5 13.3 %collective-permute-start.34 = (bf16[48,1536]{1,0:T(8,128)(2,1)S(1)}, bf16[48,1536]{1,0:T(8,128)(2,1)S(1)}, u32[]{:S(2)}, u32[]{:S(2)}) collective-permute-start(bf16[48,1536]{1,0:T(8,128)(2,1)S(1)} %get-tuple-element.128), channel_id=1, source_target_pairs={{0,1},{1,2},{2,3},{3,0},{4,5},{5,6},{6,7},{7,4},{8,9},{9,10},{10,1... | collective-permute-start | bytes 442376 | tf_op jit(solution)/shard_map/ppermute | solution.py:76
  644.1 10.5 %collective-permute-start.28 = (bf16[48,2048]{1,0:T(8,128)(2,1)S(1)}, bf16[48,2048]{1,0:T(8,128)(2,1)S(1)}, u32[]{:S(2)}, u32[]{:S(2)}) collective-permute-start(bf16[48,2048]{1,0:T(8,128)(2,1)S(1)} %get-tuple-element.123), channel_id=1, source_target_pairs={{0,3},{1,0},{2,1},{3,2},{4,7},{5,4},{6,5},{7,6},{8,11},{9,8},{10,9... | collective-permute-start | bytes 589832 | tf_op jit(solution)/shard_map/ppermute | solution.py:76
  646.0 21.6 %collective-permute-start.27 = (bf16[48,2048]{1,0:T(8,128)(2,1)S(1)}, bf16[48,2048]{1,0:T(8,128)(2,1)S(1)}, u32[]{:S(2)}, u32[]{:S(2)}) collective-permute-start(bf16[48,2048]{1,0:T(8,128)(2,1)S(1)} %get-tuple-element.122), channel_id=1, source_target_pairs={{0,2},{1,3},{2,0},{3,1},{4,6},{5,7},{6,4},{7,5},{8,10},{9,11},{10,... | collective-permute-start | bytes 589832 | tf_op jit(solution)/shard_map/ppermute | solution.py:76
  647.5 21.5 %copy-start.1 = (bf16[1120,1536]{1,0:T(8,128)(2,1)S(1)}, bf16[1120,1536]{1,0:T(8,128)(2,1)}, u32[]{:S(2)}) copy-start(bf16[1120,1536]{1,0:T(8,128)(2,1)} %param.32) | copy-start | bytes 10321924
  647.5 20.0 %collective-permute-start.26 = (bf16[48,2048]{1,0:T(8,128)(2,1)S(1)}, bf16[48,2048]{1,0:T(8,128)(2,1)S(1)}, u32[]{:S(2)}, u32[]{:S(2)}) collective-permute-start(bf16[48,2048]{1,0:T(8,128)(2,1)S(1)} %get-tuple-element.121), channel_id=1, source_target_pairs={{0,1},{1,2},{2,3},{3,0},{4,5},{5,6},{6,7},{7,4},{8,9},{9,10},{10,1... | collective-permute-start | bytes 589832 | tf_op jit(solution)/shard_map/ppermute | solution.py:76
  (55 other events, 222.6 us)

commit v4 on v3

--- a/solution.py
+++ b/solution.py
@@ -111,7 +111,6 @@
         return lax.psum_scatter(whole, "fsdp", scatter_dimension=0, tiled=True)
     rank = lax.axis_index("fsdp")
     rows = whole.shape[0] // count
-    half = whole.shape[1] // 2
     if earlier:
         whole = after(whole, *earlier)
 
@@ -119,9 +118,15 @@
         return lax.dynamic_slice_in_dim(whole, (rank ^ k) * rows, rows, 0)
 
     arrived = cross(jnp.concatenate([part(1), part(3), part(5), part(7)], 0), 1)
-    own, to_x, to_y, to_both = [
-        add_low(part(2 * i), arrived[i * rows : (i + 1) * rows]) for i in range(4)
-    ]
+    return scatter_chips(
+        [add_low(part(2 * i), arrived[i * rows : (i + 1) * rows]) for i in range(4)]
+    )
+
+
+def scatter_chips(parts):
+    own, to_x, to_y, to_both = parts
+    rows = own.shape[0]
+    half = own.shape[1] // 2
     got_x = cross(jnp.concatenate([to_x[:, :half], to_both[:, :half]], 0), 2)
     got_y = cross(jnp.concatenate([to_y[:, half:], to_both[:, half:]], 0), 4)
     last_y = cross(add_low(to_y[:, :half], got_x[rows:]), 4)
@@ -862,6 +867,350 @@
     )
 
 
+ORDER = (1, 3, 2, 0)
+
+
+def ffn_kernel(
+    normed_all, upstream_all, w_gu, w_down,
+    columns, grad_down, gu_sum, branch, down_arrived, gu_arrived,
+    normed, upstream, gu, down, hidden, d_both, partial, z_one, z_two, z_three,
+    down_x, down_y, down_last, branch_piece,
+    load, ssem, rsem,
+):
+    f = lax.axis_index("fsdp")
+    s = lax.axis_index("seq")
+    n_s = len(ORDER)
+    group, width = normed.shape
+    rows = group // n_s
+    half_rows = group // 2
+    units = down.shape[0]
+    tile = 256
+    tiles = units // tile
+    block = gu.shape[0] // 8
+    unit = units // 8
+    half = width // 2
+    plane = [f ^ k for k in range(8)]
+    full = jnp.float32
+
+    entry = pltpu.get_barrier_semaphore()
+    for k in (1, 2, 4):
+        pl.semaphore_signal(entry, inc=1, device_id={"fsdp": plane[k]}, device_id_type=MESH)
+    for j in (1, n_s - 1):
+        pl.semaphore_signal(
+            entry, inc=1, device_id={"seq": lax.rem(s + j, n_s)}, device_id_type=MESH
+        )
+
+    def here(source, target, index):
+        return pltpu.make_async_copy(source, target, load.at[index])
+
+    def there(source, target, index, **device):
+        return pltpu.make_async_remote_copy(
+            src_ref=source, dst_ref=target, send_sem=ssem.at[index], recv_sem=rsem.at[index],
+            device_id=device, device_id_type=MESH,
+        )
+
+    def part(ref, owner, size):
+        return ref.at[pl.ds(pl.multiple_of(owner * size, 16), size)]
+
+    first_loads = []
+    for p, j in enumerate(ORDER):
+        owner = lax.rem(s + n_s - j, n_s)
+        first_loads.append(here(part(normed_all, owner, rows), part(normed, p, rows), p))
+        first_loads.append(here(part(upstream_all, owner, rows), part(upstream, p, rows), 4 + p))
+
+    def tile_loads(t):
+        gate_columns = pl.ds(pl.multiple_of(t * tile, tile), tile)
+        up_columns = pl.ds(pl.multiple_of(units + t * tile, tile), tile)
+        return [
+            here(w_gu.at[:, gate_columns], gu.at[:, gate_columns], 8 + 3 * t),
+            here(w_gu.at[:, up_columns], gu.at[:, up_columns], 9 + 3 * t),
+            here(w_down.at[gate_columns], down.at[gate_columns], 10 + 3 * t),
+        ]
+
+    for copy in first_loads:
+        copy.start()
+    for t in range(tiles):
+        for copy in tile_loads(t):
+            copy.start()
+    for copy in first_loads:
+        copy.wait()
+
+    def forward(part_rows, wait):
+        def body(t, carry):
+            if wait:
+                for copy in tile_loads(t):
+                    copy.wait()
+            gate_columns = pl.ds(pl.multiple_of(t * tile, tile), tile)
+            up_columns = pl.ds(pl.multiple_of(units + t * tile, tile), tile)
+            mine = normed[part_rows]
+            gate = jnp.dot(mine, gu[:, gate_columns], preferred_element_type=full)
+            up = jnp.dot(mine, gu[:, up_columns], preferred_element_type=full)
+            d_hidden = lax.dot_general(
+                upstream[part_rows], down[gate_columns], (((1,), (1,)), ((), ())),
+                preferred_element_type=full,
+            )
+            sigma = jax.nn.sigmoid(gate)
+            activated = gate * sigma
+            hidden[part_rows, gate_columns] = (activated * up).astype(jnp.bfloat16)
+            d_both[part_rows, gate_columns] = (
+                d_hidden * up * sigma * (1.0 + gate * (1.0 - sigma))
+            ).astype(jnp.bfloat16)
+            d_both[part_rows, up_columns] = (d_hidden * activated).astype(jnp.bfloat16)
+            return carry
+
+        lax.fori_loop(0, tiles, body, 0)
+
+    def backward(part_rows):
+        def body(n, carry):
+            out_columns = pl.ds(pl.multiple_of(n * tile, tile), tile)
+            value = lax.dot_general(
+                d_both[part_rows], gu[out_columns], (((1,), (1,)), ((), ())),
+                preferred_element_type=full,
+            )
+            partial[part_rows, out_columns] = value.astype(jnp.bfloat16)
+            return carry
+
+        lax.fori_loop(0, width // tile, body, 0)
+
+    def held(j):
+        return partial.at[ORDER.index(j) * rows : (ORDER.index(j) + 1) * rows]
+
+    up_one = there(held(1), z_one, 0, seq=s + 1)
+    down_one = there(held(3), z_one, 1, seq=s - 1)
+    up_two = there(held(2), z_two.at[0], 2, seq=s + 1)
+    down_two = there(held(2), z_two.at[1], 3, seq=s - 1)
+    up_three = there(held(3), z_three.at[0], 4, seq=s + 1)
+    down_three = there(held(1), z_three.at[1], 5, seq=s - 1)
+
+    def add_to(j, arrived):
+        ref = held(j)
+        ref[...] = (ref[...].astype(full) + arrived[...].astype(full)).astype(jnp.bfloat16)
+
+    def chain_one():
+        pl.when(s == 0)(up_one.start)
+        pl.when(s == 3)(down_one.start)
+
+    def chain_two():
+        @pl.when(s == 1)
+        def _():
+            up_one.wait_recv()
+            add_to(2, z_one)
+
+        @pl.when(s == 2)
+        def _():
+            down_one.wait_recv()
+            add_to(2, z_one)
+
+        pl.when(s <= 1)(up_two.start)
+        pl.when(s >= 2)(down_two.start)
+
+    def chain_three():
+        @pl.when((s == 1) | (s == 2))
+        def _():
+            up_two.wait_recv()
+            add_to(3, z_two.at[0])
+            down_two.wait_recv()
+            add_to(1, z_two.at[1])
+
+        pl.when(s <= 2)(up_three.start)
+        pl.when(s >= 1)(down_three.start)
+
+    def chain_last():
+        columns[...] = held(0)[...].astype(full)
+
+        @pl.when(s >= 1)
+        def _():
+            up_three.wait_recv()
+            columns[...] += z_three[0].astype(full)
+
+        @pl.when(s <= 2)
+        def _():
+            down_three.wait_recv()
+            columns[...] += z_three[1].astype(full)
+
+    def chain_sent():
+        pl.when(s == 0)(up_one.wait_send)
+        pl.when(s == 3)(down_one.wait_send)
+        pl.when(s <= 1)(up_two.wait_send)
+        pl.when(s >= 2)(down_two.wait_send)
+        pl.when(s <= 2)(up_three.wait_send)
+        pl.when(s >= 1)(down_three.wait_send)
+
+    early, late = slice(0, half_rows), slice(half_rows, group)
+    forward(early, True)
+    backward(early)
+    pl.semaphore_wait(entry, 5)
+    chain_one()
+    forward(late, False)
+    backward(late)
+    chain_two()
+
+    def branch_store(n):
+        out_columns = pl.ds(pl.multiple_of(n * tile, tile), tile)
+        return here(branch_piece.at[lax.rem(n, 2)], branch.at[:, out_columns], 8 + n)
+
+    def branch_body(n, carry):
+        out_columns = pl.ds(pl.multiple_of(n * tile, tile), tile)
+        value = jnp.dot(hidden[...], down[:, out_columns], preferred_element_type=full)
+
+        @pl.when(n >= 2)
+        def _():
+            branch_store(n - 2).wait()
+
+        branch_piece[lax.rem(n, 2)] = value.astype(jnp.bfloat16)
+        branch_store(n).start()
+        return carry
+
+    lax.fori_loop(0, width // tile, branch_body, 0)
+    for n in (width // tile - 2, width // tile - 1):
+        branch_store(n).wait()
+
+    def down_body(t, carry):
+        unit_rows = pl.ds(pl.multiple_of(t * tile, tile), tile)
+        value = lax.dot_general(
+            hidden[:, unit_rows], upstream[...], (((0,), (0,)), ((), ())),
+            preferred_element_type=full,
+        )
+        down[unit_rows] = value.astype(jnp.bfloat16)
+        return carry
+
+    lax.fori_loop(0, tiles, down_body, 0)
+    down_core = [
+        there(part(down, plane[2 * i + 1], unit), down_arrived.at[i], 6 + i, fsdp=plane[1])
+        for i in range(4)
+    ]
+    for copy in down_core:
+        copy.start()
+
+    def gu_body(m, carry):
+        in_columns = pl.ds(pl.multiple_of(m * tile, tile), tile)
+        turned = normed[:, in_columns].T
+        for first in range(0, 2 * units, units // 3):
+            value = jnp.dot(turned, d_both[:, first : first + units // 3], preferred_element_type=full)
+            gu[in_columns, first : first + units // 3] = value.astype(jnp.bfloat16)
+        return carry
+
+    lax.fori_loop(0, width // tile // 2, gu_body, 0)
+
+    def add_arrived(ref, size, arrived, pieces, copies, index):
+        for i in range(4):
+            copies[i].wait_recv()
+            fetch = [
+                here(arrived.at[i, :, columns], piece, index + k)
+                for k, (columns, piece) in enumerate(pieces)
+            ]
+            for copy in fetch:
+                copy.start()
+            target = part(ref, plane[2 * i], size)
+            for copy, (columns, piece) in zip(fetch, pieces):
+                copy.wait()
+                target[:, columns] = (
+                    target[:, columns].astype(full) + piece[...].astype(full)
+                ).astype(jnp.bfloat16)
+
+    add_arrived(down, unit, down_arrived, [(pl.ds(0, width), hidden.at[:unit, :width])], down_core, 14)
+    to_x, to_y, to_both = [part(down, plane[k], unit) for k in (2, 4, 6)]
+    low_half, high_half = pl.ds(0, half), pl.ds(half, half)
+    down_first = [
+        there(to_x.at[:, low_half], down_x.at[0], 10, fsdp=plane[2]),
+        there(to_both.at[:, low_half], down_x.at[1], 11, fsdp=plane[2]),
+        there(to_y.at[:, high_half], down_y.at[0], 12, fsdp=plane[4]),
+        there(to_both.at[:, high_half], down_y.at[1], 13, fsdp=plane[4]),
+    ]
+    for copy in down_first:
+        copy.start()
+    chain_three()
+    lax.fori_loop(width // tile // 2, width // tile, gu_body, 0)
+    gu_core = [
+        there(part(gu, plane[2 * i + 1], block), gu_arrived.at[i], 16 + i, fsdp=plane[1])
+        for i in range(4)
+    ]
+    for copy in gu_core:
+        copy.start()
+    chain_last()
+    down_second = [
+        there(to_y.at[:, low_half], down_last.at[0], 14, fsdp=plane[4]),
+        there(to_x.at[:, high_half], down_last.at[1], 15, fsdp=plane[2]),
+    ]
+    down_first[1].wait_recv()
+    to_y[:, :half] = (to_y[:, :half].astype(full) + down_x[1].astype(full)).astype(jnp.bfloat16)
+    down_second[0].start()
+    down_first[3].wait_recv()
+    to_x[:, half:] = (to_x[:, half:].astype(full) + down_y[1].astype(full)).astype(jnp.bfloat16)
+    down_second[1].start()
+    gu_pieces = [
+        (pl.ds(0, units), hidden.at[:block]),
+        (pl.ds(units, units), hidden.at[block : 2 * block]),
+    ]
+    add_arrived(gu, block, gu_arrived, gu_pieces, gu_core, 20)
+    store = [here(part(gu, plane[2 * i], block), gu_sum.at[i], 16 + i) for i in range(4)]
+    for copy in store:
+        copy.start()
+    down_first[0].wait_recv()
+    down_first[2].wait_recv()
+    own = part(down, f, unit)
+    down_second[0].wait_recv()
+    grad_down[:, :half] = (
+        own[:, :half].astype(full) + down_x[0].astype(full) + down_last[0].astype(full)
+    )
+    down_second[1].wait_recv()
+    grad_down[:, half:] = (
+        own[:, half:].astype(full) + down_y[0].astype(full) + down_last[1].astype(full)
+    )
+    for copy in store:
+        copy.wait()
+    chain_sent()
+    for copy in down_core + down_first + down_second + gu_core:
+        copy.wait_send()
+
+
+def ffn(normed_all, upstream_all, w_gu, w_down):
+    group, width = normed_all.shape
+    units = w_down.shape[0]
+    rows = group // len(ORDER)
+    unit, block, half = units // 8, width // 8, width // 2
+    low, full = jnp.bfloat16, jnp.float32
+    vmem = pl.BlockSpec(memory_space=pltpu.VMEM)
+    hbm = pl.BlockSpec(memory_space=pl.ANY)
+    shape = jax.ShapeDtypeStruct
+    return pl.pallas_call(
+        ffn_kernel,
+        in_specs=[hbm] * 4,
+        out_specs=[vmem] * 2 + [hbm] * 4,
+        out_shape=[
+            shape((rows, width), full),
+            shape((unit, width), full),
+            shape((4, block, 2 * units), low),
+            shape((group, width), low),
+            shape((4, unit, width), low),
+            shape((4, block, 2 * units), low),
+        ],
+        scratch_shapes=[
+            pltpu.VMEM((group, width), low),
+            pltpu.VMEM((group, width), low),
+            pltpu.VMEM((width, 2 * units), low),
+            pltpu.VMEM((units, width), low),
+            pltpu.VMEM((group, units), low),
+            pltpu.VMEM((group, 2 * units), low),
+            pltpu.VMEM((group, width), low),
+            pltpu.VMEM((rows, width), low),
+            pltpu.VMEM((2, rows, width), low),
+            pltpu.VMEM((2, rows, width), low),
+            pltpu.VMEM((2, unit, half), low),
+            pltpu.VMEM((2, unit, half), low),
+            pltpu.VMEM((2, unit, half), low),
+            pltpu.VMEM((2, group, 256), low),
+            pltpu.SemaphoreType.DMA((36,)),
+            pltpu.SemaphoreType.DMA((20,)),
+            pltpu.SemaphoreType.DMA((20,)),
+        ],
+        compiler_params=pltpu.CompilerParams(
+            collective_id=1, has_side_effects=True, vmem_limit_bytes=63 * 2**20
+        ),
+        name="ffn",
+    )(normed_all, upstream_all, w_gu, w_down)[:4]
+
+
 def per_device(
     tokens, cotangent, lengths, balance, norm1_gain, w_query, b_query, w_key, b_key,
     w_value, b_value, w_out, norm2_gain, w_gate, w_up, w_down,
@@ -921,24 +1270,11 @@
             for j in range(seq_count)
         ]
 
-    both = jnp.dot(normed_all, weight_gu, preferred_element_type=jnp.float32)
-    gate = both[:, :padded]
-    up = both[:, padded:]
-    sigma = jax.nn.sigmoid(gate)
-    activated = gate * sigma
-    hidden = (activated * up).astype(jnp.bfloat16)
-    d_hidden = contract_columns(upstream_all, weight_down)
-    d_gate = (d_hidden * up * sigma * (1.0 + gate * (1.0 - sigma))).astype(jnp.bfloat16)
-    d_up = (d_hidden * activated).astype(jnp.bfloat16)
-    d_both = jnp.concatenate([d_gate, d_up], 1)
-    columns = contract_columns(d_both, weight_gu).astype(jnp.bfloat16)
-    columns = scatter_seq(blocks_back(columns))
-
-    grad_down = contract_rows(hidden, upstream_all).astype(jnp.bfloat16)
-    grad_down = scatter_plane(grad_down)[:unit].astype(jnp.float32)
-    grad_pair = scatter_plane(contract_rows(normed_all, d_both).astype(jnp.bfloat16))
-    branch = jnp.dot(hidden, weight_down, preferred_element_type=jnp.float32).astype(jnp.bfloat16)
-    branch = scatter_seq(blocks_back(branch), (columns,))
+    columns, grad_down, gu_sum, branch = ffn(normed_all, upstream_all, weight_gu, weight_down)
+    grad_down = grad_down[:unit]
+    grad_pair = scatter_chips(gu_sum)
+    branch = [branch[ORDER.index(j) * rows_here : (ORDER.index(j) + 1) * rows_here] for j in range(seq_count)]
+    branch = scatter_seq(branch)
     layer_out = (resid + branch).astype(jnp.bfloat16)
     grad_pair = exchange_seq(grad_pair)
     own_rows = weight_rows // seq_count

time: 678 us -> 581 us (0.86)
  Pallas kernels: 179 us -> 289 us
  matrix products: 114 us -> 9.1 us
  waiting for transfers between devices: 145 us -> 99.4 us
  other arithmetic: 95.9 us -> 55.4 us
  starting transfers between devices: 70.4 us -> 60.1 us
    pallas_call x0 -> x1, Pallas kernels: none -> 110 us  [ffn(): pl.pallas_call(ffn_kernel, in_specs=[hbm] * 4, out_specs=[vmem] * 2 + [hb...]
    dot_general x4 -> x2, matrix products: 45.5 us -> 3.7 us  [contract_columns(): lax.dot_general(left, right, (((1,), (1,)), ((), ())), preferred_element_...]
    dot_general x2 -> x0, matrix products: 32.1 us -> none  [the longest x1 21.3 us: per_device(): both = jnp.dot(normed_all, weight_gu, preferred_element_type=jnp.float32)]
    dot_general x4 -> x2, matrix products: 36.9 us -> 5.4 us  [contract_rows(): lax.dot_general(left, right, (((0,), (0,)), ((), ())), preferred_element_...]
    convert_element_type x24 -> x13, other arithmetic: 47.3 us -> 23.1 us  [add_low(): sum((value.astype(jnp.float32) for value in values)).astype(jnp.bfloat16)]
    ppermute x23 -> x17, waiting for transfers between devices: 40.4 us -> 19.5 us  [cross(): return lax.ppermute(value, 'fsdp', [(i, i ^ bits) for i in range(count)])]
    ppermute x6 -> x3, waiting for transfers between devices: 24.5 us -> 4.17 us  [scatter_seq(): lax.ppermute(send_down, 'seq', [(i, i - 1) for i in range(count - 1, max(...]
    ppermute x6 -> x3, waiting for transfers between devices: 27.9 us -> 20 us  [scatter_seq(): lax.ppermute(send_up, 'seq', [(i, i + 1) for i in range(min(step, count -...]
  transfers between devices with their start and end apart: 50 -> 38, of which waited for: 18 -> 17; matrix products, arithmetic and copies ran while one was open for 28% -> 17% of each run, Pallas kernels for 3% -> 3%
where the time goes in v4:
time: 581 us; the launch traced here: 575 us
  Pallas kernels  289 us (50%)
  waiting for transfers between devices  99.4 us (17%)
  starting transfers between devices  60.1 us (10%)
  local copies, waits for them, and re-layouts  59.7 us (10%)
  other arithmetic  55.4 us (10%)
  matrix products  9.1 us (2%)
    pallas_call x1, Pallas kernels, front(): pl.pallas_call(front_kernel, in_specs=[vmem, hbm] + [vmem] * 6 + [hbm] *...  161 us
    pallas_call x1, Pallas kernels, ffn(): pl.pallas_call(ffn_kernel, in_specs=[hbm] * 4, out_specs=[vmem] * 2 + [hb...  110 us
    ppermute x15, waiting for transfers between devices, shift(): lax.ppermute(value, 'seq', [(i, (i + step) % count) for i in range(count)])  55.7 us
    ppermute x15, starting transfers between devices, shift(): lax.ppermute(value, 'seq', [(i, (i + step) % count) for i in range(count)])  26.5 us
    convert_element_type x13, other arithmetic, add_low(): sum((value.astype(jnp.float32) for value in values)).astype(jnp.bfloat16)  23.1 us
    ppermute x3, waiting for transfers between devices, scatter_seq(): lax.ppermute(send_up, 'seq', [(i, i + 1) for i in range(min(step, count -...  20 us
    ppermute x17, waiting for transfers between devices, cross(): return lax.ppermute(value, 'fsdp', [(i, i ^ bits) for i in range(count)])  19.5 us
    pallas_call x1, Pallas kernels, attend_back(): pl.pallas_call(attend_back_kernel, grid=(HEADS,), in_specs=[pl.BlockSpec(...  17.9 us
  transfers between devices with their start and end apart: 38, of which 17 were waited for; matrix products, arithmetic and copies ran while one was open for 17% of the time, Pallas kernels for 3%

profile of v4, /device:TPU:0, one launch (start us, length us, event | category | flops | bytes accessed | tf_op | source)
XLA Modules:
  0.0 574.8 jit_solution(9857722601150422703)
XLA Ops:
  4.2 2.6 subtract_convert_fusion.1
  6.9 1.9 fusion.35
  15.2 160.7 %front.1 = (bf16[1536,4608]{1,0:T(8,128)(2,1)}, bf16[2304,1536]{1,0:T(8,128)(2,1)}, bf16[1024,1536]{1,0:T(8,128)(2,1)}, bf16[1024,1536]{1,0:T(8,128)(2,1)}, bf16...) custom-call(bf16[256,1536]{1,0:T(8,128)(2,1)} %tokens.1, ...), custom_call_target="tpu_custom_call" | custom-call | tf_op jit(solution)/shard_map/front/pallas_call | solution.py:822
  175.9 110.3 %ffn.1 = (f32[256,1536]{1,0:T(8,128)}, f32[288,1536]{1,0:T(8,128)}, bf16[4,192,4608]{2,1,0:T(8,128)(2,1)}, bf16[1024,1536]{1,0:T(8,128)(2,1)}, bf16[4,288,1536]{...) custom-call(bf16[1024,1536]{1,0:T(8,128)(2,1)} %get-tuple-element.37.normed_all, ...), custom_call_target="tpu_custom_call" | custom-call | tf_op jit(solution)/shard_map/ffn/pallas_call | solution.py:1176
  286.2 4.7 slice_bitcast_fusion.3
  291.1 1.6 pad_maximum_fusion.2
  292.7 2.2 collective-permute-start.31
  298.7 3.5 collective-permute-start
  302.2 1.6 collective-permute-start.3
  307.0 1.6 copy.33
  308.7 2.9 slice.272
  313.3 3.3 collective-permute-done
  316.6 1.7 fusion
  318.3 4.4 collective-permute-start.1
  324.7 12.1 %collective-permute-done.1 = bf16[256,1536]{1,0:T(8,128)(2,1)S(1)} collective-permute-done((bf16[256,1536]{1,0:T(8,128)(2,1)S(1)}, bf16[256,1536]{1,0:T(8,128)(2,1)S(1)}, u32[]{:S(2)}, u32[]{:S(2)}) %collective-permute-start.1) | collective-permute-done | bytes 786464 | tf_op jit(solution)/shard_map/ppermute | solution.py:174
  337.2 7.9 %collective-permute-start.2 = (bf16[256,1536]{1,0:T(8,128)(2,1)S(1)}, bf16[256,1536]{1,0:T(8,128)(2,1)S(1)}, u32[]{:S(2)}, u32[]{:S(2)}) collective-permute-start(bf16[256,1536]{1,0:T(8,128)(2,1)S(1)} %get-tuple-element.86), channel_id=1, source_target_pairs={{0,1},{1,2},{2,3},{4,5},{5,6},{6,7},{8,9},{9,10},{10,11},{12,13},{... | collective-permute-start | bytes 2359304 | tf_op jit(solution)/shard_map/ppermute | solution.py:174
  345.1 1.8 collective-permute-start.5
  346.9 2.3 add_convert_fusion.3
  349.5 2.3 add_convert_fusion.1
  351.7 1.8 collective-permute-start.34
  353.6 4.7 collective-permute-done.2
  358.2 4.2 collective-permute-done.5
  362.4 1.7 fusion.2
  364.1 3.6 convolution_convert_fusion.1
  369.2 17.9 %attend_back.1 = (bf16[256,1536]{1,0:T(8,128)(2,1)S(1)}, f32[1024,256]{1,0:T(8,128)S(1)}, f32[1024,256]{1,0:T(8,128)S(1)}) custom-call(bf16[256,1536]{1,0:T(8,128)(2,1)S(1)} %copy-done.1, bf16[1024,512]{1,0:T(8,128)(2,1)S(1)} %bitcast.41, bf16[1024,512]{1,0:T(8,128)(2,1)S(1)} %bitcast.42, f32[1024,256]{1,0:T(8,128)} %and_select_fusion.bias, ...), custom_call_target="tpu_custom_call" | custom-call | flops 12079595520 | bytes 8388608 | tf_op jit(solution)/shard_map/attend_back/pallas_call | solution.py:228
  388.5 1.5 broadcast_multiply_fusion
  391.4 3.0 copy.36
  394.7 1.7 collective-permute-start.7
  397.3 1.8 constant_dynamic-slice_fusion.3
  399.1 1.6 pad_maximum_fusion.1
  400.7 4.3 collective-permute-done.6
  405.0 9.9 %collective-permute-done.7 = bf16[256,512]{1,0:T(8,128)(2,1)S(1)} collective-permute-done((bf16[256,512]{1,0:T(8,128)(2,1)S(1)}, bf16[256,512]{1,0:T(8,128)(2,1)S(1)}, u32[]{:S(2)}, u32[]{:S(2)}) %collective-permute-start.7) | collective-permute-done | bytes 262176 | tf_op jit(solution)/shard_map/ppermute | solution.py:76
  416.8 1.8 convolution_convert_fusion
  418.9 2.6 copy-done.3
  421.5 1.8 pad_maximum_fusion
  423.3 2.3 fusion.8
  426.2 2.8 collective-permute-done.9
  430.4 2.4 collective-permute-done.10
  432.8 2.6 add_convert_fusion
  437.9 2.9 collective-permute-start.14
  442.8 4.0 collective-permute-start.37
  448.0 9.1 %collective-permute-done.35 = bf16[48,4608]{1,0:T(8,128)(2,1)S(1)} collective-permute-done((bf16[48,4608]{1,0:T(8,128)(2,1)S(1)}, bf16[48,4608]{1,0:T(8,128)(2,1)S(1)}, u32[]{:S(2)}, u32[]{:S(2)}) %collective-permute-start.35) | collective-permute-done | bytes 442400 | tf_op jit(solution)/shard_map/ppermute | solution.py:76
  457.2 15.5 %collective-permute-done.36 = bf16[48,4608]{1,0:T(8,128)(2,1)S(1)} collective-permute-done((bf16[48,4608]{1,0:T(8,128)(2,1)S(1)}, bf16[48,4608]{1,0:T(8,128)(2,1)S(1)}, u32[]{:S(2)}, u32[]{:S(2)}) %collective-permute-start.36) | collective-permute-done | bytes 442400 | tf_op jit(solution)/shard_map/ppermute | solution.py:76
  475.1 3.3 pad_maximum_fusion.4
  478.4 5.3 gather_fusion
  483.7 5.9 %reshape.195 = bf16[4,48,2,8,288]{4,3,2,1,0:T(8,128)(2,1)S(1)} reshape(bf16[4,48,2,2304]{3,2,1,0:T(2,128)(2,1)} %gather_fusion) | data formatting | bytes 3538944 | tf_op jit(solution)/shard_map/reshape | solution.py:1284
  490.1 3.0 copy.46
  493.2 3.3 add_convert_fusion.14
  497.5 1.7 collective-permute-start.24
  500.3 3.2 add_convert_fusion.7
  504.7 1.8 collective-permute-start.16
  507.8 2.2 fusion.37
  510.0 3.9 squeeze.24
  513.9 3.1 squeeze.25
  518.3 1.7 collective-permute-start.25
  521.4 9.1 %collective-permute-done.16 = bf16[384,1024]{1,0:T(8,128)(2,1)} collective-permute-done((bf16[384,1024]{1,0:T(8,128)(2,1)}, bf16[384,1024]{1,0:T(8,128)(2,1)}, u32[]{:S(2)}, u32[]{:S(2)}) %collective-permute-start.16) | collective-permute-done | bytes 786464 | tf_op jit(solution)/shard_map/ppermute | solution.py:71
  531.6 2.1 collective-permute-start.17
  535.1 4.1 collective-permute-done.25
  540.5 8.0 %collective-permute-start.28 = (bf16[48,1536]{1,0:T(8,128)(2,1)S(1)}, bf16[48,1536]{1,0:T(8,128)(2,1)S(1)}, u32[]{:S(2)}, u32[]{:S(2)}) collective-permute-start(bf16[48,1536]{1,0:T(8,128)(2,1)S(1)} %get-tuple-element.114), channel_id=1, source_target_pairs={{0,1},{1,2},{2,3},{3,0},{4,5},{5,6},{6,7},{7,4},{8,9},{9,10},{10,1... | collective-permute-start | bytes 442376 | tf_op jit(solution)/shard_map/ppermute | solution.py:76
  550.9 1.5 add_convert_fusion.15
  552.5 2.5 collective-permute-start.20
  555.1 2.4 collective-permute-start.22
  557.5 6.4 %collective-permute-done.29 = bf16[48,1536]{1,0:T(8,128)(2,1)S(1)} collective-permute-done((bf16[48,1536]{1,0:T(8,128)(2,1)S(1)}, bf16[48,1536]{1,0:T(8,128)(2,1)S(1)}, u32[]{:S(2)}, u32[]{:S(2)}) %collective-permute-start.29) | collective-permute-done | bytes 147488 | tf_op jit(solution)/shard_map/ppermute | solution.py:76
  564.6 8.2 %collective-permute-done.21 = bf16[48,2048]{1,0:T(8,128)(2,1)S(1)} collective-permute-done((bf16[48,2048]{1,0:T(8,128)(2,1)S(1)}, bf16[48,2048]{1,0:T(8,128)(2,1)S(1)}, u32[]{:S(2)}, u32[]{:S(2)}) %collective-permute-start.21) | collective-permute-done | bytes 196640 | tf_op jit(solution)/shard_map/ppermute | solution.py:76
  (235 shorter events, 55.2 us)
Async XLA Ops:
  290.9 3.9 copy-start.8
  292.7 54.2 %collective-permute-start.31 = (bf16[384,2304]{1,0:T(8,128)(2,1)}, bf16[384,2304]{1,0:T(8,128)(2,1)}, u32[]{:S(2)}, u32[]{:S(2)}) collective-permute-start(bf16[384,2304]{1,0:T(8,128)(2,1)} %pad_maximum_fusion.2), channel_id=1, source_target_pairs={{0,8},{4,12},{8,0},{12,4},{16,24},{20,28},{24,16},{28,20},{1,9},{5... | collective-permute-start | bytes 5308424 | tf_op jit(solution)/shard_map/ppermute | solution.py:71
  296.3 7.6 %copy-start.10 = (bf16[256,1536]{1,0:T(8,128)(2,1)S(1)}, bf16[256,1536]{1,0:T(8,128)(2,1)}, u32[]{:S(2)}) copy-start(bf16[256,1536]{1,0:T(8,128)(2,1)} %tokens.1) | copy-start | bytes 2359300
  296.3 53.2 %collective-permute-start.33 = (bf16[384,2304]{1,0:T(8,128)(2,1)}, bf16[384,2304]{1,0:T(8,128)(2,1)}, u32[]{:S(2)}, u32[]{:S(2)}) collective-permute-start(bf16[384,2304]{1,0:T(8,128)(2,1)} %pad_maximum_fusion.3), channel_id=1, source_target_pairs={{0,16},{4,20},{8,24},{12,28},{16,0},{20,4},{24,8},{28,12},{1,17},{... | collective-permute-start | bytes 5308424 | tf_op jit(solution)/shard_map/ppermute | solution.py:71
  297.5 6.6 %copy-start.31 = (f32[4,256,128]{2,1,0:T(8,128)S(1)}, f32[4,256,128]{2,1,0:T(8,128)}, u32[]{:S(2)}) copy-start(f32[4,256,128]{2,1,0:T(8,128)} %get-tuple-element.46) | copy-start | bytes 1572868
  297.5 6.9 %copy-start.26 = (f32[256,128]{1,0:T(8,128)S(1)}, f32[256,128]{1,0:T(8,128)}, u32[]{:S(2)}) copy-start(f32[256,128]{1,0:T(8,128)} %get-tuple-element.141.cosine) | copy-start | bytes 393220
  297.5 7.7 %copy-start.27 = (f32[256,128]{1,0:T(8,128)S(1)}, f32[256,128]{1,0:T(8,128)}, u32[]{:S(2)}) copy-start(f32[256,128]{1,0:T(8,128)} %get-tuple-element.125) | copy-start | bytes 393220
  298.7 17.9 %collective-permute-start = (bf16[256,1536]{1,0:T(8,128)(2,1)}, bf16[256,1536]{1,0:T(8,128)(2,1)}, u32[]{:S(2)}, u32[]{:S(2)}) collective-permute-start(bf16[256,1536]{1,0:T(8,128)(2,1)} %get-tuple-element.90), channel_id=1, source_target_pairs={{0,1},{4,5},{8,9},{12,13},{16,17},{20,21},{24,25},{28,29}} | collective-permute-start | bytes 2359304 | tf_op jit(solution)/shard_map/ppermute | solution.py:174
  302.2 14.4 %collective-permute-start.3 = (bf16[256,1536]{1,0:T(8,128)(2,1)}, bf16[256,1536]{1,0:T(8,128)(2,1)}, u32[]{:S(2)}, u32[]{:S(2)}) collective-permute-start(bf16[256,1536]{1,0:T(8,128)(2,1)} %get-tuple-element.91), channel_id=1, source_target_pairs={{3,2},{7,6},{11,10},{15,14},{19,18},{23,22},{27,26},{31,30}} | collective-permute-start | bytes 2359304 | tf_op jit(solution)/shard_map/ppermute | solution.py:175
  308.6 3.0 copy-start.4
  311.7 4.9 copy-start.13
  318.3 18.5 %collective-permute-start.1 = (bf16[256,1536]{1,0:T(8,128)(2,1)S(1)}, bf16[256,1536]{1,0:T(8,128)(2,1)S(1)}, u32[]{:S(2)}, u32[]{:S(2)}) collective-permute-start(bf16[256,1536]{1,0:T(8,128)(2,1)S(1)} %get-tuple-element.88), channel_id=1, source_target_pairs={{0,1},{1,2},{4,5},{5,6},{8,9},{9,10},{12,13},{13,14},{16,17},{17,1... | collective-permute-start | bytes 2359304 | tf_op jit(solution)/shard_map/ppermute | solution.py:174
  322.7 14.0 %collective-permute-start.4 = (bf16[256,1536]{1,0:T(8,128)(2,1)S(1)}, bf16[256,1536]{1,0:T(8,128)(2,1)S(1)}, u32[]{:S(2)}, u32[]{:S(2)}) collective-permute-start(bf16[256,1536]{1,0:T(8,128)(2,1)S(1)} %get-tuple-element.89), channel_id=1, source_target_pairs={{3,2},{2,1},{7,6},{6,5},{11,10},{10,9},{15,14},{14,13},{19,18},{18... | collective-permute-start | bytes 2359304 | tf_op jit(solution)/shard_map/ppermute | solution.py:175
  324.7 22.2 %copy-start.9 = (bf16[192,4608]{1,0:T(8,128)(2,1)S(1)}, bf16[192,4608]{1,0:T(8,128)(2,1)}, u32[]{:S(2)}) copy-start(bf16[192,4608]{1,0:T(8,128)(2,1)} %copy-done.8) | copy-start | bytes 5308420
  337.2 21.0 %collective-permute-start.2 = (bf16[256,1536]{1,0:T(8,128)(2,1)S(1)}, bf16[256,1536]{1,0:T(8,128)(2,1)S(1)}, u32[]{:S(2)}, u32[]{:S(2)}) collective-permute-start(bf16[256,1536]{1,0:T(8,128)(2,1)S(1)} %get-tuple-element.86), channel_id=1, source_target_pairs={{0,1},{1,2},{2,3},{4,5},{5,6},{6,7},{8,9},{9,10},{10,11},{12,13},{... | collective-permute-start | bytes 2359304 | tf_op jit(solution)/shard_map/ppermute | solution.py:174
  345.1 17.3 %collective-permute-start.5 = (bf16[256,1536]{1,0:T(8,128)(2,1)S(1)}, bf16[256,1536]{1,0:T(8,128)(2,1)S(1)}, u32[]{:S(2)}, u32[]{:S(2)}) collective-permute-start(bf16[256,1536]{1,0:T(8,128)(2,1)S(1)} %get-tuple-element.87), channel_id=1, source_target_pairs={{3,2},{2,1},{1,0},{7,6},{6,5},{5,4},{11,10},{10,9},{9,8},{15,14},{... | collective-permute-start | bytes 2359304 | tf_op jit(solution)/shard_map/ppermute | solution.py:175
  349.2 13.2 %copy-start.21 = (bf16[256,1536]{1,0:T(8,128)(2,1)S(1)}, bf16[256,1536]{1,0:T(8,128)(2,1)}, u32[]{:S(2)}) copy-start(bf16[256,1536]{1,0:T(8,128)(2,1)} %cotangent.1) | copy-start | bytes 2359300
  349.2 83.6 %collective-permute-start.32 = (bf16[192,2304]{1,0:T(8,128)(2,1)}, bf16[192,2304]{1,0:T(8,128)(2,1)}, u32[]{:S(2)}, u32[]{:S(2)}) collective-permute-start(bf16[192,2304]{1,0:T(8,128)(2,1)} %add_convert_fusion.3), channel_id=1, source_target_pairs={{0,16},{4,20},{8,24},{12,28},{16,0},{20,4},{24,8},{28,12},{1,17},{... | collective-permute-start | bytes 2654216 | tf_op jit(solution)/shard_map/ppermute | solution.py:71
  351.7 12.4 %copy-start.25 = (bf16[256,1536]{1,0:T(8,128)(2,1)S(1)}, bf16[256,1536]{1,0:T(8,128)(2,1)}, u32[]{:S(2)}) copy-start(bf16[256,1536]{1,0:T(8,128)(2,1)} %get-tuple-element.55) | copy-start | bytes 2359300
  351.7 81.1 %collective-permute-start.34 = (bf16[192,2304]{1,0:T(8,128)(2,1)}, bf16[192,2304]{1,0:T(8,128)(2,1)}, u32[]{:S(2)}, u32[]{:S(2)}) collective-permute-start(bf16[192,2304]{1,0:T(8,128)(2,1)} %add_convert_fusion.1), channel_id=1, source_target_pairs={{0,8},{4,12},{8,0},{12,4},{16,24},{20,28},{24,16},{28,20},{1,9},{5... | collective-permute-start | bytes 2654216 | tf_op jit(solution)/shard_map/ppermute | solution.py:71
  362.4 5.3 slice-start.6
  364.1 3.6 copy-start.5
  364.1 3.6 slice-start.7
  394.7 10.3 %collective-permute-start.6 = (bf16[256,512]{1,0:T(8,128)(2,1)S(1)}, bf16[256,512]{1,0:T(8,128)(2,1)S(1)}, u32[]{:S(2)}, u32[]{:S(2)}) collective-permute-start(bf16[256,512]{1,0:T(8,128)(2,1)S(1)} %get-tuple-element.104), channel_id=1, source_target_pairs={{0,3},{1,0},{2,1},{3,2},{4,7},{5,4},{6,5},{7,6},{8,11},{9,8},{10,9... | collective-permute-start | bytes 786440 | tf_op jit(solution)/shard_map/ppermute | solution.py:76
  394.7 20.1 %collective-permute-start.7 = (bf16[256,512]{1,0:T(8,128)(2,1)S(1)}, bf16[256,512]{1,0:T(8,128)(2,1)S(1)}, u32[]{:S(2)}, u32[]{:S(2)}) collective-permute-start(bf16[256,512]{1,0:T(8,128)(2,1)S(1)} %get-tuple-element.105), channel_id=1, source_target_pairs={{0,2},{1,3},{2,0},{3,1},{4,6},{5,7},{6,4},{7,5},{8,10},{9,11},{10,... | collective-permute-start | bytes 786440 | tf_op jit(solution)/shard_map/ppermute | solution.py:76
  396.4 18.4 %collective-permute-start.8 = (bf16[256,512]{1,0:T(8,128)(2,1)S(1)}, bf16[256,512]{1,0:T(8,128)(2,1)S(1)}, u32[]{:S(2)}, u32[]{:S(2)}) collective-permute-start(bf16[256,512]{1,0:T(8,128)(2,1)S(1)} %get-tuple-element.106), channel_id=1, source_target_pairs={{0,1},{1,2},{2,3},{3,0},{4,5},{5,6},{6,7},{7,4},{8,9},{9,10},{10,1... | collective-permute-start | bytes 786440 | tf_op jit(solution)/shard_map/ppermute | solution.py:76
  400.7 14.5 %copy-start.28 = (f32[256,128]{1,0:T(8,128)S(1)}, f32[256,128]{1,0:T(8,128)}, u32[]{:S(2)}) copy-start(f32[256,128]{1,0:T(8,128)} %get-tuple-element.125) | copy-start | bytes 393220
  405.0 88.2 %collective-permute-start.23 = (bf16[768,1536]{1,0:T(8,128)(2,1)}, bf16[768,1536]{1,0:T(8,128)(2,1)}, u32[]{:S(2)}, u32[]{:S(2)}) collective-permute-start(bf16[768,1536]{1,0:T(8,128)(2,1)} %pad_maximum_fusion.1), channel_id=1, source_target_pairs={{0,4},{4,0},{8,12},{12,8},{16,20},{20,16},{24,28},{28,24},{1,5},{5... | collective-permute-start | bytes 7077896 | tf_op jit(solution)/shard_map/ppermute | solution.py:71
  416.8 6.5 %slice-start.4 = ((s8[6291456]{0:T(1024)(128)(4,1)}), s8[4194304]{0:T(1024)(128)(4,1)S(1)}, s32[]{:S(2)}) async-start(s8[6291456]{0:T(1024)(128)(4,1)} %bitcast.55), calls=%async_computation.4 | async-start | bytes 8388608
  418.7 4.6 slice-start.5
  423.3 77.0 %collective-permute-start.15 = (bf16[768,2048]{1,0:T(8,128)(2,1)}, bf16[768,2048]{1,0:T(8,128)(2,1)}, u32[]{:S(2)}, u32[]{:S(2)}) collective-permute-start(bf16[768,2048]{1,0:T(8,128)(2,1)} %pad_maximum_fusion), channel_id=1, source_target_pairs={{0,4},{4,0},{8,12},{12,8},{16,20},{20,16},{24,28},{28,24},{1,5},{5... | collective-permute-start | bytes 9437192 | tf_op jit(solution)/shard_map/ppermute | solution.py:71
  423.3 5.7 copy-start.6
  425.6 3.3 collective-permute-start.9
  429.0 3.8 collective-permute-start.10
  429.0 3.8 copy-start.7
  432.8 3.8 collective-permute-start.11
  436.6 5.6 collective-permute-start.12
  436.6 5.6 collective-permute-start.13
  437.9 4.9 collective-permute-start.14
  442.2 15.0 %collective-permute-start.35 = (bf16[48,4608]{1,0:T(8,128)(2,1)S(1)}, bf16[48,4608]{1,0:T(8,128)(2,1)S(1)}, u32[]{:S(2)}, u32[]{:S(2)}) collective-permute-start(bf16[48,4608]{1,0:T(8,128)(2,1)S(1)} %get-tuple-element.93), channel_id=1, source_target_pairs={{0,1},{1,2},{2,3},{3,0},{4,5},{5,6},{6,7},{7,4},{8,9},{9,10},{10,1... | collective-permute-start | bytes 1327112 | tf_op jit(solution)/shard_map/ppermute | solution.py:76
  442.2 30.5 %collective-permute-start.36 = (bf16[48,4608]{1,0:T(8,128)(2,1)S(1)}, bf16[48,4608]{1,0:T(8,128)(2,1)S(1)}, u32[]{:S(2)}, u32[]{:S(2)}) collective-permute-start(bf16[48,4608]{1,0:T(8,128)(2,1)S(1)} %get-tuple-element.94), channel_id=1, source_target_pairs={{0,2},{1,3},{2,0},{3,1},{4,6},{5,7},{6,4},{7,5},{8,10},{9,11},{10,... | collective-permute-start | bytes 1327112 | tf_op jit(solution)/shard_map/ppermute | solution.py:76
  442.8 31.1 %collective-permute-start.37 = (bf16[48,4608]{1,0:T(8,128)(2,1)S(1)}, bf16[48,4608]{1,0:T(8,128)(2,1)}, u32[]{:S(2)}, u32[]{:S(2)}) collective-permute-start(bf16[48,4608]{1,0:T(8,128)(2,1)S(1)} %get-tuple-element.95), channel_id=1, source_target_pairs={{0,3},{1,0},{2,1},{3,2},{4,7},{5,4},{6,5},{7,6},{8,11},{9,8},{10,9... | collective-permute-start | bytes 1327112 | tf_op jit(solution)/shard_map/ppermute | solution.py:76
  489.6 3.5 slice-start
  490.1 3.1 slice-start.1
  490.1 10.2 %slice-start.2 = ((s8[6291456]{0:T(1024)(128)(4,1)}), s8[4194304]{0:T(1024)(128)(4,1)S(1)}, s32[]{:S(2)}) async-start(s8[6291456]{0:T(1024)(128)(4,1)} %bitcast.45), calls=%async_computation.2 | async-start | bytes 8388608
  493.1 7.1 %slice-start.3 = ((s8[6291456]{0:T(1024)(128)(4,1)}), s8[2097152]{0:T(1024)(128)(4,1)S(1)}, s32[]{:S(2)}) async-start(s8[6291456]{0:T(1024)(128)(4,1)} %bitcast.45), calls=%async_computation.3 | async-start | bytes 4194304
  497.5 19.5 %collective-permute-start.24 = (bf16[384,768]{1,0:T(8,128)(2,1)}, bf16[384,768]{1,0:T(8,128)(2,1)}, u32[]{:S(2)}, u32[]{:S(2)}) collective-permute-start(bf16[384,768]{1,0:T(8,128)(2,1)} %pad_maximum_fusion.9), channel_id=1, source_target_pairs={{0,8},{4,12},{8,0},{12,4},{16,24},{20,28},{24,16},{28,20},{1,9},{5... | collective-permute-start | bytes 1769480 | tf_op jit(solution)/shard_map/ppermute | solution.py:71
  500.1 19.9 %collective-permute-start.26 = (bf16[384,768]{1,0:T(8,128)(2,1)}, bf16[384,768]{1,0:T(8,128)(2,1)}, u32[]{:S(2)}, u32[]{:S(2)}) collective-permute-start(bf16[384,768]{1,0:T(8,128)(2,1)} %pad_maximum_fusion.10), channel_id=1, source_target_pairs={{0,16},{4,20},{8,24},{12,28},{16,0},{20,4},{24,8},{28,12},{1,17},{... | collective-permute-start | bytes 1769480 | tf_op jit(solution)/shard_map/ppermute | solution.py:71
  503.4 3.1 copy-start.19
  504.7 25.8 %collective-permute-start.16 = (bf16[384,1024]{1,0:T(8,128)(2,1)}, bf16[384,1024]{1,0:T(8,128)(2,1)}, u32[]{:S(2)}, u32[]{:S(2)}) collective-permute-start(bf16[384,1024]{1,0:T(8,128)(2,1)} %pad_maximum_fusion.7), channel_id=1, source_target_pairs={{0,8},{4,12},{8,0},{12,4},{16,24},{20,28},{24,16},{28,20},{1,9},{5... | collective-permute-start | bytes 2359304 | tf_op jit(solution)/shard_map/ppermute | solution.py:71
  507.5 26.3 %collective-permute-start.18 = (bf16[384,1024]{1,0:T(8,128)(2,1)}, bf16[384,1024]{1,0:T(8,128)(2,1)}, u32[]{:S(2)}, u32[]{:S(2)}) collective-permute-start(bf16[384,1024]{1,0:T(8,128)(2,1)} %pad_maximum_fusion.8), channel_id=1, source_target_pairs={{0,16},{4,20},{8,24},{12,28},{16,0},{20,4},{24,8},{28,12},{1,17},{... | collective-permute-start | bytes 2359304 | tf_op jit(solution)/shard_map/ppermute | solution.py:71
  517.0 13.5 %copy-start.20 = (bf16[192,2048]{1,0:T(8,128)(2,1)S(1)}, bf16[192,2048]{1,0:T(8,128)(2,1)}, u32[]{:S(2)}) copy-start(bf16[192,2048]{1,0:T(8,128)(2,1)} %copy-done.19) | copy-start | bytes 2359300
  517.0 16.8 %copy-start.18 = (bf16[192,2048]{1,0:T(8,128)(2,1)S(1)}, bf16[192,2048]{1,0:T(8,128)(2,1)}, u32[]{:S(2)}) copy-start(bf16[192,2048]{1,0:T(8,128)(2,1)} %copy-done.17) | copy-start | bytes 2359300
  518.3 20.9 %copy-start.24 = (bf16[192,1536]{1,0:T(8,128)(2,1)S(1)}, bf16[192,1536]{1,0:T(8,128)(2,1)}, u32[]{:S(2)}) copy-start(bf16[192,1536]{1,0:T(8,128)(2,1)} %get-tuple-element.72) | copy-start | bytes 1769476
  518.3 20.9 %collective-permute-start.25 = (bf16[192,768]{1,0:T(8,128)(2,1)S(1)}, bf16[192,768]{1,0:T(8,128)(2,1)S(1)}, u32[]{:S(2)}, u32[]{:S(2)}) collective-permute-start(bf16[192,768]{1,0:T(8,128)(2,1)S(1)} %add_convert_fusion.22), channel_id=1, source_target_pairs={{0,16},{4,20},{8,24},{12,28},{16,0},{20,4},{24,8},{28,12},{1,17},{... | collective-permute-start | bytes 884744 | tf_op jit(solution)/shard_map/ppermute | solution.py:71
  521.1 18.0 %collective-permute-start.27 = (bf16[192,768]{1,0:T(8,128)(2,1)S(1)}, bf16[192,768]{1,0:T(8,128)(2,1)S(1)}, u32[]{:S(2)}, u32[]{:S(2)}) collective-permute-start(bf16[192,768]{1,0:T(8,128)(2,1)S(1)} %add_convert_fusion.20), channel_id=1, source_target_pairs={{0,8},{4,12},{8,0},{12,4},{16,24},{20,28},{24,16},{28,20},{1,9},{5... | collective-permute-start | bytes 884744 | tf_op jit(solution)/shard_map/ppermute | solution.py:71
  531.6 19.3 %collective-permute-start.17 = (bf16[192,1024]{1,0:T(8,128)(2,1)S(1)}, bf16[192,1024]{1,0:T(8,128)(2,1)S(1)}, u32[]{:S(2)}, u32[]{:S(2)}) collective-permute-start(bf16[192,1024]{1,0:T(8,128)(2,1)S(1)} %add_convert_fusion.18), channel_id=1, source_target_pairs={{0,16},{4,20},{8,24},{12,28},{16,0},{20,4},{24,8},{28,12},{1,17},{... | collective-permute-start | bytes 1179656 | tf_op jit(solution)/shard_map/ppermute | solution.py:71
  534.9 16.0 %collective-permute-start.19 = (bf16[192,1024]{1,0:T(8,128)(2,1)S(1)}, bf16[192,1024]{1,0:T(8,128)(2,1)S(1)}, u32[]{:S(2)}, u32[]{:S(2)}) collective-permute-start(bf16[192,1024]{1,0:T(8,128)(2,1)S(1)} %add_convert_fusion.16), channel_id=1, source_target_pairs={{0,8},{4,12},{8,0},{12,4},{16,24},{20,28},{24,16},{28,20},{1,9},{5... | collective-permute-start | bytes 1179656 | tf_op jit(solution)/shard_map/ppermute | solution.py:71
  540.5 14.6 %collective-permute-start.28 = (bf16[48,1536]{1,0:T(8,128)(2,1)S(1)}, bf16[48,1536]{1,0:T(8,128)(2,1)S(1)}, u32[]{:S(2)}, u32[]{:S(2)}) collective-permute-start(bf16[48,1536]{1,0:T(8,128)(2,1)S(1)} %get-tuple-element.114), channel_id=1, source_target_pairs={{0,1},{1,2},{2,3},{3,0},{4,5},{5,6},{6,7},{7,4},{8,9},{9,10},{10,1... | collective-permute-start | bytes 442376 | tf_op jit(solution)/shard_map/ppermute | solution.py:76
  548.5 15.4 %collective-permute-start.29 = (bf16[48,1536]{1,0:T(8,128)(2,1)S(1)}, bf16[48,1536]{1,0:T(8,128)(2,1)S(1)}, u32[]{:S(2)}, u32[]{:S(2)}) collective-permute-start(bf16[48,1536]{1,0:T(8,128)(2,1)S(1)} %get-tuple-element.115), channel_id=1, source_target_pairs={{0,2},{1,3},{2,0},{3,1},{4,6},{5,7},{6,4},{7,5},{8,10},{9,11},{10,... | collective-permute-start | bytes 442376 | tf_op jit(solution)/shard_map/ppermute | solution.py:76
  549.5 14.3 %collective-permute-start.30 = (bf16[48,1536]{1,0:T(8,128)(2,1)S(1)}, bf16[48,1536]{1,0:T(8,128)(2,1)S(1)}, u32[]{:S(2)}, u32[]{:S(2)}) collective-permute-start(bf16[48,1536]{1,0:T(8,128)(2,1)S(1)} %get-tuple-element.116), channel_id=1, source_target_pairs={{0,3},{1,0},{2,1},{3,2},{4,7},{5,4},{6,5},{7,6},{8,11},{9,8},{10,9... | collective-permute-start | bytes 442376 | tf_op jit(solution)/shard_map/ppermute | solution.py:76
  552.5 12.1 %collective-permute-start.20 = (bf16[48,2048]{1,0:T(8,128)(2,1)S(1)}, bf16[48,2048]{1,0:T(8,128)(2,1)S(1)}, u32[]{:S(2)}, u32[]{:S(2)}) collective-permute-start(bf16[48,2048]{1,0:T(8,128)(2,1)S(1)} %get-tuple-element.107), channel_id=1, source_target_pairs={{0,1},{1,2},{2,3},{3,0},{4,5},{5,6},{6,7},{7,4},{8,9},{9,10},{10,1... | collective-permute-start | bytes 589832 | tf_op jit(solution)/shard_map/ppermute | solution.py:76
  555.0 17.9 %collective-permute-start.21 = (bf16[48,2048]{1,0:T(8,128)(2,1)S(1)}, bf16[48,2048]{1,0:T(8,128)(2,1)S(1)}, u32[]{:S(2)}, u32[]{:S(2)}) collective-permute-start(bf16[48,2048]{1,0:T(8,128)(2,1)S(1)} %get-tuple-element.108), channel_id=1, source_target_pairs={{0,2},{1,3},{2,0},{3,1},{4,6},{5,7},{6,4},{7,5},{8,10},{9,11},{10,... | collective-permute-start | bytes 589832 | tf_op jit(solution)/shard_map/ppermute | solution.py:76
  555.1 17.8 %collective-permute-start.22 = (bf16[48,2048]{1,0:T(8,128)(2,1)S(1)}, bf16[48,2048]{1,0:T(8,128)(2,1)S(1)}, u32[]{:S(2)}, u32[]{:S(2)}) collective-permute-start(bf16[48,2048]{1,0:T(8,128)(2,1)S(1)} %get-tuple-element.109), channel_id=1, source_target_pairs={{0,3},{1,0},{2,1},{3,2},{4,7},{5,4},{6,5},{7,6},{8,11},{9,8},{10,9... | collective-permute-start | bytes 589832 | tf_op jit(solution)/shard_map/ppermute | solution.py:76
  (20 other events, 40.2 us)

commit v5 on v4

--- a/solution.py
+++ b/solution.py
@@ -56,202 +56,6 @@
     return lax.dot_general(
         left, right, (((1,), (1,)), ((), ())), preferred_element_type=jnp.float32
     )
-
-
-def after(value, *earlier):
-    return lax.optimization_barrier((value, *earlier))[0]
-
-
-def add_low(*values):
-    return sum(value.astype(jnp.float32) for value in values).astype(jnp.bfloat16)
-
-
-def cross(value, bits):
-    count = lax.axis_size("fsdp")
-    return lax.ppermute(value, "fsdp", [(i, i ^ bits) for i in range(count)])
-
-
-def shift(value, step):
-    count = lax.axis_size("seq")
-    return lax.ppermute(value, "seq", [(i, (i + step) % count) for i in range(count)])
-
-
-def place(parts, rank):
-    rows = parts[0].shape[0]
-    whole = jnp.zeros((len(parts) * rows,) + parts[0].shape[1:], parts[0].dtype)
-    for k, part in enumerate(parts):
-        whole = lax.dynamic_update_slice_in_dim(whole, part, (rank ^ k) * rows, 0)
-    return whole
-
-
-def gather_plane(block, earlier=()):
-    if lax.axis_size("fsdp") != 8:
-        whole = lax.all_gather(block, "fsdp", axis=0, tiled=True)
-        return whole, ()
-    rank = lax.axis_index("fsdp")
-    half = block.shape[0] // 2
-    if earlier:
-        block = after(block, *earlier)
-    from_x = cross(block, 2)
-    from_y = cross(block, 4)
-    diagonal = (cross(from_x[:half], 4), cross(from_y[half:], 2))
-    from_core = cross(block, 1)
-    both = cross(jnp.concatenate([from_x, from_y], 0), 1)
-    diagonal = jnp.concatenate(diagonal, 0)
-    rows = block.shape[0]
-    parts = [
-        block, from_core, from_x, both[:rows], from_y, both[rows:], diagonal, cross(diagonal, 1),
-    ]
-    return place(parts, rank), (from_x, from_y)
-
-
-def scatter_plane(whole, earlier=()):
-    count = lax.axis_size("fsdp")
-    if count != 8:
-        return lax.psum_scatter(whole, "fsdp", scatter_dimension=0, tiled=True)
-    rank = lax.axis_index("fsdp")
-    rows = whole.shape[0] // count
-    if earlier:
-        whole = after(whole, *earlier)
-
-    def part(k):
-        return lax.dynamic_slice_in_dim(whole, (rank ^ k) * rows, rows, 0)
-
-    arrived = cross(jnp.concatenate([part(1), part(3), part(5), part(7)], 0), 1)
-    return scatter_chips(
-        [add_low(part(2 * i), arrived[i * rows : (i + 1) * rows]) for i in range(4)]
-    )
-
-
-def scatter_chips(parts):
-    own, to_x, to_y, to_both = parts
-    rows = own.shape[0]
-    half = own.shape[1] // 2
-    got_x = cross(jnp.concatenate([to_x[:, :half], to_both[:, :half]], 0), 2)
-    got_y = cross(jnp.concatenate([to_y[:, half:], to_both[:, half:]], 0), 4)
-    last_y = cross(add_low(to_y[:, :half], got_x[rows:]), 4)
-    last_x = cross(add_low(to_x[:, half:], got_y[rows:]), 2)
-    return jnp.concatenate(
-        [
-            add_low(own[:, :half], got_x[:rows], last_y),
-            add_low(own[:, half:], got_y[:rows], last_x),
-        ],
-        1,
-    )
-
-
-def chain_step(up, down, step):
-    count = lax.axis_size("seq")
-    up = lax.ppermute(up, "seq", [(i, i + 1) for i in range(step - 1, count - 1)])
-    down = lax.ppermute(down, "seq", [(i, i - 1) for i in range(1, count - step + 1)])
-    return up, down
-
-
-def gather_seq(block, pause=None):
-    count = lax.axis_size("seq")
-    rank = lax.axis_index("seq")
-    up, down = block, block
-    ups, downs = [], []
-    for step in range(1, count):
-        if pause is not None and step == count - 1:
-            up, down = pause(up), pause(down)
-        up, down = chain_step(up, down, step)
-        ups.append(up)
-        downs.append(down)
-    rest = [jnp.where(rank >= j, ups[j - 1], downs[count - j - 1]) for j in range(1, count)]
-    return [block] + rest
-
-
-def scatter_seq(parts, earlier=()):
-    count = lax.axis_size("seq")
-    up, down = None, None
-    for step in range(1, count):
-        send_up = parts[step] if up is None else add_low(parts[step], up)
-        send_down = parts[count - step] if down is None else add_low(parts[count - step], down)
-        if up is None and earlier:
-            send_up = after(send_up, *earlier)
-            send_down = after(send_down, *earlier)
-        up = lax.ppermute(send_up, "seq", [(i, i + 1) for i in range(min(step, count - 1))])
-        down = lax.ppermute(
-            send_down, "seq", [(i, i - 1) for i in range(count - 1, max(count - 1 - step, 0), -1)]
-        )
-    return parts[0].astype(jnp.float32) + up.astype(jnp.float32) + down.astype(jnp.float32)
-
-
-def exchange_seq(whole):
-    count = lax.axis_size("seq")
-    rank = lax.axis_index("seq")
-    rows = whole.shape[0] // count
-
-    def part(step):
-        return lax.dynamic_slice_in_dim(whole, ((rank + step) % count) * rows, rows, 0)
-
-    return [part(0)] + [shift(part(step), step) for step in range(1, count)]
-
-
-def attend_back_kernel(query, key, value, bias, logsum, grad, d_query, d_key, d_value):
-    scale = HEAD_DIM ** (-0.5)
-    repeat = HEADS // KV_HEADS
-    raw = lax.dot_general(
-        key[...], query[...], (((1,), (1,)), ((), ())), preferred_element_type=jnp.float32
-    )
-    probs = jnp.exp(raw * scale + bias[...] - logsum[0:1])
-    d_probs = lax.dot_general(
-        value[...], grad[...], (((1,), (1,)), ((), ())), preferred_element_type=jnp.float32
-    )
-    delta = jnp.sum(probs * d_probs, 0, keepdims=True)
-    d_score = (probs * (d_probs - delta)).astype(jnp.bfloat16)
-    turned = lax.dot_general(
-        key[...], d_score, (((0,), (0,)), ((), ())), preferred_element_type=jnp.float32
-    )
-    d_query[...] = (turned * scale).T.astype(jnp.bfloat16)
-    key_part = jnp.dot(d_score, query[...], preferred_element_type=jnp.float32) * scale
-    value_part = jnp.dot(
-        probs.astype(jnp.bfloat16), grad[...], preferred_element_type=jnp.float32
-    )
-
-    @pl.when(pl.program_id(0) % repeat == 0)
-    def _():
-        d_key[...] = key_part
-        d_value[...] = value_part
-
-    @pl.when(pl.program_id(0) % repeat != 0)
-    def _():
-        d_key[...] += key_part
-        d_value[...] += value_part
-
-
-def attend_back(queries, paired, bias, logsum, grads):
-    rows, width = queries.shape
-    group = paired.shape[0]
-    repeat = HEADS // KV_HEADS
-    return pl.pallas_call(
-        attend_back_kernel,
-        grid=(HEADS,),
-        in_specs=[
-            pl.BlockSpec((rows, HEAD_DIM), lambda h: (0, h)),
-            pl.BlockSpec((group, HEAD_DIM), lambda h: (0, h // repeat)),
-            pl.BlockSpec((group, HEAD_DIM), lambda h: (0, KV_HEADS + h // repeat)),
-            pl.BlockSpec((group, rows), lambda h: (0, 0)),
-            pl.BlockSpec((8, rows), lambda h: (h, 0)),
-            pl.BlockSpec((rows, HEAD_DIM), lambda h: (0, h)),
-        ],
-        out_specs=[
-            pl.BlockSpec((rows, HEAD_DIM), lambda h: (0, h)),
-            pl.BlockSpec((group, HEAD_DIM), lambda h: (0, h // repeat)),
-            pl.BlockSpec((group, HEAD_DIM), lambda h: (0, h // repeat)),
-        ],
-        out_shape=[
-            jax.ShapeDtypeStruct((rows, width), jnp.bfloat16),
-            jax.ShapeDtypeStruct((group, KV_HEADS * HEAD_DIM), jnp.float32),
-            jax.ShapeDtypeStruct((group, KV_HEADS * HEAD_DIM), jnp.float32),
-        ],
-        compiler_params=pltpu.CompilerParams(vmem_limit_bytes=48 * 2**20),
-        cost_estimate=pl.CostEstimate(
-            flops=10 * HEADS * rows * group * HEAD_DIM * 3, bytes_accessed=8 * 2**20, transcendentals=HEADS * rows * group
-        ),
-        name="attend_back",
-    )(queries, paired, paired, bias, logsum, grads)
 
 
 def plain_device(
@@ -455,6 +259,151 @@
         grad_pair[1],
         grad_down,
     )
+
+
+ORDER = (1, 3, 2, 0)
+
+
+class SumChain:
+    def __init__(self, partial, rows, z_one, z_two, z_three, there, index):
+        self.rank = lax.axis_index("seq")
+        s = self.rank
+
+        def held(j):
+            return partial.at[ORDER.index(j) * rows : (ORDER.index(j) + 1) * rows]
+
+        self.held, self.arrived = held, (z_one, z_two, z_three)
+        self.up = [
+            there(held(1), z_one, index, seq=s + 1),
+            there(held(2), z_two.at[0], index + 2, seq=s + 1),
+            there(held(3), z_three.at[0], index + 4, seq=s + 1),
+        ]
+        self.down = [
+            there(held(3), z_one, index + 1, seq=s - 1),
+            there(held(2), z_two.at[1], index + 3, seq=s - 1),
+            there(held(1), z_three.at[1], index + 5, seq=s - 1),
+        ]
+
+    def add(self, j, arrived):
+        ref = self.held(j)
+        total = ref[...].astype(jnp.float32) + arrived[...].astype(jnp.float32)
+        ref[...] = total.astype(jnp.bfloat16)
+
+    def one(self):
+        pl.when(self.rank == 0)(self.up[0].start)
+        pl.when(self.rank == 3)(self.down[0].start)
+
+    def two(self):
+        @pl.when(self.rank == 1)
+        def _():
+            self.up[0].wait_recv()
+            self.add(2, self.arrived[0])
+
+        @pl.when(self.rank == 2)
+        def _():
+            self.down[0].wait_recv()
+            self.add(2, self.arrived[0])
+
+        pl.when(self.rank <= 1)(self.up[1].start)
+        pl.when(self.rank >= 2)(self.down[1].start)
+
+    def three(self):
+        @pl.when((self.rank == 1) | (self.rank == 2))
+        def _():
+            self.up[1].wait_recv()
+            self.add(3, self.arrived[1].at[0])
+            self.down[1].wait_recv()
+            self.add(1, self.arrived[1].at[1])
+
+        pl.when(self.rank <= 2)(self.up[2].start)
+        pl.when(self.rank >= 1)(self.down[2].start)
+
+    def last(self, out):
+        out[...] = self.held(0)[...].astype(jnp.float32)
+
+        @pl.when(self.rank >= 1)
+        def _():
+            self.up[2].wait_recv()
+            out[...] += self.arrived[2][0].astype(jnp.float32)
+
+        @pl.when(self.rank <= 2)
+        def _():
+            self.down[2].wait_recv()
+            out[...] += self.arrived[2][1].astype(jnp.float32)
+
+    def sent(self):
+        pl.when(self.rank == 0)(self.up[0].wait_send)
+        pl.when(self.rank == 3)(self.down[0].wait_send)
+        pl.when(self.rank <= 1)(self.up[1].wait_send)
+        pl.when(self.rank >= 2)(self.down[1].wait_send)
+        pl.when(self.rank <= 2)(self.up[2].wait_send)
+        pl.when(self.rank >= 1)(self.down[2].wait_send)
+
+
+class SumPlane:
+    def __init__(self, buffer, block, plane, arrived, by_x, by_y, ended, there, index):
+        half = buffer.shape[1] // 2
+        low, high = pl.ds(0, half), pl.ds(half, half)
+
+        def part(k):
+            return buffer.at[pl.ds(pl.multiple_of(plane[k] * block, 16), block)]
+
+        self.parts = own, to_x, to_y, to_both = [part(k) for k in (0, 2, 4, 6)]
+        self.arrived, self.by_x, self.by_y, self.ended, self.half = arrived, by_x, by_y, ended, half
+        self.core = [
+            there(part(2 * i + 1), arrived.at[i], index + i, fsdp=plane[1]) for i in range(4)
+        ]
+        self.first = [
+            there(to_both.at[:, low], by_x.at[1], index + 5, fsdp=plane[2]),
+            there(to_both.at[:, high], by_y.at[1], index + 7, fsdp=plane[4]),
+            there(to_x.at[:, low], by_x.at[0], index + 4, fsdp=plane[2]),
+            there(to_y.at[:, high], by_y.at[0], index + 6, fsdp=plane[4]),
+        ]
+        self.second = [
+            there(to_y.at[:, low], ended.at[0], index + 8, fsdp=plane[4]),
+            there(to_x.at[:, high], ended.at[1], index + 9, fsdp=plane[2]),
+        ]
+
+    def start_core(self):
+        for copy in self.core:
+            copy.start()
+
+    def start_first(self):
+        for i in (3, 1, 2, 0):
+            self.core[i].wait_recv()
+            part = self.parts[i]
+            total = part[...].astype(jnp.float32) + self.arrived[i].astype(jnp.float32)
+            part[...] = total.astype(jnp.bfloat16)
+        for copy in self.first:
+            copy.start()
+
+    def start_second(self):
+        half = self.half
+        _, to_x, to_y, _ = self.parts
+        self.first[0].wait_recv()
+        total = to_y[:, :half].astype(jnp.float32) + self.by_x[1].astype(jnp.float32)
+        to_y[:, :half] = total.astype(jnp.bfloat16)
+        self.second[0].start()
+        self.first[1].wait_recv()
+        total = to_x[:, half:].astype(jnp.float32) + self.by_y[1].astype(jnp.float32)
+        to_x[:, half:] = total.astype(jnp.bfloat16)
+        self.second[1].start()
+
+    def finish(self):
+        half = self.half
+        own = self.parts[0]
+        self.first[2].wait_recv()
+        self.second[0].wait_recv()
+        total = own[:, :half].astype(jnp.float32) + self.by_x[0].astype(jnp.float32)
+        own[:, :half] = (total + self.ended[0].astype(jnp.float32)).astype(jnp.bfloat16)
+        self.first[3].wait_recv()
+        self.second[1].wait_recv()
+        total = own[:, half:].astype(jnp.float32) + self.by_y[0].astype(jnp.float32)
+        own[:, half:] = (total + self.ended[1].astype(jnp.float32)).astype(jnp.bfloat16)
+
+    def sent(self):
+        for copy in self.core + self.first + self.second:
+            copy.wait_send()
 
 
 def front_kernel(
@@ -867,9 +816,6 @@
     )
 
 
-ORDER = (1, 3, 2, 0)
-
-
 def ffn_kernel(
     normed_all, upstream_all, w_gu, w_down,
     columns, grad_down, gu_sum, branch, down_arrived, gu_arrived,
@@ -972,78 +918,15 @@
 
         lax.fori_loop(0, width // tile, body, 0)
 
-    def held(j):
-        return partial.at[ORDER.index(j) * rows : (ORDER.index(j) + 1) * rows]
-
-    up_one = there(held(1), z_one, 0, seq=s + 1)
-    down_one = there(held(3), z_one, 1, seq=s - 1)
-    up_two = there(held(2), z_two.at[0], 2, seq=s + 1)
-    down_two = there(held(2), z_two.at[1], 3, seq=s - 1)
-    up_three = there(held(3), z_three.at[0], 4, seq=s + 1)
-    down_three = there(held(1), z_three.at[1], 5, seq=s - 1)
-
-    def add_to(j, arrived):
-        ref = held(j)
-        ref[...] = (ref[...].astype(full) + arrived[...].astype(full)).astype(jnp.bfloat16)
-
-    def chain_one():
-        pl.when(s == 0)(up_one.start)
-        pl.when(s == 3)(down_one.start)
-
-    def chain_two():
-        @pl.when(s == 1)
-        def _():
-            up_one.wait_recv()
-            add_to(2, z_one)
-
-        @pl.when(s == 2)
-        def _():
-            down_one.wait_recv()
-            add_to(2, z_one)
-
-        pl.when(s <= 1)(up_two.start)
-        pl.when(s >= 2)(down_two.start)
-
-    def chain_three():
-        @pl.when((s == 1) | (s == 2))
-        def _():
-            up_two.wait_recv()
-            add_to(3, z_two.at[0])
-            down_two.wait_recv()
-            add_to(1, z_two.at[1])
-
-        pl.when(s <= 2)(up_three.start)
-        pl.when(s >= 1)(down_three.start)
-
-    def chain_last():
-        columns[...] = held(0)[...].astype(full)
-
-        @pl.when(s >= 1)
-        def _():
-            up_three.wait_recv()
-            columns[...] += z_three[0].astype(full)
-
-        @pl.when(s <= 2)
-        def _():
-            down_three.wait_recv()
-            columns[...] += z_three[1].astype(full)
-
-    def chain_sent():
-        pl.when(s == 0)(up_one.wait_send)
-        pl.when(s == 3)(down_one.wait_send)
-        pl.when(s <= 1)(up_two.wait_send)
-        pl.when(s >= 2)(down_two.wait_send)
-        pl.when(s <= 2)(up_three.wait_send)
-        pl.when(s >= 1)(down_three.wait_send)
-
+    chain = SumChain(partial, rows, z_one, z_two, z_three, there, 0)
     early, late = slice(0, half_rows), slice(half_rows, group)
     forward(early, True)
     backward(early)
     pl.semaphore_wait(entry, 5)
-    chain_one()
+    chain.one()
     forward(late, False)
     backward(late)
-    chain_two()
+    chain.two()
 
     def branch_store(n):
         out_columns = pl.ds(pl.multiple_of(n * tile, tile), tile)
@@ -1119,7 +1002,7 @@
     ]
     for copy in down_first:
         copy.start()
-    chain_three()
+    chain.three()
     lax.fori_loop(width // tile // 2, width // tile, gu_body, 0)
     gu_core = [
         there(part(gu, plane[2 * i + 1], block), gu_arrived.at[i], 16 + i, fsdp=plane[1])
@@ -1127,7 +1010,7 @@
     ]
     for copy in gu_core:
         copy.start()
-    chain_last()
+    chain.last(columns)
     down_second = [
         there(to_y.at[:, low_half], down_last.at[0], 14, fsdp=plane[4]),
         there(to_x.at[:, high_half], down_last.at[1], 15, fsdp=plane[2]),
@@ -1159,7 +1042,7 @@
     )
     for copy in store:
         copy.wait()
-    chain_sent()
+    chain.sent()
     for copy in down_core + down_first + down_second + gu_core:
         copy.wait_send()
 
@@ -1211,6 +1094,435 @@
     )(normed_all, upstream_all, w_gu, w_down)[:4]
 
 
+def back_kernel(
+    columns, resid, gain_two, cotangent, attended, queries, paired, slots, slot_row, first_row,
+    logsum, normeworking, tokens, gain_one, cosine, sine, w_out, w_qkv, gu_sum, branch,
+    layer, input_rows, vector, grad_out, grad_qkv, gu_rows,
+    out_w, qkv, gu_own, gu_to_y, gu_to_x, gu_x, gu_y, gu_ended,
+    branch_v, z_one, z_two, z_three, working, bias, d_branch, d_attended, d_qkv, d_resid,
+    keys_grad, values_grad, dkv, dkv_in,
+    out_arrived, out_x, out_y, out_ended, qkv_arrived, qkv_x, qkv_y, qkv_ended,
+    out_in, qkv_in, vector_in,
+    load, ssem, rsem,
+):
+    f = lax.axis_index("fsdp")
+    s = lax.axis_index("seq")
+    rows, width = tokens.shape
+    n_s = paired.shape[0]
+    kv_width = KV_HEADS * HEAD_DIM
+    repeat = HEADS // KV_HEADS
+    scale = HEAD_DIM ** (-0.5)
+    block = width // 8
+    piece = block // n_s
+    units = gu_sum.shape[2] // 2
+    tile = 256
+    full, low = jnp.float32, jnp.bfloat16
+    plane = [f ^ k for k in range(8)]
+
+    entry = pltpu.get_barrier_semaphore()
+    for k in (1, 2, 4):
+        pl.semaphore_signal(entry, inc=1, device_id={"fsdp": plane[k]}, device_id_type=MESH)
+    for j in range(1, n_s):
+        pl.semaphore_signal(
+            entry, inc=1, device_id={"seq": lax.rem(s + j, n_s)}, device_id_type=MESH
+        )
+
+    def here(source, target, index):
+        return pltpu.make_async_copy(source, target, load.at[index])
+
+    def there(source, target, index, **device):
+        return pltpu.make_async_remote_copy(
+            src_ref=source, dst_ref=target, send_sem=ssem.at[index], recv_sem=rsem.at[index],
+            device_id=device, device_id_type=MESH,
+        )
+
+    low_units, high_units = pl.ds(0, units), pl.ds(units, units)
+    load_branch = here(branch, branch_v, 0)
+    load_out = here(w_out, out_w, 1)
+    load_gu = [
+        here(gu_sum.at[0], gu_own, 2),
+        here(gu_sum.at[2, :, low_units], gu_to_y, 3),
+        here(gu_sum.at[1, :, high_units], gu_to_x, 4),
+    ]
+    load_qkv = here(w_qkv, qkv, 5)
+    load_columns = here(columns, working, 7)
+    for copy in [load_columns, load_branch, load_out] + load_gu + [load_qkv]:
+        copy.start()
+
+    gu_first = [
+        there(gu_sum.at[3, :, low_units], gu_x.at[1], 0, fsdp=plane[2]),
+        there(gu_sum.at[3, :, high_units], gu_y.at[1], 1, fsdp=plane[4]),
+        there(gu_sum.at[1, :, low_units], gu_x.at[0], 2, fsdp=plane[2]),
+        there(gu_sum.at[2, :, high_units], gu_y.at[0], 3, fsdp=plane[4]),
+    ]
+    gu_second = [
+        there(gu_to_y, gu_ended.at[0], 4, fsdp=plane[4]),
+        there(gu_to_x, gu_ended.at[1], 5, fsdp=plane[2]),
+    ]
+
+    def around(j):
+        return {"seq": lax.rem(s + j, n_s)}
+
+    def rows_for(ref, first, j):
+        owner = lax.rem(s + j, n_s)
+        return ref.at[pl.ds(pl.multiple_of(first + owner * piece, 16), piece)]
+
+    gu_send = [there(rows_for(gu_own, 0, j), gu_rows.at[j], 5 + j, **around(j)) for j in range(1, n_s)]
+    dkv_send = [
+        [
+            there(dkv.at[g, lax.rem(s + j, n_s)], dkv_in.at[g, j], 8 + 3 * g + j, **around(j))
+            for j in range(1, n_s)
+        ]
+        for g in range(KV_HEADS)
+    ]
+    chain = SumChain(branch_v, rows, z_one, z_two, z_three, there, 16)
+    sum_out = SumPlane(out_w, block, plane, out_arrived, out_x, out_y, out_ended, there, 24)
+    sum_qkv = SumPlane(qkv, block, plane, qkv_arrived, qkv_x, qkv_y, qkv_ended, there, 36)
+    out_send = [there(rows_for(out_w, f * block, j), out_in.at[j], 47 + j, **around(j)) for j in range(1, n_s)]
+    qkv_send = [there(rows_for(qkv, f * block, j), qkv_in.at[j], 51 + j, **around(j)) for j in range(1, n_s)]
+    vector_send = [
+        there(vector_in.at[0], vector_in.at[1], 56, fsdp=plane[1]),
+        there(vector_in.at[2], vector_in.at[3], 57, fsdp=plane[2]),
+        there(vector_in.at[4], vector_in.at[5], 58, fsdp=plane[4]),
+    ] + [there(vector_in.at[6], vector_in.at[6 + j], 58 + j, **around(j)) for j in range(1, n_s)]
+
+    pl.semaphore_wait(entry, 3 + n_s - 1)
+    for copy in gu_first:
+        copy.start()
+    load_branch.wait()
+    chain.one()
+
+    def norm_back(value, gain, grad):
+        root = lax.rsqrt(jnp.mean(value * value, -1, keepdims=True) + epsilon)
+        scaled = gain * grad
+        inner = jnp.mean(scaled * value, -1, keepdims=True)
+        gain_grad = jnp.sum(grad * (value * root), 0, keepdims=True)
+        return root * scaled - value * (root * root * root * inner), gain_grad
+
+    load_columns.wait()
+    d_norm, gain_two_grad = norm_back(resid[...], gain_two[...], working[...])
+    d_total = cotangent[...].astype(full) + d_norm
+    d_branch[...] = d_total.astype(low)
+    d_resid[...] = d_total
+    for j in range(n_s):
+        keys_slot = slots[j]
+        keys_slot = jnp.concatenate([keys_slot] * (rows // 128), 1)
+        ok = (keys_slot <= slot_row[0:1]) & (keys_slot >= first_row[0:1])
+        bias[j * rows : (j + 1) * rows] = jnp.where(ok, 0.0, -1e30)
+    load_out.wait()
+    for n in range(width // tile):
+        value = lax.dot_general(
+            d_branch[...], out_w[n * tile : (n + 1) * tile], (((1,), (1,)), ((), ())),
+            preferred_element_type=full,
+        )
+        d_attended[:, n * tile : (n + 1) * tile] = value.astype(low)
+
+    def turned_back(value):
+        return value * cosine[...] + pltpu.roll(value * sine[...], HEAD_DIM // 2, 1)
+
+    for g in range(KV_HEADS):
+        keys = paired[:, :, g * HEAD_DIM : (g + 1) * HEAD_DIM].reshape(n_s * rows, HEAD_DIM)
+        values = paired[:, :, kv_width + g * HEAD_DIM : kv_width + (g + 1) * HEAD_DIM]
+        values = values.reshape(n_s * rows, HEAD_DIM)
+        keys_grad[...] = jnp.zeros_like(keys_grad)
+        values_grad[...] = jnp.zeros_like(values_grad)
+
+        def head(i, carry, g=g, keys=keys, values=values):
+            h = g * repeat + i
+            head_columns = pl.ds(pl.multiple_of(h * HEAD_DIM, HEAD_DIM), HEAD_DIM)
+            query = queries[:, head_columns]
+            grad = d_attended[:, head_columns]
+            raw = lax.dot_general(
+                keys, query, (((1,), (1,)), ((), ())), preferred_element_type=full
+            )
+            logs = logsum[pl.ds(pl.multiple_of(h * 8, 8), 8)][0:1]
+            probs = jnp.exp(raw * scale + bias[...] - logs)
+            d_probs = lax.dot_general(
+                values, grad, (((1,), (1,)), ((), ())), preferred_element_type=full
+            )
+            delta = jnp.sum(probs * d_probs, 0, keepdims=True)
+            d_score = (probs * (d_probs - delta)).astype(low)
+            turned = lax.dot_general(
+                keys, d_score, (((0,), (0,)), ((), ())), preferred_element_type=full
+            )
+            d_qkv[:, head_columns] = turned_back((turned * scale).T).astype(low)
+            keys_grad[...] += jnp.dot(d_score, query, preferred_element_type=full) * scale
+            values_grad[...] += jnp.dot(probs.astype(low), grad, preferred_element_type=full)
+            return carry
+
+        lax.fori_loop(0, repeat, head, 0)
+        dkv[g, :, :, :HEAD_DIM] = keys_grad[...].astype(low).reshape(n_s, rows, HEAD_DIM)
+        dkv[g, :, :, HEAD_DIM:] = values_grad[...].astype(low).reshape(n_s, rows, HEAD_DIM)
+        for copy in dkv_send[g]:
+            copy.start()
+
+    turned = attended[...].T
+    for n in range(width // tile):
+        n_columns = slice(n * tile, (n + 1) * tile)
+        value = jnp.dot(turned, d_branch[:, n_columns], preferred_element_type=full)
+        out_w[:, n_columns] = value.astype(low)
+    sum_out.start_core()
+    load_qkv.wait()
+
+    def back_one(first, count, start):
+        for n in range(width // tile):
+            n_rows = slice(n * tile, (n + 1) * tile)
+            value = lax.dot_general(
+                d_qkv[:, first : first + count], qkv[n_rows, first : first + count],
+                (((1,), (1,)), ((), ())), preferred_element_type=full,
+            )
+            working[:, n_rows] = value if start else working[:, n_rows] + value
+
+    back_one(0, width, True)
+    normed_turned = normeworking[...].T
+    for n in range(width // tile):
+        n_columns = slice(n * tile, (n + 1) * tile)
+        value = jnp.dot(normed_turned, d_qkv[:, n_columns], preferred_element_type=full)
+        qkv[:, n_columns] = value.astype(low)
+    sum_out.start_first()
+
+    for g in range(KV_HEADS):
+        for copy in dkv_send[g]:
+            copy.wait_recv()
+        total = dkv[g, s].astype(full)
+        for j in range(1, n_s):
+            total = total + dkv_in[g, j].astype(full)
+        key_columns = slice(width + g * HEAD_DIM, width + (g + 1) * HEAD_DIM)
+        value_columns = slice(width + kv_width + g * HEAD_DIM, width + kv_width + (g + 1) * HEAD_DIM)
+        d_qkv[:, key_columns] = turned_back(total[:, :HEAD_DIM]).astype(low)
+        d_qkv[:, value_columns] = total[:, HEAD_DIM:].astype(low)
+    chain.two()
+    back_one(width, 2 * kv_width, False)
+    value = jnp.dot(normed_turned, d_qkv[:, width:], preferred_element_type=full)
+    qkv[:, width:] = value.astype(low)
+    sum_qkv.start_core()
+
+    for copy in load_gu:
+        copy.wait()
+    gu_first[0].wait_recv()
+    gu_to_y[...] = (gu_to_y[...].astype(full) + gu_x[1].astype(full)).astype(low)
+    gu_second[0].start()
+    gu_first[1].wait_recv()
+    gu_to_x[...] = (gu_to_x[...].astype(full) + gu_y[1].astype(full)).astype(low)
+    gu_second[1].start()
+
+    d_norm, gain_one_grad = norm_back(tokens[...].astype(full), gain_one[...], working[...])
+    input_rows[...] = (d_resid[...] + d_norm).astype(low)
+    bias_grad = jnp.sum(d_qkv[...].astype(full), 0, keepdims=True)
+    vectors = jnp.concatenate([gain_one_grad, gain_two_grad, bias_grad], 1)
+    part = vectors.shape[1] // 8
+    for r in range(8):
+        vector_in[0, r : r + 1] = vectors[:, r * part : (r + 1) * part]
+    vector_send[0].start()
+    sum_qkv.start_first()
+    vector_send[0].wait_recv()
+    vector_in[2] = vector_in[0] + vector_in[1]
+    vector_send[1].start()
+    chain.three()
+    sum_out.start_second()
+
+    gu_first[2].wait_recv()
+    gu_second[0].wait_recv()
+    total = gu_own[:, :units].astype(full) + gu_x[0].astype(full) + gu_ended[0].astype(full)
+    gu_own[:, :units] = total.astype(low)
+    gu_first[3].wait_recv()
+    gu_second[1].wait_recv()
+    total = gu_own[:, units:].astype(full) + gu_y[0].astype(full) + gu_ended[1].astype(full)
+    gu_own[:, units:] = total.astype(low)
+    for copy in gu_send:
+        copy.start()
+    keep_rows = here(rows_for(gu_own, 0, 0), gu_rows.at[0], 6)
+    keep_rows.start()
+    vector_send[1].wait_recv()
+    vector_in[4] = vector_in[2] + vector_in[3]
+    vector_send[2].start()
+
+    sum_out.finish()
+    for copy in out_send:
+        copy.start()
+    sum_qkv.start_second()
+    vector_send[2].wait_recv()
+    vector_in[6] = vector_in[4] + vector_in[5]
+    for copy in vector_send[3:]:
+        copy.start()
+    chain.last(working)
+    layer[...] = (resid[...] + working[...]).astype(low)
+    sum_qkv.finish()
+    for copy in qkv_send:
+        copy.start()
+
+    def gathered(own, copies, arrived, out):
+        total = own[...].astype(full)
+        for copy in copies:
+            copy.wait_recv()
+        for j in range(1, n_s):
+            total = total + arrived[j].astype(full)
+        out[...] = total
+
+    gathered(rows_for(out_w, f * block, 0), out_send, out_in, grad_out)
+    for copy in vector_send[3:]:
+        copy.wait_recv()
+    vector[...] = vector_in[6] + vector_in[7] + vector_in[8] + vector_in[9]
+    gathered(rows_for(qkv, f * block, 0), qkv_send, qkv_in, grad_qkv)
+    for copy in gu_send:
+        copy.wait_recv()
+    keep_rows.wait()
+    chain.sent()
+    sum_out.sent()
+    sum_qkv.sent()
+    for copy in gu_first + gu_second + gu_send + out_send + qkv_send + vector_send:
+        copy.wait_send()
+    for g in range(KV_HEADS):
+        for copy in dkv_send[g]:
+            copy.wait_send()
+
+
+def back(
+    columns, resid, gain_two, cotangent, attended, queries, paired, slots, slot, first_row,
+    logsum, normeworking, tokens, gain_one, cosine, sine, w_out, w_qkv, gu_sum, branch,
+):
+    rows, width = tokens.shape
+    n_s = paired.shape[0]
+    group = n_s * rows
+    kv_width = KV_HEADS * HEAD_DIM
+    qkv_width = width + 2 * kv_width
+    block = width // 8
+    piece = block // n_s
+    units = gu_sum.shape[2] // 2
+    low, full = jnp.bfloat16, jnp.float32
+    slot_row = jnp.broadcast_to(slot.astype(full)[None], (8, rows))
+    first_f = jnp.broadcast_to(first_row.astype(full)[None], (8, rows))
+    half = HEAD_DIM // 2
+    sine = jnp.concatenate([-sine[:, :half], sine[:, half:]], 1)
+    vmem = pl.BlockSpec(memory_space=pltpu.VMEM)
+    hbm = pl.BlockSpec(memory_space=pl.ANY)
+    shape = jax.ShapeDtypeStruct
+    vectors = (2 * width + qkv_width) // 8
+    return pl.pallas_call(
+        back_kernel,
+        in_specs=[hbm] + [vmem] * 15 + [hbm] * 4,
+        out_specs=[vmem] * 5 + [hbm],
+        out_shape=[
+            shape((rows, width), low),
+            shape((rows, width), low),
+            shape((8, vectors), full),
+            shape((piece, width), full),
+            shape((piece, qkv_width), full),
+            shape((n_s, piece, 2 * units), low),
+        ],
+        scratch_shapes=[
+            pltpu.VMEM((width, width), low),
+            pltpu.VMEM((width, qkv_width), low),
+            pltpu.VMEM((block, 2 * units), low),
+            pltpu.VMEM((block, units), low),
+            pltpu.VMEM((block, units), low),
+            pltpu.VMEM((2, block, units), low),
+            pltpu.VMEM((2, block, units), low),
+            pltpu.VMEM((2, block, units), low),
+            pltpu.VMEM((group, width), low),
+            pltpu.VMEM((rows, width), low),
+            pltpu.VMEM((2, rows, width), low),
+            pltpu.VMEM((2, rows, width), low),
+            pltpu.VMEM((rows, width), full),
+            pltpu.VMEM((group, rows), full),
+            pltpu.VMEM((rows, width), low),
+            pltpu.VMEM((rows, width), low),
+            pltpu.VMEM((rows, qkv_width), low),
+            pltpu.VMEM((rows, width), full),
+            pltpu.VMEM((group, HEAD_DIM), full),
+            pltpu.VMEM((group, HEAD_DIM), full),
+            pltpu.VMEM((KV_HEADS, n_s, rows, 2 * HEAD_DIM), low),
+            pltpu.VMEM((KV_HEADS, n_s, rows, 2 * HEAD_DIM), low),
+            pltpu.VMEM((4, block, width), low),
+            pltpu.VMEM((2, block, width // 2), low),
+            pltpu.VMEM((2, block, width // 2), low),
+            pltpu.VMEM((2, block, width // 2), low),
+            pltpu.VMEM((4, block, qkv_width), low),
+            pltpu.VMEM((2, block, qkv_width // 2), low),
+            pltpu.VMEM((2, block, qkv_width // 2), low),
+            pltpu.VMEM((2, block, qkv_width // 2), low),
+            pltpu.VMEM((n_s, piece, width), low),
+            pltpu.VMEM((n_s, piece, qkv_width), low),
+            pltpu.VMEM((10, 8, vectors), full),
+            pltpu.SemaphoreType.DMA((8,)),
+            pltpu.SemaphoreType.DMA((64,)),
+            pltpu.SemaphoreType.DMA((64,)),
+        ],
+        compiler_params=pltpu.CompilerParams(
+            collective_id=2, has_side_effects=True, vmem_limit_bytes=63 * 2**20
+        ),
+        name="back",
+    )(
+        columns, resid, gain_two, cotangent, attended, queries, paired, slots, slot_row, first_f,
+        logsum, normeworking, tokens, gain_one, cosine, sine, w_out, w_qkv, gu_sum, branch,
+    )
+
+
+def finish_kernel(
+    layer, input_rows, grad_out, grad_qkv, grad_down, gu_rows,
+    layer_out, input_grad, out_out, query_out, key_out, value_out, down_out, gate_out, up_out,
+):
+    s = lax.axis_index("seq")
+    n_s = gu_rows.shape[0]
+    width = grad_out.shape[1]
+    kv_width = KV_HEADS * HEAD_DIM
+    unit_pad = grad_down.shape[0]
+    unit = down_out.shape[0]
+    units = gu_rows.shape[2] // 2
+    layer_out[...] = layer[...]
+    input_grad[...] = input_rows[...]
+    out_out[...] = grad_out[...]
+    query_out[...] = grad_qkv[:, :width]
+    key_out[...] = grad_qkv[:, width : width + kv_width]
+    value_out[...] = grad_qkv[:, width + kv_width :]
+    down_out[...] = grad_down[:unit]
+    window = 512
+    lanes = lax.broadcasted_iota(jnp.int32, (gu_rows.shape[1], 128), 1)
+    for base, out in ((0, gate_out), (units, up_out)):
+        for f in range(units // unit_pad):
+            for owner in range(n_s):
+                source = base + f * unit_pad
+                begin = min(source // 128 * 128, 2 * units - window)
+                target = (f * n_s + owner) * unit
+                first = target // 128 * 128
+                slot = lax.rem(s + n_s - owner, n_s)
+                value = gu_rows[slot, :, begin : begin + window].astype(jnp.float32)
+                turn = ((target - first) - (source - begin)) % window
+                if turn:
+                    value = pltpu.roll(value, turn, 1)
+                for t in range(first, min(target + unit, out.shape[1]), 128):
+                    part = value[:, t - first : t - first + 128]
+                    if t < target:
+                        part = jnp.where(lanes >= target - t, part, out[:, t : t + 128])
+                    out[:, t : t + 128] = part
+
+
+def finish(layer, input_rows, grad_out, grad_qkv, grad_down, gu_rows, unit, hidden_width):
+    piece, width = grad_out.shape
+    kv_width = KV_HEADS * HEAD_DIM
+    low, full = jnp.bfloat16, jnp.float32
+    shape = jax.ShapeDtypeStruct
+    vmem = pl.BlockSpec(memory_space=pltpu.VMEM)
+    return pl.pallas_call(
+        finish_kernel,
+        in_specs=[vmem] * 6,
+        out_specs=[vmem] * 9,
+        out_shape=[
+            shape(layer.shape, low),
+            shape(layer.shape, low),
+            shape((piece, width), full),
+            shape((piece, width), full),
+            shape((piece, kv_width), full),
+            shape((piece, kv_width), full),
+            shape((unit, width), full),
+            shape((piece, hidden_width), full),
+            shape((piece, hidden_width), full),
+        ],
+        compiler_params=pltpu.CompilerParams(vmem_limit_bytes=48 * 2**20),
+        name="finish",
+    )(layer, input_rows, grad_out, grad_qkv, grad_down, gu_rows)
+
+
 def per_device(
     tokens, cotangent, lengths, balance, norm1_gain, w_query, b_query, w_key, b_key,
     w_value, b_value, w_out, norm2_gain, w_gate, w_up, w_down,
@@ -1222,14 +1534,11 @@
     rows_here, width = tokens.shape
     group = seq_count * rows_here
     kv_width = KV_HEADS * HEAD_DIM
-    qkv_width = width + 2 * kv_width
     hidden_width = w_gate.shape[1]
     unit = hidden_width // (fsdp_count * seq_count)
-    own_units = hidden_width // seq_count
-    padded = fsdp_count * (-(-unit // 16) * 16)
+    unit_pad = -(-unit // 16) * 16
     weight_rows = w_gate.shape[0]
 
-    unit_pad = -(-unit // 16) * 16
     pair_bias = jnp.concatenate([jnp.tile(b_key, fsdp_count), jnp.tile(b_value, fsdp_count)])
     small = jnp.concatenate([norm1_gain] * 2 + [norm2_gain] * 2 + [b_query] * 2 + [pair_bias])
     place_of = np.concatenate(
@@ -1254,84 +1563,16 @@
         tokens, cotangent, small, slot, first_row, cosine, sine,
         (w_query, w_key, w_value, w_out, w_gate, w_up), down_own,
     )
-    gain_one, gain_two = gain_one[0], gain_two[0]
-    paired = paired.reshape(group, 2 * kv_width)
-    slots_all = slots_all[:, :, 0].reshape(group)
-    slot = slot.astype(jnp.float32)
-    allowed = (slots_all[:, None] <= slot[None, :]) & (
-        slots_all[:, None] >= first_row.astype(jnp.float32)[None, :]
-    )
-    bias = jnp.where(allowed, 0.0, -1e30).astype(jnp.float32)
-    inputs = tokens.astype(jnp.float32)
-
-    def blocks_back(value):
-        return [
-            lax.dynamic_slice_in_dim(value, ((seq_rank - j) % seq_count) * rows_here, rows_here, 0)
-            for j in range(seq_count)
-        ]
-
     columns, grad_down, gu_sum, branch = ffn(normed_all, upstream_all, weight_gu, weight_down)
-    grad_down = grad_down[:unit]
-    grad_pair = scatter_chips(gu_sum)
-    branch = [branch[ORDER.index(j) * rows_here : (ORDER.index(j) + 1) * rows_here] for j in range(seq_count)]
-    branch = scatter_seq(branch)
-    layer_out = (resid + branch).astype(jnp.bfloat16)
-    grad_pair = exchange_seq(grad_pair)
-    own_rows = weight_rows // seq_count
-    grad_pair = jnp.stack(grad_pair, 0).reshape(seq_count, own_rows, 2, padded)
-    order = (seq_rank - jnp.arange(seq_count)) % seq_count
-    grad_pair = grad_pair[order]
-    grad_pair = grad_pair.reshape(seq_count, own_rows, 2, fsdp_count, unit_pad)[..., :unit]
-    grad_pair = grad_pair.transpose(2, 1, 3, 0, 4).astype(jnp.float32)
-    grad_pair = grad_pair.reshape(2, own_rows, hidden_width)
-
-    _, pull_two = jax.vjp(norm_piece, resid, gain_two)
-    d_resid_norm, grad_gain_two = pull_two(columns)
-    d_resid = cotangent.astype(jnp.float32) + d_resid_norm
-    d_branch = d_resid.astype(jnp.bfloat16)
-    d_attended = contract_columns(d_branch, weight_out).astype(jnp.bfloat16)
-    d_queries, d_keys, d_values = attend_back(queries, paired, bias, logsum, d_attended)
-    d_paired = jnp.concatenate([d_keys, d_values], 1).astype(jnp.bfloat16)
-    d_paired = blocks_back(d_paired)
-    d_paired = sum(
-        part.astype(jnp.float32)
-        for part in [d_paired[0]] + [shift(d_paired[j], -j) for j in range(1, seq_count)]
-    )
-    d_query_pre = rotate_back(
-        d_queries.astype(jnp.float32).reshape(rows_here, HEADS, HEAD_DIM), cosine, sine
-    ).astype(jnp.bfloat16)
-    d_key_pre = rotate_back(
-        d_paired[:, :kv_width].reshape(rows_here, KV_HEADS, HEAD_DIM), cosine, sine
-    ).astype(jnp.bfloat16)
-    d_value_pre = d_paired[:, kv_width:].astype(jnp.bfloat16)
-    d_qkv = jnp.concatenate(
-        [
-            d_query_pre.reshape(rows_here, width),
-            d_key_pre.reshape(rows_here, kv_width),
-            d_value_pre,
-        ],
-        1,
-    )
-    grad_out = contract_rows(attended, d_branch).astype(jnp.bfloat16)
-    grad_qkv = contract_rows(normed_one, d_qkv).astype(jnp.bfloat16)
-    grad_bias = jnp.sum(d_qkv.astype(jnp.float32), 0)
-    d_normed_one = contract_columns(d_qkv, weight_qkv)
-    _, pull_one = jax.vjp(norm_piece, inputs, gain_one)
-    d_input_norm, grad_gain_one = pull_one(d_normed_one)
-    input_grad = (d_resid + d_input_norm).astype(jnp.bfloat16)
-
-    def summed(value):
-        return sum(part.astype(jnp.float32) for part in exchange_seq(scatter_plane(value)))
-
-    grad_out = summed(grad_out)
-    grad_qkv = summed(grad_qkv)
-    vectors = jnp.concatenate([grad_gain_one, grad_gain_two, grad_bias], 0)
-    if fsdp_count == 8:
-        for bits in (1, 2, 4):
-            vectors = vectors + cross(vectors, bits)
-        vectors = vectors + sum(shift(vectors, j) for j in range(1, seq_count))
-    else:
-        vectors = lax.psum(vectors, ("fsdp", "seq"))
+    layer, input_rows, vectors, grad_out, grad_qkv, gu_rows = back(
+        columns, resid, gain_two, cotangent, attended, queries, paired, slots_all, slot, first_row,
+        logsum, normed_one, tokens, gain_one, cosine, sine, weight_out, weight_qkv, gu_sum, branch,
+    )
+    (
+        layer_out, input_grad, grad_out, grad_query, grad_key, grad_value, grad_down, grad_gate,
+        grad_up,
+    ) = finish(layer, input_rows, grad_out, grad_qkv, grad_down, gu_rows, unit, hidden_width)
+    vectors = vectors.reshape(-1)
     own = width // (fsdp_count * seq_count)
     first = (fsdp_rank * seq_count + seq_rank) * own
 
@@ -1343,16 +1584,16 @@
         layer_out,
         input_grad,
         own_part(0),
-        grad_qkv[:, :width],
+        grad_query,
         own_part(biases),
-        grad_qkv[:, width : width + kv_width],
+        grad_key,
         vectors[biases + width : biases + width + kv_width],
-        grad_qkv[:, width + kv_width :],
+        grad_value,
         vectors[biases + width + kv_width :],
         grad_out,
         own_part(width),
-        grad_pair[0],
-        grad_pair[1],
+        grad_gate,
+        grad_up,
         grad_down,
     )
 

time: 581 us -> 457 us (0.79)
  Pallas kernels: 289 us -> 421 us
  waiting for transfers between devices: 99.4 us -> 0 us
  starting transfers between devices: 60.1 us -> 0 us
  other arithmetic: 55.4 us -> 8.14 us
  local copies, waits for them, and re-layouts: 59.7 us -> 19.3 us
  matrix products: 9.1 us -> 0 us
    pallas_call x1 -> x2, Pallas kernels: 17.9 us -> 150 us  [the longest x1 146 us: back(): pl.pallas_call(back_kernel, in_specs=[hbm] + [vmem] * 15 + [hbm] * 4, out...]
    ppermute x38 -> x0, waiting for transfers between devices: 99.4 us -> none  [the longest x15 55.7 us: shift(): lax.ppermute(value, 'seq', [(i, (i + step) % count) for i in range(count)])]
    ppermute x38 -> x0, starting transfers between devices: 60.1 us -> none  [the longest x15 26.5 us: shift(): lax.ppermute(value, 'seq', [(i, (i + step) % count) for i in range(count)])]
    convert_element_type x17 -> x0, other arithmetic: 25.3 us -> none  [the longest x13 23.1 us: add_low(): sum((value.astype(jnp.float32) for value in values)).astype(jnp.bfloat16)]
    concatenate x16 -> x1, other arithmetic: 12.9 us -> 0.84 us  [rope_tables(): cosine = jnp.concatenate([jnp.cos(angle), jnp.cos(angle)], -1)]
    dot_general x4 -> x0, matrix products: 9.1 us -> none  [the longest x2 5.4 us: contract_rows(): lax.dot_general(left, right, (((0,), (0,)), ((), ())), preferred_element_...]
    slice x17 -> x0, local copies, waits for them, and re-layouts: 8.38 us -> none  [the longest x1 2.87 us: per_device(): grad_down = grad_down[:unit]]
    squeeze x2 -> x0, local copies, waits for them, and re-layouts: 6.96 us -> none  [the longest x1 3.88 us: per_device(): grad_pair[0]]
  transfers between devices with their start and end apart: 38 -> 0, of which waited for: 17 -> 0; matrix products, arithmetic and copies ran while one was open for 17% -> 0% of each run, Pallas kernels for 3% -> 0%
where the time goes in v5:
time: 457 us; the launch traced here: 449 us
  Pallas kernels  421 us (92%)
  local copies, waits for them, and re-layouts  19.3 us (4%)
  other arithmetic  8.14 us (2%)
    pallas_call x1, Pallas kernels, front(): pl.pallas_call(front_kernel, in_specs=[vmem, hbm] + [vmem] * 6 + [hbm] *...  161 us
    pallas_call x1, Pallas kernels, back(): pl.pallas_call(back_kernel, in_specs=[hbm] + [vmem] * 15 + [hbm] * 4, out...  146 us
    pallas_call x1, Pallas kernels, ffn(): pl.pallas_call(ffn_kernel, in_specs=[hbm] * 4, out_specs=[vmem] * 2 + [hb...  110 us

profile of v5, /device:TPU:0, one launch (start us, length us, event | category | flops | bytes accessed | tf_op | source)
XLA Modules:
  0.0 449.2 jit_solution(2162000080791728662)
XLA Ops:
  0.7 0.7 tile.20
  1.3 0.1 tile.21
  1.4 0.7 tile.8
  2.1 0.1 tile.9
  2.1 4.1 concatenate.10
  6.2 0.7 or_select_fusion
  6.9 0.6 broadcast_in_dim.21.small
  7.6 0.8 reduce-window.9
  8.4 0.7 bitcast_subtract_fusion
  9.1 0.6 fusion.6
  9.6 2.6 subtract_convert_fusion
  12.3 0.5 fusion
  12.8 0.8 pad_maximum_fusion
  13.7 1.9 fusion.3
  15.6 0.6 broadcast_in_dim.23.slot_row
  16.2 0.8 broadcast_in_dim.22.slot_keys
  17.0 0.6 broadcast_in_dim.25.first_row
  17.6 1.2 constant_dynamic-slice_fusion
  18.8 1.0 pad.4.w_down
  19.8 160.6 %front.1 = (bf16[1536,4608]{1,0:T(8,128)(2,1)}, bf16[2304,1536]{1,0:T(8,128)(2,1)}, bf16[1024,1536]{1,0:T(8,128)(2,1)}, bf16[1024,1536]{1,0:T(8,128)(2,1)}, bf16...) custom-call(bf16[256,1536]{1,0:T(8,128)(2,1)} %tokens.3, ...), custom_call_target="tpu_custom_call" | custom-call | tf_op jit(solution)/shard_map/front/pallas_call | solution.py:771
  180.4 110.4 %ffn.1 = (f32[256,1536]{1,0:T(8,128)}, f32[288,1536]{1,0:T(8,128)}, bf16[4,192,4608]{2,1,0:T(8,128)(2,1)}, bf16[1024,1536]{1,0:T(8,128)(2,1)}, bf16[4,288,1536]{...) custom-call(bf16[1024,1536]{1,0:T(8,128)(2,1)} %get-tuple-element.48.normed_all, ...), custom_call_target="tpu_custom_call" | custom-call | tf_op jit(solution)/shard_map/ffn/pallas_call | solution.py:1059
  290.8 145.7 %back.1 = (bf16[256,1536]{1,0:T(8,128)(2,1)}, bf16[256,1536]{1,0:T(8,128)(2,1)}, f32[8,640]{1,0:T(8,128)}, f32[48,1536]{1,0:T(8,128)}, f32[48,2048]{1,0:T(8,128)}, /*index=5*/bf16[4,48,4608]{2,1,0:T(8,128)(2,1)}) custom-call(f32[256,1536]{1,0:T(8,128)} %get-tuple-element.52.columns, f32[256,1536]{1,0:T(8,128)} %get-tuple-element.53.resid, ...), custom_call_target="tpu_custom_call" | custom-call | tf_op jit(solution)/shard_map/back/pallas_call | solution.py:1401
  436.5 0.0 copy-start
  436.5 1.5 copy-done
  438.0 0.0 copy-start.1
  438.0 1.5 copy-done.1
  439.5 0.0 copy-start.2
  439.5 1.1 copy-done.2
  440.6 0.0 copy-start.3
  440.6 1.1 copy-done.3
  441.7 0.0 copy-start.4
  441.8 1.0 copy-done.4
  442.7 0.0 copy-start.5
  442.7 1.0 copy-done.5
  443.7 0.0 copy-start.6
  443.7 3.8 finish.1
  447.6 0.0 copy-done.6
  447.6 0.6 fusion.4
  448.2 0.6 fusion.5
  (2 shorter events, 0.0 us)
Async XLA Ops:
  436.5 1.5 copy-start
  438.0 1.5 copy-start.1
  439.5 1.1 copy-start.2
  440.6 1.1 copy-start.3
  441.7 1.0 copy-start.4
  442.7 1.0 copy-start.5
  443.7 3.8 copy-start.6

commit v6 on v5

--- a/solution.py
+++ b/solution.py
@@ -293,7 +293,7 @@
         pl.when(self.rank == 0)(self.up[0].start)
         pl.when(self.rank == 3)(self.down[0].start)
 
-    def two(self):
+    def add_one(self):
         @pl.when(self.rank == 1)
         def _():
             self.up[0].wait_recv()
@@ -304,6 +304,7 @@
             self.down[0].wait_recv()
             self.add(2, self.arrived[0])
 
+    def two(self):
         pl.when(self.rank <= 1)(self.up[1].start)
         pl.when(self.rank >= 2)(self.down[1].start)
 
@@ -331,9 +332,11 @@
             self.down[2].wait_recv()
             out[...] += self.arrived[2][1].astype(jnp.float32)
 
-    def sent(self):
+    def one_sent(self):
         pl.when(self.rank == 0)(self.up[0].wait_send)
         pl.when(self.rank == 3)(self.down[0].wait_send)
+
+    def sent(self):
         pl.when(self.rank <= 1)(self.up[1].wait_send)
         pl.when(self.rank >= 2)(self.down[1].wait_send)
         pl.when(self.rank <= 2)(self.up[2].wait_send)
@@ -818,9 +821,9 @@
 
 def ffn_kernel(
     normed_all, upstream_all, w_gu, w_down,
-    columns, grad_down, gu_sum, branch, down_arrived, gu_arrived,
+    columns, grad_down, gu_sum, gu_far, branch, down_arrived, gu_arrived,
     normed, upstream, gu, down, hidden, d_both, partial, z_one, z_two, z_three,
-    down_x, down_y, down_last, branch_piece,
+    down_x, down_y, down_last, down_piece,
     load, ssem, rsem,
 ):
     f = lax.axis_index("fsdp")
@@ -832,6 +835,7 @@
     units = down.shape[0]
     tile = 256
     tiles = units // tile
+    wide = 768
     block = gu.shape[0] // 8
     unit = units // 8
     half = width // 2
@@ -865,8 +869,8 @@
         first_loads.append(here(part(upstream_all, owner, rows), part(upstream, p, rows), 4 + p))
 
     def tile_loads(t):
-        gate_columns = pl.ds(pl.multiple_of(t * tile, tile), tile)
-        up_columns = pl.ds(pl.multiple_of(units + t * tile, tile), tile)
+        gate_columns = pl.ds(pl.multiple_of(t * wide, wide), wide)
+        up_columns = pl.ds(pl.multiple_of(units + t * wide, wide), wide)
         return [
             here(w_gu.at[:, gate_columns], gu.at[:, gate_columns], 8 + 3 * t),
             here(w_gu.at[:, up_columns], gu.at[:, up_columns], 9 + 3 * t),
@@ -875,7 +879,7 @@
 
     for copy in first_loads:
         copy.start()
-    for t in range(tiles):
+    for t in range(units // wide):
         for copy in tile_loads(t):
             copy.start()
     for copy in first_loads:
@@ -886,8 +890,8 @@
             if wait:
                 for copy in tile_loads(t):
                     copy.wait()
-            gate_columns = pl.ds(pl.multiple_of(t * tile, tile), tile)
-            up_columns = pl.ds(pl.multiple_of(units + t * tile, tile), tile)
+            gate_columns = pl.ds(pl.multiple_of(t * wide, wide), wide)
+            up_columns = pl.ds(pl.multiple_of(units + t * wide, wide), wide)
             mine = normed[part_rows]
             gate = jnp.dot(mine, gu[:, gate_columns], preferred_element_type=full)
             up = jnp.dot(mine, gu[:, up_columns], preferred_element_type=full)
@@ -904,11 +908,11 @@
             d_both[part_rows, up_columns] = (d_hidden * activated).astype(jnp.bfloat16)
             return carry
 
-        lax.fori_loop(0, tiles, body, 0)
+        lax.fori_loop(0, units // wide, body, 0)
 
     def backward(part_rows):
         def body(n, carry):
-            out_columns = pl.ds(pl.multiple_of(n * tile, tile), tile)
+            out_columns = pl.ds(pl.multiple_of(n * 512, 512), 512)
             value = lax.dot_general(
                 d_both[part_rows], gu[out_columns], (((1,), (1,)), ((), ())),
                 preferred_element_type=full,
@@ -916,37 +920,19 @@
             partial[part_rows, out_columns] = value.astype(jnp.bfloat16)
             return carry
 
-        lax.fori_loop(0, width // tile, body, 0)
+        lax.fori_loop(0, width // 512, body, 0)
 
     chain = SumChain(partial, rows, z_one, z_two, z_three, there, 0)
     early, late = slice(0, half_rows), slice(half_rows, group)
+    pieces = [(first, min(group, units - first)) for first in range(0, units, group)]
     forward(early, True)
     backward(early)
     pl.semaphore_wait(entry, 5)
     chain.one()
     forward(late, False)
     backward(late)
+    chain.add_one()
     chain.two()
-
-    def branch_store(n):
-        out_columns = pl.ds(pl.multiple_of(n * tile, tile), tile)
-        return here(branch_piece.at[lax.rem(n, 2)], branch.at[:, out_columns], 8 + n)
-
-    def branch_body(n, carry):
-        out_columns = pl.ds(pl.multiple_of(n * tile, tile), tile)
-        value = jnp.dot(hidden[...], down[:, out_columns], preferred_element_type=full)
-
-        @pl.when(n >= 2)
-        def _():
-            branch_store(n - 2).wait()
-
-        branch_piece[lax.rem(n, 2)] = value.astype(jnp.bfloat16)
-        branch_store(n).start()
-        return carry
-
-    lax.fori_loop(0, width // tile, branch_body, 0)
-    for n in (width // tile - 2, width // tile - 1):
-        branch_store(n).wait()
 
     def down_body(t, carry):
         unit_rows = pl.ds(pl.multiple_of(t * tile, tile), tile)
@@ -973,25 +959,26 @@
             gu[in_columns, first : first + units // 3] = value.astype(jnp.bfloat16)
         return carry
 
-    lax.fori_loop(0, width // tile // 2, gu_body, 0)
-
-    def add_arrived(ref, size, arrived, pieces, copies, index):
-        for i in range(4):
-            copies[i].wait_recv()
-            fetch = [
-                here(arrived.at[i, :, columns], piece, index + k)
-                for k, (columns, piece) in enumerate(pieces)
-            ]
-            for copy in fetch:
-                copy.start()
-            target = part(ref, plane[2 * i], size)
-            for copy, (columns, piece) in zip(fetch, pieces):
-                copy.wait()
-                target[:, columns] = (
-                    target[:, columns].astype(full) + piece[...].astype(full)
-                ).astype(jnp.bfloat16)
-
-    add_arrived(down, unit, down_arrived, [(pl.ds(0, width), hidden.at[:unit, :width])], down_core, 14)
+    lax.fori_loop(0, 2, gu_body, 0)
+
+    def add_arrived(i, ref, size, arrived, pieces, copies, index):
+        copies[i].wait_recv()
+        fetch = [
+            here(arrived.at[i, :, columns], piece, index + k)
+            for k, (columns, piece) in enumerate(pieces)
+        ]
+        for copy in fetch:
+            copy.start()
+        target = part(ref, plane[2 * i], size)
+        for copy, (columns, piece) in zip(fetch, pieces):
+            copy.wait()
+            target[:, columns] = (
+                target[:, columns].astype(full) + piece[...].astype(full)
+            ).astype(jnp.bfloat16)
+
+    down_pieces = [(pl.ds(0, width), down_piece)]
+    for i in (3, 1, 2, 0):
+        add_arrived(i, down, unit, down_arrived, down_pieces, down_core, 14)
     to_x, to_y, to_both = [part(down, plane[k], unit) for k in (2, 4, 6)]
     low_half, high_half = pl.ds(0, half), pl.ds(half, half)
     down_first = [
@@ -1003,14 +990,44 @@
     for copy in down_first:
         copy.start()
     chain.three()
-    lax.fori_loop(width // tile // 2, width // tile, gu_body, 0)
+    lax.fori_loop(2, width // tile, gu_body, 0)
     gu_core = [
         there(part(gu, plane[2 * i + 1], block), gu_arrived.at[i], 16 + i, fsdp=plane[1])
         for i in range(4)
     ]
     for copy in gu_core:
         copy.start()
+
+    again = [
+        here(
+            w_down.at[first : first + count],
+            d_both.at[:count, i * width : (i + 1) * width], 24 + i,
+        )
+        for i, (first, count) in enumerate(pieces)
+    ]
+    for copy in again:
+        copy.start()
+    for copy in again:
+        copy.wait()
+
+    def branch_body(n, carry):
+        out_columns = pl.ds(pl.multiple_of(n * wide, wide), wide)
+        for m in range(2):
+            mine = slice(m * half_rows, (m + 1) * half_rows)
+            value = jnp.zeros((half_rows, wide), full)
+            for i, (first, count) in enumerate(pieces):
+                columns_here = pl.ds(pl.multiple_of(i * width + n * wide, wide), wide)
+                value += jnp.dot(
+                    hidden[mine, first : first + count], d_both[:count, columns_here],
+                    preferred_element_type=full,
+                )
+            upstream[mine, out_columns] = value.astype(jnp.bfloat16)
+        return carry
+
+    lax.fori_loop(0, width // wide, branch_body, 0)
     chain.last(columns)
+    chain_branch = SumChain(upstream, rows, z_one, z_two, z_three, there, 22)
+    chain_branch.one()
     down_second = [
         there(to_y.at[:, low_half], down_last.at[0], 14, fsdp=plane[4]),
         there(to_x.at[:, high_half], down_last.at[1], 15, fsdp=plane[2]),
@@ -1025,8 +1042,17 @@
         (pl.ds(0, units), hidden.at[:block]),
         (pl.ds(units, units), hidden.at[block : 2 * block]),
     ]
-    add_arrived(gu, block, gu_arrived, gu_pieces, gu_core, 20)
-    store = [here(part(gu, plane[2 * i], block), gu_sum.at[i], 16 + i) for i in range(4)]
+    add_arrived(3, gu, block, gu_arrived, gu_pieces, gu_core, 20)
+    far = part(gu, plane[6], block)
+    gu_first = [
+        there(far.at[:, pl.ds(0, units)], gu_far.at[0], 20, fsdp=plane[2]),
+        there(far.at[:, pl.ds(units, units)], gu_far.at[1], 21, fsdp=plane[4]),
+    ]
+    for copy in gu_first:
+        copy.start()
+    for i in (1, 2, 0):
+        add_arrived(i, gu, block, gu_arrived, gu_pieces, gu_core, 20)
+    store = [here(part(gu, plane[2 * i], block), gu_sum.at[i], 16 + i) for i in range(3)]
     for copy in store:
         copy.start()
     down_first[0].wait_recv()
@@ -1040,11 +1066,18 @@
     grad_down[:, half:] = (
         own[:, half:].astype(full) + down_y[0].astype(full) + down_last[1].astype(full)
     )
-    for copy in store:
+    chain_branch.add_one()
+    chain_branch.one_sent()
+    store_branch = here(upstream, branch, 27)
+    store_branch.start()
+    chain.one_sent()
+    chain.sent()
+    for copy in down_core + down_first + down_second + gu_core + gu_first:
+        copy.wait_send()
+    for copy in gu_first:
+        copy.wait_recv()
+    for copy in store + [store_branch]:
         copy.wait()
-    chain.sent()
-    for copy in down_core + down_first + down_second + gu_core:
-        copy.wait_send()
 
 
 def ffn(normed_all, upstream_all, w_gu, w_down):
@@ -1059,11 +1092,12 @@
     return pl.pallas_call(
         ffn_kernel,
         in_specs=[hbm] * 4,
-        out_specs=[vmem] * 2 + [hbm] * 4,
+        out_specs=[vmem] * 2 + [hbm] * 5,
         out_shape=[
             shape((rows, width), full),
             shape((unit, width), full),
-            shape((4, block, 2 * units), low),
+            shape((3, block, 2 * units), low),
+            shape((2, block, units), low),
             shape((group, width), low),
             shape((4, unit, width), low),
             shape((4, block, 2 * units), low),
@@ -1082,21 +1116,21 @@
             pltpu.VMEM((2, unit, half), low),
             pltpu.VMEM((2, unit, half), low),
             pltpu.VMEM((2, unit, half), low),
-            pltpu.VMEM((2, group, 256), low),
+            pltpu.VMEM((unit, width), low),
             pltpu.SemaphoreType.DMA((36,)),
-            pltpu.SemaphoreType.DMA((20,)),
-            pltpu.SemaphoreType.DMA((20,)),
+            pltpu.SemaphoreType.DMA((28,)),
+            pltpu.SemaphoreType.DMA((28,)),
         ],
         compiler_params=pltpu.CompilerParams(
             collective_id=1, has_side_effects=True, vmem_limit_bytes=63 * 2**20
         ),
         name="ffn",
-    )(normed_all, upstream_all, w_gu, w_down)[:4]
+    )(normed_all, upstream_all, w_gu, w_down)[:5]
 
 
 def back_kernel(
     columns, resid, gain_two, cotangent, attended, queries, paired, slots, slot_row, first_row,
-    logsum, normeworking, tokens, gain_one, cosine, sine, w_out, w_qkv, gu_sum, branch,
+    logsum, normed_one, tokens, gain_one, cosine, sine, w_out, w_qkv, gu_sum, gu_far, branch,
     layer, input_rows, vector, grad_out, grad_qkv, gu_rows,
     out_w, qkv, gu_own, gu_to_y, gu_to_x, gu_x, gu_y, gu_ended,
     branch_v, z_one, z_two, z_three, working, bias, d_branch, d_attended, d_qkv, d_resid,
@@ -1143,6 +1177,8 @@
         here(gu_sum.at[0], gu_own, 2),
         here(gu_sum.at[2, :, low_units], gu_to_y, 3),
         here(gu_sum.at[1, :, high_units], gu_to_x, 4),
+        here(gu_far.at[0], gu_x.at[1], 8),
+        here(gu_far.at[1], gu_y.at[1], 9),
     ]
     load_qkv = here(w_qkv, qkv, 5)
     load_columns = here(columns, working, 7)
@@ -1150,8 +1186,6 @@
         copy.start()
 
     gu_first = [
-        there(gu_sum.at[3, :, low_units], gu_x.at[1], 0, fsdp=plane[2]),
-        there(gu_sum.at[3, :, high_units], gu_y.at[1], 1, fsdp=plane[4]),
         there(gu_sum.at[1, :, low_units], gu_x.at[0], 2, fsdp=plane[2]),
         there(gu_sum.at[2, :, high_units], gu_y.at[0], 3, fsdp=plane[4]),
     ]
@@ -1190,7 +1224,13 @@
     for copy in gu_first:
         copy.start()
     load_branch.wait()
-    chain.one()
+    chain.two()
+    for copy in load_gu:
+        copy.wait()
+    gu_to_y[...] = (gu_to_y[...].astype(full) + gu_x[1].astype(full)).astype(low)
+    gu_second[0].start()
+    gu_to_x[...] = (gu_to_x[...].astype(full) + gu_y[1].astype(full)).astype(low)
+    gu_second[1].start()
 
     def norm_back(value, gain, grad):
         root = lax.rsqrt(jnp.mean(value * value, -1, keepdims=True) + epsilon)
@@ -1274,7 +1314,7 @@
             working[:, n_rows] = value if start else working[:, n_rows] + value
 
     back_one(0, width, True)
-    normed_turned = normeworking[...].T
+    normed_turned = normed_one[...].T
     for n in range(width // tile):
         n_columns = slice(n * tile, (n + 1) * tile)
         value = jnp.dot(normed_turned, d_qkv[:, n_columns], preferred_element_type=full)
@@ -1291,20 +1331,11 @@
         value_columns = slice(width + kv_width + g * HEAD_DIM, width + kv_width + (g + 1) * HEAD_DIM)
         d_qkv[:, key_columns] = turned_back(total[:, :HEAD_DIM]).astype(low)
         d_qkv[:, value_columns] = total[:, HEAD_DIM:].astype(low)
-    chain.two()
     back_one(width, 2 * kv_width, False)
     value = jnp.dot(normed_turned, d_qkv[:, width:], preferred_element_type=full)
     qkv[:, width:] = value.astype(low)
     sum_qkv.start_core()
-
-    for copy in load_gu:
-        copy.wait()
-    gu_first[0].wait_recv()
-    gu_to_y[...] = (gu_to_y[...].astype(full) + gu_x[1].astype(full)).astype(low)
-    gu_second[0].start()
-    gu_first[1].wait_recv()
-    gu_to_x[...] = (gu_to_x[...].astype(full) + gu_y[1].astype(full)).astype(low)
-    gu_second[1].start()
+    chain.three()
 
     d_norm, gain_one_grad = norm_back(tokens[...].astype(full), gain_one[...], working[...])
     input_rows[...] = (d_resid[...] + d_norm).astype(low)
@@ -1318,14 +1349,12 @@
     vector_send[0].wait_recv()
     vector_in[2] = vector_in[0] + vector_in[1]
     vector_send[1].start()
-    chain.three()
-    sum_out.start_second()
-
-    gu_first[2].wait_recv()
+
+    gu_first[0].wait_recv()
     gu_second[0].wait_recv()
     total = gu_own[:, :units].astype(full) + gu_x[0].astype(full) + gu_ended[0].astype(full)
     gu_own[:, :units] = total.astype(low)
-    gu_first[3].wait_recv()
+    gu_first[1].wait_recv()
     gu_second[1].wait_recv()
     total = gu_own[:, units:].astype(full) + gu_y[0].astype(full) + gu_ended[1].astype(full)
     gu_own[:, units:] = total.astype(low)
@@ -1333,14 +1362,15 @@
         copy.start()
     keep_rows = here(rows_for(gu_own, 0, 0), gu_rows.at[0], 6)
     keep_rows.start()
+    sum_out.start_second()
     vector_send[1].wait_recv()
     vector_in[4] = vector_in[2] + vector_in[3]
     vector_send[2].start()
 
+    sum_qkv.start_second()
     sum_out.finish()
     for copy in out_send:
         copy.start()
-    sum_qkv.start_second()
     vector_send[2].wait_recv()
     vector_in[6] = vector_in[4] + vector_in[5]
     for copy in vector_send[3:]:
@@ -1379,7 +1409,7 @@
 
 def back(
     columns, resid, gain_two, cotangent, attended, queries, paired, slots, slot, first_row,
-    logsum, normeworking, tokens, gain_one, cosine, sine, w_out, w_qkv, gu_sum, branch,
+    logsum, normed_one, tokens, gain_one, cosine, sine, w_out, w_qkv, gu_sum, gu_far, branch,
 ):
     rows, width = tokens.shape
     n_s = paired.shape[0]
@@ -1400,7 +1430,7 @@
     vectors = (2 * width + qkv_width) // 8
     return pl.pallas_call(
         back_kernel,
-        in_specs=[hbm] + [vmem] * 15 + [hbm] * 4,
+        in_specs=[hbm] + [vmem] * 15 + [hbm] * 5,
         out_specs=[vmem] * 5 + [hbm],
         out_shape=[
             shape((rows, width), low),
@@ -1444,7 +1474,7 @@
             pltpu.VMEM((n_s, piece, width), low),
             pltpu.VMEM((n_s, piece, qkv_width), low),
             pltpu.VMEM((10, 8, vectors), full),
-            pltpu.SemaphoreType.DMA((8,)),
+            pltpu.SemaphoreType.DMA((10,)),
             pltpu.SemaphoreType.DMA((64,)),
             pltpu.SemaphoreType.DMA((64,)),
         ],
@@ -1454,7 +1484,7 @@
         name="back",
     )(
         columns, resid, gain_two, cotangent, attended, queries, paired, slots, slot_row, first_f,
-        logsum, normeworking, tokens, gain_one, cosine, sine, w_out, w_qkv, gu_sum, branch,
+        logsum, normed_one, tokens, gain_one, cosine, sine, w_out, w_qkv, gu_sum, gu_far, branch,
     )
 
 
@@ -1518,7 +1548,7 @@
             shape((piece, hidden_width), full),
             shape((piece, hidden_width), full),
         ],
-        compiler_params=pltpu.CompilerParams(vmem_limit_bytes=48 * 2**20),
+        compiler_params=pltpu.CompilerParams(vmem_limit_bytes=63 * 2**20),
         name="finish",
     )(layer, input_rows, grad_out, grad_qkv, grad_down, gu_rows)
 
@@ -1563,10 +1593,11 @@
         tokens, cotangent, small, slot, first_row, cosine, sine,
         (w_query, w_key, w_value, w_out, w_gate, w_up), down_own,
     )
-    columns, grad_down, gu_sum, branch = ffn(normed_all, upstream_all, weight_gu, weight_down)
+    columns, grad_down, gu_sum, gu_far, branch = ffn(normed_all, upstream_all, weight_gu, weight_down)
     layer, input_rows, vectors, grad_out, grad_qkv, gu_rows = back(
         columns, resid, gain_two, cotangent, attended, queries, paired, slots_all, slot, first_row,
-        logsum, normed_one, tokens, gain_one, cosine, sine, weight_out, weight_qkv, gu_sum, branch,
+        logsum, normed_one, tokens, gain_one, cosine, sine, weight_out, weight_qkv, gu_sum, gu_far,
+        branch,
     )
     (
         layer_out, input_grad, grad_out, grad_query, grad_key, grad_value, grad_down, grad_gate,

time: 457 us -> 451 us (0.987)
  local copies, waits for them, and re-layouts: 19.3 us -> 12.1 us
    pallas_call x1, Pallas kernels: 146 us -> 133 us  [back(): pl.pallas_call(back_kernel, in_specs=[hbm] + [vmem] * 15 + [hbm] * 5, out...]
    pallas_call x1, Pallas kernels: 110 us -> 122 us  [ffn(): pl.pallas_call(ffn_kernel, in_specs=[hbm] * 4, out_specs=[vmem] * 2 + [hb...]
    unnamed x14 -> x2, local copies, waits for them, and re-layouts: 7.17 us -> 0.01 us
where the time goes in v6:
time: 451 us; the launch traced here: 443 us
  Pallas kernels  422 us (94%)
  local copies, waits for them, and re-layouts  12.1 us (3%)
  other arithmetic  8.14 us (2%)
    pallas_call x1, Pallas kernels, front(): pl.pallas_call(front_kernel, in_specs=[vmem, hbm] + [vmem] * 6 + [hbm] *...  161 us
    pallas_call x1, Pallas kernels, back(): pl.pallas_call(back_kernel, in_specs=[hbm] + [vmem] * 15 + [hbm] * 5, out...  133 us
    pallas_call x1, Pallas kernels, ffn(): pl.pallas_call(ffn_kernel, in_specs=[hbm] * 4, out_specs=[vmem] * 2 + [hb...  122 us

profile of v6, /device:TPU:0, one launch (start us, length us, event | category | flops | bytes accessed | tf_op | source)
XLA Modules:
  0.0 443.4 jit_solution(7224310418816444442)
XLA Ops:
  0.7 0.7 tile.20
  1.3 0.1 tile.21
  1.4 0.7 tile.8
  2.1 0.1 tile.9
  2.1 4.1 concatenate.10
  6.2 0.7 or_select_fusion
  6.9 0.6 broadcast_in_dim.21.small
  7.6 0.8 reduce-window.9
  8.4 0.7 bitcast_subtract_fusion
  9.1 0.6 fusion.6
  9.6 2.6 subtract_convert_fusion
  12.3 0.5 fusion
  12.8 0.8 pad_maximum_fusion
  13.7 1.9 fusion.3
  15.6 0.6 broadcast_in_dim.23.slot_row
  16.2 0.8 broadcast_in_dim.22.slot_keys
  17.0 0.6 broadcast_in_dim.25.first_row
  17.6 1.2 constant_dynamic-slice_fusion
  18.8 1.0 pad.4.w_down
  19.8 160.6 %front.1 = (bf16[1536,4608]{1,0:T(8,128)(2,1)}, bf16[2304,1536]{1,0:T(8,128)(2,1)}, bf16[1024,1536]{1,0:T(8,128)(2,1)}, bf16[1024,1536]{1,0:T(8,128)(2,1)}, bf16...) custom-call(bf16[256,1536]{1,0:T(8,128)(2,1)} %tokens.3, ...), custom_call_target="tpu_custom_call" | custom-call | tf_op jit(solution)/shard_map/front/pallas_call | solution.py:774
  180.4 122.2 %ffn.1 = (f32[256,1536]{1,0:T(8,128)}, f32[288,1536]{1,0:T(8,128)}, bf16[3,192,4608]{2,1,0:T(8,128)(2,1)}, bf16[2,192,2304]{2,1,0:T(8,128)(2,1)}, bf16[1024,1536...) custom-call(bf16[1024,1536]{1,0:T(8,128)(2,1)} %get-tuple-element.49.normed_all, ...), custom_call_target="tpu_custom_call" | custom-call | tf_op jit(solution)/shard_map/ffn/pallas_call | solution.py:1092
  302.6 132.8 %back.1 = (bf16[256,1536]{1,0:T(8,128)(2,1)}, bf16[256,1536]{1,0:T(8,128)(2,1)}, f32[8,640]{1,0:T(8,128)}, f32[48,1536]{1,0:T(8,128)}, f32[48,2048]{1,0:T(8,128)}, /*index=5*/bf16[4,48,4608]{2,1,0:T(8,128)(2,1)}) custom-call(f32[256,1536]{1,0:T(8,128)} %get-tuple-element.53.columns, f32[256,1536]{1,0:T(8,128)} %get-tuple-element.54.resid, ...), custom_call_target="tpu_custom_call" | custom-call | tf_op jit(solution)/shard_map/back/pallas_call | solution.py:1431
  435.4 0.0 copy-start
  435.4 6.6 %finish.1 = (bf16[256,1536]{1,0:T(8,128)(2,1)}, bf16[256,1536]{1,0:T(8,128)(2,1)}, f32[48,1536]{1,0:T(8,128)}, f32[48,1536]{1,0:T(8,128)}, f32[48,256]{1,0:T(8,1...) custom-call(bf16[256,1536]{1,0:T(8,128)(2,1)} %get-tuple-element.68.layer, ...), custom_call_target="tpu_custom_call" | custom-call | tf_op jit(solution)/shard_map/finish/pallas_call | solution.py:1536
  442.0 0.0 copy-done
  442.0 0.6 fusion.4
  442.6 0.6 fusion.5
  (2 shorter events, 0.0 us)
Async XLA Ops:
  435.4 6.6 %copy-start = (f32[8,640]{1,0:T(8,128)S(1)}, f32[8,640]{1,0:T(8,128)}, u32[]{:S(2)}) copy-start(f32[8,640]{1,0:T(8,128)} %get-tuple-element.76) | copy-start | bytes 61444

commit v7 on v6

--- a/solution.py
+++ b/solution.py
@@ -410,19 +410,24 @@
 
 
 def front_kernel(
-    tokens, cotangent, small, slot_keys, slot_row, first_row, cosine, sine,
+    lengths, tokens, cotangent, small, balance, inverse,
     w_query, w_key, w_value, w_out, w_gate, w_up, w_down,
-    gu_all, down_all, upstream_all, normed_all, qkv_out, out_out,
+    gu_all, down_all, upstream_all, normed_all, hidden, factor_gate, factor_up, qkv_out, out_out,
     queries, paired_out, slots_out, logsum, attended, resid, normed_one, gain_one, gain_two,
-    qkv, out_w, gate_v, up_v, gu_own, kv, small_all, slots_all, bias, normed_own,
+    slot_row, first_row, cosine, sine,
+    qkv, out_w, gate_v, up_v, gu, normed, kv, small_own, small_all, slots_all, bias,
+    down_raw, down_own, hidden_v, gate_part, up_part,
     local, ssem, rsem, zsend, zrecv,
 ):
     f = lax.axis_index("fsdp")
     s = lax.axis_index("seq")
     rows, width = tokens.shape
     n_f, n_s = 8, slots_all.shape[0]
+    group = n_s * rows
     block = w_query.shape[0]
-    unit = w_down.shape[0]
+    unit_pad = down_own.shape[0]
+    unit = w_gate.shape[1] // (n_f * n_s)
+    units = n_f * unit_pad
     kv_width = KV_HEADS * HEAD_DIM
     qkv_width = width + 2 * kv_width
     scale = HEAD_DIM ** (-0.5)
@@ -543,32 +548,51 @@
                 pl.when(can_up)(up.wait_send)
                 pl.when(can_down)(down.wait_send)
 
+    own_block = pl.ds(pl.multiple_of(f * block, 16), block)
     pieces = [
-        here(w_query, qkv.at[pl.ds(pl.multiple_of(f * block, 16), block), pl.ds(0, width)], 5),
-        here(w_key, qkv.at[pl.ds(pl.multiple_of(f * block, 16), block), pl.ds(width, kv_width)], 6),
-        here(w_value, qkv.at[pl.ds(pl.multiple_of(f * block, 16), block), pl.ds(width + kv_width, kv_width)], 7),
+        here(w_query, qkv.at[own_block, pl.ds(0, width)], 5),
+        here(w_key, qkv.at[own_block, pl.ds(width, kv_width)], 6),
+        here(w_value, qkv.at[own_block, pl.ds(width + kv_width, kv_width)], 7),
         here(cotangent, own_rows(upstream_all, s, rows), 8),
     ]
     load_gate = here(w_gate, gate_v, 9)
     load_up = here(w_up, up_v, 10)
+    first_unit = pl.multiple_of(s * unit // 16 * 16, 16)
+    load_down = here(w_down.at[pl.ds(first_unit, unit_pad)], down_raw, 15)
     for copy in pieces:
         copy.start()
     load_gate.start()
     load_up.start()
-    small_all[f] = small[...]
-    slots_all[s] = slot_keys[...]
+    load_down.start()
+
+    slot = (balance[...] & (group - 1)).astype(jnp.float32)
+    second = lengths[0, 0].astype(jnp.float32)
+    third = (lengths[0, 0] + lengths[0, 1]).astype(jnp.float32)
+    first = jnp.where(slot >= third, third, jnp.where(slot >= second, second, 0.0))
+    slot_row[...] = jnp.broadcast_to(slot, slot_row.shape)
+    first_row[...] = jnp.broadcast_to(first, first_row.shape)
+    slots_all[s] = jnp.broadcast_to(slot, (128, rows)).T
+    lanes = lax.broadcasted_iota(jnp.int32, small.shape, 1)
+    sorts = lax.broadcasted_iota(jnp.int32, small.shape, 0)
+    small_own[...] = jnp.where(
+        sorts < 3,
+        pltpu.roll(small[...], lax.rem(f, 2) * block, 1),
+        pltpu.roll(small[...], f * (kv_width // n_f), 1),
+    )
+    small_all[f] = small_own[...]
 
     gather_qkv = Gather(None, qkv, block, 0)
     gather_out = Gather(w_out, out_w, block, 8)
-    gather_gu = Gather(gu_own, gu_all, block, 16)
-    gather_down = Gather(w_down, down_all, unit, 24)
+    gather_gu = Gather(None, gu, block, 16)
+    gather_down = Gather(down_own, down_all, unit_pad, 24)
     chain_up = Chain(upstream_all, 0)
-    chain_normed = Chain(normed_all, 6)
+    chain_normed = Chain(normed, 6)
     send_small = [
-        there(small, small_all.at[f], 32 + k, fsdp=plane[k]) for k in range(1, n_f)
+        there(small_own, small_all.at[f], 32 + k, fsdp=plane[k]) for k in range(1, n_f)
     ]
     send_slots = [
-        there(slot_keys, slots_all.at[s], 40 + j, seq=lax.rem(s + j, n_s)) for j in range(1, n_s)
+        there(slots_all.at[s], slots_all.at[s], 40 + j, seq=lax.rem(s + j, n_s))
+        for j in range(1, n_s)
     ]
     send_kv = [
         there(kv.at[s], kv.at[s], 44 + j, seq=lax.rem(s + j, n_s)) for j in range(1, n_s)
@@ -584,28 +608,37 @@
 
     load_gate.wait()
     load_up.wait()
-    pick_units(gate_v, up_v, gu_own, w_gate.shape[1] // n_f, w_gate.shape[1] // (n_f * n_s), unit)
+    pick_units(gate_v, up_v, gu.at[own_block], w_gate.shape[1] // n_f, unit, unit_pad)
+    load_down.wait()
+    raw = down_raw[...].astype(jnp.float32)
+    shifted = jnp.concatenate([raw[8:], jnp.zeros((8, width), jnp.float32)], 0)
+    raw = jnp.where(lax.rem(s * unit, 16) == 0, raw, shifted)
+    inside = lax.broadcasted_iota(jnp.int32, raw.shape, 0) < unit
+    down_own[...] = jnp.where(inside, raw, 0.0).astype(jnp.bfloat16)
+
+    position = slots_all[s] - jnp.broadcast_to(first, (128, rows)).T
+    angle = position * inverse[...]
+    cosine[...] = jnp.cos(angle)
+    sine[...] = jnp.where(
+        lax.broadcasted_iota(jnp.int32, angle.shape, 1) < HEAD_DIM // 2, -1.0, 1.0
+    ) * jnp.sin(angle)
 
     for copy in send_small + send_slots:
         copy.wait_recv()
-    third = 2 * block
-    for i in range(n_f // 2):
-        columns = slice(i * third, (i + 1) * third)
-        gain_one[:, columns] = (
-            small_all[2 * i, 0:1, :third].astype(jnp.float32)
-            + small_all[2 * i + 1, 0:1, :third].astype(jnp.float32)
+    def joined(sort):
+        return jnp.concatenate(
+            [
+                small_all[2 * i, sort : sort + 1] + small_all[2 * i + 1, sort : sort + 1]
+                for i in range(n_f // 2)
+            ],
+            1,
         )
-        gain_two[:, columns] = (
-            small_all[2 * i, 0:1, third : 2 * third].astype(jnp.float32)
-            + small_all[2 * i + 1, 0:1, third : 2 * third].astype(jnp.float32)
-        )
-    bias_query = [
-        small_all[2 * i, 0:1, 2 * third : 3 * third].astype(jnp.float32)
-        + small_all[2 * i + 1, 0:1, 2 * third : 3 * third].astype(jnp.float32)
-        for i in range(n_f // 2)
-    ]
-    bias_query = jnp.concatenate(bias_query, 1)
-    bias_pair = sum(small_all[i, 0:1, 3 * third :].astype(jnp.float32) for i in range(n_f))
+
+    gain_one[...] = joined(0)
+    gain_two[...] = joined(1)
+    bias_query = joined(2)
+    bias_key = sum(small_all[i, 3:4, :kv_width] for i in range(n_f))
+    bias_value = sum(small_all[i, 4:5, :kv_width] for i in range(n_f))
 
     inputs = tokens[...].astype(jnp.float32)
     root = lax.rsqrt(jnp.mean(inputs * inputs, -1, keepdims=True) + epsilon)
@@ -613,14 +646,14 @@
     for j in range(n_s):
         keys_slot = slots_all[j]
         keys_slot = jnp.concatenate([keys_slot] * (rows // 128), 1)
-        ok = (keys_slot <= slot_row[0:1]) & (keys_slot >= first_row[0:1])
+        ok = (keys_slot <= slot) & (keys_slot >= first)
         bias[j * rows : (j + 1) * rows] = jnp.where(ok, 0.0, -1e30)
 
     gather_qkv.forward()
-    gather_out.start()
     chain_up.receive(1)
     chain_up.send(2)
     gather_qkv.last()
+    gather_out.start()
     gather_qkv.finish()
     save_qkv = here(qkv, qkv_out, 11)
     save_qkv.start()
@@ -628,19 +661,19 @@
     def turned(value):
         return value * cosine[...] + pltpu.roll(value, HEAD_DIM // 2, 1) * sine[...]
 
-    normed = normed_one[...]
-    pair = jnp.dot(normed, qkv[:, width : width + kv_width], preferred_element_type=jnp.float32)
-    pair = pair + bias_pair[:, :kv_width]
+    rows_low = normed_one[...]
+    pair = jnp.dot(rows_low, qkv[:, width : width + kv_width], preferred_element_type=jnp.float32)
+    pair = pair + bias_key
     for g in range(KV_HEADS):
         columns = slice(g * HEAD_DIM, (g + 1) * HEAD_DIM)
         kv[s, :, columns] = turned(pair[:, columns]).astype(jnp.bfloat16)
-    pair = jnp.dot(normed, qkv[:, width + kv_width :], preferred_element_type=jnp.float32)
-    kv[s, :, kv_width:] = (pair + bias_pair[:, kv_width:]).astype(jnp.bfloat16)
+    pair = jnp.dot(rows_low, qkv[:, width + kv_width :], preferred_element_type=jnp.float32)
+    kv[s, :, kv_width:] = (pair + bias_value).astype(jnp.bfloat16)
     for copy in send_kv:
         copy.start()
     for g in range(HEADS // 2):
         columns = slice(g * 2 * HEAD_DIM, (g + 1) * 2 * HEAD_DIM)
-        pair = jnp.dot(normed, qkv[:, columns], preferred_element_type=jnp.float32)
+        pair = jnp.dot(rows_low, qkv[:, columns], preferred_element_type=jnp.float32)
         pair = pair + bias_query[:, columns]
         for h in range(2):
             part = turned(pair[:, h * HEAD_DIM : (h + 1) * HEAD_DIM]).astype(jnp.bfloat16)
@@ -695,28 +728,76 @@
         resid[:, columns] = tokens[:, columns].astype(jnp.float32) + part
     value = resid[...]
     root = lax.rsqrt(jnp.mean(value * value, -1, keepdims=True) + epsilon)
-    normed_own[...] = (value * root * gain_two[...]).astype(jnp.bfloat16)
-    place_normed = here(normed_own, own_rows(normed_all, s, rows), 14)
-    place_normed.start()
-    place_normed.wait()
+    own_tokens = pl.ds(pl.multiple_of(s * rows, rows), rows)
+    normed[own_tokens] = (value * root * gain_two[...]).astype(jnp.bfloat16)
     chain_normed.send(1)
 
+    wide = hidden_v.shape[2]
+    count = units // wide
+
+    def saves(owner, t, slot):
+        place = (
+            pl.ds(pl.multiple_of(owner * rows, rows), rows),
+            pl.ds(pl.multiple_of(t * wide, wide), wide),
+        )
+        return [
+            here(part.at[slot], whole.at[place], 16 + 3 * slot + i)
+            for i, (part, whole) in enumerate(
+                ((hidden_v, hidden), (gate_part, factor_gate), (up_part, factor_up))
+            )
+        ]
+
+    def feed(owner, done):
+        def body(t, carry):
+            slot = lax.rem(t + done, 2)
+            mine = normed[pl.ds(pl.multiple_of(owner * rows, rows), rows)]
+            gate_columns = pl.ds(pl.multiple_of(t * wide, wide), wide)
+            up_columns = pl.ds(pl.multiple_of(units + t * wide, wide), wide)
+            gate = jnp.dot(mine, gu[:, gate_columns], preferred_element_type=jnp.float32)
+            up = jnp.dot(mine, gu[:, up_columns], preferred_element_type=jnp.float32)
+            sigma = jax.nn.sigmoid(gate)
+            activated = gate * sigma
+
+            @pl.when(t + done >= 2)
+            def _():
+                for copy in saves(owner, t, slot):
+                    copy.wait()
+
+            hidden_v[slot] = (activated * up).astype(jnp.bfloat16)
+            gate_part[slot] = (up * sigma * (1.0 + gate * (1.0 - sigma))).astype(jnp.bfloat16)
+            up_part[slot] = activated.astype(jnp.bfloat16)
+            for copy in saves(owner, t, slot):
+                copy.start()
+            return carry
+
+        lax.fori_loop(0, count, body, 0)
+
     gather_gu.forward()
-    gather_down.start()
     chain_normed.receive(1)
     chain_normed.send(2)
     gather_gu.last()
+    gather_down.start()
+    gather_gu.finish()
+    save_gu = here(gu, gu_all, 22)
+    save_gu.start()
+    feed(s, 0)
     chain_normed.receive(2)
     chain_normed.send(3)
+    feed(s ^ 1, count)
+    gather_down.forward()
+    feed(s ^ 2, 2 * count)
+    chain_normed.receive(3)
+    save_normed = here(normed, normed_all, 23)
+    save_normed.start()
+    gather_down.last()
+    feed(s ^ 3, 3 * count)
+    for t in (count - 2, count - 1):
+        for copy in saves(s ^ 3, t, (t + 3 * count) % 2):
+            copy.wait()
     chain_up.receive(3)
-    gather_down.forward()
-    gather_gu.finish()
-    gather_down.last()
-    chain_normed.receive(3)
     gather_down.finish()
-    save_qkv.wait()
-    save_kv.wait()
-    save_out.wait()
+    for copy in (save_qkv, save_kv, save_out, save_gu, save_normed):
+        copy.wait()
     for part in (gather_qkv, gather_out, gather_gu, gather_down, chain_up, chain_normed):
         part.sent()
     for copy in send_small + send_slots + send_kv:
@@ -751,35 +832,41 @@
         out[:, first : first + tile] = total.astype(jnp.bfloat16)
 
 
-def front(tokens, cotangent, small, slot, first_row, cosine, sine, weights, w_down_own):
+def front(tokens, cotangent, lengths, balance, vectors, weights):
     rows, width = tokens.shape
     n_s = lax.axis_size("seq")
-    w_query, w_key, w_value, w_out, w_gate, w_up = weights
+    w_query, w_key, w_value, w_out, w_gate, w_up, w_down = weights
     block = w_query.shape[0]
-    unit = w_down_own.shape[0]
+    unit_pad = -(-w_down.shape[0] // n_s // 16) * 16
     kv_width = KV_HEADS * HEAD_DIM
     qkv_width = width + 2 * kv_width
-    units = 8 * unit
+    units = 8 * unit_pad
     group = n_s * rows
+    wide = 768
     low, full = jnp.bfloat16, jnp.float32
-    slot_f = slot.astype(full)
-    slot_keys = jnp.broadcast_to(slot_f[:, None], (rows, 128))
-    slot_row = jnp.broadcast_to(slot_f[None], (8, rows))
-    first_f = jnp.broadcast_to(first_row.astype(full)[None], (8, rows))
+    small = sum(
+        jnp.pad(v.astype(full)[None], ((i, 7 - i), (0, 2 * block - v.shape[0])))
+        for i, v in enumerate(vectors)
+    )
     half = HEAD_DIM // 2
-    sine = jnp.concatenate([-sine[:, :half], sine[:, half:]], 1)
+    inverse = rope_base ** (-(np.arange(half, dtype=np.float32) * np.float32(2.0 / HEAD_DIM)))
+    inverse = jnp.asarray(np.concatenate([inverse, inverse])[None], full)
+    smem = pl.BlockSpec(memory_space=pltpu.SMEM)
     vmem = pl.BlockSpec(memory_space=pltpu.VMEM)
     hbm = pl.BlockSpec(memory_space=pl.ANY)
     shape = jax.ShapeDtypeStruct
     return pl.pallas_call(
         front_kernel,
-        in_specs=[vmem, hbm] + [vmem] * 6 + [hbm] * 7,
-        out_specs=[hbm] * 6 + [vmem, hbm] + [vmem] * 7,
+        in_specs=[smem, vmem, hbm, vmem, vmem, vmem] + [hbm] * 7,
+        out_specs=[hbm] * 9 + [vmem, hbm] + [vmem] * 11,
         out_shape=[
-            shape((8 * block, 2 * units), low),
+            shape((width, 2 * units), low),
             shape((units, width), low),
             shape((group, width), low),
             shape((group, width), low),
+            shape((group, units), low),
+            shape((group, units), low),
+            shape((group, units), low),
             shape((width, qkv_width), low),
             shape((width, width), low),
             shape((rows, width), low),
@@ -791,36 +878,46 @@
             shape((rows, width), low),
             shape((1, width), full),
             shape((1, width), full),
+            shape((8, rows), full),
+            shape((8, rows), full),
+            shape((rows, HEAD_DIM), full),
+            shape((rows, HEAD_DIM), full),
         ],
         scratch_shapes=[
             pltpu.VMEM((width, qkv_width), low),
             pltpu.VMEM((width, width), low),
             pltpu.VMEM(w_gate.shape, low),
             pltpu.VMEM(w_up.shape, low),
-            pltpu.VMEM((block, 2 * units), low),
+            pltpu.VMEM((width, 2 * units), low),
+            pltpu.VMEM((group, width), low),
             pltpu.VMEM((n_s, rows, 2 * kv_width), low),
-            pltpu.VMEM((8,) + small.shape, low),
+            pltpu.VMEM((8, 2 * block), full),
+            pltpu.VMEM((8, 8, 2 * block), full),
             pltpu.VMEM((n_s, rows, 128), full),
             pltpu.VMEM((group, rows), full),
-            pltpu.VMEM((rows, width), low),
-            pltpu.SemaphoreType.DMA((16,)),
+            pltpu.VMEM((unit_pad, width), low),
+            pltpu.VMEM((unit_pad, width), low),
+            pltpu.VMEM((2, rows, wide), low),
+            pltpu.VMEM((2, rows, wide), low),
+            pltpu.VMEM((2, rows, wide), low),
+            pltpu.SemaphoreType.DMA((24,)),
             pltpu.SemaphoreType.DMA((48,)),
             pltpu.SemaphoreType.DMA((48,)),
             pltpu.SemaphoreType.DMA((12,)),
             pltpu.SemaphoreType.DMA((12,)),
         ],
         compiler_params=pltpu.CompilerParams(
-            collective_id=0, has_side_effects=True, vmem_limit_bytes=56 * 2**20
+            collective_id=0, has_side_effects=True, vmem_limit_bytes=62 * 2**20
         ),
         name="front",
     )(
-        tokens, cotangent, small, slot_keys, slot_row, first_f, cosine, sine,
-        w_query, w_key, w_value, w_out, w_gate, w_up, w_down_own,
+        lengths, tokens, cotangent, small, balance.reshape(1, rows), inverse,
+        w_query, w_key, w_value, w_out, w_gate, w_up, w_down,
     )
 
 
 def ffn_kernel(
-    normed_all, upstream_all, w_gu, w_down,
+    normed_all, upstream_all, w_gu, w_down, hidden_all, factor_gate, factor_up,
     columns, grad_down, gu_sum, gu_far, branch, down_arrived, gu_arrived,
     normed, upstream, gu, down, hidden, d_both, partial, z_one, z_two, z_three,
     down_x, down_y, down_last, down_piece,
@@ -862,56 +959,69 @@
     def part(ref, owner, size):
         return ref.at[pl.ds(pl.multiple_of(owner * size, 16), size)]
 
-    first_loads = []
-    for p, j in enumerate(ORDER):
-        owner = lax.rem(s + n_s - j, n_s)
-        first_loads.append(here(part(normed_all, owner, rows), part(normed, p, rows), p))
-        first_loads.append(here(part(upstream_all, owner, rows), part(upstream, p, rows), 4 + p))
-
-    def tile_loads(t):
-        gate_columns = pl.ds(pl.multiple_of(t * wide, wide), wide)
-        up_columns = pl.ds(pl.multiple_of(units + t * wide, wide), wide)
+    early, late = range(0, n_s // 2), range(n_s // 2, n_s)
+
+    def rows_of(p):
+        return pl.ds(p * rows, rows)
+
+    def row_loads(p):
+        owner = lax.rem(s + n_s - ORDER[p], n_s)
+        mine = rows_of(p)
         return [
-            here(w_gu.at[:, gate_columns], gu.at[:, gate_columns], 8 + 3 * t),
-            here(w_gu.at[:, up_columns], gu.at[:, up_columns], 9 + 3 * t),
-            here(w_down.at[gate_columns], down.at[gate_columns], 10 + 3 * t),
+            here(part(upstream_all, owner, rows), upstream.at[mine], 5 * p),
+            here(part(factor_gate, owner, rows), d_both.at[mine, pl.ds(0, units)], 5 * p + 1),
+            here(part(factor_up, owner, rows), d_both.at[mine, pl.ds(units, units)], 5 * p + 2),
+            here(part(hidden_all, owner, rows), hidden.at[mine], 5 * p + 3),
+            here(part(normed_all, owner, rows), normed.at[mine], 5 * p + 4),
         ]
 
-    for copy in first_loads:
+    def down_load(t):
+        mine = pl.ds(pl.multiple_of(t * wide, wide), wide)
+        return here(w_down.at[mine], down.at[mine], 20 + t)
+
+    def gu_load(n):
+        mine = pl.ds(pl.multiple_of(n * 512, 512), 512)
+        return here(w_gu.at[mine], gu.at[mine], 23 + n)
+
+    loads = [row_loads(p) for p in range(n_s)]
+    order = [loads[0][0], loads[1][0], down_load(0)]
+    order += [loads[p][i] for i in (1, 2) for p in early]
+    order += [down_load(t) for t in range(1, units // wide)]
+    order += [gu_load(n) for n in range(width // 512)]
+    order += [loads[p][i] for i in (0, 1, 2) for p in late]
+    order += [loads[p][i] for i in (3, 4) for p in range(n_s)]
+    for copy in order:
         copy.start()
-    for t in range(units // wide):
-        for copy in tile_loads(t):
-            copy.start()
-    for copy in first_loads:
-        copy.wait()
-
-    def forward(part_rows, wait):
+
+    def forward(blocks, wait):
+        for p in blocks:
+            for copy in loads[p][:3]:
+                copy.wait()
+        mine = pl.ds(blocks[0] * rows, len(blocks) * rows)
+
         def body(t, carry):
             if wait:
-                for copy in tile_loads(t):
-                    copy.wait()
+                down_load(t).wait()
             gate_columns = pl.ds(pl.multiple_of(t * wide, wide), wide)
             up_columns = pl.ds(pl.multiple_of(units + t * wide, wide), wide)
-            mine = normed[part_rows]
-            gate = jnp.dot(mine, gu[:, gate_columns], preferred_element_type=full)
-            up = jnp.dot(mine, gu[:, up_columns], preferred_element_type=full)
             d_hidden = lax.dot_general(
-                upstream[part_rows], down[gate_columns], (((1,), (1,)), ((), ())),
+                upstream[mine], down[gate_columns], (((1,), (1,)), ((), ())),
                 preferred_element_type=full,
             )
-            sigma = jax.nn.sigmoid(gate)
-            activated = gate * sigma
-            hidden[part_rows, gate_columns] = (activated * up).astype(jnp.bfloat16)
-            d_both[part_rows, gate_columns] = (
-                d_hidden * up * sigma * (1.0 + gate * (1.0 - sigma))
-            ).astype(jnp.bfloat16)
-            d_both[part_rows, up_columns] = (d_hidden * activated).astype(jnp.bfloat16)
+            value = d_hidden * d_both[mine, gate_columns].astype(full)
+            d_both[mine, gate_columns] = value.astype(jnp.bfloat16)
+            value = d_hidden * d_both[mine, up_columns].astype(full)
+            d_both[mine, up_columns] = value.astype(jnp.bfloat16)
             return carry
 
         lax.fori_loop(0, units // wide, body, 0)
 
-    def backward(part_rows):
+    def backward(blocks, wait):
+        part_rows = pl.ds(blocks[0] * rows, len(blocks) * rows)
+
         def body(n, carry):
+            if wait:
+                gu_load(n).wait()
             out_columns = pl.ds(pl.multiple_of(n * 512, 512), 512)
             value = lax.dot_general(
                 d_both[part_rows], gu[out_columns], (((1,), (1,)), ((), ())),
@@ -923,16 +1033,19 @@
         lax.fori_loop(0, width // 512, body, 0)
 
     chain = SumChain(partial, rows, z_one, z_two, z_three, there, 0)
-    early, late = slice(0, half_rows), slice(half_rows, group)
     pieces = [(first, min(group, units - first)) for first in range(0, units, group)]
     forward(early, True)
-    backward(early)
+    backward(early, True)
     pl.semaphore_wait(entry, 5)
     chain.one()
     forward(late, False)
-    backward(late)
+    backward(late, False)
     chain.add_one()
     chain.two()
+
+    for p in range(n_s):
+        loads[p][3].wait()
+        loads[p][4].wait()
 
     def down_body(t, carry):
         unit_rows = pl.ds(pl.multiple_of(t * tile, tile), tile)
@@ -978,7 +1091,7 @@
 
     down_pieces = [(pl.ds(0, width), down_piece)]
     for i in (3, 1, 2, 0):
-        add_arrived(i, down, unit, down_arrived, down_pieces, down_core, 14)
+        add_arrived(i, down, unit, down_arrived, down_pieces, down_core, 26)
     to_x, to_y, to_both = [part(down, plane[k], unit) for k in (2, 4, 6)]
     low_half, high_half = pl.ds(0, half), pl.ds(half, half)
     down_first = [
@@ -1001,7 +1114,7 @@
     again = [
         here(
             w_down.at[first : first + count],
-            d_both.at[:count, i * width : (i + 1) * width], 24 + i,
+            d_both.at[:count, i * width : (i + 1) * width], 32 + i,
         )
         for i, (first, count) in enumerate(pieces)
     ]
@@ -1042,7 +1155,7 @@
         (pl.ds(0, units), hidden.at[:block]),
         (pl.ds(units, units), hidden.at[block : 2 * block]),
     ]
-    add_arrived(3, gu, block, gu_arrived, gu_pieces, gu_core, 20)
+    add_arrived(3, gu, block, gu_arrived, gu_pieces, gu_core, 27)
     far = part(gu, plane[6], block)
     gu_first = [
         there(far.at[:, pl.ds(0, units)], gu_far.at[0], 20, fsdp=plane[2]),
@@ -1051,8 +1164,8 @@
     for copy in gu_first:
         copy.start()
     for i in (1, 2, 0):
-        add_arrived(i, gu, block, gu_arrived, gu_pieces, gu_core, 20)
-    store = [here(part(gu, plane[2 * i], block), gu_sum.at[i], 16 + i) for i in range(3)]
+        add_arrived(i, gu, block, gu_arrived, gu_pieces, gu_core, 27)
+    store = [here(part(gu, plane[2 * i], block), gu_sum.at[i], 29 + i) for i in range(3)]
     for copy in store:
         copy.start()
     down_first[0].wait_recv()
@@ -1068,7 +1181,7 @@
     )
     chain_branch.add_one()
     chain_branch.one_sent()
-    store_branch = here(upstream, branch, 27)
+    store_branch = here(upstream, branch, 35)
     store_branch.start()
     chain.one_sent()
     chain.sent()
@@ -1080,7 +1193,7 @@
         copy.wait()
 
 
-def ffn(normed_all, upstream_all, w_gu, w_down):
+def ffn(normed_all, upstream_all, w_gu, w_down, hidden, factor_gate, factor_up):
     group, width = normed_all.shape
     units = w_down.shape[0]
     rows = group // len(ORDER)
@@ -1091,7 +1204,7 @@
     shape = jax.ShapeDtypeStruct
     return pl.pallas_call(
         ffn_kernel,
-        in_specs=[hbm] * 4,
+        in_specs=[hbm] * 7,
         out_specs=[vmem] * 2 + [hbm] * 5,
         out_shape=[
             shape((rows, width), full),
@@ -1125,7 +1238,7 @@
             collective_id=1, has_side_effects=True, vmem_limit_bytes=63 * 2**20
         ),
         name="ffn",
-    )(normed_all, upstream_all, w_gu, w_down)[:5]
+    )(normed_all, upstream_all, w_gu, w_down, hidden, factor_gate, factor_up)[:5]
 
 
 def back_kernel(
@@ -1408,7 +1521,7 @@
 
 
 def back(
-    columns, resid, gain_two, cotangent, attended, queries, paired, slots, slot, first_row,
+    columns, resid, gain_two, cotangent, attended, queries, paired, slots, slot_row, first_row,
     logsum, normed_one, tokens, gain_one, cosine, sine, w_out, w_qkv, gu_sum, gu_far, branch,
 ):
     rows, width = tokens.shape
@@ -1420,10 +1533,6 @@
     piece = block // n_s
     units = gu_sum.shape[2] // 2
     low, full = jnp.bfloat16, jnp.float32
-    slot_row = jnp.broadcast_to(slot.astype(full)[None], (8, rows))
-    first_f = jnp.broadcast_to(first_row.astype(full)[None], (8, rows))
-    half = HEAD_DIM // 2
-    sine = jnp.concatenate([-sine[:, :half], sine[:, half:]], 1)
     vmem = pl.BlockSpec(memory_space=pltpu.VMEM)
     hbm = pl.BlockSpec(memory_space=pl.ANY)
     shape = jax.ShapeDtypeStruct
@@ -1483,7 +1592,7 @@
         ),
         name="back",
     )(
-        columns, resid, gain_two, cotangent, attended, queries, paired, slots, slot_row, first_f,
+        columns, resid, gain_two, cotangent, attended, queries, paired, slots, slot_row, first_row,
         logsum, normed_one, tokens, gain_one, cosine, sine, w_out, w_qkv, gu_sum, gu_far, branch,
     )
 
@@ -1562,40 +1671,22 @@
     seq_rank = lax.axis_index("seq")
     fsdp_rank = lax.axis_index("fsdp")
     rows_here, width = tokens.shape
-    group = seq_count * rows_here
     kv_width = KV_HEADS * HEAD_DIM
     hidden_width = w_gate.shape[1]
     unit = hidden_width // (fsdp_count * seq_count)
-    unit_pad = -(-unit // 16) * 16
-    weight_rows = w_gate.shape[0]
-
-    pair_bias = jnp.concatenate([jnp.tile(b_key, fsdp_count), jnp.tile(b_value, fsdp_count)])
-    small = jnp.concatenate([norm1_gain] * 2 + [norm2_gain] * 2 + [b_query] * 2 + [pair_bias])
-    place_of = np.concatenate(
-        [np.repeat([0, 1], weight_rows)] * 3 + [8 + np.repeat(np.arange(8), b_key.shape[0])] * 2
-    )
-    place_of = jnp.asarray(place_of, jnp.int32)
-    mine = (place_of == fsdp_rank % 2) | (place_of == 8 + fsdp_rank)
-    small = jnp.broadcast_to(jnp.where(mine, small, 0)[None], (16, small.shape[0]))
-
-    slot = balance % group
-    seq_lengths = lengths[0]
-    starts = jnp.cumsum(seq_lengths) - seq_lengths
-    segment = segment_of(slot, starts)
-    first_row = jnp.where(segment == 0, starts[0], jnp.where(segment == 1, starts[1], starts[2]))
-    cosine, sine = rope_tables(slot - first_row)
-    down_own = lax.dynamic_slice_in_dim(w_down, seq_rank * unit, unit, 0)
-    down_own = jnp.pad(down_own, ((0, unit_pad - unit), (0, 0)))
     (
-        weight_gu, weight_down, upstream_all, normed_all, weight_qkv, weight_out,
-        queries, paired, slots_all, logsum, attended, resid, normed_one, gain_one, gain_two,
+        weight_gu, weight_down, upstream_all, normed_all, hidden, factor_gate, factor_up,
+        weight_qkv, weight_out, queries, paired, slots, logsum, attended, resid, normed_one,
+        gain_one, gain_two, slot_row, first_row, cosine, sine,
     ) = front(
-        tokens, cotangent, small, slot, first_row, cosine, sine,
-        (w_query, w_key, w_value, w_out, w_gate, w_up), down_own,
-    )
-    columns, grad_down, gu_sum, gu_far, branch = ffn(normed_all, upstream_all, weight_gu, weight_down)
+        tokens, cotangent, lengths, balance, (norm1_gain, norm2_gain, b_query, b_key, b_value),
+        (w_query, w_key, w_value, w_out, w_gate, w_up, w_down),
+    )
+    columns, grad_down, gu_sum, gu_far, branch = ffn(
+        normed_all, upstream_all, weight_gu, weight_down, hidden, factor_gate, factor_up
+    )
     layer, input_rows, vectors, grad_out, grad_qkv, gu_rows = back(
-        columns, resid, gain_two, cotangent, attended, queries, paired, slots_all, slot, first_row,
+        columns, resid, gain_two, cotangent, attended, queries, paired, slots, slot_row, first_row,
         logsum, normed_one, tokens, gain_one, cosine, sine, weight_out, weight_qkv, gu_sum, gu_far,
         branch,
     )

time: 451 us -> 431 us (0.956)
  local copies, waits for them, and re-layouts: 12.1 us -> 3.15 us
  other arithmetic: 8.14 us -> 1.28 us
    pallas_call x2, Pallas kernels: 283 us -> 276 us  [the longest x1 167 us: front(): pl.pallas_call(front_kernel, in_specs=[smem, vmem, hbm, vmem, vmem, vmem]...]
    convert_element_type x2 -> x0, other arithmetic: 4.58 us -> none  [the longest x1 2.63 us: rope_tables(): angle = position.astype(jnp.float32)[:, None] * inverse[None, :]]
where the time goes in v7:
time: 431 us; the launch traced here: 425 us
  Pallas kernels  419 us (97%)
    pallas_call x1, Pallas kernels, front(): pl.pallas_call(front_kernel, in_specs=[smem, vmem, hbm, vmem, vmem, vmem]...  167 us
    pallas_call x1, Pallas kernels, back(): pl.pallas_call(back_kernel, in_specs=[hbm] + [vmem] * 15 + [hbm] * 5, out...  137 us
    pallas_call x1, Pallas kernels, ffn(): pl.pallas_call(ffn_kernel, in_specs=[hbm] * 7, out_specs=[vmem] * 2 + [hb...  110 us

profile of v7, /device:TPU:0, one launch (start us, length us, event | category | flops | bytes accessed | tf_op | source)
XLA Modules:
  0.0 424.8 jit_solution(6837511412030119462)
XLA Ops:
  0.6 0.7 broadcast_in_dim.20
  1.3 0.7 broadcast_in_dim.21
  2.0 0.7 broadcast_in_dim.22
  2.6 1.3 convert_add_fusion.small
  3.9 166.6 %front.1 = (bf16[1536,4608]{1,0:T(8,128)(2,1)}, bf16[2304,1536]{1,0:T(8,128)(2,1)}, bf16[1024,1536]{1,0:T(8,128)(2,1)}, bf16[1024,1536]{1,0:T(8,128)(2,1)}, bf16...) custom-call(s32[1,3]{1,0:T(1,128)} %lengths.1, ...), custom_call_target="tpu_custom_call" | custom-call | tf_op jit(solution)/shard_map/front/pallas_call | solution.py:858
  170.6 109.7 %ffn.1 = (f32[256,1536]{1,0:T(8,128)}, f32[288,1536]{1,0:T(8,128)}, bf16[3,192,4608]{2,1,0:T(8,128)(2,1)}, bf16[2,192,2304]{2,1,0:T(8,128)(2,1)}, bf16[1024,1536...) custom-call(bf16[1024,1536]{1,0:T(8,128)(2,1)} %get-tuple-element.56.normed_all, ...), custom_call_target="tpu_custom_call" | custom-call | tf_op jit(solution)/shard_map/ffn/pallas_call | solution.py:1205
  280.3 136.6 %back.1 = (bf16[256,1536]{1,0:T(8,128)(2,1)}, bf16[256,1536]{1,0:T(8,128)(2,1)}, f32[8,640]{1,0:T(8,128)}, f32[48,1536]{1,0:T(8,128)}, f32[48,2048]{1,0:T(8,128)}, /*index=5*/bf16[4,48,4608]{2,1,0:T(8,128)(2,1)}) custom-call(f32[256,1536]{1,0:T(8,128)} %get-tuple-element.63.columns, f32[256,1536]{1,0:T(8,128)} %get-tuple-element.64.resid, ...), custom_call_target="tpu_custom_call" | custom-call | tf_op jit(solution)/shard_map/back/pallas_call | solution.py:1540
  416.8 0.0 copy-start
  416.8 6.6 %finish.1 = (bf16[256,1536]{1,0:T(8,128)(2,1)}, bf16[256,1536]{1,0:T(8,128)(2,1)}, f32[48,1536]{1,0:T(8,128)}, f32[48,1536]{1,0:T(8,128)}, f32[48,256]{1,0:T(8,1...) custom-call(bf16[256,1536]{1,0:T(8,128)(2,1)} %get-tuple-element.82.layer, ...), custom_call_target="tpu_custom_call" | custom-call | tf_op jit(solution)/shard_map/finish/pallas_call | solution.py:1645
  423.4 0.0 copy-done
  423.4 0.6 fusion
  424.0 0.6 fusion.1
  (1 shorter events, 0.0 us)
Async XLA Ops:
  416.8 6.6 %copy-start = (f32[8,640]{1,0:T(8,128)S(1)}, f32[8,640]{1,0:T(8,128)}, u32[]{:S(2)}) copy-start(f32[8,640]{1,0:T(8,128)} %get-tuple-element.90) | copy-start | bytes 61444

commit v8 on v7

--- a/solution.py
+++ b/solution.py
@@ -265,13 +265,9 @@
 
 
 class SumChain:
-    def __init__(self, partial, rows, z_one, z_two, z_three, there, index):
+    def __init__(self, held, z_one, z_two, z_three, there, index):
         self.rank = lax.axis_index("seq")
         s = self.rank
-
-        def held(j):
-            return partial.at[ORDER.index(j) * rows : (ORDER.index(j) + 1) * rows]
-
         self.held, self.arrived = held, (z_one, z_two, z_three)
         self.up = [
             there(held(1), z_one, index, seq=s + 1),
@@ -409,13 +405,20 @@
             copy.wait_send()
 
 
+def in_order(partial, rows):
+    def held(j):
+        return partial.at[ORDER.index(j) * rows : (ORDER.index(j) + 1) * rows]
+
+    return held
+
+
 def front_kernel(
     lengths, tokens, cotangent, small, balance, inverse,
     w_query, w_key, w_value, w_out, w_gate, w_up, w_down,
     gu_all, down_all, upstream_all, normed_all, hidden, factor_gate, factor_up, qkv_out, out_out,
     queries, paired_out, slots_out, logsum, attended, resid, normed_one, gain_one, gain_two,
     slot_row, first_row, cosine, sine,
-    qkv, out_w, gate_v, up_v, gu, normed, kv, small_own, small_all, slots_all, bias,
+    q_w, kv_w, out_w, gate_v, up_v, gu, normed, kv, small_own, small_all, slots_all, bias,
     down_raw, down_own, hidden_v, gate_part, up_part,
     local, ssem, rsem, zsend, zrecv,
 ):
@@ -550,9 +553,9 @@
 
     own_block = pl.ds(pl.multiple_of(f * block, 16), block)
     pieces = [
-        here(w_query, qkv.at[own_block, pl.ds(0, width)], 5),
-        here(w_key, qkv.at[own_block, pl.ds(width, kv_width)], 6),
-        here(w_value, qkv.at[own_block, pl.ds(width + kv_width, kv_width)], 7),
+        here(w_key, kv_w.at[own_block, pl.ds(0, kv_width)], 6),
+        here(w_value, kv_w.at[own_block, pl.ds(kv_width, kv_width)], 7),
+        here(w_query, q_w.at[own_block], 5),
         here(cotangent, own_rows(upstream_all, s, rows), 8),
     ]
     load_gate = here(w_gate, gate_v, 9)
@@ -581,41 +584,31 @@
     )
     small_all[f] = small_own[...]
 
-    gather_qkv = Gather(None, qkv, block, 0)
-    gather_out = Gather(w_out, out_w, block, 8)
-    gather_gu = Gather(None, gu, block, 16)
-    gather_down = Gather(down_own, down_all, unit_pad, 24)
+    gather_kv = Gather(None, kv_w, block, 0)
+    gather_q = Gather(None, q_w, block, 8)
+    gather_out = Gather(w_out, out_w, block, 16)
+    gather_gu = Gather(None, gu, block, 24)
+    gather_down = Gather(down_own, down_all, unit_pad, 32)
     chain_up = Chain(upstream_all, 0)
     chain_normed = Chain(normed, 6)
     send_small = [
-        there(small_own, small_all.at[f], 32 + k, fsdp=plane[k]) for k in range(1, n_f)
+        there(small_own, small_all.at[f], 40 + k, fsdp=plane[k]) for k in range(1, n_f)
     ]
     send_slots = [
-        there(slots_all.at[s], slots_all.at[s], 40 + j, seq=lax.rem(s + j, n_s))
+        there(slots_all.at[s], slots_all.at[s], 48 + j, seq=lax.rem(s + j, n_s))
         for j in range(1, n_s)
     ]
     send_kv = [
-        there(kv.at[s], kv.at[s], 44 + j, seq=lax.rem(s + j, n_s)) for j in range(1, n_s)
+        there(kv.at[s], kv.at[s], 52 + j, seq=lax.rem(s + j, n_s)) for j in range(1, n_s)
     ]
-    for copy in pieces[:3]:
+    for copy in pieces[:2]:
         copy.wait()
     pl.semaphore_wait(entry, n_f - 1 + n_s - 1)
-    gather_qkv.start()
+    gather_kv.start()
     for copy in send_small + send_slots:
         copy.start()
-    pieces[3].wait()
-    chain_up.send(1)
-
-    load_gate.wait()
-    load_up.wait()
-    pick_units(gate_v, up_v, gu.at[own_block], w_gate.shape[1] // n_f, unit, unit_pad)
-    load_down.wait()
-    raw = down_raw[...].astype(jnp.float32)
-    shifted = jnp.concatenate([raw[8:], jnp.zeros((8, width), jnp.float32)], 0)
-    raw = jnp.where(lax.rem(s * unit, 16) == 0, raw, shifted)
-    inside = lax.broadcasted_iota(jnp.int32, raw.shape, 0) < unit
-    down_own[...] = jnp.where(inside, raw, 0.0).astype(jnp.bfloat16)
-
+    for copy in pieces[2:]:
+        copy.wait()
     position = slots_all[s] - jnp.broadcast_to(first, (128, rows)).T
     angle = position * inverse[...]
     cosine[...] = jnp.cos(angle)
@@ -625,6 +618,7 @@
 
     for copy in send_small + send_slots:
         copy.wait_recv()
+
     def joined(sort):
         return jnp.concatenate(
             [
@@ -643,49 +637,60 @@
     inputs = tokens[...].astype(jnp.float32)
     root = lax.rsqrt(jnp.mean(inputs * inputs, -1, keepdims=True) + epsilon)
     normed_one[...] = (inputs * root * gain_one[...]).astype(jnp.bfloat16)
+    gather_kv.forward()
+    gather_q.start()
+    gather_kv.last()
+    gather_kv.finish()
+
+    def turned(value):
+        return value * cosine[...] + pltpu.roll(value, HEAD_DIM // 2, 1) * sine[...]
+
+    rows_low = normed_one[...]
+    pair = jnp.dot(rows_low, kv_w[:, :kv_width], preferred_element_type=jnp.float32)
+    pair = pair + bias_key
+    for g in range(KV_HEADS):
+        columns = slice(g * HEAD_DIM, (g + 1) * HEAD_DIM)
+        kv[s, :, columns] = turned(pair[:, columns]).astype(jnp.bfloat16)
+    pair = jnp.dot(rows_low, kv_w[:, kv_width:], preferred_element_type=jnp.float32)
+    kv[s, :, kv_width:] = (pair + bias_value).astype(jnp.bfloat16)
+    for copy in send_kv:
+        copy.start()
+    save_kv_w = here(kv_w, qkv_out.at[:, pl.ds(width, 2 * kv_width)], 11)
+    save_kv_w.start()
+
+    load_gate.wait()
+    load_up.wait()
+    pick_units(gate_v, up_v, gu.at[own_block], w_gate.shape[1] // n_f, unit, unit_pad)
+    gather_q.forward()
+    load_down.wait()
+    raw = down_raw[...].astype(jnp.float32)
+    shifted = jnp.concatenate([raw[8:], jnp.zeros((8, width), jnp.float32)], 0)
+    raw = jnp.where(lax.rem(s * unit, 16) == 0, raw, shifted)
+    inside = lax.broadcasted_iota(jnp.int32, raw.shape, 0) < unit
+    down_own[...] = jnp.where(inside, raw, 0.0).astype(jnp.bfloat16)
+
     for j in range(n_s):
         keys_slot = slots_all[j]
         keys_slot = jnp.concatenate([keys_slot] * (rows // 128), 1)
         ok = (keys_slot <= slot) & (keys_slot >= first)
         bias[j * rows : (j + 1) * rows] = jnp.where(ok, 0.0, -1e30)
 
-    gather_qkv.forward()
-    chain_up.receive(1)
-    chain_up.send(2)
-    gather_qkv.last()
+    gather_q.last()
     gather_out.start()
-    gather_qkv.finish()
-    save_qkv = here(qkv, qkv_out, 11)
-    save_qkv.start()
-
-    def turned(value):
-        return value * cosine[...] + pltpu.roll(value, HEAD_DIM // 2, 1) * sine[...]
-
-    rows_low = normed_one[...]
-    pair = jnp.dot(rows_low, qkv[:, width : width + kv_width], preferred_element_type=jnp.float32)
-    pair = pair + bias_key
-    for g in range(KV_HEADS):
-        columns = slice(g * HEAD_DIM, (g + 1) * HEAD_DIM)
-        kv[s, :, columns] = turned(pair[:, columns]).astype(jnp.bfloat16)
-    pair = jnp.dot(rows_low, qkv[:, width + kv_width :], preferred_element_type=jnp.float32)
-    kv[s, :, kv_width:] = (pair + bias_value).astype(jnp.bfloat16)
-    for copy in send_kv:
-        copy.start()
+    gather_q.finish()
+    save_q_w = here(q_w, qkv_out.at[:, pl.ds(0, width)], 0)
+    save_q_w.start()
     for g in range(HEADS // 2):
         columns = slice(g * 2 * HEAD_DIM, (g + 1) * 2 * HEAD_DIM)
-        pair = jnp.dot(rows_low, qkv[:, columns], preferred_element_type=jnp.float32)
+        pair = jnp.dot(rows_low, q_w[:, columns], preferred_element_type=jnp.float32)
         pair = pair + bias_query[:, columns]
         for h in range(2):
             part = turned(pair[:, h * HEAD_DIM : (h + 1) * HEAD_DIM]).astype(jnp.bfloat16)
             queries[:, (2 * g + h) * HEAD_DIM : (2 * g + h + 1) * HEAD_DIM] = part
 
-    gather_out.forward()
-    gather_gu.start()
-    chain_up.receive(2)
-    gather_out.last()
     for copy in send_kv:
         copy.wait_recv()
-    chain_up.send(3)
+    chain_up.send(1)
     save_kv = here(kv, paired_out, 12)
     save_kv.start()
     slots_out[...] = slots_all[...]
@@ -717,7 +722,11 @@
             return carry
 
         lax.fori_loop(0, repeat, head, 0)
-
+        if g == 0:
+            gather_out.forward()
+
+    gather_out.last()
+    gather_gu.start()
     gather_out.finish()
     save_out = here(out_w, out_out, 13)
     save_out.start()
@@ -772,33 +781,37 @@
 
         lax.fori_loop(0, count, body, 0)
 
+    chain_normed.receive(1)
+    chain_up.receive(1)
+    chain_up.send(2)
     gather_gu.forward()
-    chain_normed.receive(1)
+    chain_up.receive(2)
     chain_normed.send(2)
+    chain_normed.receive(2)
+    chain_normed.send(3)
     gather_gu.last()
     gather_down.start()
     gather_gu.finish()
     save_gu = here(gu, gu_all, 22)
     save_gu.start()
     feed(s, 0)
-    chain_normed.receive(2)
-    chain_normed.send(3)
     feed(s ^ 1, count)
-    gather_down.forward()
-    feed(s ^ 2, 2 * count)
     chain_normed.receive(3)
+    chain_up.send(3)
     save_normed = here(normed, normed_all, 23)
     save_normed.start()
+    feed(s ^ 2, 2 * count)
+    gather_down.forward()
+    feed(s ^ 3, 3 * count)
     gather_down.last()
-    feed(s ^ 3, 3 * count)
     for t in (count - 2, count - 1):
         for copy in saves(s ^ 3, t, (t + 3 * count) % 2):
             copy.wait()
     chain_up.receive(3)
     gather_down.finish()
-    for copy in (save_qkv, save_kv, save_out, save_gu, save_normed):
+    for copy in (save_kv_w, save_q_w, save_kv, save_out, save_gu, save_normed):
         copy.wait()
-    for part in (gather_qkv, gather_out, gather_gu, gather_down, chain_up, chain_normed):
+    for part in (gather_kv, gather_q, gather_out, gather_gu, gather_down, chain_up, chain_normed):
         part.sent()
     for copy in send_small + send_slots + send_kv:
         copy.wait_send()
@@ -884,7 +897,8 @@
             shape((rows, HEAD_DIM), full),
         ],
         scratch_shapes=[
-            pltpu.VMEM((width, qkv_width), low),
+            pltpu.VMEM((width, width), low),
+            pltpu.VMEM((width, 2 * kv_width), low),
             pltpu.VMEM((width, width), low),
             pltpu.VMEM(w_gate.shape, low),
             pltpu.VMEM(w_up.shape, low),
@@ -901,8 +915,8 @@
             pltpu.VMEM((2, rows, wide), low),
             pltpu.VMEM((2, rows, wide), low),
             pltpu.SemaphoreType.DMA((24,)),
-            pltpu.SemaphoreType.DMA((48,)),
-            pltpu.SemaphoreType.DMA((48,)),
+            pltpu.SemaphoreType.DMA((56,)),
+            pltpu.SemaphoreType.DMA((56,)),
             pltpu.SemaphoreType.DMA((12,)),
             pltpu.SemaphoreType.DMA((12,)),
         ],
@@ -1032,7 +1046,7 @@
 
         lax.fori_loop(0, width // 512, body, 0)
 
-    chain = SumChain(partial, rows, z_one, z_two, z_three, there, 0)
+    chain = SumChain(in_order(partial, rows), z_one, z_two, z_three, there, 0)
     pieces = [(first, min(group, units - first)) for first in range(0, units, group)]
     forward(early, True)
     backward(early, True)
@@ -1139,7 +1153,7 @@
 
     lax.fori_loop(0, width // wide, branch_body, 0)
     chain.last(columns)
-    chain_branch = SumChain(upstream, rows, z_one, z_two, z_three, there, 22)
+    chain_branch = SumChain(in_order(upstream, rows), z_one, z_two, z_three, there, 22)
     chain_branch.one()
     down_second = [
         there(to_y.at[:, low_half], down_last.at[0], 14, fsdp=plane[4]),
@@ -1249,7 +1263,7 @@
     branch_v, z_one, z_two, z_three, working, bias, d_branch, d_attended, d_qkv, d_resid,
     keys_grad, values_grad, dkv, dkv_in,
     out_arrived, out_x, out_y, out_ended, qkv_arrived, qkv_x, qkv_y, qkv_ended,
-    out_in, qkv_in, vector_in,
+    out_one, out_two, out_three, qkv_one, qkv_two, qkv_three, vector_in,
     load, ssem, rsem,
 ):
     f = lax.axis_index("fsdp")
@@ -1322,16 +1336,20 @@
         ]
         for g in range(KV_HEADS)
     ]
-    chain = SumChain(branch_v, rows, z_one, z_two, z_three, there, 16)
+    chain = SumChain(in_order(branch_v, rows), z_one, z_two, z_three, there, 16)
     sum_out = SumPlane(out_w, block, plane, out_arrived, out_x, out_y, out_ended, there, 24)
     sum_qkv = SumPlane(qkv, block, plane, qkv_arrived, qkv_x, qkv_y, qkv_ended, there, 36)
-    out_send = [there(rows_for(out_w, f * block, j), out_in.at[j], 47 + j, **around(j)) for j in range(1, n_s)]
-    qkv_send = [there(rows_for(qkv, f * block, j), qkv_in.at[j], 51 + j, **around(j)) for j in range(1, n_s)]
+
+    def own_part(ref):
+        return lambda j: rows_for(ref, f * block, n_s - j)
+
+    chain_out = SumChain(own_part(out_w), out_one, out_two, out_three, there, 48)
+    chain_qkv = SumChain(own_part(qkv), qkv_one, qkv_two, qkv_three, there, 54)
     vector_send = [
-        there(vector_in.at[0], vector_in.at[1], 56, fsdp=plane[1]),
-        there(vector_in.at[2], vector_in.at[3], 57, fsdp=plane[2]),
-        there(vector_in.at[4], vector_in.at[5], 58, fsdp=plane[4]),
-    ] + [there(vector_in.at[6], vector_in.at[6 + j], 58 + j, **around(j)) for j in range(1, n_s)]
+        there(vector_in.at[0], vector_in.at[1], 60, fsdp=plane[1]),
+        there(vector_in.at[2], vector_in.at[3], 61, fsdp=plane[2]),
+        there(vector_in.at[4], vector_in.at[5], 62, fsdp=plane[4]),
+    ] + [there(vector_in.at[6], vector_in.at[6 + j], 62 + j, **around(j)) for j in range(1, n_s)]
 
     pl.semaphore_wait(entry, 3 + n_s - 1)
     for copy in gu_first:
@@ -1482,38 +1500,36 @@
 
     sum_qkv.start_second()
     sum_out.finish()
-    for copy in out_send:
-        copy.start()
+    chain_out.one()
     vector_send[2].wait_recv()
     vector_in[6] = vector_in[4] + vector_in[5]
     for copy in vector_send[3:]:
         copy.start()
+    chain_out.add_one()
+    chain_out.two()
+    sum_qkv.finish()
+    chain_qkv.one()
+    chain_out.three()
     chain.last(working)
     layer[...] = (resid[...] + working[...]).astype(low)
-    sum_qkv.finish()
-    for copy in qkv_send:
-        copy.start()
-
-    def gathered(own, copies, arrived, out):
-        total = own[...].astype(full)
-        for copy in copies:
-            copy.wait_recv()
-        for j in range(1, n_s):
-            total = total + arrived[j].astype(full)
-        out[...] = total
-
-    gathered(rows_for(out_w, f * block, 0), out_send, out_in, grad_out)
+    chain_qkv.add_one()
+    chain_qkv.two()
     for copy in vector_send[3:]:
         copy.wait_recv()
     vector[...] = vector_in[6] + vector_in[7] + vector_in[8] + vector_in[9]
-    gathered(rows_for(qkv, f * block, 0), qkv_send, qkv_in, grad_qkv)
+    chain_out.last(grad_out)
+    chain_qkv.three()
+    chain_qkv.last(grad_qkv)
     for copy in gu_send:
         copy.wait_recv()
     keep_rows.wait()
+    for part in (chain_out, chain_qkv):
+        part.one_sent()
+        part.sent()
     chain.sent()
     sum_out.sent()
     sum_qkv.sent()
-    for copy in gu_first + gu_second + gu_send + out_send + qkv_send + vector_send:
+    for copy in gu_first + gu_second + gu_send + vector_send:
         copy.wait_send()
     for g in range(KV_HEADS):
         for copy in dkv_send[g]:
@@ -1580,12 +1596,16 @@
             pltpu.VMEM((2, block, qkv_width // 2), low),
             pltpu.VMEM((2, block, qkv_width // 2), low),
             pltpu.VMEM((2, block, qkv_width // 2), low),
-            pltpu.VMEM((n_s, piece, width), low),
-            pltpu.VMEM((n_s, piece, qkv_width), low),
+            pltpu.VMEM((piece, width), low),
+            pltpu.VMEM((2, piece, width), low),
+            pltpu.VMEM((2, piece, width), low),
+            pltpu.VMEM((piece, qkv_width), low),
+            pltpu.VMEM((2, piece, qkv_width), low),
+            pltpu.VMEM((2, piece, qkv_width), low),
             pltpu.VMEM((10, 8, vectors), full),
             pltpu.SemaphoreType.DMA((10,)),
-            pltpu.SemaphoreType.DMA((64,)),
-            pltpu.SemaphoreType.DMA((64,)),
+            pltpu.SemaphoreType.DMA((68,)),
+            pltpu.SemaphoreType.DMA((68,)),
         ],
         compiler_params=pltpu.CompilerParams(
             collective_id=2, has_side_effects=True, vmem_limit_bytes=63 * 2**20

time: 431 us -> 427 us (level)
    pallas_call x1, Pallas kernels: 137 us -> 127 us  [back(): pl.pallas_call(back_kernel, in_specs=[hbm] + [vmem] * 15 + [hbm] * 5, out...]
    pallas_call x1, Pallas kernels: 167 us -> 175 us  [front(): pl.pallas_call(front_kernel, in_specs=[smem, vmem, hbm, vmem, vmem, vmem]...]
where the time goes in v8:
time: 427 us; the launch traced here: 422 us
  Pallas kernels  417 us (98%)
    pallas_call x1, Pallas kernels, front(): pl.pallas_call(front_kernel, in_specs=[smem, vmem, hbm, vmem, vmem, vmem]...  175 us
    pallas_call x1, Pallas kernels, back(): pl.pallas_call(back_kernel, in_specs=[hbm] + [vmem] * 15 + [hbm] * 5, out...  127 us
    pallas_call x1, Pallas kernels, ffn(): pl.pallas_call(ffn_kernel, in_specs=[hbm] * 7, out_specs=[vmem] * 2 + [hb...  108 us

profile of v8, /device:TPU:0, one launch (start us, length us, event | category | flops | bytes accessed | tf_op | source)
XLA Modules:
  0.0 422.5 jit_solution(18045221182082804851)
XLA Ops:
  0.6 0.7 broadcast_in_dim.20
  1.3 0.7 broadcast_in_dim.21
  2.0 0.7 broadcast_in_dim.22
  2.6 1.3 convert_add_fusion.small
  3.9 174.8 %front.1 = (bf16[1536,4608]{1,0:T(8,128)(2,1)}, bf16[2304,1536]{1,0:T(8,128)(2,1)}, bf16[1024,1536]{1,0:T(8,128)(2,1)}, bf16[1024,1536]{1,0:T(8,128)(2,1)}, bf16...) custom-call(s32[1,3]{1,0:T(1,128)} %lengths.1, ...), custom_call_target="tpu_custom_call" | custom-call | tf_op jit(solution)/shard_map/front/pallas_call | solution.py:871
  178.8 108.5 %ffn.1 = (f32[256,1536]{1,0:T(8,128)}, f32[288,1536]{1,0:T(8,128)}, bf16[3,192,4608]{2,1,0:T(8,128)(2,1)}, bf16[2,192,2304]{2,1,0:T(8,128)(2,1)}, bf16[1024,1536...) custom-call(bf16[1024,1536]{1,0:T(8,128)(2,1)} %get-tuple-element.56.normed_all, ...), custom_call_target="tpu_custom_call" | custom-call | tf_op jit(solution)/shard_map/ffn/pallas_call | solution.py:1219
  287.3 127.2 %back.1 = (bf16[256,1536]{1,0:T(8,128)(2,1)}, bf16[256,1536]{1,0:T(8,128)(2,1)}, f32[8,640]{1,0:T(8,128)}, f32[48,1536]{1,0:T(8,128)}, f32[48,2048]{1,0:T(8,128)}, /*index=5*/bf16[4,48,4608]{2,1,0:T(8,128)(2,1)}) custom-call(f32[256,1536]{1,0:T(8,128)} %get-tuple-element.63.columns, f32[256,1536]{1,0:T(8,128)} %get-tuple-element.64.resid, ...), custom_call_target="tpu_custom_call" | custom-call | tf_op jit(solution)/shard_map/back/pallas_call | solution.py:1556
  414.5 0.0 copy-start
  414.5 6.6 %finish.1 = (bf16[256,1536]{1,0:T(8,128)(2,1)}, bf16[256,1536]{1,0:T(8,128)(2,1)}, f32[48,1536]{1,0:T(8,128)}, f32[48,1536]{1,0:T(8,128)}, f32[48,256]{1,0:T(8,1...) custom-call(bf16[256,1536]{1,0:T(8,128)(2,1)} %get-tuple-element.82.layer, ...), custom_call_target="tpu_custom_call" | custom-call | tf_op jit(solution)/shard_map/finish/pallas_call | solution.py:1665
  421.1 0.0 copy-done
  421.1 0.6 fusion
  421.7 0.6 fusion.1
  (1 shorter events, 0.0 us)
Async XLA Ops:
  414.5 6.6 %copy-start = (f32[8,640]{1,0:T(8,128)S(1)}, f32[8,640]{1,0:T(8,128)}, u32[]{:S(2)}) copy-start(f32[8,640]{1,0:T(8,128)} %get-tuple-element.90) | copy-start | bytes 61444

commit v9 on v8

--- a/solution.py
+++ b/solution.py
@@ -419,7 +419,7 @@
     queries, paired_out, slots_out, logsum, attended, resid, normed_one, gain_one, gain_two,
     slot_row, first_row, cosine, sine,
     q_w, kv_w, out_w, gate_v, up_v, gu, normed, kv, small_own, small_all, slots_all, bias,
-    down_raw, down_own, hidden_v, gate_part, up_part,
+    cotangent_v, down_raw, down_own, hidden_v, gate_part, up_part,
     local, ssem, rsem, zsend, zrecv,
 ):
     f = lax.axis_index("fsdp")
@@ -515,19 +515,20 @@
                 copy.wait_send()
 
     class Chain:
-        def __init__(self, target, index):
+        def __init__(self, target, index, own=None):
             self.steps = []
             for step in range(1, n_s):
                 up = own_rows(target, s - (step - 1), rows)
                 down = own_rows(target, s + (step - 1), rows)
+                source = own if own is not None and step == 1 else up
                 i = index + 2 * (step - 1)
                 self.steps.append((
                     pltpu.make_async_remote_copy(
-                        src_ref=up, dst_ref=up, send_sem=zsend.at[i], recv_sem=zrecv.at[i],
+                        src_ref=source, dst_ref=up, send_sem=zsend.at[i], recv_sem=zrecv.at[i],
                         device_id={"seq": s + 1}, device_id_type=MESH,
                     ),
                     pltpu.make_async_remote_copy(
-                        src_ref=down, dst_ref=down, send_sem=zsend.at[i + 1], recv_sem=zrecv.at[i + 1],
+                        src_ref=down if source is up else source, dst_ref=down, send_sem=zsend.at[i + 1], recv_sem=zrecv.at[i + 1],
                         device_id={"seq": s - 1}, device_id_type=MESH,
                     ),
                     (s >= step - 1) & (s < n_s - 1),
@@ -556,7 +557,7 @@
         here(w_key, kv_w.at[own_block, pl.ds(0, kv_width)], 6),
         here(w_value, kv_w.at[own_block, pl.ds(kv_width, kv_width)], 7),
         here(w_query, q_w.at[own_block], 5),
-        here(cotangent, own_rows(upstream_all, s, rows), 8),
+        here(cotangent, cotangent_v, 8),
     ]
     load_gate = here(w_gate, gate_v, 9)
     load_up = here(w_up, up_v, 10)
@@ -589,7 +590,7 @@
     gather_out = Gather(w_out, out_w, block, 16)
     gather_gu = Gather(None, gu, block, 24)
     gather_down = Gather(down_own, down_all, unit_pad, 32)
-    chain_up = Chain(upstream_all, 0)
+    chain_up = Chain(upstream_all, 0, cotangent_v)
     chain_normed = Chain(normed, 6)
     send_small = [
         there(small_own, small_all.at[f], 40 + k, fsdp=plane[k]) for k in range(1, n_f)
@@ -609,6 +610,9 @@
         copy.start()
     for copy in pieces[2:]:
         copy.wait()
+    chain_up.send(1)
+    save_own = here(cotangent_v, own_rows(upstream_all, s, rows), 8)
+    save_own.start()
     position = slots_all[s] - jnp.broadcast_to(first, (128, rows)).T
     angle = position * inverse[...]
     cosine[...] = jnp.cos(angle)
@@ -688,9 +692,10 @@
             part = turned(pair[:, h * HEAD_DIM : (h + 1) * HEAD_DIM]).astype(jnp.bfloat16)
             queries[:, (2 * g + h) * HEAD_DIM : (2 * g + h + 1) * HEAD_DIM] = part
 
+    chain_up.receive(1)
     for copy in send_kv:
         copy.wait_recv()
-    chain_up.send(1)
+    chain_up.send(2)
     save_kv = here(kv, paired_out, 12)
     save_kv.start()
     slots_out[...] = slots_all[...]
@@ -781,12 +786,10 @@
 
         lax.fori_loop(0, count, body, 0)
 
+    chain_up.receive(2)
     chain_normed.receive(1)
-    chain_up.receive(1)
-    chain_up.send(2)
+    chain_normed.send(2)
     gather_gu.forward()
-    chain_up.receive(2)
-    chain_normed.send(2)
     chain_normed.receive(2)
     chain_normed.send(3)
     gather_gu.last()
@@ -794,12 +797,12 @@
     gather_gu.finish()
     save_gu = here(gu, gu_all, 22)
     save_gu.start()
-    feed(s, 0)
-    feed(s ^ 1, count)
     chain_normed.receive(3)
     chain_up.send(3)
     save_normed = here(normed, normed_all, 23)
     save_normed.start()
+    feed(s, 0)
+    feed(s ^ 1, count)
     feed(s ^ 2, 2 * count)
     gather_down.forward()
     feed(s ^ 3, 3 * count)
@@ -809,7 +812,7 @@
             copy.wait()
     chain_up.receive(3)
     gather_down.finish()
-    for copy in (save_kv_w, save_q_w, save_kv, save_out, save_gu, save_normed):
+    for copy in (save_own, save_kv_w, save_q_w, save_kv, save_out, save_gu, save_normed):
         copy.wait()
     for part in (gather_kv, gather_q, gather_out, gather_gu, gather_down, chain_up, chain_normed):
         part.sent()
@@ -909,6 +912,7 @@
             pltpu.VMEM((8, 8, 2 * block), full),
             pltpu.VMEM((n_s, rows, 128), full),
             pltpu.VMEM((group, rows), full),
+            pltpu.VMEM((rows, width), low),
             pltpu.VMEM((unit_pad, width), low),
             pltpu.VMEM((unit_pad, width), low),
             pltpu.VMEM((2, rows, wide), low),

time: 427 us -> 423 us (level)
  Pallas kernels: 417 us -> 412 us
    pallas_call x1, Pallas kernels: 175 us -> 165 us  [front(): pl.pallas_call(front_kernel, in_specs=[smem, vmem, hbm, vmem, vmem, vmem]...]
where the time goes in v9:
time: 423 us; the launch traced here: 417 us
  Pallas kernels  412 us (97%)
    pallas_call x1, Pallas kernels, front(): pl.pallas_call(front_kernel, in_specs=[smem, vmem, hbm, vmem, vmem, vmem]...  165 us
    pallas_call x1, Pallas kernels, back(): pl.pallas_call(back_kernel, in_specs=[hbm] + [vmem] * 15 + [hbm] * 5, out...  130 us
    pallas_call x1, Pallas kernels, ffn(): pl.pallas_call(ffn_kernel, in_specs=[hbm] * 7, out_specs=[vmem] * 2 + [hb...  110 us

profile of v9, /device:TPU:0, one launch (start us, length us, event | category | flops | bytes accessed | tf_op | source)
XLA Modules:
  0.0 417.1 jit_solution(12902100856645338365)
XLA Ops:
  0.6 0.7 broadcast_in_dim.20
  1.3 0.7 broadcast_in_dim.21
  2.0 0.7 broadcast_in_dim.22
  2.6 1.3 convert_add_fusion.small
  3.9 164.5 %front.1 = (bf16[1536,4608]{1,0:T(8,128)(2,1)}, bf16[2304,1536]{1,0:T(8,128)(2,1)}, bf16[1024,1536]{1,0:T(8,128)(2,1)}, bf16[1024,1536]{1,0:T(8,128)(2,1)}, bf16...) custom-call(s32[1,3]{1,0:T(1,128)} %lengths.1, ...), custom_call_target="tpu_custom_call" | custom-call | tf_op jit(solution)/shard_map/front/pallas_call | solution.py:874
  168.4 110.5 %ffn.1 = (f32[256,1536]{1,0:T(8,128)}, f32[288,1536]{1,0:T(8,128)}, bf16[3,192,4608]{2,1,0:T(8,128)(2,1)}, bf16[2,192,2304]{2,1,0:T(8,128)(2,1)}, bf16[1024,1536...) custom-call(bf16[1024,1536]{1,0:T(8,128)(2,1)} %get-tuple-element.56.normed_all, ...), custom_call_target="tpu_custom_call" | custom-call | tf_op jit(solution)/shard_map/ffn/pallas_call | solution.py:1223
  278.9 130.2 %back.1 = (bf16[256,1536]{1,0:T(8,128)(2,1)}, bf16[256,1536]{1,0:T(8,128)(2,1)}, f32[8,640]{1,0:T(8,128)}, f32[48,1536]{1,0:T(8,128)}, f32[48,2048]{1,0:T(8,128)}, /*index=5*/bf16[4,48,4608]{2,1,0:T(8,128)(2,1)}) custom-call(f32[256,1536]{1,0:T(8,128)} %get-tuple-element.63.columns, f32[256,1536]{1,0:T(8,128)} %get-tuple-element.64.resid, ...), custom_call_target="tpu_custom_call" | custom-call | tf_op jit(solution)/shard_map/back/pallas_call | solution.py:1560
  409.1 0.0 copy-start
  409.1 6.6 %finish.1 = (bf16[256,1536]{1,0:T(8,128)(2,1)}, bf16[256,1536]{1,0:T(8,128)(2,1)}, f32[48,1536]{1,0:T(8,128)}, f32[48,1536]{1,0:T(8,128)}, f32[48,256]{1,0:T(8,1...) custom-call(bf16[256,1536]{1,0:T(8,128)(2,1)} %get-tuple-element.82.layer, ...), custom_call_target="tpu_custom_call" | custom-call | tf_op jit(solution)/shard_map/finish/pallas_call | solution.py:1669
  415.7 0.0 copy-done
  415.7 0.6 fusion
  416.3 0.6 fusion.1
  (1 shorter events, 0.0 us)
Async XLA Ops:
  409.1 6.6 %copy-start = (f32[8,640]{1,0:T(8,128)S(1)}, f32[8,640]{1,0:T(8,128)}, u32[]{:S(2)}) copy-start(f32[8,640]{1,0:T(8,128)} %get-tuple-element.90) | copy-start | bytes 61444

commit v10 on v9

--- a/solution.py
+++ b/solution.py
@@ -304,7 +304,7 @@
         pl.when(self.rank <= 1)(self.up[1].start)
         pl.when(self.rank >= 2)(self.down[1].start)
 
-    def three(self):
+    def add_two(self):
         @pl.when((self.rank == 1) | (self.rank == 2))
         def _():
             self.up[1].wait_recv()
@@ -312,6 +312,7 @@
             self.down[1].wait_recv()
             self.add(1, self.arrived[1].at[1])
 
+    def three(self):
         pl.when(self.rank <= 2)(self.up[2].start)
         pl.when(self.rank >= 1)(self.down[2].start)
 
@@ -332,9 +333,11 @@
         pl.when(self.rank == 0)(self.up[0].wait_send)
         pl.when(self.rank == 3)(self.down[0].wait_send)
 
-    def sent(self):
+    def two_sent(self):
         pl.when(self.rank <= 1)(self.up[1].wait_send)
         pl.when(self.rank >= 2)(self.down[1].wait_send)
+
+    def three_sent(self):
         pl.when(self.rank <= 2)(self.up[2].wait_send)
         pl.when(self.rank >= 1)(self.down[2].wait_send)
 
@@ -666,6 +669,7 @@
     load_up.wait()
     pick_units(gate_v, up_v, gu.at[own_block], w_gate.shape[1] // n_f, unit, unit_pad)
     gather_q.forward()
+    gather_out.start()
     load_down.wait()
     raw = down_raw[...].astype(jnp.float32)
     shifted = jnp.concatenate([raw[8:], jnp.zeros((8, width), jnp.float32)], 0)
@@ -680,7 +684,6 @@
         bias[j * rows : (j + 1) * rows] = jnp.where(ok, 0.0, -1e30)
 
     gather_q.last()
-    gather_out.start()
     gather_q.finish()
     save_q_w = here(q_w, qkv_out.at[:, pl.ds(0, width)], 0)
     save_q_w.start()
@@ -692,6 +695,7 @@
             part = turned(pair[:, h * HEAD_DIM : (h + 1) * HEAD_DIM]).astype(jnp.bfloat16)
             queries[:, (2 * g + h) * HEAD_DIM : (2 * g + h + 1) * HEAD_DIM] = part
 
+    gather_out.forward()
     chain_up.receive(1)
     for copy in send_kv:
         copy.wait_recv()
@@ -728,10 +732,9 @@
 
         lax.fori_loop(0, repeat, head, 0)
         if g == 0:
-            gather_out.forward()
-
-    gather_out.last()
-    gather_gu.start()
+            gather_out.last()
+            gather_gu.start()
+
     gather_out.finish()
     save_out = here(out_w, out_out, 13)
     save_out.start()
@@ -936,7 +939,7 @@
 
 def ffn_kernel(
     normed_all, upstream_all, w_gu, w_down, hidden_all, factor_gate, factor_up,
-    columns, grad_down, gu_sum, gu_far, branch, down_arrived, gu_arrived,
+    columns, grad_down, gu_sum, branch, down_arrived, gu_arrived,
     normed, upstream, gu, down, hidden, d_both, partial, z_one, z_two, z_three,
     down_x, down_y, down_last, down_piece,
     load, ssem, rsem,
@@ -1120,8 +1123,10 @@
     ]
     for copy in down_first:
         copy.start()
+    lax.fori_loop(2, width // tile - 1, gu_body, 0)
+    chain.add_two()
     chain.three()
-    lax.fori_loop(2, width // tile, gu_body, 0)
+    lax.fori_loop(width // tile - 1, width // tile, gu_body, 0)
     gu_core = [
         there(part(gu, plane[2 * i + 1], block), gu_arrived.at[i], 16 + i, fsdp=plane[1])
         for i in range(4)
@@ -1132,7 +1137,7 @@
     again = [
         here(
             w_down.at[first : first + count],
-            d_both.at[:count, i * width : (i + 1) * width], 32 + i,
+            d_both.at[:count, i * width : (i + 1) * width], 33 + i,
         )
         for i, (first, count) in enumerate(pieces)
     ]
@@ -1173,19 +1178,10 @@
         (pl.ds(0, units), hidden.at[:block]),
         (pl.ds(units, units), hidden.at[block : 2 * block]),
     ]
-    add_arrived(3, gu, block, gu_arrived, gu_pieces, gu_core, 27)
-    far = part(gu, plane[6], block)
-    gu_first = [
-        there(far.at[:, pl.ds(0, units)], gu_far.at[0], 20, fsdp=plane[2]),
-        there(far.at[:, pl.ds(units, units)], gu_far.at[1], 21, fsdp=plane[4]),
-    ]
-    for copy in gu_first:
-        copy.start()
-    for i in (1, 2, 0):
+    store = [here(part(gu, plane[2 * i], block), gu_sum.at[i], 29 + i) for i in range(4)]
+    for i in (3, 1, 2, 0):
         add_arrived(i, gu, block, gu_arrived, gu_pieces, gu_core, 27)
-    store = [here(part(gu, plane[2 * i], block), gu_sum.at[i], 29 + i) for i in range(3)]
-    for copy in store:
-        copy.start()
+        store[i].start()
     down_first[0].wait_recv()
     down_first[2].wait_recv()
     own = part(down, f, unit)
@@ -1199,14 +1195,13 @@
     )
     chain_branch.add_one()
     chain_branch.one_sent()
-    store_branch = here(upstream, branch, 35)
+    store_branch = here(upstream, branch, 36)
     store_branch.start()
     chain.one_sent()
-    chain.sent()
-    for copy in down_core + down_first + down_second + gu_core + gu_first:
+    chain.two_sent()
+    chain.three_sent()
+    for copy in down_core + down_first + down_second + gu_core:
         copy.wait_send()
-    for copy in gu_first:
-        copy.wait_recv()
     for copy in store + [store_branch]:
         copy.wait()
 
@@ -1223,12 +1218,11 @@
     return pl.pallas_call(
         ffn_kernel,
         in_specs=[hbm] * 7,
-        out_specs=[vmem] * 2 + [hbm] * 5,
+        out_specs=[vmem] * 2 + [hbm] * 4,
         out_shape=[
             shape((rows, width), full),
             shape((unit, width), full),
-            shape((3, block, 2 * units), low),
-            shape((2, block, units), low),
+            shape((4, block, 2 * units), low),
             shape((group, width), low),
             shape((4, unit, width), low),
             shape((4, block, 2 * units), low),
@@ -1248,7 +1242,7 @@
             pltpu.VMEM((2, unit, half), low),
             pltpu.VMEM((2, unit, half), low),
             pltpu.VMEM((unit, width), low),
-            pltpu.SemaphoreType.DMA((36,)),
+            pltpu.SemaphoreType.DMA((40,)),
             pltpu.SemaphoreType.DMA((28,)),
             pltpu.SemaphoreType.DMA((28,)),
         ],
@@ -1256,12 +1250,12 @@
             collective_id=1, has_side_effects=True, vmem_limit_bytes=63 * 2**20
         ),
         name="ffn",
-    )(normed_all, upstream_all, w_gu, w_down, hidden, factor_gate, factor_up)[:5]
+    )(normed_all, upstream_all, w_gu, w_down, hidden, factor_gate, factor_up)[:4]
 
 
 def back_kernel(
     columns, resid, gain_two, cotangent, attended, queries, paired, slots, slot_row, first_row,
-    logsum, normed_one, tokens, gain_one, cosine, sine, w_out, w_qkv, gu_sum, gu_far, branch,
+    logsum, normed_one, tokens, gain_one, cosine, sine, w_out, w_qkv, gu_sum, branch,
     layer, input_rows, vector, grad_out, grad_qkv, gu_rows,
     out_w, qkv, gu_own, gu_to_y, gu_to_x, gu_x, gu_y, gu_ended,
     branch_v, z_one, z_two, z_three, working, bias, d_branch, d_attended, d_qkv, d_resid,
@@ -1308,8 +1302,6 @@
         here(gu_sum.at[0], gu_own, 2),
         here(gu_sum.at[2, :, low_units], gu_to_y, 3),
         here(gu_sum.at[1, :, high_units], gu_to_x, 4),
-        here(gu_far.at[0], gu_x.at[1], 8),
-        here(gu_far.at[1], gu_y.at[1], 9),
     ]
     load_qkv = here(w_qkv, qkv, 5)
     load_columns = here(columns, working, 7)
@@ -1317,6 +1309,8 @@
         copy.start()
 
     gu_first = [
+        there(gu_sum.at[3, :, low_units], gu_x.at[1], 0, fsdp=plane[2]),
+        there(gu_sum.at[3, :, high_units], gu_y.at[1], 1, fsdp=plane[4]),
         there(gu_sum.at[1, :, low_units], gu_x.at[0], 2, fsdp=plane[2]),
         there(gu_sum.at[2, :, high_units], gu_y.at[0], 3, fsdp=plane[4]),
     ]
@@ -1360,12 +1354,6 @@
         copy.start()
     load_branch.wait()
     chain.two()
-    for copy in load_gu:
-        copy.wait()
-    gu_to_y[...] = (gu_to_y[...].astype(full) + gu_x[1].astype(full)).astype(low)
-    gu_second[0].start()
-    gu_to_x[...] = (gu_to_x[...].astype(full) + gu_y[1].astype(full)).astype(low)
-    gu_second[1].start()
 
     def norm_back(value, gain, grad):
         root = lax.rsqrt(jnp.mean(value * value, -1, keepdims=True) + epsilon)
@@ -1454,6 +1442,14 @@
         n_columns = slice(n * tile, (n + 1) * tile)
         value = jnp.dot(normed_turned, d_qkv[:, n_columns], preferred_element_type=full)
         qkv[:, n_columns] = value.astype(low)
+    for copy in load_gu:
+        copy.wait()
+    gu_first[0].wait_recv()
+    gu_to_y[...] = (gu_to_y[...].astype(full) + gu_x[1].astype(full)).astype(low)
+    gu_second[0].start()
+    gu_first[1].wait_recv()
+    gu_to_x[...] = (gu_to_x[...].astype(full) + gu_y[1].astype(full)).astype(low)
+    gu_second[1].start()
     sum_out.start_first()
 
     for g in range(KV_HEADS):
@@ -1470,6 +1466,7 @@
     value = jnp.dot(normed_turned, d_qkv[:, width:], preferred_element_type=full)
     qkv[:, width:] = value.astype(low)
     sum_qkv.start_core()
+    chain.add_two()
     chain.three()
 
     d_norm, gain_one_grad = norm_back(tokens[...].astype(full), gain_one[...], working[...])
@@ -1485,11 +1482,11 @@
     vector_in[2] = vector_in[0] + vector_in[1]
     vector_send[1].start()
 
-    gu_first[0].wait_recv()
+    gu_first[2].wait_recv()
     gu_second[0].wait_recv()
     total = gu_own[:, :units].astype(full) + gu_x[0].astype(full) + gu_ended[0].astype(full)
     gu_own[:, :units] = total.astype(low)
-    gu_first[1].wait_recv()
+    gu_first[3].wait_recv()
     gu_second[1].wait_recv()
     total = gu_own[:, units:].astype(full) + gu_y[0].astype(full) + gu_ended[1].astype(full)
     gu_own[:, units:] = total.astype(low)
@@ -1513,6 +1510,7 @@
     chain_out.two()
     sum_qkv.finish()
     chain_qkv.one()
+    chain_out.add_two()
     chain_out.three()
     chain.last(working)
     layer[...] = (resid[...] + working[...]).astype(low)
@@ -1522,6 +1520,7 @@
         copy.wait_recv()
     vector[...] = vector_in[6] + vector_in[7] + vector_in[8] + vector_in[9]
     chain_out.last(grad_out)
+    chain_qkv.add_two()
     chain_qkv.three()
     chain_qkv.last(grad_qkv)
     for copy in gu_send:
@@ -1529,8 +1528,10 @@
     keep_rows.wait()
     for part in (chain_out, chain_qkv):
         part.one_sent()
-        part.sent()
-    chain.sent()
+        part.two_sent()
+        part.three_sent()
+    chain.two_sent()
+    chain.three_sent()
     sum_out.sent()
     sum_qkv.sent()
     for copy in gu_first + gu_second + gu_send + vector_send:
@@ -1542,7 +1543,7 @@
 
 def back(
     columns, resid, gain_two, cotangent, attended, queries, paired, slots, slot_row, first_row,
-    logsum, normed_one, tokens, gain_one, cosine, sine, w_out, w_qkv, gu_sum, gu_far, branch,
+    logsum, normed_one, tokens, gain_one, cosine, sine, w_out, w_qkv, gu_sum, branch,
 ):
     rows, width = tokens.shape
     n_s = paired.shape[0]
@@ -1559,7 +1560,7 @@
     vectors = (2 * width + qkv_width) // 8
     return pl.pallas_call(
         back_kernel,
-        in_specs=[hbm] + [vmem] * 15 + [hbm] * 5,
+        in_specs=[hbm] + [vmem] * 15 + [hbm] * 4,
         out_specs=[vmem] * 5 + [hbm],
         out_shape=[
             shape((rows, width), low),
@@ -1617,7 +1618,7 @@
         name="back",
     )(
         columns, resid, gain_two, cotangent, attended, queries, paired, slots, slot_row, first_row,
-        logsum, normed_one, tokens, gain_one, cosine, sine, w_out, w_qkv, gu_sum, gu_far, branch,
+        logsum, normed_one, tokens, gain_one, cosine, sine, w_out, w_qkv, gu_sum, branch,
     )
 
 
@@ -1706,13 +1707,12 @@
         tokens, cotangent, lengths, balance, (norm1_gain, norm2_gain, b_query, b_key, b_value),
         (w_query, w_key, w_value, w_out, w_gate, w_up, w_down),
     )
-    columns, grad_down, gu_sum, gu_far, branch = ffn(
+    columns, grad_down, gu_sum, branch = ffn(
         normed_all, upstream_all, weight_gu, weight_down, hidden, factor_gate, factor_up
     )
     layer, input_rows, vectors, grad_out, grad_qkv, gu_rows = back(
         columns, resid, gain_two, cotangent, attended, queries, paired, slots, slot_row, first_row,
-        logsum, normed_one, tokens, gain_one, cosine, sine, weight_out, weight_qkv, gu_sum, gu_far,
-        branch,
+        logsum, normed_one, tokens, gain_one, cosine, sine, weight_out, weight_qkv, gu_sum, branch,
     )
     (
         layer_out, input_grad, grad_out, grad_query, grad_key, grad_value, grad_down, grad_gate,

time: 423 us -> 419 us (level)
    pallas_call x1, Pallas kernels: 130 us -> 137 us  [back(): pl.pallas_call(back_kernel, in_specs=[hbm] + [vmem] * 15 + [hbm] * 4, out...]
    pallas_call x1, Pallas kernels: 165 us -> 159 us  [front(): pl.pallas_call(front_kernel, in_specs=[smem, vmem, hbm, vmem, vmem, vmem]...]
    pallas_call x1, Pallas kernels: 110 us -> 105 us  [ffn(): pl.pallas_call(ffn_kernel, in_specs=[hbm] * 7, out_specs=[vmem] * 2 + [hb...]
where the time goes in v10:
time: 419 us; the launch traced here: 413 us
  Pallas kernels  408 us (97%)
    pallas_call x1, Pallas kernels, front(): pl.pallas_call(front_kernel, in_specs=[smem, vmem, hbm, vmem, vmem, vmem]...  159 us
    pallas_call x1, Pallas kernels, back(): pl.pallas_call(back_kernel, in_specs=[hbm] + [vmem] * 15 + [hbm] * 4, out...  137 us
    pallas_call x1, Pallas kernels, ffn(): pl.pallas_call(ffn_kernel, in_specs=[hbm] * 7, out_specs=[vmem] * 2 + [hb...  105 us

profile of v10, /device:TPU:0, one launch (start us, length us, event | category | flops | bytes accessed | tf_op | source)
XLA Modules:
  0.0 413.3 jit_solution(7159669672224422221)
XLA Ops:
  0.6 0.7 broadcast_in_dim.20
  1.3 0.7 broadcast_in_dim.21
  2.0 0.7 broadcast_in_dim.22
  2.6 1.3 convert_add_fusion.small
  3.9 158.5 %front.1 = (bf16[1536,4608]{1,0:T(8,128)(2,1)}, bf16[2304,1536]{1,0:T(8,128)(2,1)}, bf16[1024,1536]{1,0:T(8,128)(2,1)}, bf16[1024,1536]{1,0:T(8,128)(2,1)}, bf16...) custom-call(s32[1,3]{1,0:T(1,128)} %lengths.1, ...), custom_call_target="tpu_custom_call" | custom-call | tf_op jit(solution)/shard_map/front/pallas_call | solution.py:877
  162.5 105.5 %ffn.1 = (f32[256,1536]{1,0:T(8,128)}, f32[288,1536]{1,0:T(8,128)}, bf16[4,192,4608]{2,1,0:T(8,128)(2,1)}, bf16[1024,1536]{1,0:T(8,128)(2,1)}, bf16[4,288,1536]{...) custom-call(bf16[1024,1536]{1,0:T(8,128)(2,1)} %get-tuple-element.55.normed_all, ...), custom_call_target="tpu_custom_call" | custom-call | tf_op jit(solution)/shard_map/ffn/pallas_call | solution.py:1218
  267.9 137.4 %back.1 = (bf16[256,1536]{1,0:T(8,128)(2,1)}, bf16[256,1536]{1,0:T(8,128)(2,1)}, f32[8,640]{1,0:T(8,128)}, f32[48,1536]{1,0:T(8,128)}, f32[48,2048]{1,0:T(8,128)}, /*index=5*/bf16[4,48,4608]{2,1,0:T(8,128)(2,1)}) custom-call(f32[256,1536]{1,0:T(8,128)} %get-tuple-element.62.columns, f32[256,1536]{1,0:T(8,128)} %get-tuple-element.63.resid, ...), custom_call_target="tpu_custom_call" | custom-call | tf_op jit(solution)/shard_map/back/pallas_call | solution.py:1561
  405.3 0.0 copy-start
  405.3 6.6 %finish.1 = (bf16[256,1536]{1,0:T(8,128)(2,1)}, bf16[256,1536]{1,0:T(8,128)(2,1)}, f32[48,1536]{1,0:T(8,128)}, f32[48,1536]{1,0:T(8,128)}, f32[48,256]{1,0:T(8,1...) custom-call(bf16[256,1536]{1,0:T(8,128)(2,1)} %get-tuple-element.80.layer, ...), custom_call_target="tpu_custom_call" | custom-call | tf_op jit(solution)/shard_map/finish/pallas_call | solution.py:1670
  411.9 0.0 copy-done
  411.9 0.6 fusion
  412.5 0.6 fusion.1
  (1 shorter events, 0.0 us)
Async XLA Ops:
  405.3 6.6 %copy-start = (f32[8,640]{1,0:T(8,128)S(1)}, f32[8,640]{1,0:T(8,128)}, u32[]{:S(2)}) copy-start(f32[8,640]{1,0:T(8,128)} %get-tuple-element.88) | copy-start | bytes 61444

commit v11 on v10

--- a/solution.py
+++ b/solution.py
@@ -282,8 +282,7 @@
 
     def add(self, j, arrived):
         ref = self.held(j)
-        total = ref[...].astype(jnp.float32) + arrived[...].astype(jnp.float32)
-        ref[...] = total.astype(jnp.bfloat16)
+        ref[...] = ref[...] + arrived[...]
 
     def one(self):
         pl.when(self.rank == 0)(self.up[0].start)
@@ -304,7 +303,7 @@
         pl.when(self.rank <= 1)(self.up[1].start)
         pl.when(self.rank >= 2)(self.down[1].start)
 
-    def add_two(self):
+    def three(self):
         @pl.when((self.rank == 1) | (self.rank == 2))
         def _():
             self.up[1].wait_recv()
@@ -312,7 +311,6 @@
             self.down[1].wait_recv()
             self.add(1, self.arrived[1].at[1])
 
-    def three(self):
         pl.when(self.rank <= 2)(self.up[2].start)
         pl.when(self.rank >= 1)(self.down[2].start)
 
@@ -333,11 +331,9 @@
         pl.when(self.rank == 0)(self.up[0].wait_send)
         pl.when(self.rank == 3)(self.down[0].wait_send)
 
-    def two_sent(self):
+    def sent(self):
         pl.when(self.rank <= 1)(self.up[1].wait_send)
         pl.when(self.rank >= 2)(self.down[1].wait_send)
-
-    def three_sent(self):
         pl.when(self.rank <= 2)(self.up[2].wait_send)
         pl.when(self.rank >= 1)(self.down[2].wait_send)
 
@@ -374,8 +370,7 @@
         for i in (3, 1, 2, 0):
             self.core[i].wait_recv()
             part = self.parts[i]
-            total = part[...].astype(jnp.float32) + self.arrived[i].astype(jnp.float32)
-            part[...] = total.astype(jnp.bfloat16)
+            part[...] = part[...] + self.arrived[i]
         for copy in self.first:
             copy.start()
 
@@ -383,12 +378,10 @@
         half = self.half
         _, to_x, to_y, _ = self.parts
         self.first[0].wait_recv()
-        total = to_y[:, :half].astype(jnp.float32) + self.by_x[1].astype(jnp.float32)
-        to_y[:, :half] = total.astype(jnp.bfloat16)
+        to_y[:, :half] = to_y[:, :half] + self.by_x[1]
         self.second[0].start()
         self.first[1].wait_recv()
-        total = to_x[:, half:].astype(jnp.float32) + self.by_y[1].astype(jnp.float32)
-        to_x[:, half:] = total.astype(jnp.bfloat16)
+        to_x[:, half:] = to_x[:, half:] + self.by_y[1]
         self.second[1].start()
 
     def finish(self):
@@ -1082,8 +1075,8 @@
         there(part(down, plane[2 * i + 1], unit), down_arrived.at[i], 6 + i, fsdp=plane[1])
         for i in range(4)
     ]
-    for copy in down_core:
-        copy.start()
+    for i in (3, 1, 2, 0):
+        down_core[i].start()
 
     def gu_body(m, carry):
         in_columns = pl.ds(pl.multiple_of(m * tile, tile), tile)
@@ -1095,24 +1088,34 @@
 
     lax.fori_loop(0, 2, gu_body, 0)
 
-    def add_arrived(i, ref, size, arrived, pieces, copies, index):
-        copies[i].wait_recv()
-        fetch = [
-            here(arrived.at[i, :, columns], piece, index + k)
-            for k, (columns, piece) in enumerate(pieces)
-        ]
-        for copy in fetch:
-            copy.start()
-        target = part(ref, plane[2 * i], size)
-        for copy, (columns, piece) in zip(fetch, pieces):
-            copy.wait()
-            target[:, columns] = (
-                target[:, columns].astype(full) + piece[...].astype(full)
-            ).astype(jnp.bfloat16)
-
-    down_pieces = [(pl.ds(0, width), down_piece)]
-    for i in (3, 1, 2, 0):
-        add_arrived(i, down, unit, down_arrived, down_pieces, down_core, 26)
+    class Arrivals:
+        def __init__(self, ref, size, arrived, copies, turns, index):
+            self.ref, self.size, self.copies = ref, size, copies
+            self.pieces = {}
+            for n, i in enumerate((3, 1, 2, 0)):
+                self.pieces[i] = [
+                    (here(arrived.at[i, :, columns], piece, index + 3 * (n % 2) + k), columns, piece)
+                    for k, (columns, piece) in enumerate(turns[n % 2])
+                ]
+
+        def fetch(self, i):
+            self.copies[i].wait_recv()
+            for copy, _, _ in self.pieces[i]:
+                copy.start()
+
+        def add(self, i):
+            target = part(self.ref, plane[2 * i], self.size)
+            for copy, columns, piece in self.pieces[i]:
+                copy.wait()
+                target[:, columns] = target[:, columns] + piece[...]
+
+    down_turns = [[(pl.ds(0, width), piece)] for piece in (down_piece.at[0], down_piece.at[1])]
+    down_sum = Arrivals(down, unit, down_arrived, down_core, down_turns, 26)
+    down_sum.fetch(3)
+    for i, following in ((3, 1), (1, 2), (2, 0), (0, None)):
+        if following is not None:
+            down_sum.fetch(following)
+        down_sum.add(i)
     to_x, to_y, to_both = [part(down, plane[k], unit) for k in (2, 4, 6)]
     low_half, high_half = pl.ds(0, half), pl.ds(half, half)
     down_first = [
@@ -1123,21 +1126,19 @@
     ]
     for copy in down_first:
         copy.start()
-    lax.fori_loop(2, width // tile - 1, gu_body, 0)
-    chain.add_two()
     chain.three()
-    lax.fori_loop(width // tile - 1, width // tile, gu_body, 0)
+    lax.fori_loop(2, width // tile, gu_body, 0)
     gu_core = [
         there(part(gu, plane[2 * i + 1], block), gu_arrived.at[i], 16 + i, fsdp=plane[1])
         for i in range(4)
     ]
-    for copy in gu_core:
-        copy.start()
+    for i in (3, 1, 2, 0):
+        gu_core[i].start()
 
     again = [
         here(
             w_down.at[first : first + count],
-            d_both.at[:count, i * width : (i + 1) * width], 33 + i,
+            d_both.at[:count, i * width : (i + 1) * width], 36 + i,
         )
         for i, (first, count) in enumerate(pieces)
     ]
@@ -1169,18 +1170,22 @@
         there(to_x.at[:, high_half], down_last.at[1], 15, fsdp=plane[2]),
     ]
     down_first[1].wait_recv()
-    to_y[:, :half] = (to_y[:, :half].astype(full) + down_x[1].astype(full)).astype(jnp.bfloat16)
+    to_y[:, :half] = to_y[:, :half] + down_x[1]
     down_second[0].start()
     down_first[3].wait_recv()
-    to_x[:, half:] = (to_x[:, half:].astype(full) + down_y[1].astype(full)).astype(jnp.bfloat16)
+    to_x[:, half:] = to_x[:, half:] + down_y[1]
     down_second[1].start()
-    gu_pieces = [
-        (pl.ds(0, units), hidden.at[:block]),
-        (pl.ds(units, units), hidden.at[block : 2 * block]),
+    gu_turns = [
+        [(pl.ds(k * units, units), hidden.at[(2 * n + k) * block : (2 * n + k + 1) * block]) for k in range(2)]
+        for n in range(2)
     ]
-    store = [here(part(gu, plane[2 * i], block), gu_sum.at[i], 29 + i) for i in range(4)]
-    for i in (3, 1, 2, 0):
-        add_arrived(i, gu, block, gu_arrived, gu_pieces, gu_core, 27)
+    gu_arrivals = Arrivals(gu, block, gu_arrived, gu_core, gu_turns, 26)
+    store = [here(part(gu, plane[2 * i], block), gu_sum.at[i], 32 + i) for i in range(4)]
+    gu_arrivals.fetch(3)
+    for i, following in ((3, 1), (1, 2), (2, 0), (0, None)):
+        if following is not None:
+            gu_arrivals.fetch(following)
+        gu_arrivals.add(i)
         store[i].start()
     down_first[0].wait_recv()
     down_first[2].wait_recv()
@@ -1195,11 +1200,10 @@
     )
     chain_branch.add_one()
     chain_branch.one_sent()
-    store_branch = here(upstream, branch, 36)
+    store_branch = here(upstream, branch, 39)
     store_branch.start()
     chain.one_sent()
-    chain.two_sent()
-    chain.three_sent()
+    chain.sent()
     for copy in down_core + down_first + down_second + gu_core:
         copy.wait_send()
     for copy in store + [store_branch]:
@@ -1241,7 +1245,7 @@
             pltpu.VMEM((2, unit, half), low),
             pltpu.VMEM((2, unit, half), low),
             pltpu.VMEM((2, unit, half), low),
-            pltpu.VMEM((unit, width), low),
+            pltpu.VMEM((2, unit, width), low),
             pltpu.SemaphoreType.DMA((40,)),
             pltpu.SemaphoreType.DMA((28,)),
             pltpu.SemaphoreType.DMA((28,)),
@@ -1445,10 +1449,10 @@
     for copy in load_gu:
         copy.wait()
     gu_first[0].wait_recv()
-    gu_to_y[...] = (gu_to_y[...].astype(full) + gu_x[1].astype(full)).astype(low)
+    gu_to_y[...] = gu_to_y[...] + gu_x[1]
     gu_second[0].start()
     gu_first[1].wait_recv()
-    gu_to_x[...] = (gu_to_x[...].astype(full) + gu_y[1].astype(full)).astype(low)
+    gu_to_x[...] = gu_to_x[...] + gu_y[1]
     gu_second[1].start()
     sum_out.start_first()
 
@@ -1466,7 +1470,6 @@
     value = jnp.dot(normed_turned, d_qkv[:, width:], preferred_element_type=full)
     qkv[:, width:] = value.astype(low)
     sum_qkv.start_core()
-    chain.add_two()
     chain.three()
 
     d_norm, gain_one_grad = norm_back(tokens[...].astype(full), gain_one[...], working[...])
@@ -1510,7 +1513,6 @@
     chain_out.two()
     sum_qkv.finish()
     chain_qkv.one()
-    chain_out.add_two()
     chain_out.three()
     chain.last(working)
     layer[...] = (resid[...] + working[...]).astype(low)
@@ -1520,7 +1522,6 @@
         copy.wait_recv()
     vector[...] = vector_in[6] + vector_in[7] + vector_in[8] + vector_in[9]
     chain_out.last(grad_out)
-    chain_qkv.add_two()
     chain_qkv.three()
     chain_qkv.last(grad_qkv)
     for copy in gu_send:
@@ -1528,10 +1529,8 @@
     keep_rows.wait()
     for part in (chain_out, chain_qkv):
         part.one_sent()
-        part.two_sent()
-        part.three_sent()
-    chain.two_sent()
-    chain.three_sent()
+        part.sent()
+    chain.sent()
     sum_out.sent()
     sum_qkv.sent()
     for copy in gu_first + gu_second + gu_send + vector_send:

time: 419 us -> 404 us (0.964)
  Pallas kernels: 408 us -> 394 us
    pallas_call x1, Pallas kernels: 105 us -> 97 us  [ffn(): pl.pallas_call(ffn_kernel, in_specs=[hbm] * 7, out_specs=[vmem] * 2 + [hb...]
    pallas_call x1, Pallas kernels: 137 us -> 132 us  [back(): pl.pallas_call(back_kernel, in_specs=[hbm] + [vmem] * 15 + [hbm] * 4, out...]
where the time goes in v11:
time: 404 us; the launch traced here: 399 us
  Pallas kernels  394 us (98%)
    pallas_call x1, Pallas kernels, front(): pl.pallas_call(front_kernel, in_specs=[smem, vmem, hbm, vmem, vmem, vmem]...  159 us
    pallas_call x1, Pallas kernels, back(): pl.pallas_call(back_kernel, in_specs=[hbm] + [vmem] * 15 + [hbm] * 4, out...  132 us
    pallas_call x1, Pallas kernels, ffn(): pl.pallas_call(ffn_kernel, in_specs=[hbm] * 7, out_specs=[vmem] * 2 + [hb...  97 us

profile of v11, /device:TPU:0, one launch (start us, length us, event | category | flops | bytes accessed | tf_op | source)
XLA Modules:
  0.0 399.0 jit_solution(17917655904906739309)
XLA Ops:
  0.6 0.7 broadcast_in_dim.20
  1.3 0.7 broadcast_in_dim.21
  2.0 0.7 broadcast_in_dim.22
  2.6 1.3 convert_add_fusion.small
  3.9 158.5 %front.1 = (bf16[1536,4608]{1,0:T(8,128)(2,1)}, bf16[2304,1536]{1,0:T(8,128)(2,1)}, bf16[1024,1536]{1,0:T(8,128)(2,1)}, bf16[1024,1536]{1,0:T(8,128)(2,1)}, bf16...) custom-call(s32[1,3]{1,0:T(1,128)} %lengths.1, ...), custom_call_target="tpu_custom_call" | custom-call | tf_op jit(solution)/shard_map/front/pallas_call | solution.py:870
  162.4 97.0 %ffn.1 = (f32[256,1536]{1,0:T(8,128)}, f32[288,1536]{1,0:T(8,128)}, bf16[4,192,4608]{2,1,0:T(8,128)(2,1)}, bf16[1024,1536]{1,0:T(8,128)(2,1)}, bf16[4,288,1536]{...) custom-call(bf16[1024,1536]{1,0:T(8,128)(2,1)} %get-tuple-element.55.normed_all, ...), custom_call_target="tpu_custom_call" | custom-call | tf_op jit(solution)/shard_map/ffn/pallas_call | solution.py:1222
  259.4 131.6 %back.1 = (bf16[256,1536]{1,0:T(8,128)(2,1)}, bf16[256,1536]{1,0:T(8,128)(2,1)}, f32[8,640]{1,0:T(8,128)}, f32[48,1536]{1,0:T(8,128)}, f32[48,2048]{1,0:T(8,128)}, /*index=5*/bf16[4,48,4608]{2,1,0:T(8,128)(2,1)}) custom-call(f32[256,1536]{1,0:T(8,128)} %get-tuple-element.62.columns, f32[256,1536]{1,0:T(8,128)} %get-tuple-element.63.resid, ...), custom_call_target="tpu_custom_call" | custom-call | tf_op jit(solution)/shard_map/back/pallas_call | solution.py:1560
  391.0 0.0 copy-start
  391.0 6.6 %finish.1 = (bf16[256,1536]{1,0:T(8,128)(2,1)}, bf16[256,1536]{1,0:T(8,128)(2,1)}, f32[48,1536]{1,0:T(8,128)}, f32[48,1536]{1,0:T(8,128)}, f32[48,256]{1,0:T(8,1...) custom-call(bf16[256,1536]{1,0:T(8,128)(2,1)} %get-tuple-element.80.layer, ...), custom_call_target="tpu_custom_call" | custom-call | tf_op jit(solution)/shard_map/finish/pallas_call | solution.py:1669
  397.6 0.0 copy-done
  397.6 0.6 fusion
  398.2 0.6 fusion.1
  (1 shorter events, 0.0 us)
Async XLA Ops:
  391.0 6.6 %copy-start = (f32[8,640]{1,0:T(8,128)S(1)}, f32[8,640]{1,0:T(8,128)}, u32[]{:S(2)}) copy-start(f32[8,640]{1,0:T(8,128)} %get-tuple-element.88) | copy-start | bytes 61444

commit v12 on v11

--- a/solution.py
+++ b/solution.py
@@ -793,12 +793,12 @@
     gather_gu.finish()
     save_gu = here(gu, gu_all, 22)
     save_gu.start()
+    feed(s, 0)
+    feed(s ^ 1, count)
     chain_normed.receive(3)
     chain_up.send(3)
     save_normed = here(normed, normed_all, 23)
     save_normed.start()
-    feed(s, 0)
-    feed(s ^ 1, count)
     feed(s ^ 2, 2 * count)
     gather_down.forward()
     feed(s ^ 3, 3 * count)
@@ -1078,6 +1078,15 @@
     for i in (3, 1, 2, 0):
         down_core[i].start()
 
+    again_in = [upstream] + [
+        d_both.at[:count, i * width : (i + 1) * width] for i, (_, count) in enumerate(pieces[1:])
+    ]
+    again = [
+        here(w_down.at[first : first + count], place, 36 + i)
+        for i, ((first, count), place) in enumerate(zip(pieces, again_in))
+    ]
+    again[0].start()
+
     def gu_body(m, carry):
         in_columns = pl.ds(pl.multiple_of(m * tile, tile), tile)
         turned = normed[:, in_columns].T
@@ -1135,14 +1144,7 @@
     for i in (3, 1, 2, 0):
         gu_core[i].start()
 
-    again = [
-        here(
-            w_down.at[first : first + count],
-            d_both.at[:count, i * width : (i + 1) * width], 36 + i,
-        )
-        for i, (first, count) in enumerate(pieces)
-    ]
-    for copy in again:
+    for copy in again[1:]:
         copy.start()
     for copy in again:
         copy.wait()
@@ -1153,17 +1155,16 @@
             mine = slice(m * half_rows, (m + 1) * half_rows)
             value = jnp.zeros((half_rows, wide), full)
             for i, (first, count) in enumerate(pieces):
-                columns_here = pl.ds(pl.multiple_of(i * width + n * wide, wide), wide)
                 value += jnp.dot(
-                    hidden[mine, first : first + count], d_both[:count, columns_here],
+                    hidden[mine, first : first + count], again_in[i][:, out_columns],
                     preferred_element_type=full,
                 )
-            upstream[mine, out_columns] = value.astype(jnp.bfloat16)
+            normed[mine, out_columns] = value.astype(jnp.bfloat16)
         return carry
 
     lax.fori_loop(0, width // wide, branch_body, 0)
     chain.last(columns)
-    chain_branch = SumChain(in_order(upstream, rows), z_one, z_two, z_three, there, 22)
+    chain_branch = SumChain(in_order(normed, rows), z_one, z_two, z_three, there, 22)
     chain_branch.one()
     down_second = [
         there(to_y.at[:, low_half], down_last.at[0], 14, fsdp=plane[4]),
@@ -1200,7 +1201,7 @@
     )
     chain_branch.add_one()
     chain_branch.one_sent()
-    store_branch = here(upstream, branch, 39)
+    store_branch = here(normed, branch, 39)
     store_branch.start()
     chain.one_sent()
     chain.sent()
@@ -1624,6 +1625,7 @@
 def finish_kernel(
     layer, input_rows, grad_out, grad_qkv, grad_down, gu_rows,
     layer_out, input_grad, out_out, query_out, key_out, value_out, down_out, gate_out, up_out,
+    layer_v, input_v, out_v, qkv_v, down_v, gu_v, gate_v, up_v, load, store,
 ):
     s = lax.axis_index("seq")
     n_s = gu_rows.shape[0]
@@ -1632,16 +1634,32 @@
     unit_pad = grad_down.shape[0]
     unit = down_out.shape[0]
     units = gu_rows.shape[2] // 2
-    layer_out[...] = layer[...]
-    input_grad[...] = input_rows[...]
-    out_out[...] = grad_out[...]
-    query_out[...] = grad_qkv[:, :width]
-    key_out[...] = grad_qkv[:, width : width + kv_width]
-    value_out[...] = grad_qkv[:, width + kv_width :]
-    down_out[...] = grad_down[:unit]
+    moves = [
+        (layer, layer_v, [(layer_v, layer_out)]),
+        (input_rows, input_v, [(input_v, input_grad)]),
+        (grad_down, down_v, [(down_v.at[:unit], down_out)]),
+        (grad_out, out_v, [(out_v, out_out)]),
+        (grad_qkv, qkv_v, [
+            (qkv_v.at[:, :width], query_out),
+            (qkv_v.at[:, width : width + kv_width], key_out),
+            (qkv_v.at[:, width + kv_width :], value_out),
+        ]),
+    ]
+    load_gu = pltpu.make_async_copy(gu_rows, gu_v, load.at[0])
+    load_gu.start()
+    loads, stores = [], []
+    for i, (source, place, _) in enumerate(moves):
+        loads.append(pltpu.make_async_copy(source, place, load.at[1 + i]))
+        loads[-1].start()
+    for copy, (_, _, parts) in zip(loads, moves):
+        copy.wait()
+        for source, target in parts:
+            stores.append(pltpu.make_async_copy(source, target, store.at[len(stores)]))
+            stores[-1].start()
+    load_gu.wait()
     window = 512
     lanes = lax.broadcasted_iota(jnp.int32, (gu_rows.shape[1], 128), 1)
-    for base, out in ((0, gate_out), (units, up_out)):
+    for base, out, target_out in ((0, gate_v, gate_out), (units, up_v, up_out)):
         for f in range(units // unit_pad):
             for owner in range(n_s):
                 source = base + f * unit_pad
@@ -1649,7 +1667,7 @@
                 target = (f * n_s + owner) * unit
                 first = target // 128 * 128
                 slot = lax.rem(s + n_s - owner, n_s)
-                value = gu_rows[slot, :, begin : begin + window].astype(jnp.float32)
+                value = gu_v[slot, :, begin : begin + window].astype(jnp.float32)
                 turn = ((target - first) - (source - begin)) % window
                 if turn:
                     value = pltpu.roll(value, turn, 1)
@@ -1658,6 +1676,10 @@
                     if t < target:
                         part = jnp.where(lanes >= target - t, part, out[:, t : t + 128])
                     out[:, t : t + 128] = part
+        stores.append(pltpu.make_async_copy(out, target_out, store.at[len(stores)]))
+        stores[-1].start()
+    for copy in stores:
+        copy.wait()
 
 
 def finish(layer, input_rows, grad_out, grad_qkv, grad_down, gu_rows, unit, hidden_width):
@@ -1665,11 +1687,12 @@
     kv_width = KV_HEADS * HEAD_DIM
     low, full = jnp.bfloat16, jnp.float32
     shape = jax.ShapeDtypeStruct
-    vmem = pl.BlockSpec(memory_space=pltpu.VMEM)
+    hbm = pl.BlockSpec(memory_space=pl.ANY)
+    wide = pltpu.VMEM((piece, hidden_width), full)
     return pl.pallas_call(
         finish_kernel,
-        in_specs=[vmem] * 6,
-        out_specs=[vmem] * 9,
+        in_specs=[hbm] * 6,
+        out_specs=[hbm] * 9,
         out_shape=[
             shape(layer.shape, low),
             shape(layer.shape, low),
@@ -1681,6 +1704,10 @@
             shape((piece, hidden_width), full),
             shape((piece, hidden_width), full),
         ],
+        scratch_shapes=[
+            pltpu.VMEM(value.shape, value.dtype)
+            for value in (layer, input_rows, grad_out, grad_qkv, grad_down, gu_rows)
+        ] + [wide, wide, pltpu.SemaphoreType.DMA((6,)), pltpu.SemaphoreType.DMA((9,))],
         compiler_params=pltpu.CompilerParams(vmem_limit_bytes=63 * 2**20),
         name="finish",
     )(layer, input_rows, grad_out, grad_qkv, grad_down, gu_rows)

time: 404 us -> 399 us (0.988)
  Pallas kernels: 394 us -> 389 us
where the time goes in v12:
time: 399 us; the launch traced here: 394 us
  Pallas kernels  389 us (97%)
    pallas_call x1, Pallas kernels, front(): pl.pallas_call(front_kernel, in_specs=[smem, vmem, hbm, vmem, vmem, vmem]...  157 us
    pallas_call x1, Pallas kernels, back(): pl.pallas_call(back_kernel, in_specs=[hbm] + [vmem] * 15 + [hbm] * 4, out...  132 us
    pallas_call x1, Pallas kernels, ffn(): pl.pallas_call(ffn_kernel, in_specs=[hbm] * 7, out_specs=[vmem] * 2 + [hb...  94 us

profile of v12, /device:TPU:0, one launch (start us, length us, event | category | flops | bytes accessed | tf_op | source)
XLA Modules:
  0.0 394.1 jit_solution(14214755338565132980)
XLA Ops:
  0.6 0.7 broadcast_in_dim.20
  1.3 0.7 broadcast_in_dim.21
  2.0 0.7 broadcast_in_dim.22
  2.6 1.3 convert_add_fusion.small
  3.9 157.1 %front.1 = (bf16[1536,4608]{1,0:T(8,128)(2,1)}, bf16[2304,1536]{1,0:T(8,128)(2,1)}, bf16[1024,1536]{1,0:T(8,128)(2,1)}, bf16[1024,1536]{1,0:T(8,128)(2,1)}, bf16...) custom-call(s32[1,3]{1,0:T(1,128)} %lengths.1, ...), custom_call_target="tpu_custom_call" | custom-call | tf_op jit(solution)/shard_map/front/pallas_call | solution.py:870
  161.0 94.0 %ffn.1 = (f32[256,1536]{1,0:T(8,128)}, f32[288,1536]{1,0:T(8,128)}, bf16[4,192,4608]{2,1,0:T(8,128)(2,1)}, bf16[1024,1536]{1,0:T(8,128)(2,1)}, bf16[4,288,1536]{...) custom-call(bf16[1024,1536]{1,0:T(8,128)(2,1)} %get-tuple-element.55.normed_all, ...), custom_call_target="tpu_custom_call" | custom-call | tf_op jit(solution)/shard_map/ffn/pallas_call | solution.py:1223
  255.1 132.2 %back.1 = (bf16[256,1536]{1,0:T(8,128)(2,1)}, bf16[256,1536]{1,0:T(8,128)(2,1)}, f32[8,640]{1,0:T(8,128)}, f32[48,1536]{1,0:T(8,128)}, f32[48,2048]{1,0:T(8,128)}, /*index=5*/bf16[4,48,4608]{2,1,0:T(8,128)(2,1)}) custom-call(f32[256,1536]{1,0:T(8,128)} %get-tuple-element.62.columns, f32[256,1536]{1,0:T(8,128)} %get-tuple-element.63.resid, ...), custom_call_target="tpu_custom_call" | custom-call | tf_op jit(solution)/shard_map/back/pallas_call | solution.py:1561
  387.3 0.0 copy-start
  387.3 5.4 %finish.1 = (bf16[256,1536]{1,0:T(8,128)(2,1)}, bf16[256,1536]{1,0:T(8,128)(2,1)}, f32[48,1536]{1,0:T(8,128)}, f32[48,1536]{1,0:T(8,128)}, f32[48,256]{1,0:T(8,1...) custom-call(bf16[256,1536]{1,0:T(8,128)(2,1)} %get-tuple-element.80.layer, ...), custom_call_target="tpu_custom_call" | custom-call | tf_op jit(solution)/shard_map/finish/pallas_call | solution.py:1692
  392.7 0.0 copy-done
  392.7 0.6 fusion
  393.3 0.6 fusion.1
  (1 shorter events, 0.0 us)
Async XLA Ops:
  387.3 5.4 %copy-start = (f32[8,640]{1,0:T(8,128)S(1)}, f32[8,640]{1,0:T(8,128)}, u32[]{:S(2)}) copy-start(f32[8,640]{1,0:T(8,128)} %get-tuple-element.88) | copy-start | bytes 61444

commit v13 on v12

--- a/solution.py
+++ b/solution.py
@@ -261,7 +261,7 @@
     )
 
 
-ORDER = (1, 3, 2, 0)
+SEQ = 4
 
 
 class SumChain:
@@ -303,7 +303,7 @@
         pl.when(self.rank <= 1)(self.up[1].start)
         pl.when(self.rank >= 2)(self.down[1].start)
 
-    def three(self):
+    def add_two(self):
         @pl.when((self.rank == 1) | (self.rank == 2))
         def _():
             self.up[1].wait_recv()
@@ -311,6 +311,7 @@
             self.down[1].wait_recv()
             self.add(1, self.arrived[1].at[1])
 
+    def three(self):
         pl.when(self.rank <= 2)(self.up[2].start)
         pl.when(self.rank >= 1)(self.down[2].start)
 
@@ -331,9 +332,11 @@
         pl.when(self.rank == 0)(self.up[0].wait_send)
         pl.when(self.rank == 3)(self.down[0].wait_send)
 
-    def sent(self):
+    def two_sent(self):
         pl.when(self.rank <= 1)(self.up[1].wait_send)
         pl.when(self.rank >= 2)(self.down[1].wait_send)
+
+    def three_sent(self):
         pl.when(self.rank <= 2)(self.up[2].wait_send)
         pl.when(self.rank >= 1)(self.down[2].wait_send)
 
@@ -401,9 +404,17 @@
             copy.wait_send()
 
 
+def block_at(place):
+    far = 2 * (lax.axis_index("seq") // 2)
+    return (1 + far, 2, 3 - far, 0)[place]
+
+
 def in_order(partial, rows):
+    far = 2 * (lax.axis_index("seq") // 2)
+    places = {0: 3, 1: far, 2: 1, 3: 2 - far}
+
     def held(j):
-        return partial.at[ORDER.index(j) * rows : (ORDER.index(j) + 1) * rows]
+        return partial.at[pl.ds(pl.multiple_of(places[j] * rows, rows), rows)]
 
     return held
 
@@ -559,11 +570,8 @@
     load_up = here(w_up, up_v, 10)
     first_unit = pl.multiple_of(s * unit // 16 * 16, 16)
     load_down = here(w_down.at[pl.ds(first_unit, unit_pad)], down_raw, 15)
-    for copy in pieces:
+    for copy in pieces[:2]:
         copy.start()
-    load_gate.start()
-    load_up.start()
-    load_down.start()
 
     slot = (balance[...] & (group - 1)).astype(jnp.float32)
     second = lengths[0, 0].astype(jnp.float32)
@@ -600,6 +608,8 @@
     ]
     for copy in pieces[:2]:
         copy.wait()
+    for copy in pieces[2:]:
+        copy.start()
     pl.semaphore_wait(entry, n_f - 1 + n_s - 1)
     gather_kv.start()
     for copy in send_small + send_slots:
@@ -607,6 +617,9 @@
     for copy in pieces[2:]:
         copy.wait()
     chain_up.send(1)
+    load_gate.start()
+    load_up.start()
+    load_down.start()
     save_own = here(cotangent_v, own_rows(upstream_all, s, rows), 8)
     save_own.start()
     position = slots_all[s] - jnp.broadcast_to(first, (128, rows)).T
@@ -939,7 +952,7 @@
 ):
     f = lax.axis_index("fsdp")
     s = lax.axis_index("seq")
-    n_s = len(ORDER)
+    n_s = SEQ
     group, width = normed.shape
     rows = group // n_s
     half_rows = group // 2
@@ -973,13 +986,13 @@
     def part(ref, owner, size):
         return ref.at[pl.ds(pl.multiple_of(owner * size, 16), size)]
 
-    early, late = range(0, n_s // 2), range(n_s // 2, n_s)
+    early, late = (0,), (1, 2, 3)
 
     def rows_of(p):
         return pl.ds(p * rows, rows)
 
     def row_loads(p):
-        owner = lax.rem(s + n_s - ORDER[p], n_s)
+        owner = lax.rem(s + n_s - block_at(p), n_s)
         mine = rows_of(p)
         return [
             here(part(upstream_all, owner, rows), upstream.at[mine], 5 * p),
@@ -998,19 +1011,21 @@
         return here(w_gu.at[mine], gu.at[mine], 23 + n)
 
     loads = [row_loads(p) for p in range(n_s)]
-    order = [loads[0][0], loads[1][0], down_load(0)]
+    order = [loads[0][0], down_load(0)]
     order += [loads[p][i] for i in (1, 2) for p in early]
     order += [down_load(t) for t in range(1, units // wide)]
-    order += [gu_load(n) for n in range(width // 512)]
-    order += [loads[p][i] for i in (0, 1, 2) for p in late]
-    order += [loads[p][i] for i in (3, 4) for p in range(n_s)]
+    second = [gu_load(n) for n in range(width // 512)]
+    second += [loads[p][i] for i in (0, 1, 2) for p in late]
+    third = [loads[p][i] for i in (3, 4) for p in range(n_s)]
     for copy in order:
         copy.start()
 
-    def forward(blocks, wait):
+    def forward(blocks, wait, following):
         for p in blocks:
             for copy in loads[p][:3]:
                 copy.wait()
+        for copy in following:
+            copy.start()
         mine = pl.ds(blocks[0] * rows, len(blocks) * rows)
 
         def body(t, carry):
@@ -1048,12 +1063,14 @@
 
     chain = SumChain(in_order(partial, rows), z_one, z_two, z_three, there, 0)
     pieces = [(first, min(group, units - first)) for first in range(0, units, group)]
-    forward(early, True)
-    backward(early, True)
+    forward((0,), True, second)
+    backward((0,), True)
     pl.semaphore_wait(entry, 5)
     chain.one()
-    forward(late, False)
-    backward(late, False)
+    forward((1,), False, third)
+    backward((1,), False)
+    forward((2, 3), False, ())
+    backward((2, 3), False)
     chain.add_one()
     chain.two()
 
@@ -1135,6 +1152,7 @@
     ]
     for copy in down_first:
         copy.start()
+    chain.add_two()
     chain.three()
     lax.fori_loop(2, width // tile, gu_body, 0)
     gu_core = [
@@ -1204,7 +1222,8 @@
     store_branch = here(normed, branch, 39)
     store_branch.start()
     chain.one_sent()
-    chain.sent()
+    chain.two_sent()
+    chain.three_sent()
     for copy in down_core + down_first + down_second + gu_core:
         copy.wait_send()
     for copy in store + [store_branch]:
@@ -1214,7 +1233,7 @@
 def ffn(normed_all, upstream_all, w_gu, w_down, hidden, factor_gate, factor_up):
     group, width = normed_all.shape
     units = w_down.shape[0]
-    rows = group // len(ORDER)
+    rows = group // SEQ
     unit, block, half = units // 8, width // 8, width // 2
     low, full = jnp.bfloat16, jnp.float32
     vmem = pl.BlockSpec(memory_space=pltpu.VMEM)
@@ -1259,14 +1278,16 @@
 
 
 def back_kernel(
-    columns, resid, gain_two, cotangent, attended, queries, paired, slots, slot_row, first_row,
-    logsum, normed_one, tokens, gain_one, cosine, sine, w_out, w_qkv, gu_sum, branch,
+    gain_two, slot_row, first_row, logsum, gain_one, cosine, sine, slots,
+    resid_in, cotangent_in, attended_in, queries_in, paired_in, normed_in, tokens_in,
+    columns, w_out, w_qkv, gu_sum, branch,
     layer, input_rows, vector, grad_out, grad_qkv, gu_rows,
+    resid, cotangent, attended, queries, paired, normed_one, tokens,
     out_w, qkv, gu_own, gu_to_y, gu_to_x, gu_x, gu_y, gu_ended,
     branch_v, z_one, z_two, z_three, working, bias, d_branch, d_attended, d_qkv, d_resid,
     keys_grad, values_grad, dkv, dkv_in,
     out_arrived, out_x, out_y, out_ended, qkv_arrived, qkv_x, qkv_y, qkv_ended,
-    out_one, out_two, out_three, qkv_one, qkv_two, qkv_three, vector_in,
+    out_in, qkv_one, qkv_two, qkv_three, vector_in,
     load, ssem, rsem,
 ):
     f = lax.axis_index("fsdp")
@@ -1310,7 +1331,15 @@
     ]
     load_qkv = here(w_qkv, qkv, 5)
     load_columns = here(columns, working, 7)
-    for copy in [load_columns, load_branch, load_out] + load_gu + [load_qkv]:
+    load_rows = [
+        here(source, place, 10 + i)
+        for i, (source, place) in enumerate((
+            (resid_in, resid), (cotangent_in, cotangent), (attended_in, attended),
+            (queries_in, queries), (paired_in, paired), (normed_in, normed_one),
+            (tokens_in, tokens),
+        ))
+    ]
+    for copy in [load_columns] + load_rows[:2] + [load_branch]:
         copy.start()
 
     gu_first = [
@@ -1346,7 +1375,9 @@
     def own_part(ref):
         return lambda j: rows_for(ref, f * block, n_s - j)
 
-    chain_out = SumChain(own_part(out_w), out_one, out_two, out_three, there, 48)
+    out_send = [
+        there(own_part(out_w)(n_s - j), out_in.at[j], 47 + j, **around(j)) for j in range(1, n_s)
+    ]
     chain_qkv = SumChain(own_part(qkv), qkv_one, qkv_two, qkv_three, there, 54)
     vector_send = [
         there(vector_in.at[0], vector_in.at[1], 60, fsdp=plane[1]),
@@ -1368,6 +1399,10 @@
         return root * scaled - value * (root * root * root * inner), gain_grad
 
     load_columns.wait()
+    for copy in load_rows[:2]:
+        copy.wait()
+    for copy in [load_out] + load_rows[2:] + load_gu + [load_qkv]:
+        copy.start()
     d_norm, gain_two_grad = norm_back(resid[...], gain_two[...], working[...])
     d_total = cotangent[...].astype(full) + d_norm
     d_branch[...] = d_total.astype(low)
@@ -1378,6 +1413,8 @@
         ok = (keys_slot <= slot_row[0:1]) & (keys_slot >= first_row[0:1])
         bias[j * rows : (j + 1) * rows] = jnp.where(ok, 0.0, -1e30)
     load_out.wait()
+    for copy in load_rows[2:]:
+        copy.wait()
     for n in range(width // tile):
         value = lax.dot_general(
             d_branch[...], out_w[n * tile : (n + 1) * tile], (((1,), (1,)), ((), ())),
@@ -1455,7 +1492,6 @@
     gu_first[1].wait_recv()
     gu_to_x[...] = gu_to_x[...] + gu_y[1]
     gu_second[1].start()
-    sum_out.start_first()
 
     for g in range(KV_HEADS):
         for copy in dkv_send[g]:
@@ -1471,6 +1507,7 @@
     value = jnp.dot(normed_turned, d_qkv[:, width:], preferred_element_type=full)
     qkv[:, width:] = value.astype(low)
     sum_qkv.start_core()
+    chain.add_two()
     chain.three()
 
     d_norm, gain_one_grad = norm_back(tokens[...].astype(full), gain_one[...], working[...])
@@ -1485,6 +1522,7 @@
     vector_send[0].wait_recv()
     vector_in[2] = vector_in[0] + vector_in[1]
     vector_send[1].start()
+    sum_out.start_first()
 
     gu_first[2].wait_recv()
     gu_second[0].wait_recv()
@@ -1498,43 +1536,47 @@
         copy.start()
     keep_rows = here(rows_for(gu_own, 0, 0), gu_rows.at[0], 6)
     keep_rows.start()
-    sum_out.start_second()
     vector_send[1].wait_recv()
     vector_in[4] = vector_in[2] + vector_in[3]
     vector_send[2].start()
-
     sum_qkv.start_second()
-    sum_out.finish()
-    chain_out.one()
+    sum_out.start_second()
     vector_send[2].wait_recv()
     vector_in[6] = vector_in[4] + vector_in[5]
     for copy in vector_send[3:]:
         copy.start()
-    chain_out.add_one()
-    chain_out.two()
     sum_qkv.finish()
     chain_qkv.one()
-    chain_out.three()
     chain.last(working)
     layer[...] = (resid[...] + working[...]).astype(low)
     chain_qkv.add_one()
     chain_qkv.two()
+    sum_out.finish()
+    for copy in out_send:
+        copy.start()
     for copy in vector_send[3:]:
         copy.wait_recv()
     vector[...] = vector_in[6] + vector_in[7] + vector_in[8] + vector_in[9]
-    chain_out.last(grad_out)
+    chain_qkv.add_two()
     chain_qkv.three()
     chain_qkv.last(grad_qkv)
+    total = own_part(out_w)(0)[...].astype(full)
+    for copy in out_send:
+        copy.wait_recv()
+    for j in range(1, n_s):
+        total = total + out_in[j].astype(full)
+    grad_out[...] = total
     for copy in gu_send:
         copy.wait_recv()
     keep_rows.wait()
-    for part in (chain_out, chain_qkv):
-        part.one_sent()
-        part.sent()
-    chain.sent()
+    chain_qkv.one_sent()
+    chain_qkv.two_sent()
+    chain_qkv.three_sent()
+    chain.two_sent()
+    chain.three_sent()
     sum_out.sent()
     sum_qkv.sent()
-    for copy in gu_first + gu_second + gu_send + vector_send:
+    for copy in gu_first + gu_second + gu_send + out_send + vector_send:
         copy.wait_send()
     for g in range(KV_HEADS):
         for copy in dkv_send[g]:
@@ -1560,7 +1602,7 @@
     vectors = (2 * width + qkv_width) // 8
     return pl.pallas_call(
         back_kernel,
-        in_specs=[hbm] + [vmem] * 15 + [hbm] * 4,
+        in_specs=[vmem] * 8 + [hbm] * 12,
         out_specs=[vmem] * 5 + [hbm],
         out_shape=[
             shape((rows, width), low),
@@ -1571,6 +1613,13 @@
             shape((n_s, piece, 2 * units), low),
         ],
         scratch_shapes=[
+            pltpu.VMEM((rows, width), full),
+            pltpu.VMEM((rows, width), low),
+            pltpu.VMEM((rows, width), low),
+            pltpu.VMEM((rows, width), low),
+            pltpu.VMEM(paired.shape, low),
+            pltpu.VMEM((rows, width), low),
+            pltpu.VMEM((rows, width), low),
             pltpu.VMEM((width, width), low),
             pltpu.VMEM((width, qkv_width), low),
             pltpu.VMEM((block, 2 * units), low),
@@ -1601,14 +1650,12 @@
             pltpu.VMEM((2, block, qkv_width // 2), low),
             pltpu.VMEM((2, block, qkv_width // 2), low),
             pltpu.VMEM((2, block, qkv_width // 2), low),
-            pltpu.VMEM((piece, width), low),
-            pltpu.VMEM((2, piece, width), low),
-            pltpu.VMEM((2, piece, width), low),
+            pltpu.VMEM((n_s, piece, width), low),
             pltpu.VMEM((piece, qkv_width), low),
             pltpu.VMEM((2, piece, qkv_width), low),
             pltpu.VMEM((2, piece, qkv_width), low),
             pltpu.VMEM((10, 8, vectors), full),
-            pltpu.SemaphoreType.DMA((10,)),
+            pltpu.SemaphoreType.DMA((18,)),
             pltpu.SemaphoreType.DMA((68,)),
             pltpu.SemaphoreType.DMA((68,)),
         ],
@@ -1617,8 +1664,9 @@
         ),
         name="back",
     )(
-        columns, resid, gain_two, cotangent, attended, queries, paired, slots, slot_row, first_row,
-        logsum, normed_one, tokens, gain_one, cosine, sine, w_out, w_qkv, gu_sum, branch,
+        gain_two, slot_row, first_row, logsum, gain_one, cosine, sine, slots,
+        resid, cotangent, attended, queries, paired, normed_one, tokens,
+        columns, w_out, w_qkv, gu_sum, branch,
     )
 
 

time: 399 us -> 396 us (level)
  Pallas kernels: 389 us -> 385 us
where the time goes in v13:
time: 396 us; the launch traced here: 390 us
  Pallas kernels  385 us (97%)
    pallas_call x1, Pallas kernels, front(): pl.pallas_call(front_kernel, in_specs=[smem, vmem, hbm, vmem, vmem, vmem]...  157 us
    pallas_call x1, Pallas kernels, back(): pl.pallas_call(back_kernel, in_specs=[vmem] * 8 + [hbm] * 12, out_specs=[...  130 us
    pallas_call x1, Pallas kernels, ffn(): pl.pallas_call(ffn_kernel, in_specs=[hbm] * 7, out_specs=[vmem] * 2 + [hb...  92.6 us

profile of v13, /device:TPU:0, one launch (start us, length us, event | category | flops | bytes accessed | tf_op | source)
XLA Modules:
  0.0 390.5 jit_solution(6374173643147616836)
XLA Ops:
  0.6 0.7 broadcast_in_dim.20
  1.3 0.7 broadcast_in_dim.21
  2.0 0.7 broadcast_in_dim.22
  2.6 1.3 convert_add_fusion.small
  3.9 157.1 %front.1 = (bf16[1536,4608]{1,0:T(8,128)(2,1)}, bf16[2304,1536]{1,0:T(8,128)(2,1)}, bf16[1024,1536]{1,0:T(8,128)(2,1)}, bf16[1024,1536]{1,0:T(8,128)(2,1)}, bf16...) custom-call(s32[1,3]{1,0:T(1,128)} %lengths.1, ...), custom_call_target="tpu_custom_call" | custom-call | tf_op jit(solution)/shard_map/front/pallas_call | solution.py:883
  161.0 92.6 %ffn.1 = (f32[256,1536]{1,0:T(8,128)}, f32[288,1536]{1,0:T(8,128)}, bf16[4,192,4608]{2,1,0:T(8,128)(2,1)}, bf16[1024,1536]{1,0:T(8,128)(2,1)}, bf16[4,288,1536]{...) custom-call(bf16[1024,1536]{1,0:T(8,128)(2,1)} %get-tuple-element.68.normed_all, ...), custom_call_target="tpu_custom_call" | custom-call | tf_op jit(solution)/shard_map/ffn/pallas_call | solution.py:1242
  253.6 130.1 %back.1 = (bf16[256,1536]{1,0:T(8,128)(2,1)}, bf16[256,1536]{1,0:T(8,128)(2,1)}, f32[8,640]{1,0:T(8,128)}, f32[48,1536]{1,0:T(8,128)}, f32[48,2048]{1,0:T(8,128)}, /*index=5*/bf16[4,48,4608]{2,1,0:T(8,128)(2,1)}) custom-call(f32[1,1536]{1,0:T(1,128)} %get-tuple-element.55.gain_two, f32[8,256]{1,0:T(8,128)} %get-tuple-element.56.slot_row, ...), custom_call_target="tpu_custom_call" | custom-call | tf_op jit(solution)/shard_map/back/pallas_call | solution.py:1603
  383.7 0.0 copy-start
  383.7 5.4 %finish.1 = (bf16[256,1536]{1,0:T(8,128)(2,1)}, bf16[256,1536]{1,0:T(8,128)(2,1)}, f32[48,1536]{1,0:T(8,128)}, f32[48,1536]{1,0:T(8,128)}, f32[48,256]{1,0:T(8,1...) custom-call(bf16[256,1536]{1,0:T(8,128)(2,1)} %get-tuple-element.80.layer, ...), custom_call_target="tpu_custom_call" | custom-call | tf_op jit(solution)/shard_map/finish/pallas_call | solution.py:1740
  389.1 0.0 copy-done
  389.1 0.6 fusion
  389.7 0.6 fusion.1
  (1 shorter events, 0.0 us)
Async XLA Ops:
  383.7 5.4 %copy-start = (f32[8,640]{1,0:T(8,128)S(1)}, f32[8,640]{1,0:T(8,128)}, u32[]{:S(2)}) copy-start(f32[8,640]{1,0:T(8,128)} %get-tuple-element.88) | copy-start | bytes 61444

commit v14 on v13

--- a/solution.py
+++ b/solution.py
@@ -702,6 +702,7 @@
             queries[:, (2 * g + h) * HEAD_DIM : (2 * g + h + 1) * HEAD_DIM] = part
 
     gather_out.forward()
+    gather_gu.start()
     chain_up.receive(1)
     for copy in send_kv:
         copy.wait_recv()
@@ -739,7 +740,6 @@
         lax.fori_loop(0, repeat, head, 0)
         if g == 0:
             gather_out.last()
-            gather_gu.start()
 
     gather_out.finish()
     save_out = here(out_w, out_out, 13)
@@ -812,8 +812,8 @@
     chain_up.send(3)
     save_normed = here(normed, normed_all, 23)
     save_normed.start()
+    gather_down.forward()
     feed(s ^ 2, 2 * count)
-    gather_down.forward()
     feed(s ^ 3, 3 * count)
     gather_down.last()
     for t in (count - 2, count - 1):
@@ -1113,6 +1113,8 @@
         return carry
 
     lax.fori_loop(0, 2, gu_body, 0)
+    chain.add_two()
+    chain.three()
 
     class Arrivals:
         def __init__(self, ref, size, arrived, copies, turns, index):
@@ -1152,8 +1154,6 @@
     ]
     for copy in down_first:
         copy.start()
-    chain.add_two()
-    chain.three()
     lax.fori_loop(2, width // tile, gu_body, 0)
     gu_core = [
         there(part(gu, plane[2 * i + 1], block), gu_arrived.at[i], 16 + i, fsdp=plane[1])
@@ -1522,8 +1522,6 @@
     vector_send[0].wait_recv()
     vector_in[2] = vector_in[0] + vector_in[1]
     vector_send[1].start()
-    sum_out.start_first()
-
     gu_first[2].wait_recv()
     gu_second[0].wait_recv()
     total = gu_own[:, :units].astype(full) + gu_x[0].astype(full) + gu_ended[0].astype(full)
@@ -1536,6 +1534,8 @@
         copy.start()
     keep_rows = here(rows_for(gu_own, 0, 0), gu_rows.at[0], 6)
     keep_rows.start()
+    sum_out.start_first()
+
     vector_send[1].wait_recv()
     vector_in[4] = vector_in[2] + vector_in[3]
     vector_send[2].start()

time: 396 us -> 390 us (0.985)
  Pallas kernels: 385 us -> 378 us
    pallas_call x1, Pallas kernels: 157 us -> 153 us  [front(): pl.pallas_call(front_kernel, in_specs=[smem, vmem, hbm, vmem, vmem, vmem]...]
where the time goes in v14:
time: 390 us; the launch traced here: 384 us
  Pallas kernels  378 us (97%)
    pallas_call x1, Pallas kernels, front(): pl.pallas_call(front_kernel, in_specs=[smem, vmem, hbm, vmem, vmem, vmem]...  153 us
    pallas_call x1, Pallas kernels, back(): pl.pallas_call(back_kernel, in_specs=[vmem] * 8 + [hbm] * 12, out_specs=[...  128 us
    pallas_call x1, Pallas kernels, ffn(): pl.pallas_call(ffn_kernel, in_specs=[hbm] * 7, out_specs=[vmem] * 2 + [hb...  92 us

profile of v14, /device:TPU:0, one launch (start us, length us, event | category | flops | bytes accessed | tf_op | source)
XLA Modules:
  0.0 383.5 jit_solution(36690065435248834)
XLA Ops:
  0.6 0.7 broadcast_in_dim.20
  1.3 0.7 broadcast_in_dim.21
  2.0 0.7 broadcast_in_dim.22
  2.6 1.3 convert_add_fusion.small
  3.9 153.1 %front.1 = (bf16[1536,4608]{1,0:T(8,128)(2,1)}, bf16[2304,1536]{1,0:T(8,128)(2,1)}, bf16[1024,1536]{1,0:T(8,128)(2,1)}, bf16[1024,1536]{1,0:T(8,128)(2,1)}, bf16...) custom-call(s32[1,3]{1,0:T(1,128)} %lengths.1, ...), custom_call_target="tpu_custom_call" | custom-call | tf_op jit(solution)/shard_map/front/pallas_call | solution.py:883
  157.0 92.0 %ffn.1 = (f32[256,1536]{1,0:T(8,128)}, f32[288,1536]{1,0:T(8,128)}, bf16[4,192,4608]{2,1,0:T(8,128)(2,1)}, bf16[1024,1536]{1,0:T(8,128)(2,1)}, bf16[4,288,1536]{...) custom-call(bf16[1024,1536]{1,0:T(8,128)(2,1)} %get-tuple-element.68.normed_all, ...), custom_call_target="tpu_custom_call" | custom-call | tf_op jit(solution)/shard_map/ffn/pallas_call | solution.py:1242
  249.1 127.7 %back.1 = (bf16[256,1536]{1,0:T(8,128)(2,1)}, bf16[256,1536]{1,0:T(8,128)(2,1)}, f32[8,640]{1,0:T(8,128)}, f32[48,1536]{1,0:T(8,128)}, f32[48,2048]{1,0:T(8,128)}, /*index=5*/bf16[4,48,4608]{2,1,0:T(8,128)(2,1)}) custom-call(f32[1,1536]{1,0:T(1,128)} %get-tuple-element.55.gain_two, f32[8,256]{1,0:T(8,128)} %get-tuple-element.56.slot_row, ...), custom_call_target="tpu_custom_call" | custom-call | tf_op jit(solution)/shard_map/back/pallas_call | solution.py:1603
  376.7 0.0 copy-start
  376.8 5.4 %finish.1 = (bf16[256,1536]{1,0:T(8,128)(2,1)}, bf16[256,1536]{1,0:T(8,128)(2,1)}, f32[48,1536]{1,0:T(8,128)}, f32[48,1536]{1,0:T(8,128)}, f32[48,256]{1,0:T(8,1...) custom-call(bf16[256,1536]{1,0:T(8,128)(2,1)} %get-tuple-element.80.layer, ...), custom_call_target="tpu_custom_call" | custom-call | tf_op jit(solution)/shard_map/finish/pallas_call | solution.py:1740
  382.1 0.0 copy-done
  382.2 0.6 fusion
  382.8 0.6 fusion.1
  (1 shorter events, 0.0 us)
Async XLA Ops:
  376.7 5.4 %copy-start = (f32[8,640]{1,0:T(8,128)S(1)}, f32[8,640]{1,0:T(8,128)}, u32[]{:S(2)}) copy-start(f32[8,640]{1,0:T(8,128)} %get-tuple-element.88) | copy-start | bytes 61444

commit v15 on v14

--- a/solution.py
+++ b/solution.py
@@ -1287,7 +1287,7 @@
     branch_v, z_one, z_two, z_three, working, bias, d_branch, d_attended, d_qkv, d_resid,
     keys_grad, values_grad, dkv, dkv_in,
     out_arrived, out_x, out_y, out_ended, qkv_arrived, qkv_x, qkv_y, qkv_ended,
-    out_in, qkv_one, qkv_two, qkv_three, vector_in,
+    out_one, out_two, out_three, qkv_one, qkv_two, qkv_three, vector_in,
     load, ssem, rsem,
 ):
     f = lax.axis_index("fsdp")
@@ -1375,9 +1375,7 @@
     def own_part(ref):
         return lambda j: rows_for(ref, f * block, n_s - j)
 
-    out_send = [
-        there(own_part(out_w)(n_s - j), out_in.at[j], 47 + j, **around(j)) for j in range(1, n_s)
-    ]
+    chain_out = SumChain(own_part(out_w), out_one, out_two, out_three, there, 48)
     chain_qkv = SumChain(own_part(qkv), qkv_one, qkv_two, qkv_three, there, 54)
     vector_send = [
         there(vector_in.at[0], vector_in.at[1], 60, fsdp=plane[1]),
@@ -1552,31 +1550,30 @@
     chain_qkv.add_one()
     chain_qkv.two()
     sum_out.finish()
-    for copy in out_send:
-        copy.start()
+    chain_out.one()
     for copy in vector_send[3:]:
         copy.wait_recv()
     vector[...] = vector_in[6] + vector_in[7] + vector_in[8] + vector_in[9]
     chain_qkv.add_two()
     chain_qkv.three()
+    chain_out.add_one()
+    chain_out.two()
     chain_qkv.last(grad_qkv)
-    total = own_part(out_w)(0)[...].astype(full)
-    for copy in out_send:
-        copy.wait_recv()
-    for j in range(1, n_s):
-        total = total + out_in[j].astype(full)
-    grad_out[...] = total
+    chain_out.add_two()
+    chain_out.three()
+    chain_out.last(grad_out)
     for copy in gu_send:
         copy.wait_recv()
     keep_rows.wait()
-    chain_qkv.one_sent()
-    chain_qkv.two_sent()
-    chain_qkv.three_sent()
+    for part in (chain_qkv, chain_out):
+        part.one_sent()
+        part.two_sent()
+        part.three_sent()
     chain.two_sent()
     chain.three_sent()
     sum_out.sent()
     sum_qkv.sent()
-    for copy in gu_first + gu_second + gu_send + out_send + vector_send:
+    for copy in gu_first + gu_second + gu_send + vector_send:
         copy.wait_send()
     for g in range(KV_HEADS):
         for copy in dkv_send[g]:
@@ -1650,7 +1647,9 @@
             pltpu.VMEM((2, block, qkv_width // 2), low),
             pltpu.VMEM((2, block, qkv_width // 2), low),
             pltpu.VMEM((2, block, qkv_width // 2), low),
-            pltpu.VMEM((n_s, piece, width), low),
+            pltpu.VMEM((piece, width), low),
+            pltpu.VMEM((2, piece, width), low),
+            pltpu.VMEM((2, piece, width), low),
             pltpu.VMEM((piece, qkv_width), low),
             pltpu.VMEM((2, piece, qkv_width), low),
             pltpu.VMEM((2, piece, qkv_width), low),

time: 390 us -> 391 us (level)
  no operation moved by 1% of the time
where the time goes in v15:
time: 391 us; the launch traced here: 386 us
  Pallas kernels  380 us (97%)
    pallas_call x1, Pallas kernels, front(): pl.pallas_call(front_kernel, in_specs=[smem, vmem, hbm, vmem, vmem, vmem]...  153 us
    pallas_call x1, Pallas kernels, back(): pl.pallas_call(back_kernel, in_specs=[vmem] * 8 + [hbm] * 12, out_specs=[...  130 us
    pallas_call x1, Pallas kernels, ffn(): pl.pallas_call(ffn_kernel, in_specs=[hbm] * 7, out_specs=[vmem] * 2 + [hb...  92 us

profile of v15, /device:TPU:0, one launch (start us, length us, event | category | flops | bytes accessed | tf_op | source)
XLA Modules:
  0.0 385.7 jit_solution(5631547019665533481)
XLA Ops:
  0.6 0.7 broadcast_in_dim.20
  1.3 0.7 broadcast_in_dim.21
  2.0 0.7 broadcast_in_dim.22
  2.6 1.3 convert_add_fusion.small
  3.9 153.1 %front.1 = (bf16[1536,4608]{1,0:T(8,128)(2,1)}, bf16[2304,1536]{1,0:T(8,128)(2,1)}, bf16[1024,1536]{1,0:T(8,128)(2,1)}, bf16[1024,1536]{1,0:T(8,128)(2,1)}, bf16...) custom-call(s32[1,3]{1,0:T(1,128)} %lengths.1, ...), custom_call_target="tpu_custom_call" | custom-call | tf_op jit(solution)/shard_map/front/pallas_call | solution.py:883
  157.0 92.0 %ffn.1 = (f32[256,1536]{1,0:T(8,128)}, f32[288,1536]{1,0:T(8,128)}, bf16[4,192,4608]{2,1,0:T(8,128)(2,1)}, bf16[1024,1536]{1,0:T(8,128)(2,1)}, bf16[4,288,1536]{...) custom-call(bf16[1024,1536]{1,0:T(8,128)(2,1)} %get-tuple-element.68.normed_all, ...), custom_call_target="tpu_custom_call" | custom-call | tf_op jit(solution)/shard_map/ffn/pallas_call | solution.py:1242
  249.1 129.8 %back.1 = (bf16[256,1536]{1,0:T(8,128)(2,1)}, bf16[256,1536]{1,0:T(8,128)(2,1)}, f32[8,640]{1,0:T(8,128)}, f32[48,1536]{1,0:T(8,128)}, f32[48,2048]{1,0:T(8,128)}, /*index=5*/bf16[4,48,4608]{2,1,0:T(8,128)(2,1)}) custom-call(f32[1,1536]{1,0:T(1,128)} %get-tuple-element.55.gain_two, f32[8,256]{1,0:T(8,128)} %get-tuple-element.56.slot_row, ...), custom_call_target="tpu_custom_call" | custom-call | tf_op jit(solution)/shard_map/back/pallas_call | solution.py:1600
  378.9 0.0 copy-start
  378.9 5.4 %finish.1 = (bf16[256,1536]{1,0:T(8,128)(2,1)}, bf16[256,1536]{1,0:T(8,128)(2,1)}, f32[48,1536]{1,0:T(8,128)}, f32[48,1536]{1,0:T(8,128)}, f32[48,256]{1,0:T(8,1...) custom-call(bf16[256,1536]{1,0:T(8,128)(2,1)} %get-tuple-element.80.layer, ...), custom_call_target="tpu_custom_call" | custom-call | tf_op jit(solution)/shard_map/finish/pallas_call | solution.py:1739
  384.3 0.0 copy-done
  384.3 0.6 fusion
  384.9 0.6 fusion.1
  (1 shorter events, 0.0 us)
Async XLA Ops:
  378.9 5.4 %copy-start = (f32[8,640]{1,0:T(8,128)S(1)}, f32[8,640]{1,0:T(8,128)}, u32[]{:S(2)}) copy-start(f32[8,640]{1,0:T(8,128)} %get-tuple-element.88) | copy-start | bytes 61444
